TPU v7x, 128 devices: a whole 4x4x4 slice. The times are simulated.
128 devices in a mesh: genome: 32 (over z, y, core), indiv: 4 (over x).
Axes of the slice: x: 4, y: 4, z: 4, core: 2. Of those that a mesh axis runs over, the one named last changes fastest.
Arguments:
- indiv_factors: float32 [8192, 256], P('indiv'), may hold values from -1.5 to 1.5
- variant_factors: float32 [32768, 256], P('genome'), may hold values from -1.5 to 1.5
- dosage_tiles: bfloat16 [32, 4, 64, 128, 128], P('genome', 'indiv'), may hold values from -6 to 6
- block_rows: int32 [32, 4, 64], P('genome', 'indiv'), may hold values from 0 to 15, as said below
- block_cols: int32 [32, 4, 64], P('genome', 'indiv'), may hold values from 0 to 7, as said below
- live_blocks: int32 [32, 4], P('genome', 'indiv'), may hold values from 1 to 64, as said below
Outputs:
- variant_new: float32 [32768, 256], P('genome')
- indiv_new: float32 [8192, 256], P('indiv')
Inputs may be any that keep to these rules, and one draw needn't show every extreme that they name: `block_rows`: block row of each slot, counted in blocks of 128 individuals inside the slot's row group; the live slots of one slab and group name distinct (row, column) pairs. `block_cols`: block column of each slot, counted in blocks of 128 variants inside the slot's slab. Slots below live_blocks[g, i] are typed and the later ones are ignored; in every draw some slab and group has all 64 slots typed.
All inputs are finite; a program needn't handle non-finite values.
Results may differ from a plain program's by a relative error of at most 0.003.
The roundings to bfloat16 on the way count: a program that leaves them out, or rounds other values in their place, can miss the bound.
Values may be sent and summed in bfloat16 or wider, within the bound.
No kernel may reach another device: no remote copies, remote signals or barrier semaphores. Data moves between devices by JAX's collectives and lax.ppermute only.
A program may use at most 128 MiB of HBM per device.

v0:
```python
import math

import jax
import jax.numpy as jnp
from jax import lax
from jax.sharding import PartitionSpec as P

CG_STEPS = 2


smooth_weight = 32.0
ridge_weight = 1.0
highest = lax.Precision.HIGHEST


def extended_2(block, sides, width):
    for axis, dim in sides:
        count = lax.axis_size(axis)
        forward = [(i, i + 1) for i in range(count - 1)]
        backward = [(target, source) for source, target in forward]
        low = lax.ppermute(
            lax.slice_in_dim(block, block.shape[dim] - width, None, axis=dim), axis, forward
        )
        high = lax.ppermute(lax.slice_in_dim(block, 0, width, axis=dim), axis, backward)
        block = jnp.concatenate([low, block, high], axis=dim)
    return block


def block_pass(left_blocks, right_blocks, tiles, row_ids, col_ids, live_count, subtract, to_left):
    slot_count = row_ids.shape[0]
    group_size = math.gcd(slot_count, 16)
    rounds = (live_count + group_size - 1) // group_size
    offsets = jnp.arange(group_size, dtype=jnp.int32)
    target = left_blocks if to_left else right_blocks

    def advance(turn_index, running):
        first_slot = turn_index * group_size
        row_part = lax.dynamic_slice_in_dim(row_ids, first_slot, group_size, 0)
        col_part = lax.dynamic_slice_in_dim(col_ids, first_slot, group_size, 0)
        tile_part = lax.dynamic_slice_in_dim(tiles, first_slot, group_size, 0)
        left_part = left_blocks[row_part]
        right_part = right_blocks[col_part]
        product = jnp.einsum(
            "sir,sjr->sij", left_part, right_part, preferred_element_type=jnp.float32
        )
        if subtract:
            product = product - tile_part.astype(jnp.float32)
        keeping = first_slot + offsets < live_count
        masked = jnp.where(keeping[:, None, None], product, 0.0)
        if to_left:
            contrib = jnp.einsum(
                "sij,sjr->sir", masked, right_part.astype(jnp.float32), precision=highest
            )
            return running.at[row_part].add(contrib)
        contrib = jnp.einsum(
            "sij,sir->sjr", masked, left_part.astype(jnp.float32), precision=highest
        )
        return running.at[col_part].add(contrib)

    running = lax.fori_loop(0, rounds, advance, jnp.zeros(target.shape, jnp.float32))
    return running.reshape(-1, target.shape[2])


def conjugate(start, operator, summed_over):
    resid = -operator(start, True)
    direction = resid
    solution = start
    norm_now = summed_over(jnp.sum(resid * resid))
    for turn_index in range(CG_STEPS):
        applied = operator(direction, False)
        step_size = norm_now / summed_over(jnp.sum(direction * applied))
        solution = solution + step_size * direction
        resid = resid - step_size * applied
        if turn_index + 1 < CG_STEPS:
            norm_next = summed_over(jnp.sum(resid * resid))
            direction = resid + norm_next / norm_now * direction
            norm_now = norm_next
    return solution


def on_device(indiv_factors, variant_factors, dosage_tiles, block_rows, block_cols, live_blocks):
    tiles = dosage_tiles[0, 0]
    row_ids = block_rows[0, 0]
    col_ids = block_cols[0, 0]
    live_count = live_blocks[0, 0]
    block_size = tiles.shape[1]
    factor_rank = indiv_factors.shape[1]

    def blocked(values):
        return values.astype(jnp.bfloat16).reshape(-1, block_size, factor_rank)

    indiv_blocks = blocked(indiv_factors)

    def banded(values):
        extended = extended_2(values, (("genome", 0),), 1)
        return 2.0 * values - extended[:-2] - extended[2:]

    def variant_data(direction, subtract):
        partial_term = block_pass(
            indiv_blocks, blocked(direction), tiles, row_ids, col_ids, live_count, subtract, False
        )
        return lax.psum(partial_term, "indiv")

    def variant_apply(direction, subtract):
        return (
            variant_data(direction, subtract)
            + smooth_weight * banded(direction)
            + ridge_weight * direction
        )

    def variant_total(value):
        return lax.psum(value, "genome")

    variant_new = conjugate(variant_factors, variant_apply, variant_total)
    variant_blocks = blocked(variant_new)

    def indiv_total(value):
        return lax.psum(value, "indiv")

    def indiv_apply(direction, subtract):
        partial_term = block_pass(
            blocked(direction), variant_blocks, tiles, row_ids, col_ids, live_count, subtract, True
        )
        summed = lax.psum(partial_term, "genome")
        return summed + ridge_weight * direction

    indiv_new = conjugate(indiv_factors, indiv_apply, indiv_total)
    return (variant_new, indiv_new)


def solution(mesh):
    return jax.shard_map(
        on_device,
        mesh=mesh,
        in_specs=(
            P("indiv", None),
            P("genome", None),
            P("genome", "indiv", None, None, None),
            P("genome", "indiv", None),
            P("genome", "indiv", None),
            P("genome", "indiv"),
        ),
        out_specs=(P("genome", None), P("indiv", None)),
        check_vma=False,
    )
```

profile of v0, /device:TPU:0, one launch (start us, length us, event | category | flops | bytes accessed | tf_op | source)
XLA Modules:
  0.0 1030.4 jit_solution(11684756296934902843)
XLA Ops:
  7.9 2.1 convert_element_type.35
  11.8 27.5 %while.66 = (s32[]{:T(128)}, f32[8,128,256]{2,1,0:T(8,128)S(1)}, s32[]{:T(128)}, s32[64]{0:T(128)S(1)}, s32[]{:T(128)}, /*index=5*/s32[64]{0:T(128)S(1)}, bf16[1...) while((s32[]{:T(128)}, f32[8,128,256]{2,1,0:T(8,128)S(1)}, ...), condition=%wide.region_2.3_spmd.clone, body=%wide.region_0.2_spmd.clone.sunk | while | flops 940836992 | bytes 20456220 | solution.py:60
  15.3 2.6 gather_fusion.1
  19.7 2.3 fusion.117
  22.0 3.5 scatter_fusion
  29.0 2.6 gather_fusion.1
  33.4 2.3 fusion.117
  35.8 3.5 scatter_fusion
  43.6 3.6 collective-permute-done.1
  47.2 68.8 %all-reduce.9.cloned.1.call-done = f32[1024,256]{1,0:T(8,128)} async-done(((f32[1024,256]{1,0:T(8,128)}), f32[1024,256]{1,0:T(8,128)}) %all-reduce.9.cloned.1.call-update) | async-done | bytes 1048592 | tf_op jit(solution)/shard_map/psum | solution.py:102
  116.0 3.9 negate_convert_fusion.1
  120.0 23.0 %while.67 = (s32[]{:T(128)}, f32[8,128,256]{2,1,0:T(8,128)S(1)}, s32[]{:T(128)}, s32[64]{0:T(128)S(1)}, s32[]{:T(128)}, /*index=5*/s32[64]{0:T(128)S(1)}, bf16[1...) while((s32[]{:T(128)}, f32[8,128,256]{2,1,0:T(8,128)S(1)}, ...), condition=%wide.region_8.9_spmd.clone, body=%wide.region_6.8_spmd.clone.sunk | while | flops 940312704 | bytes 17834768 | solution.py:60
  121.4 2.6 gather_fusion.3
  125.7 2.3 fusion.123
  128.0 3.5 scatter_fusion.1
  132.9 2.6 gather_fusion.3
  137.2 2.3 fusion.123
  139.5 3.5 scatter_fusion.1
  144.1 2.2 multiply_reduce_fusion.5
  148.9 3.4 collective-permute-done.3
  152.3 61.3 %all-reduce.11.cloned.1.call-done = f32[1024,256]{1,0:T(8,128)} async-done(((f32[1024,256]{1,0:T(8,128)}), f32[1024,256]{1,0:T(8,128)}) %all-reduce.11.cloned.1.call-update) | async-done | bytes 1048592 | tf_op jit(solution)/shard_map/psum | solution.py:102
  213.6 2.3 multiply_reduce_fusion.4
  215.9 66.5 %all-reduce = (f32[]{:T(128)}, f32[]{:T(128)}) all-reduce(f32[]{:T(128)} %get-tuple-element.563, f32[]{:T(128)} %multiply_reduce_fusion.4), channel_id=1, replica_groups=mesh['genome'=32,'indiv'=4] {'genome'}, use_global_device_ids=true, to_apply=%region_5.6 | all-reduce | flops 2 | bytes 16 | tf_op jit(solution)/shard_map/psum | solution.py:112
  284.9 63.3 %psum.102 = f32[]{:T(128)} all-reduce(f32[]{:T(128)} %multiply_reduce_fusion.3), channel_id=1, replica_groups=mesh['genome'=32,'indiv'=4] {'genome'}, use_global_device_ids=true, to_apply=%region_13.14 | all-reduce | flops 1 | bytes 8 | tf_op jit(solution)/shard_map/psum | solution.py:112
  351.2 23.2 %while.68 = (s32[]{:T(128)}, f32[8,128,256]{2,1,0:T(8,128)S(1)}, s32[]{:T(128)}, s32[64]{0:T(128)S(1)}, s32[]{:T(128)}, /*index=5*/s32[64]{0:T(128)S(1)}, bf16[1...) while((s32[]{:T(128)}, f32[8,128,256]{2,1,0:T(8,128)S(1)}, ...), condition=%wide.region_16.17_spmd.clone, body=%wide.region_14.16_spmd.clone.sunk | while | flops 940312704 | bytes 17834768 | solution.py:60
  352.8 2.6 gather_fusion.5
  357.1 2.3 fusion.129
  359.4 3.5 scatter_fusion.2
  364.3 2.6 gather_fusion.5
  368.6 2.3 fusion.129
  370.9 3.5 scatter_fusion.2
  380.6 58.2 %all-reduce.13.cloned.1.call-done = f32[1024,256]{1,0:T(8,128)} async-done(((f32[1024,256]{1,0:T(8,128)}), f32[1024,256]{1,0:T(8,128)}) %all-reduce.13.cloned.1.call-update) | async-done | bytes 1048592 | tf_op jit(solution)/shard_map/psum | solution.py:102
  438.8 3.4 fusion.21
  442.2 66.5 %psum.104 = f32[]{:T(128)} all-reduce(f32[]{:T(128)} %fusion.21), channel_id=1, replica_groups=mesh['genome'=32,'indiv'=4] {'genome'}, use_global_device_ids=true, to_apply=%region_19.20 | all-reduce | flops 1 | bytes 8 | tf_op jit(solution)/shard_map/psum | solution.py:112
  510.0 2.7 fusion.37
  514.2 24.0 %while.69 = (s32[]{:T(128)}, f32[16,128,256]{2,1,0:T(8,128)}, s32[]{:T(128)}, s32[64]{0:T(128)S(1)}, s32[]{:T(128)}, /*index=5*/bf16[16,128,256]{2,1,0:T(8,128)(...) while((s32[]{:T(128)}, f32[16,128,256]{2,1,0:T(8,128)}, ...), condition=%wide.region_22.23_spmd.clone, body=%wide.region_20.22_spmd.clone.sunk | while | flops 940836992 | bytes 18359068 | solution.py:60
  519.0 2.3 fusion.136
  521.3 4.9 scatter_fusion.3
  531.0 2.3 fusion.136
  533.3 4.9 scatter_fusion.3
  538.3 126.1 %all-reduce.15.cloned.1.call-done = f32[2048,256]{1,0:T(8,128)} async-done(((f32[2048,256]{1,0:T(8,128)}), f32[2048,256]{1,0:T(8,128)}) %all-reduce.15.cloned.1.call-update) | async-done | bytes 2097168 | tf_op jit(solution)/shard_map/psum | solution.py:124
  664.4 4.2 negate_convert_fusion
  670.1 21.9 %while.70 = (s32[]{:T(128)}, f32[16,128,256]{2,1,0:T(8,128)}, s32[]{:T(128)}, s32[64]{0:T(128)S(1)}, s32[]{:T(128)}, /*index=5*/bf16[16,128,256]{2,1,0:T(8,128)(...) while((s32[]{:T(128)}, f32[16,128,256]{2,1,0:T(8,128)}, ...), condition=%wide.region_28.29_spmd.clone, body=%wide.region_26.28_spmd.clone.sunk | while | flops 940312704 | bytes 17834768 | solution.py:60
  671.5 1.8 gather_fusion.8
  673.8 2.3 fusion.142
  676.1 4.9 scatter_fusion.4
  682.4 1.8 gather_fusion.8
  684.7 2.3 fusion.142
  687.0 5.0 scatter_fusion.4
  692.1 128.5 %all-reduce.17.cloned.1.call-done = f32[2048,256]{1,0:T(8,128)} async-done(((f32[2048,256]{1,0:T(8,128)}), f32[2048,256]{1,0:T(8,128)}) %all-reduce.17.cloned.1.call-update) | async-done | bytes 2097168 | tf_op jit(solution)/shard_map/psum | solution.py:124
  820.6 3.4 multiply_reduce_fusion.1
  824.0 11.0 %all-reduce.1 = (f32[]{:T(128)}, f32[]{:T(128)}) all-reduce(f32[]{:T(128)} %get-tuple-element.434, f32[]{:T(128)} %get-tuple-element.433), channel_id=1, replica_groups=mesh['genome'=32,'indiv'=4] {'indiv'}, use_global_device_ids=true, to_apply=%region_25.26 | all-reduce | flops 2 | bytes 16 | tf_op jit(solution)/shard_map/psum | solution.py:118
  836.2 3.4 multiply_reduce_fusion
  839.6 8.6 psum.109
  849.5 3.7 fusion.36
  854.7 21.9 %while.71 = (s32[]{:T(128)}, f32[16,128,256]{2,1,0:T(8,128)}, s32[]{:T(128)}, s32[64]{0:T(128)S(1)}, s32[]{:T(128)}, /*index=5*/bf16[16,128,256]{2,1,0:T(8,128)(...) while((s32[]{:T(128)}, f32[16,128,256]{2,1,0:T(8,128)}, ...), condition=%wide.region_36.37_spmd.clone, body=%wide.region_34.36_spmd.clone.sunk | while | flops 940312704 | bytes 17834768 | solution.py:60
  858.4 2.3 fusion.148
  860.7 4.9 scatter_fusion.5
  869.2 2.3 fusion.148
  871.5 5.0 scatter_fusion.5
  876.6 127.0 %all-reduce.19.cloned.1.call-done = f32[2048,256]{1,0:T(8,128)} async-done(((f32[2048,256]{1,0:T(8,128)}), f32[2048,256]{1,0:T(8,128)}) %all-reduce.19.cloned.1.call-update) | async-done | bytes 2097168 | tf_op jit(solution)/shard_map/psum | solution.py:124
  1003.6 3.4 fusion.20
  1007.0 11.0 %psum.111 = f32[]{:T(128)} all-reduce(f32[]{:T(128)} %fusion.20), channel_id=1, replica_groups=mesh['genome'=32,'indiv'=4] {'indiv'}, use_global_device_ids=true, to_apply=%region_39.40 | all-reduce | flops 1 | bytes 8 | tf_op jit(solution)/shard_map/psum | solution.py:118
  1019.3 4.2 multiply_add_fusion
  (130 shorter events, 66.4 us)
Async XLA Ops:
  7.2 108.9 %all-reduce.9.cloned.1.call-start = ((), (), s32[]{:S(2)}) async-start(), calls=%async_computation | async-start | bytes 2097152 | tf_op jit(solution)/shard_map/psum | solution.py:102
  9.9 1.8 copy-start.6
  9.9 1.8 copy-start.7
  39.3 1.0 copy-start
  40.3 173.3 %all-reduce.11.cloned.1.call-start = ((), (), s32[]{:S(2)}) async-start(), calls=%async_computation.1 | async-start | bytes 2097152 | tf_op jit(solution)/shard_map/psum | solution.py:102
  41.0 2.6 collective-permute-start
  42.3 4.9 collective-permute-start.1
  143.0 1.0 copy-start.1
  144.0 294.7 %all-reduce.13.cloned.1.call-start = ((), (), s32[]{:S(2)}) async-start(), calls=%async_computation.2 | async-start | bytes 2097152 | tf_op jit(solution)/shard_map/psum | solution.py:102
  146.3 2.6 collective-permute-start.2
  147.6 4.8 collective-permute-start.3
  213.6 70.2 %copy-start.5 = (f32[1024,256]{1,0:T(8,128)S(1)}, f32[1024,256]{1,0:T(8,128)}, u32[]{:S(2)}) copy-start(f32[1024,256]{1,0:T(8,128)} %all-reduce.11.cloned.1.call-done) | copy-start | bytes 3145732
  374.4 1.0 copy-start.2
  375.4 134.5 %copy-start.4 = (f32[1024,256]{1,0:T(8,128)S(1)}, f32[1024,256]{1,0:T(8,128)}, u32[]{:S(2)}) copy-start(f32[1024,256]{1,0:T(8,128)} %param.19) | copy-start | bytes 3145732
  375.4 289.0 %all-reduce.15.cloned.1.call-start = ((), (), s32[]{:S(2)}) async-start(), calls=%async_computation.3 | async-start | bytes 4194304 | tf_op jit(solution)/shard_map/psum | solution.py:124
  376.3 2.6 collective-permute-start.4
  377.6 3.0 collective-permute-start.5
  538.2 282.4 %all-reduce.17.cloned.1.call-start = ((), (), s32[]{:S(2)}) async-start(), calls=%async_computation.4 | async-start | bytes 4194304 | tf_op jit(solution)/shard_map/psum | solution.py:124
  692.1 311.5 %all-reduce.19.cloned.1.call-start = ((), (), s32[]{:S(2)}) async-start(), calls=%async_computation.5 | async-start | bytes 4194304 | tf_op jit(solution)/shard_map/psum | solution.py:124
  876.6 127.0 %copy-start.3 = (f32[2048,256]{1,0:T(8,128)S(1)}, f32[2048,256]{1,0:T(8,128)}, u32[]{:S(2)}) copy-start(f32[2048,256]{1,0:T(8,128)} %get-tuple-element.540) | copy-start | bytes 6291460
Sparse Core Ops, SparseCore 0:
  40.4 75.6 all-reduce.8
  144.2 69.3 all-reduce.10
  375.5 63.1 all-reduce.12
  538.3 126.0 all-reduce.14
  692.2 128.3 all-reduce.16
  876.7 126.8 all-reduce.18
where the time goes:
time: 1030 us
  waiting for transfers between devices  579 us (56%)
  blocking collectives  227 us (22%)
  other arithmetic  103 us (10%)
  local copies, waits for them, and re-layouts  47.1 us (5%)
  matrix products  43.4 us (4%)
  between operations  22.7 us (2%)
    psum x3, waiting for transfers between devices, indiv_apply(): summed = lax.psum(partial_term, 'genome')  382 us
    psum x3, blocking collectives, variant_total(): return lax.psum(value, 'genome')  196 us
    psum x3, waiting for transfers between devices, variant_data(): return lax.psum(partial_term, 'indiv')  188 us
    psum x3, blocking collectives, indiv_total(): return lax.psum(value, 'indiv')  30.7 us
    scatter-add x6, other arithmetic, advance(): return running.at[row_part].add(contrib)  29.5 us
    scatter-add x6, other arithmetic, advance(): return running.at[col_part].add(contrib)  21 us
  transfers between devices with their start and end apart: 12, of which 9 were waited for; matrix products, arithmetic and copies ran while one was open for 0% of the time, Pallas kernels for 0%

commit v1 on v0

v1 whole, which is shorter than its diff:
```python
import jax
import jax.numpy as jnp
import numpy as np
from jax import lax
from jax.experimental import pallas as pl
from jax.experimental.pallas import tpu as pltpu
from jax.sharding import Mesh
from jax.sharding import PartitionSpec as P

BS = 128
R = 256
ROWS = 16
COLS = 8
smooth_weight = 32.0
ridge_weight = 1.0
f32, bf16, f16 = jnp.float32, jnp.bfloat16, jnp.float16
ALL = ("z", "y", "c", "x")
GEN = ("z", "y", "c")
CHIP = ("z", "y")
PAY_V = 2 * BS + 2 * BS + 16
PAY_I = BS + 8
VMEM_LIMIT = 48 * 1024 * 1024


def params():
    return pltpu.CompilerParams(vmem_limit_bytes=VMEM_LIMIT)


def smem():
    return pl.BlockSpec(memory_space=pltpu.SMEM)


def vmem():
    return pl.BlockSpec(memory_space=pltpu.VMEM)


def row_col():
    rows = lax.broadcasted_iota(jnp.int32, (BS, BS), 0)
    cols = lax.broadcasted_iota(jnp.int32, (BS, BS), 1)
    return rows, cols


def pack(gram):
    rows, cols = row_col()
    upper = gram[:BS, :BS]
    lower = gram[BS:, BS:]
    mixed = jnp.where(rows <= cols, upper, lower)
    diag = jnp.sum(jnp.where(rows == cols, lower, 0.0), axis=0, keepdims=True)
    return mixed, gram[:BS, BS:], diag


def unpack(mixed, cross, diag):
    rows, cols = row_col()
    turned = mixed.T
    upper = jnp.where(rows <= cols, mixed, turned)
    lower = jnp.where(rows > cols, mixed, jnp.where(rows < cols, turned, diag))
    top = jnp.concatenate([upper, cross], axis=1)
    bottom = jnp.concatenate([cross.T, lower], axis=1)
    return jnp.concatenate([top, bottom], axis=0)


def split(matrix):
    high = matrix.astype(bf16)
    return high, (matrix - high.astype(f32)).astype(bf16)


def times(values, high, low):
    rounded = values.astype(bf16)
    return jnp.dot(rounded, high, preferred_element_type=f32) + jnp.dot(
        rounded, low, preferred_element_type=f32
    )


def set_mask(row_ids, col_ids, live, mask):
    def clear(k, carry):
        mask[k] = 0.0
        return carry

    lax.fori_loop(0, ROWS * COLS, clear, 0)

    def mark(s, carry):
        mask[row_ids[s] * COLS + col_ids[s]] = 1.0
        return carry

    lax.fori_loop(0, live, mark, 0)


def variant_sums(row_ids, col_ids, meta, tiles, factors, pay, turned, rounded, grams, diags, mask):
    live, me, odd = meta[0], meta[1], meta[2]
    set_mask(row_ids, col_ids, live, mask)

    def place(part):
        owner = jnp.where(odd == 1, 3 - part, part)
        return lax.rem(owner - me + 4, 4)

    pay[...] = jnp.zeros_like(pay)
    for r in range(ROWS):
        block = factors[r * BS : (r + 1) * BS, :]
        rounded[r] = block.astype(bf16)
        turned[r] = block.T.astype(bf16)
    for r in range(ROWS):
        gram = jnp.dot(turned[r], rounded[r], preferred_element_type=f32)
        mixed, cross, diag = pack(gram)
        grams[r, :, :BS] = mixed
        grams[r, :, BS:] = cross
        diags[r : r + 1, :] = diag

    def slots(step, carry):
        for k in range(4):
            s = step * 4 + k
            r, c = row_ids[s], col_ids[s]
            weight = jnp.where(s < live, 1.0, 0.0)
            product = weight * jnp.dot(turned[r], tiles[s], preferred_element_type=f32)
            at = place(c // 2)
            rows = pl.ds(pl.multiple_of(2 * BS + lax.rem(c, 2) * BS, BS), BS)
            pay[at, rows, :BS] += product[:BS]
            pay[at, rows, BS:] += product[BS:]
        return carry

    lax.fori_loop(0, (live + 3) // 4, slots, 0)

    for c in range(COLS):
        at = place(c // 2)
        weights = [mask[r * COLS + c] for r in range(ROWS)]
        base = (c % 2) * BS
        for half in range(4):
            rows = slice(half * 32, (half + 1) * 32)
            total = weights[0] * grams[0, rows, :]
            for r in range(1, ROWS):
                total += weights[r] * grams[r, rows, :]
            pay[at, base + half * 32 : base + (half + 1) * 32, :] = total
        total = weights[0] * diags[0:1, :]
        for r in range(1, ROWS):
            total += weights[r] * diags[r : r + 1, :]
        pay[at, 4 * BS + c % 2 : 4 * BS + c % 2 + 1, :BS] = total


def band_of(values, before, after, ext):
    n = values.shape[0]
    ext[7:8, :] = before
    ext[8 : 8 + n, :] = values
    ext[8 + n : 9 + n, :] = after
    return 2.0 * values - ext[7 : 7 + n, :] - ext[9 : 9 + n, :]


def variant_start(meta, total, start, low, high, resid, applied, g_high, g_low, edge, ext):
    part = meta[0]
    n = 2 * BS
    first = pl.multiple_of(part * n, n)
    mine = start[pl.ds(first, n), :]
    before8 = start[pl.ds(pl.multiple_of(jnp.maximum(first - 8, 0), 8), 8), :]
    after8 = start[pl.ds(pl.multiple_of(jnp.minimum(first + n, 3 * n + n - 8), 8), 8), :]
    before = jnp.where(part == 0, low[7:8, :], before8[7:8, :])
    after = jnp.where(part == 3, high[0:1, :], after8[0:1, :])
    banded = band_of(mine, before, after, ext)
    for k in range(2):
        gram = unpack(
            total[k * BS : (k + 1) * BS, :BS],
            total[k * BS : (k + 1) * BS, BS:],
            total[4 * BS + k : 4 * BS + k + 1, :BS],
        )
        up, down = split(gram)
        g_high[k] = up
        g_low[k] = down
        rows = slice(k * BS, (k + 1) * BS)
        data = total[(2 + k) * BS : (3 + k) * BS, :]
        data = jnp.concatenate([data[:, :BS].T, data[:, BS:].T], axis=1)
        resid[rows, :] = (
            data
            - times(mine[rows], up, down)
            - ridge_weight * mine[rows]
            - smooth_weight * banded[rows]
        )
    value = resid[...]
    zero = jnp.zeros((1, R), f32)
    banded = band_of(value, zero, zero, ext)
    for k in range(2):
        rows = slice(k * BS, (k + 1) * BS)
        applied[rows, :] = (
            times(value[rows], g_high[k], g_low[k])
            + ridge_weight * value[rows]
            + smooth_weight * banded[rows]
        )
    edge[...] = jnp.zeros_like(edge)
    edge[0:1, :] = resid[0:1, :]
    edge[1:2, :] = applied[0:1, :]
    edge[2:3, :] = resid[n - 1 : n, :]
    edge[3:4, :] = applied[n - 1 : n, :]


def as_row(values):
    lanes = lax.broadcasted_iota(jnp.int32, (8, BS), 1)
    row = jnp.zeros((8, BS), f32)
    for k, value in enumerate(values):
        row = jnp.where(lanes == k, value, row)
    return row


def total_of(values):
    return jnp.sum(jnp.sum(values, axis=0, keepdims=True), axis=1, keepdims=True)


def largest(values):
    return jnp.max(jnp.max(jnp.abs(values), axis=0, keepdims=True), axis=1, keepdims=True)


def variant_moments(meta, resid, applied, g_high, g_low, edge_before, edge_after, again, moments, ext):
    has_before, has_after = meta[1], meta[2]
    n = 2 * BS
    value = resid[...]
    again[...] = applied[...]
    again[0:1, :] = again[0:1, :] - smooth_weight * edge_before[2:3, :]
    again[n - 1 : n, :] = again[n - 1 : n, :] - smooth_weight * edge_after[0:1, :]
    first = again[...]
    zero = jnp.zeros((1, R), f32)
    before = jnp.where(has_before == 1, edge_before[3:4, :] - smooth_weight * value[0:1, :], zero)
    after = jnp.where(has_after == 1, edge_after[1:2, :] - smooth_weight * value[n - 1 : n, :], zero)
    banded = band_of(first, before, after, ext)
    data = jnp.concatenate(
        [times(first[k * BS : (k + 1) * BS], g_high[k], g_low[k]) for k in range(2)], axis=0
    )
    second = data + ridge_weight * first + smooth_weight * banded
    moments[...] = as_row(
        [
            total_of(value * value),
            total_of(value * first),
            total_of(first * first),
            total_of(first * second),
            largest(value),
            largest(first),
        ]
    )


def coefficients(table):
    sums = jnp.sum(table, axis=0, keepdims=True)
    peaks = jnp.max(table, axis=0, keepdims=True)
    rr, ra, aa, aaa = (sums[:, k : k + 1] for k in range(4))
    first = rr / ra
    rr_next = rr - 2.0 * first * ra + first * first * aa
    ratio = rr_next / rr
    curve = (
        (1.0 + ratio) * (1.0 + ratio) * ra
        - 2.0 * (1.0 + ratio) * first * aa
        + first * first * aaa
    )
    second = rr_next / curve
    on_resid = first + second * (1.0 + ratio)
    on_applied = second * first
    bound = jnp.abs(on_resid) * peaks[:, 4:5] + jnp.abs(on_applied) * peaks[:, 5:6]
    return on_resid, on_applied, bound


def indiv_sums(
    row_ids, col_ids, meta, table, start, tiles,
    resid0, resid1, resid2, resid3, again0, again1, again2, again3,
    new, pay, scales, turned, rounded, grams, diags, mask,
):
    live, me, odd, core = meta[0], meta[1], meta[2], meta[3]
    set_mask(row_ids, col_ids, live, mask)
    on_resid, on_applied, bound = coefficients(table[...])
    n = 2 * BS
    resids, agains = (resid0, resid1, resid2, resid3), (again0, again1, again2, again3)
    for k in range(4):
        owner = lax.rem(me - k + 4, 4)
        part = jnp.where(odd == 1, 3 - owner, owner)
        rows = pl.ds(pl.multiple_of(part * n, n), n)
        new[rows, :] = start[rows, :] + on_resid * resids[k][...] - on_applied * agains[k][...]
    top = bound + 1.5
    scale_e = 30000.0 / (2.0 * 6.0 * COLS * BS * top)
    scale_h = 30000.0 / (2.0 * COLS * BS * top * top)
    scales[...] = as_row([1.0 / scale_e, 1.0 / scale_h])
    pay[...] = jnp.zeros_like(pay)
    for c in range(COLS):
        block = new[c * BS : (c + 1) * BS, :]
        rounded[c] = block.astype(bf16)
        turned[c] = block.T.astype(bf16)
    for c in range(COLS):
        gram = jnp.dot(turned[c], rounded[c], preferred_element_type=f32) * scale_h
        mixed, cross, diag = pack(gram)
        grams[c, :, :BS] = mixed
        grams[c, :, BS:] = cross
        diags[c : c + 1, :] = diag

    def slots(step, carry):
        for k in range(4):
            s = step * 4 + k
            r, c = row_ids[s], col_ids[s]
            weight = jnp.where(s < live, scale_e, 0.0)
            product = weight * jnp.dot(tiles[s], rounded[c], preferred_element_type=f32)
            pay[core, r, :BS, :] += product
        return carry

    lax.fori_loop(0, (live + 3) // 4, slots, 0)
    other = 1 - core
    for r in range(ROWS):
        weights = [mask[r * COLS + c] for c in range(COLS)]
        for half in range(4):
            rows = slice(half * 32, (half + 1) * 32)
            total = weights[0] * grams[0, rows, :]
            for c in range(1, COLS):
                total += weights[c] * grams[c, rows, :]
            pay[other, r, rows, :] = total
        total = weights[0] * diags[0:1, :]
        for c in range(1, COLS):
            total += weights[c] * diags[c : c + 1, :]
        pay[other, r, BS : BS + 1, :BS] = total


def indiv_moments(meta, mine, theirs, start, scales, resid, applied, moments):
    core = meta[0]
    own, far = mine[...], theirs[...]
    data = jnp.where(core == 0, own, far) * scales[0:1, 0:1]
    packed = jnp.where(core == 0, far, own) * scales[0:1, 1:2]
    high, low = split(unpack(packed[:BS, :BS], packed[:BS, BS:], packed[BS : BS + 1, :BS]))
    begin = start[...]
    value = data[:BS, :] - times(begin, high, low) - ridge_weight * begin
    first = times(value, high, low) + ridge_weight * value
    second = times(first, high, low) + ridge_weight * first
    resid[...] = value
    applied[...] = first
    moments[...] = as_row(
        [
            total_of(value * value),
            total_of(value * first),
            total_of(first * first),
            total_of(first * second),
            largest(value),
            largest(first),
        ]
    )


def indiv_update(meta, table, resid, applied, update, scales):
    on_resid, on_applied, bound = coefficients(table[...])
    bound = jnp.maximum(bound, 1e-30)
    rows = pl.ds(pl.multiple_of(meta[0] * (BS // 2), BS // 2), BS // 2)
    update[...] = (on_resid * resid[rows, :] - on_applied * applied[rows, :]) * (30000.0 / bound)
    scales[...] = as_row([bound / 30000.0])


def ring(step):
    return [(k, (k + step) % 4) for k in range(4)]


def on_device(indiv_factors, variant_factors, dosage_tiles, block_rows, block_cols, live_blocks):
    tiles = dosage_tiles[0, 0]
    row_ids = block_rows[0, 0]
    col_ids = block_cols[0, 0]
    live = live_blocks[0, 0]
    me = lax.axis_index("x")
    core = lax.axis_index("c")
    chip = lax.axis_index(CHIP)
    slab = lax.axis_index(GEN)
    odd = core
    part = jnp.where(odd == 1, 3 - me, me)

    slabs = 32
    low = lax.ppermute(variant_factors[-8:], GEN, [(k, k + 1) for k in range(slabs - 1)])
    high = lax.ppermute(variant_factors[:8], GEN, [(k + 1, k) for k in range(slabs - 1)])

    meta = jnp.stack([live, me, odd, core]).astype(jnp.int32)
    pay = pl.pallas_call(
        variant_sums,
        out_shape=jax.ShapeDtypeStruct((4, PAY_V, R), f32),
        in_specs=[smem(), smem(), smem(), vmem(), vmem()],
        out_specs=vmem(),
        scratch_shapes=[
            pltpu.VMEM((ROWS, R, BS), bf16),
            pltpu.VMEM((ROWS, BS, R), bf16),
            pltpu.VMEM((ROWS, BS, R), f32),
            pltpu.VMEM((ROWS, BS), f32),
            pltpu.SMEM((ROWS * COLS,), f32),
        ],
        compiler_params=params(),
    )(row_ids, col_ids, meta, tiles, indiv_factors)
    got = [
        lax.ppermute(pay[k].astype(f16), "x", ring(k)) for k in (1, 2, 3)
    ]
    total = pay[0] + got[0].astype(f32) + got[1].astype(f32) + got[2].astype(f32)

    def device(position):
        at, place = divmod(position, 4)
        return at * 4 + (3 - place if at % 2 else place)

    line = [device(k) for k in range(4 * slabs)]
    position = slab * 4 + part
    meta_line = jnp.stack(
        [part, (position > 0).astype(jnp.int32), (position < 4 * slabs - 1).astype(jnp.int32)]
    ).astype(jnp.int32)
    square = jax.ShapeDtypeStruct((2 * BS, R), f32)
    halves = jax.ShapeDtypeStruct((2, R, R), bf16)
    resid, applied, g_high, g_low, edge = pl.pallas_call(
        variant_start,
        out_shape=(square, square, halves, halves, jax.ShapeDtypeStruct((8, R), f32)),
        in_specs=[smem()] + [vmem()] * 4,
        out_specs=(vmem(),) * 5,
        scratch_shapes=[pltpu.VMEM((2 * BS + 16, R), f32)],
        compiler_params=params(),
    )(meta_line, total, variant_factors, low, high)
    edge_before = lax.ppermute(edge, ALL, list(zip(line[:-1], line[1:])))
    edge_after = lax.ppermute(edge, ALL, list(zip(line[1:], line[:-1])))
    resids = [resid] + [lax.ppermute(resid, "x", ring(k)) for k in (1, 2, 3)]
    again, moments = pl.pallas_call(
        variant_moments,
        out_shape=(square, jax.ShapeDtypeStruct((8, BS), f32)),
        in_specs=[smem()] + [vmem()] * 6,
        out_specs=(vmem(),) * 2,
        scratch_shapes=[pltpu.VMEM((2 * BS + 16, R), f32)],
        compiler_params=params(),
    )(meta_line, resid, applied, g_high, g_low, edge_before, edge_after)
    agains = [again] + [lax.ppermute(again, "x", ring(k)) for k in (1, 2, 3)]
    table = lax.all_to_all(
        jnp.broadcast_to(moments[None, :1], (4 * slabs, 1, BS)), ALL, 0, 0
    ).reshape(4 * slabs, BS)

    variant_new, pay, scales = pl.pallas_call(
        indiv_sums,
        out_shape=(
            jax.ShapeDtypeStruct((COLS * BS, R), f32),
            jax.ShapeDtypeStruct((2, ROWS, PAY_I, R), f32),
            jax.ShapeDtypeStruct((8, BS), f32),
        ),
        in_specs=[smem()] * 3 + [vmem()] * 11,
        out_specs=(vmem(),) * 3,
        scratch_shapes=[
            pltpu.VMEM((COLS, R, BS), bf16),
            pltpu.VMEM((COLS, BS, R), bf16),
            pltpu.VMEM((COLS, BS, R), f32),
            pltpu.VMEM((COLS, BS), f32),
            pltpu.SMEM((ROWS * COLS,), f32),
        ],
        compiler_params=params(),
    )(row_ids, col_ids, meta, table, variant_factors, tiles, *resids, *agains)

    swap = [(0, 1), (1, 0)]
    from_other = lax.ppermute(pay[1].astype(f16), "c", swap)
    of_chip = (pay[0] + from_other.astype(f32)).astype(f16)
    arrived = lax.all_to_all(of_chip, CHIP, 0, 0)
    mine = jnp.sum(arrived.astype(f32), axis=0)
    theirs = lax.ppermute(mine, "c", swap)
    begin = lax.dynamic_slice_in_dim(indiv_factors, chip * BS, BS, 0)
    meta_core = core.astype(jnp.int32).reshape(1)
    block = jax.ShapeDtypeStruct((BS, R), f32)
    row = jax.ShapeDtypeStruct((8, BS), f32)
    resid, applied, moments = pl.pallas_call(
        indiv_moments,
        out_shape=(block, block, row),
        in_specs=[smem()] + [vmem()] * 4,
        out_specs=(vmem(),) * 3,
        compiler_params=params(),
    )(meta_core, mine, theirs, begin, scales)
    chips = 64
    table = lax.all_to_all(
        jnp.broadcast_to(moments[None, :1], (chips, 1, BS)), ("z", "y", "x"), 0, 0
    ).reshape(chips, BS)
    update, scales = pl.pallas_call(
        indiv_update,
        out_shape=(jax.ShapeDtypeStruct((BS // 2, R), f32), row),
        in_specs=[smem()] + [vmem()] * 3,
        out_specs=(vmem(),) * 2,
        compiler_params=params(),
    )(meta_core, table, resid, applied)
    sent = jnp.broadcast_to(update.astype(f16)[None], (ROWS, BS // 2, R))
    ours = lax.all_to_all(sent, CHIP, 0, 0)
    far = lax.ppermute(ours, "c", swap)
    first = jnp.where(core == 0, ours, far)
    last = jnp.where(core == 0, far, ours)
    change = jnp.concatenate([first, last], axis=1).reshape(ROWS * BS, R)
    indiv_new = indiv_factors + change.astype(f32) * scales[0, 0]
    return variant_new, indiv_new


def solution(mesh):
    grid = np.asarray(mesh.devices).reshape(4, 4, 2, 4)
    inner = Mesh(grid, ALL)
    return jax.shard_map(
        on_device,
        mesh=inner,
        in_specs=(
            P("x", None),
            P(GEN, None),
            P(GEN, "x", None, None, None),
            P(GEN, "x", None),
            P(GEN, "x", None),
            P(GEN, "x"),
        ),
        out_specs=(P(GEN, None), P("x", None)),
        check_vma=False,
    )
```

time: 1030 us -> 149 us (0.14)
  waiting for transfers between devices: 579 us -> 10.5 us
  blocking collectives: 227 us -> 74.3 us
  other arithmetic: 103 us -> 10.2 us
  matrix products: 43.4 us -> 0 us
  local copies, waits for them, and re-layouts: 47.1 us -> 5.33 us
  starting transfers between devices: 7.95 us -> 29.7 us
  between operations: 22.7 us -> 1.54 us
  Pallas kernels: 0 us -> 16.1 us
    psum x6 -> x0, waiting for transfers between devices: 570 us -> none  [the longest x3 382 us: indiv_apply(): summed = lax.psum(partial_term, 'genome')]
    psum x6 -> x0, blocking collectives: 227 us -> none  [the longest x3 196 us: variant_total(): return lax.psum(value, 'genome')]
    all_to_all x0 -> x4, blocking collectives: none -> 74.3 us  [the longest x1 22.1 us: on_device(): lax.all_to_all(jnp.broadcast_to(moments[None, :1], (4 * slabs, 1, BS)), A...]
    scatter-add x12 -> x0, other arithmetic: 50.5 us -> none  [the longest x6 29.5 us: advance(): return running.at[row_part].add(contrib)]
    dot_general x24 -> x0, matrix products: 43.4 us -> none  [the longest x12 15.5 us: advance(): jnp.einsum('sir,sjr->sij', left_part, right_part, preferred_element_type=...]
    gather x24 -> x0, local copies, waits for them, and re-layouts: 33.7 us -> none  [the longest x12 19.4 us: advance(): right_part = right_blocks[col_part]]
    ppermute x6 -> x16, starting transfers between devices: 7.71 us -> 29.7 us  [the longest x3 7.48 us: on_device(): resids = [resid] + [lax.ppermute(resid, 'x', ring(k)) for k in (1, 2, 3)]]
    reduce_sum x7 -> x1, other arithmetic: 19.2 us -> 0.15 us  [on_device(): mine = jnp.sum(arrived.astype(f32), axis=0)]
  transfers between devices with their start and end apart: 12 -> 16, of which waited for: 9 -> 5; matrix products, arithmetic and copies ran while one was open for 0% -> 1% of each run, Pallas kernels for 0% -> 1%
where the time goes in v1:
time: 149 us; the launch traced here: 148 us
  blocking collectives  74.3 us (50%)
  starting transfers between devices  29.7 us (20%)
  Pallas kernels  16.1 us (11%)
  waiting for transfers between devices  10.5 us (7%)
  other arithmetic  10.2 us (7%)
  local copies, waits for them, and re-layouts  5.33 us (4%)
  between operations  1.54 us (1%)
    all_to_all x1, blocking collectives, on_device(): lax.all_to_all(jnp.broadcast_to(moments[None, :1], (4 * slabs, 1, BS)), A...  22.1 us
    all_to_all x1, blocking collectives, on_device(): arrived = lax.all_to_all(of_chip, CHIP, 0, 0)  22 us
    all_to_all x1, blocking collectives, on_device(): lax.all_to_all(jnp.broadcast_to(moments[None, :1], (chips, 1, BS)), ('z',...  16.6 us
    all_to_all x1, blocking collectives, on_device(): ours = lax.all_to_all(sent, CHIP, 0, 0)  13.7 us
    ppermute x3, starting transfers between devices, on_device(): resids = [resid] + [lax.ppermute(resid, 'x', ring(k)) for k in (1, 2, 3)]  7.48 us
    pallas_call x1, Pallas kernels, on_device(): pl.pallas_call(indiv_sums, out_shape=(jax.ShapeDtypeStruct((COLS * BS, R)...  7.09 us
    ppermute x3, starting transfers between devices, on_device(): got = [lax.ppermute(pay[k].astype(f16), 'x', ring(k)) for k in (1, 2, 3)]  6.55 us
    pallas_call x1, Pallas kernels, on_device(): pl.pallas_call(variant_sums, out_shape=jax.ShapeDtypeStruct((4, PAY_V, R)...  5.96 us
  transfers between devices with their start and end apart: 16, of which 5 were waited for; matrix products, arithmetic and copies ran while one was open for 1% of the time, Pallas kernels for 1%

profile of v1, /device:TPU:0, one launch (start us, length us, event | category | flops | bytes accessed | tf_op | source)
XLA Modules:
  0.0 147.6 jit_solution(16746665890910129749)
XLA Ops:
  1.3 0.1 pad_add_fusion.meta
  1.4 1.6 %copy-done = f32[2048,256]{1,0:T(8,128)S(1)} copy-done((f32[2048,256]{1,0:T(8,128)S(1)}, f32[2048,256]{1,0:T(8,128)}, u32[]{:S(2)}) %copy-start) | copy-done | bytes 2097176
  3.0 1.6 %copy-done.2 = bf16[1,1,64,128,128]{4,3,2,1,0:T(8,128)(2,1)S(1)} copy-done((bf16[1,1,64,128,128]{4,3,2,1,0:T(8,128)(2,1)S(1)}, bf16[1,1,64,128,128]{4,3,2,1,0:T(8,128)(2,1)}, u32[]{:S(2)}) %copy-start.2) | copy-done | bytes 2097176
  4.5 0.7 copy-done.5
  5.2 0.7 copy-done.7
  5.9 6.0 %shard_map.77 = f32[4,528,256]{2,1,0:T(8,128)} custom-call(s32[64]{0:T(128)S(1)} %bitcast.43, s32[64]{0:T(128)S(1)} %bitcast.45, s32[4]{0:T(128)S(1)} %pad_add_fusion.meta, bf16[64,128,128]{2,1,0:T(8,128)(2,1)S(1)} %bitcast.39, f32[2048,256]{1,0:T(8,128)S(1)} %copy-done), custom_call_target="tpu_custom_call" | custom-call | tf_op jit(solution)/shard_map/pallas_call | solution.py:363
  11.8 1.9 %convert.10 = f16[4,528,256]{2,1,0:T(8,128)(2,1)S(1)} convert(f32[4,528,256]{2,1,0:T(8,128)} %shard_map.77) | non-fusion elementwise | flops 540672 | bytes 3244032 | tf_op jit(solution)/shard_map/convert.5
  13.7 0.2 slice_bitcast_fusion.3
  13.9 1.6 %collective-permute-start = (f16[528,256]{1,0:T(8,128)(2,1)S(1)}, f16[528,256]{1,0:T(8,128)(2,1)S(1)}, u32[]{:S(2)}, u32[]{:S(2)}) collective-permute-start(f16[528,256]{1,0:T(8,128)(2,1)S(1)} %get-tuple-element.32), channel_id=1, source_target_pairs={{0,1},{1,2},{2,3},{3,0},{4,5},{5,6},{6,7},{7,4},{8,9},{9,10},{10,1... | collective-permute-start | bytes 811016 | tf_op jit(solution)/shard_map/ppermute | solution.py:378
  15.5 2.7 %collective-permute-start.1 = (f16[528,256]{1,0:T(8,128)(2,1)S(1)}, f16[528,256]{1,0:T(8,128)(2,1)S(1)}, u32[]{:S(2)}, u32[]{:S(2)}) collective-permute-start(f16[528,256]{1,0:T(8,128)(2,1)S(1)} %get-tuple-element.34), channel_id=1, source_target_pairs={{0,2},{1,3},{2,0},{3,1},{4,6},{5,7},{6,4},{7,5},{8,10},{9,11},{10,... | collective-permute-start | bytes 811016 | tf_op jit(solution)/shard_map/ppermute | solution.py:378
  18.2 2.2 %collective-permute-start.2 = (f16[528,256]{1,0:T(8,128)(2,1)S(1)}, f16[528,256]{1,0:T(8,128)(2,1)S(1)}, u32[]{:S(2)}, u32[]{:S(2)}) collective-permute-start(f16[528,256]{1,0:T(8,128)(2,1)S(1)} %get-tuple-element.33), channel_id=1, source_target_pairs={{0,3},{1,0},{2,1},{3,2},{4,7},{5,4},{6,5},{7,6},{8,11},{9,8},{10,9... | collective-permute-start | bytes 811016 | tf_op jit(solution)/shard_map/ppermute | solution.py:378
  20.4 0.0 copy-done.4
  20.4 2.9 %collective-permute-start.3 = (f32[8,256]{1,0:T(8,128)S(1)}, f32[8,256]{1,0:T(8,128)S(1)}, u32[]{:S(2)}, u32[]{:S(2)}) collective-permute-start(f32[8,256]{1,0:T(8,128)S(1)} %get-tuple-element.38), channel_id=1, source_target_pairs={{0,4},{4,8},{8,12},{12,16},{16,20},{20,24},{24,28},{28,32},{32,36}... | collective-permute-start | bytes 24584 | tf_op jit(solution)/shard_map/ppermute | solution.py:359
  23.3 1.3 collective-permute-start.4
  24.6 0.1 pad_add_fusion.1.meta
  24.7 0.0 collective-permute-done
  24.7 4.9 %collective-permute-done.1 = f16[528,256]{1,0:T(8,128)(2,1)S(1)} collective-permute-done((f16[528,256]{1,0:T(8,128)(2,1)S(1)}, f16[528,256]{1,0:T(8,128)(2,1)S(1)}, u32[]{:S(2)}, u32[]{:S(2)}) %collective-permute-start.1) | collective-permute-done | bytes 270368 | tf_op jit(solution)/shard_map/ppermute | solution.py:378
  29.7 0.5 collective-permute-done.2
  30.1 1.2 fusion.4.total
  31.3 0.0 collective-permute-done.3.low
  31.3 0.0 collective-permute-done.4.high
  31.3 1.1 shard_map.78
  32.4 2.1 %collective-permute-start.7 = (f32[256,256]{1,0:T(8,128)S(1)}, f32[256,256]{1,0:T(8,128)S(1)}, u32[]{:S(2)}, u32[]{:S(2)}) collective-permute-start(f32[256,256]{1,0:T(8,128)S(1)} %get-tuple-element.17.resid.resid0), channel_id=1, source_target_pairs={{0,1},{1,2},{2,3},{3,0},{4,5},{5,6},{6,7},{7,4},{8,9},{9,10},{10,1... | collective-permute-start | bytes 786440 | tf_op jit(solution)/shard_map/ppermute | solution.py:403
  34.5 4.2 %collective-permute-start.5 = (f32[8,256]{1,0:T(8,128)S(1)}, f32[8,256]{1,0:T(8,128)S(1)}, u32[]{:S(2)}, u32[]{:S(2)}) collective-permute-start(f32[8,256]{1,0:T(8,128)S(1)} %get-tuple-element.21), channel_id=1, source_target_pairs={{0,1},{1,2},{2,3},{3,7},{7,6},{6,5},{5,4},{4,8},{8,9},{9,10},{10,1... | collective-permute-start | bytes 24584 | tf_op jit(solution)/shard_map/ppermute | solution.py:401
  38.8 1.3 collective-permute-start.6
  40.1 3.5 %collective-permute-start.8 = (f32[256,256]{1,0:T(8,128)S(1)}, f32[256,256]{1,0:T(8,128)S(1)}, u32[]{:S(2)}, u32[]{:S(2)}) collective-permute-start(f32[256,256]{1,0:T(8,128)S(1)} %get-tuple-element.17.resid.resid0), channel_id=1, source_target_pairs={{0,2},{1,3},{2,0},{3,1},{4,6},{5,7},{6,4},{7,5},{8,10},{9,11},{10,... | collective-permute-start | bytes 786440 | tf_op jit(solution)/shard_map/ppermute | solution.py:403
  43.6 1.9 %collective-permute-start.9 = (f32[256,256]{1,0:T(8,128)S(1)}, f32[256,256]{1,0:T(8,128)S(1)}, u32[]{:S(2)}, u32[]{:S(2)}) collective-permute-start(f32[256,256]{1,0:T(8,128)S(1)} %get-tuple-element.17.resid.resid0), channel_id=1, source_target_pairs={{0,3},{1,0},{2,1},{3,2},{4,7},{5,4},{6,5},{7,6},{8,11},{9,8},{10,9... | collective-permute-start | bytes 786440 | tf_op jit(solution)/shard_map/ppermute | solution.py:403
  45.5 0.0 collective-permute-done.5.edge_before
  45.5 0.0 collective-permute-done.6.edge_after
  45.5 0.9 shard_map.79
  46.4 0.2 collective-permute-start.10
  46.6 1.3 collective-permute-start.11
  47.9 0.0 collective-permute-done.7.resid1
  47.9 1.8 %collective-permute-start.12 = (f32[256,256]{1,0:T(8,128)S(1)}, f32[256,256]{1,0:T(8,128)S(1)}, u32[]{:S(2)}, u32[]{:S(2)}) collective-permute-start(f32[256,256]{1,0:T(8,128)S(1)} %get-tuple-element.23.again0), channel_id=1, source_target_pairs={{0,3},{1,0},{2,1},{3,2},{4,7},{5,4},{6,5},{7,6},{8,11},{9,8},{10,9... | collective-permute-start | bytes 786440 | tf_op jit(solution)/shard_map/ppermute | solution.py:412
  49.7 22.1 %all_to_all.20 = f32[128,1,128]{2,1,0:T(1,128)S(1)} all-to-all(f32[128,1,128]{2,1,0:T(1,128)S(1)} %broadcast_in_dim.11), channel_id=1, replica_groups=mesh['z'=4,'y'=4,'c'=2,'x'=4] {'z','y','c','x'}, dimensions={0} | all-to-all | bytes 131072 | tf_op jit(solution)/shard_map/all_to_all | solution.py:413
  71.8 0.0 collective-permute-done.8.resid2
  71.8 0.0 collective-permute-done.9.resid3
  71.8 0.0 collective-permute-done.10.again1
  71.8 0.0 collective-permute-done.11.again2
  71.8 0.0 collective-permute-done.12.again3
  71.8 0.0 copy-done.3
  71.8 0.0 copy-done.6
  71.9 0.0 copy-done.8
  71.9 7.1 %shard_map.80 = (f32[1024,256]{1,0:T(8,128)}, f32[2,16,136,256]{3,2,1,0:T(8,128)}, f32[8,128]{1,0:T(8,128)S(1)}) custom-call(s32[64]{0:T(128)S(1)} %bitcast.44, s32[64]{0:T(128)S(1)} %bitcast.46, s32[4]{0:T(128)S(1)} %pad_add_fusion.meta, f32[128,128]{1,0:T(8,128)S(1)} %bitcast.41, f32[1024,256]{1,0:T(8,128)S(1)} %copy-done.4, ...), custom_call_target="tpu_custom_call" | custom-call | tf_op jit(solution)/shard_map/pallas_call | solution.py:417
  79.0 1.8 %fusion.1 = f16[16,136,256]{2,1,0:T(8,128)(2,1)S(1)} fusion(f32[2,16,136,256]{3,2,1,0:T(8,128)} %get-tuple-element.25), kind=kLoop, calls=%fused_computation.6 | loop fusion | flops 557056 | bytes 3342336 | tf_op jit(solution)/shard_map/convert_element_type | solution.py:437
  80.8 2.4 %collective-permute-start.13 = (f16[16,136,256]{2,1,0:T(8,128)(2,1)S(1)}, f16[16,136,256]{2,1,0:T(8,128)(2,1)S(1)}, u32[]{:S(2)}, u32[]{:S(2)}) collective-permute-start(f16[16,136,256]{2,1,0:T(8,128)(2,1)S(1)} %fusion.1), channel_id=1, source_target_pairs={{0,4},{4,0},{1,5},{5,1},{2,6},{6,2},{3,7},{7,3},{8,12},{12,8},{9,1... | collective-permute-start | bytes 3342344 | tf_op jit(solution)/shard_map/ppermute | solution.py:437
  83.2 2.4 %collective-permute-done.13 = f16[16,136,256]{2,1,0:T(8,128)(2,1)S(1)} collective-permute-done((f16[16,136,256]{2,1,0:T(8,128)(2,1)S(1)}, f16[16,136,256]{2,1,0:T(8,128)(2,1)S(1)}, u32[]{:S(2)}, u32[]{:S(2)}) %collective-permute-start.13) | collective-permute-done | bytes 1114144 | tf_op jit(solution)/shard_map/ppermute | solution.py:437
  85.6 2.0 %fusion = f16[16,136,256]{2,1,0:T(8,128)(2,1)S(1)} fusion(f16[16,136,256]{2,1,0:T(8,128)(2,1)S(1)} %collective-permute-done.13, f32[2,16,136,256]{3,2,1,0:T(8,128)} %get-tuple-element.25), kind=kLoop, calls=%fused_computation.2 | loop fusion | flops 1671168 | bytes 4456448 | tf_op jit(solution)/shard_map/convert_element_type | solution.py:438
  87.6 0.0 copy-start.1
  87.7 22.0 %all_to_all.21 = f16[16,136,256]{2,1,0:T(8,128)(2,1)S(1)} all-to-all(f16[16,136,256]{2,1,0:T(8,128)(2,1)S(1)} %fusion), channel_id=1, replica_groups=mesh['z'=4,'y'=4,'c'=2,'x'=4] {'z','y'}, dimensions={0} | all-to-all | bytes 2228224 | tf_op jit(solution)/shard_map/all_to_all | solution.py:439
  109.6 0.2 convert_reduce_fusion.mine
  109.8 0.3 collective-permute-start.14
  110.1 0.0 copy-done.1
  110.1 1.3 collective-permute-done.14.theirs
  111.4 0.8 shard_map.81
  112.2 16.6 %all_to_all.22 = f32[64,1,128]{2,1,0:T(1,128)S(1)} all-to-all(f32[64,1,128]{2,1,0:T(1,128)S(1)} %broadcast_in_dim.25), channel_id=1, replica_groups=mesh['z'=4,'y'=4,'c'=2,'x'=4] {'z','y','x'}, dimensions={0} | all-to-all | bytes 65536 | tf_op jit(solution)/shard_map/all_to_all | solution.py:454
  128.8 0.2 shard_map.82
  129.0 13.7 %all_to_all.23 = f16[16,64,256]{2,1,0:T(8,128)(2,1)S(1)} all-to-all(f16[16,64,256]{2,1,0:T(8,128)(2,1)S(1)} %broadcast_in_dim.26), channel_id=1, replica_groups=mesh['z'=4,'y'=4,'c'=2,'x'=4] {'z','y'}, dimensions={0} | all-to-all | bytes 1048576 | tf_op jit(solution)/shard_map/all_to_all | solution.py:465
  142.7 0.0 collective-permute-start.15
  142.7 0.5 slice.47
  143.2 1.4 collective-permute-done.15
  144.6 0.3 broadcast_select_fusion.1
  144.9 0.9 convert_multiply_fusion
  145.8 1.8 %bitcast_add_fusion.1 = f32[2048,256]{1,0:T(8,128)} fusion(f32[2048,256]{1,0:T(8,128)S(1)} %copy-done.1, f32[16,128,256]{2,1,0:T(8,128)S(1)} %convert_multiply_fusion), kind=kLoop, calls=%fused_computation.4 | loop fusion | flops 524288 | bytes 6291456 | tf_op jit(solution)/shard_map/add | solution.py:470
  (16 shorter events, 0.2 us)
Async XLA Ops:
  1.4 1.6 %copy-start = (f32[2048,256]{1,0:T(8,128)S(1)}, f32[2048,256]{1,0:T(8,128)}, u32[]{:S(2)}) copy-start(f32[2048,256]{1,0:T(8,128)} %factors.1) | copy-start | bytes 6291460
  3.0 1.6 %copy-start.2 = (bf16[1,1,64,128,128]{4,3,2,1,0:T(8,128)(2,1)S(1)}, bf16[1,1,64,128,128]{4,3,2,1,0:T(8,128)(2,1)}, u32[]{:S(2)}) copy-start(bf16[1,1,64,128,128]{4,3,2,1,0:T(8,128)(2,1)} %param.8) | copy-start | bytes 6291460
  4.5 0.7 copy-start.5
  5.2 0.7 copy-start.7
  11.8 8.6 %copy-start.4 = (f32[1024,256]{1,0:T(8,128)S(1)}, f32[1024,256]{1,0:T(8,128)}, u32[]{:S(2)}) copy-start(f32[1024,256]{1,0:T(8,128)} %start.3) | copy-start | bytes 3145732
  13.9 10.9 %collective-permute-start = (f16[528,256]{1,0:T(8,128)(2,1)S(1)}, f16[528,256]{1,0:T(8,128)(2,1)S(1)}, u32[]{:S(2)}, u32[]{:S(2)}) collective-permute-start(f16[528,256]{1,0:T(8,128)(2,1)S(1)} %get-tuple-element.32), channel_id=1, source_target_pairs={{0,1},{1,2},{2,3},{3,0},{4,5},{5,6},{6,7},{7,4},{8,9},{9,10},{10,1... | collective-permute-start | bytes 811016 | tf_op jit(solution)/shard_map/ppermute | solution.py:378
  15.5 14.2 %collective-permute-start.1 = (f16[528,256]{1,0:T(8,128)(2,1)S(1)}, f16[528,256]{1,0:T(8,128)(2,1)S(1)}, u32[]{:S(2)}, u32[]{:S(2)}) collective-permute-start(f16[528,256]{1,0:T(8,128)(2,1)S(1)} %get-tuple-element.34), channel_id=1, source_target_pairs={{0,2},{1,3},{2,0},{3,1},{4,6},{5,7},{6,4},{7,5},{8,10},{9,11},{10,... | collective-permute-start | bytes 811016 | tf_op jit(solution)/shard_map/ppermute | solution.py:378
  18.2 11.9 %collective-permute-start.2 = (f16[528,256]{1,0:T(8,128)(2,1)S(1)}, f16[528,256]{1,0:T(8,128)(2,1)S(1)}, u32[]{:S(2)}, u32[]{:S(2)}) collective-permute-start(f16[528,256]{1,0:T(8,128)(2,1)S(1)} %get-tuple-element.33), channel_id=1, source_target_pairs={{0,3},{1,0},{2,1},{3,2},{4,7},{5,4},{6,5},{7,6},{8,11},{9,8},{10,9... | collective-permute-start | bytes 811016 | tf_op jit(solution)/shard_map/ppermute | solution.py:378
  20.4 10.9 %collective-permute-start.3 = (f32[8,256]{1,0:T(8,128)S(1)}, f32[8,256]{1,0:T(8,128)S(1)}, u32[]{:S(2)}, u32[]{:S(2)}) collective-permute-start(f32[8,256]{1,0:T(8,128)S(1)} %get-tuple-element.38), channel_id=1, source_target_pairs={{0,4},{4,8},{8,12},{12,16},{16,20},{20,24},{24,28},{28,32},{32,36}... | collective-permute-start | bytes 24584 | tf_op jit(solution)/shard_map/ppermute | solution.py:359
  23.3 8.0 %collective-permute-start.4 = (f32[8,256]{1,0:T(8,128)S(1)}, f32[8,256]{1,0:T(8,128)S(1)}, u32[]{:S(2)}, u32[]{:S(2)}) collective-permute-start(f32[8,256]{1,0:T(8,128)S(1)} %get-tuple-element.37), channel_id=1, source_target_pairs={{4,0},{8,4},{12,8},{16,12},{20,16},{24,20},{28,24},{32,28},{36,32}... | collective-permute-start | bytes 24584 | tf_op jit(solution)/shard_map/ppermute | solution.py:360
  24.7 47.1 %copy-start.3 = (bf16[1,1,64,128,128]{4,3,2,1,0:T(8,128)(2,1)S(1)}, bf16[1,1,64,128,128]{4,3,2,1,0:T(8,128)(2,1)}, u32[]{:S(2)}) copy-start(bf16[1,1,64,128,128]{4,3,2,1,0:T(8,128)(2,1)} %param.8) | copy-start | bytes 6291460
  24.7 47.1 %copy-start.6 = (s32[1,1,64]{2,1,0:T(1,128)S(1)}, s32[1,1,64]{2,1,0:T(1,128)}, u32[]{:S(2)}) copy-start(s32[1,1,64]{2,1,0:T(1,128)} %param.9) | copy-start | bytes 772
  24.7 47.1 %copy-start.8 = (s32[1,1,64]{2,1,0:T(1,128)S(1)}, s32[1,1,64]{2,1,0:T(1,128)}, u32[]{:S(2)}) copy-start(s32[1,1,64]{2,1,0:T(1,128)} %param.10) | copy-start | bytes 772
  32.4 15.5 %collective-permute-start.7 = (f32[256,256]{1,0:T(8,128)S(1)}, f32[256,256]{1,0:T(8,128)S(1)}, u32[]{:S(2)}, u32[]{:S(2)}) collective-permute-start(f32[256,256]{1,0:T(8,128)S(1)} %get-tuple-element.17.resid.resid0), channel_id=1, source_target_pairs={{0,1},{1,2},{2,3},{3,0},{4,5},{5,6},{6,7},{7,4},{8,9},{9,10},{10,1... | collective-permute-start | bytes 786440 | tf_op jit(solution)/shard_map/ppermute | solution.py:403
  34.5 11.0 %collective-permute-start.5 = (f32[8,256]{1,0:T(8,128)S(1)}, f32[8,256]{1,0:T(8,128)S(1)}, u32[]{:S(2)}, u32[]{:S(2)}) collective-permute-start(f32[8,256]{1,0:T(8,128)S(1)} %get-tuple-element.21), channel_id=1, source_target_pairs={{0,1},{1,2},{2,3},{3,7},{7,6},{6,5},{5,4},{4,8},{8,9},{9,10},{10,1... | collective-permute-start | bytes 24584 | tf_op jit(solution)/shard_map/ppermute | solution.py:401
  38.8 6.7 %collective-permute-start.6 = (f32[8,256]{1,0:T(8,128)S(1)}, f32[8,256]{1,0:T(8,128)S(1)}, u32[]{:S(2)}, u32[]{:S(2)}) collective-permute-start(f32[8,256]{1,0:T(8,128)S(1)} %get-tuple-element.21), channel_id=1, source_target_pairs={{1,0},{2,1},{3,2},{7,3},{6,7},{5,6},{4,5},{8,4},{9,8},{10,9},{11,1... | collective-permute-start | bytes 24584 | tf_op jit(solution)/shard_map/ppermute | solution.py:402
  40.1 31.7 %collective-permute-start.8 = (f32[256,256]{1,0:T(8,128)S(1)}, f32[256,256]{1,0:T(8,128)S(1)}, u32[]{:S(2)}, u32[]{:S(2)}) collective-permute-start(f32[256,256]{1,0:T(8,128)S(1)} %get-tuple-element.17.resid.resid0), channel_id=1, source_target_pairs={{0,2},{1,3},{2,0},{3,1},{4,6},{5,7},{6,4},{7,5},{8,10},{9,11},{10,... | collective-permute-start | bytes 786440 | tf_op jit(solution)/shard_map/ppermute | solution.py:403
  43.6 28.2 %collective-permute-start.9 = (f32[256,256]{1,0:T(8,128)S(1)}, f32[256,256]{1,0:T(8,128)S(1)}, u32[]{:S(2)}, u32[]{:S(2)}) collective-permute-start(f32[256,256]{1,0:T(8,128)S(1)} %get-tuple-element.17.resid.resid0), channel_id=1, source_target_pairs={{0,3},{1,0},{2,1},{3,2},{4,7},{5,4},{6,5},{7,6},{8,11},{9,8},{10,9... | collective-permute-start | bytes 786440 | tf_op jit(solution)/shard_map/ppermute | solution.py:403
  46.4 25.4 %collective-permute-start.10 = (f32[256,256]{1,0:T(8,128)S(1)}, f32[256,256]{1,0:T(8,128)S(1)}, u32[]{:S(2)}, u32[]{:S(2)}) collective-permute-start(f32[256,256]{1,0:T(8,128)S(1)} %get-tuple-element.23.again0), channel_id=1, source_target_pairs={{0,1},{1,2},{2,3},{3,0},{4,5},{5,6},{6,7},{7,4},{8,9},{9,10},{10,1... | collective-permute-start | bytes 786440 | tf_op jit(solution)/shard_map/ppermute | solution.py:412
  46.6 25.2 %collective-permute-start.11 = (f32[256,256]{1,0:T(8,128)S(1)}, f32[256,256]{1,0:T(8,128)S(1)}, u32[]{:S(2)}, u32[]{:S(2)}) collective-permute-start(f32[256,256]{1,0:T(8,128)S(1)} %get-tuple-element.23.again0), channel_id=1, source_target_pairs={{0,2},{1,3},{2,0},{3,1},{4,6},{5,7},{6,4},{7,5},{8,10},{9,11},{10,... | collective-permute-start | bytes 786440 | tf_op jit(solution)/shard_map/ppermute | solution.py:412
  47.9 23.9 %collective-permute-start.12 = (f32[256,256]{1,0:T(8,128)S(1)}, f32[256,256]{1,0:T(8,128)S(1)}, u32[]{:S(2)}, u32[]{:S(2)}) collective-permute-start(f32[256,256]{1,0:T(8,128)S(1)} %get-tuple-element.23.again0), channel_id=1, source_target_pairs={{0,3},{1,0},{2,1},{3,2},{4,7},{5,4},{6,5},{7,6},{8,11},{9,8},{10,9... | collective-permute-start | bytes 786440 | tf_op jit(solution)/shard_map/ppermute | solution.py:412
  80.8 4.8 %collective-permute-start.13 = (f16[16,136,256]{2,1,0:T(8,128)(2,1)S(1)}, f16[16,136,256]{2,1,0:T(8,128)(2,1)S(1)}, u32[]{:S(2)}, u32[]{:S(2)}) collective-permute-start(f16[16,136,256]{2,1,0:T(8,128)(2,1)S(1)} %fusion.1), channel_id=1, source_target_pairs={{0,4},{4,0},{1,5},{5,1},{2,6},{6,2},{3,7},{7,3},{8,12},{12,8},{9,1... | collective-permute-start | bytes 3342344 | tf_op jit(solution)/shard_map/ppermute | solution.py:437
  87.6 22.4 %copy-start.1 = (f32[2048,256]{1,0:T(8,128)S(1)}, f32[2048,256]{1,0:T(8,128)}, u32[]{:S(2)}) copy-start(f32[2048,256]{1,0:T(8,128)} %factors.1) | copy-start | bytes 6291460
  109.8 1.6 %collective-permute-start.14 = (f32[136,256]{1,0:T(8,128)S(1)}, f32[136,256]{1,0:T(8,128)S(1)}, u32[]{:S(2)}, u32[]{:S(2)}) collective-permute-start(f32[136,256]{1,0:T(8,128)S(1)} %convert_reduce_fusion.mine), channel_id=1, source_target_pairs={{0,4},{4,0},{1,5},{5,1},{2,6},{6,2},{3,7},{7,3},{8,12},{12,8},{9,1... | collective-permute-start | bytes 417800 | tf_op jit(solution)/shard_map/ppermute | solution.py:441
  142.7 1.9 %collective-permute-start.15 = (f16[16,64,256]{2,1,0:T(8,128)(2,1)S(1)}, f16[16,64,256]{2,1,0:T(8,128)(2,1)S(1)}, u32[]{:S(2)}, u32[]{:S(2)}) collective-permute-start(f16[16,64,256]{2,1,0:T(8,128)(2,1)S(1)} %all_to_all.23), channel_id=1, source_target_pairs={{0,4},{4,0},{1,5},{5,1},{2,6},{6,2},{3,7},{7,3},{8,12},{12,8},{9,1... | collective-permute-start | bytes 1572872 | tf_op jit(solution)/shard_map/ppermute | solution.py:466

commit v2 on v1

v2 whole, which is shorter than its diff:
```python
import jax
import jax.numpy as jnp
import numpy as np
from jax import lax
from jax.experimental import pallas as pl
from jax.experimental.pallas import tpu as pltpu
from jax.sharding import Mesh
from jax.sharding import PartitionSpec as P

BS = 128
R = 256
NB = 64
ROWS = 16
COLS = 8
smooth_weight = 32.0
ridge_weight = 1.0
f32, bf16, f16 = jnp.float32, jnp.bfloat16, jnp.float16
ALL = ("z", "y", "c", "x")
GEN = ("z", "y", "c")
CHIP = ("z", "y")
PAY_V = 2 * BS + 2 * BS + 16
PAY_I = BS + 8
VMEM_LIMIT = 48 * 1024 * 1024


def row_col():
    rows = lax.broadcasted_iota(jnp.int32, (BS, BS), 0)
    cols = lax.broadcasted_iota(jnp.int32, (BS, BS), 1)
    return rows, cols


def pack(gram):
    rows, cols = row_col()
    upper = gram[:BS, :BS]
    lower = gram[BS:, BS:]
    mixed = jnp.where(rows <= cols, upper, lower)
    diag = jnp.sum(jnp.where(rows == cols, lower, 0.0), axis=0, keepdims=True)
    return mixed, gram[:BS, BS:], diag


def unpack(mixed, cross, diag):
    rows, cols = row_col()
    turned = mixed.T
    upper = jnp.where(rows <= cols, mixed, turned)
    lower = jnp.where(rows > cols, mixed, jnp.where(rows < cols, turned, diag))
    top = jnp.concatenate([upper, cross], axis=1)
    bottom = jnp.concatenate([cross.T, lower], axis=1)
    return jnp.concatenate([top, bottom], axis=0)


def split(matrix):
    high = matrix.astype(bf16)
    return high, (matrix - high.astype(f32)).astype(bf16)


def times(values, high, low):
    rounded = values.astype(bf16)
    return jnp.dot(rounded, high, preferred_element_type=f32) + jnp.dot(
        rounded, low, preferred_element_type=f32
    )


def set_mask(row_ids, col_ids, live, mask):
    def clear(k, carry):
        mask[k] = 0.0
        return carry

    lax.fori_loop(0, ROWS * COLS, clear, 0)

    def mark(s, carry):
        mask[row_ids[0, 0, s] * COLS + col_ids[0, 0, s]] = 1.0
        return carry

    lax.fori_loop(0, live, mark, 0)


def variant_sums(
    row_ids, col_ids, meta, tiles_hbm, factors_hbm, own, far, dense_hbm, mask,
    tiles, factors, dense, turned, rounded, grams, diags, sems,
):
    live, me, odd = meta[0], meta[1], meta[2]
    quarter = ROWS * BS // 4
    loads = [
        pltpu.make_async_copy(
            factors_hbm.at[pl.ds(k * quarter, quarter), :],
            factors.at[pl.ds(k * quarter, quarter), :],
            sems.at[k],
        )
        for k in range(4)
    ]
    load_tiles = pltpu.make_async_copy(tiles_hbm.at[0, 0], tiles, sems.at[4])
    for load in loads:
        load.start()
    load_tiles.start()
    dense[...] = jnp.zeros_like(dense)
    set_mask(row_ids, col_ids, live, mask)
    for r in range(ROWS):
        if r % 4 == 0:
            loads[r // 4].wait()
        block = factors[r * BS : (r + 1) * BS, :]
        rounded[r] = block.astype(bf16)
        turned[:, r * BS : (r + 1) * BS] = block.T.astype(bf16)
        gram = jnp.dot(turned[:, r * BS : (r + 1) * BS], rounded[r], preferred_element_type=f32)
        mixed, cross, diag = pack(gram)
        grams[r, :, :BS] = mixed
        grams[r, :, BS:] = cross
        diags[r : r + 1, :] = diag
    load_tiles.wait()

    def scatter(s, carry):
        rows = pl.ds(pl.multiple_of(row_ids[0, 0, s] * BS, BS), BS)
        cols = pl.ds(pl.multiple_of(col_ids[0, 0, s] * BS, BS), BS)
        dense[rows, cols] = tiles[s]
        return carry

    lax.fori_loop(0, live, scatter, 0)
    keep = pltpu.make_async_copy(dense, dense_hbm, sems.at[5])
    keep.start()
    zero = jnp.zeros((16, R), f32)
    for k in range(4):
        at = lax.rem(me + k, 4)
        part = jnp.where(odd == 1, 3 - at, at)
        out = own if k == 0 else far.at[k - 1]
        cols = pl.ds(pl.multiple_of(part * 2 * BS, 2 * BS), 2 * BS)
        out[2 * BS : 4 * BS, :] = jnp.dot(
            turned[...], dense[:, cols], preferred_element_type=f32
        )
        out[4 * BS :, :] = zero
        for j in range(2):
            weights = [mask[r * COLS + part * 2 + j] for r in range(ROWS)]
            for piece in range(4):
                rows = slice(piece * 32, (piece + 1) * 32)
                total = weights[0] * grams[0, rows, :]
                for r in range(1, ROWS):
                    total += weights[r] * grams[r, rows, :]
                out[j * BS + piece * 32 : j * BS + (piece + 1) * 32, :] = total
            total = weights[0] * diags[0:1, :]
            for r in range(1, ROWS):
                total += weights[r] * diags[r : r + 1, :]
            out[4 * BS + j : 4 * BS + j + 1, :BS] = total
    keep.wait()


def band_of(values, before, after, ext):
    n = values.shape[0]
    ext[7:8, :] = before
    ext[8 : 8 + n, :] = values
    ext[8 + n : 9 + n, :] = after
    return 2.0 * values - ext[7 : 7 + n, :] - ext[9 : 9 + n, :]


def variant_start(meta, total, start, low, high, resid, applied, g_high, g_low, edge, ext):
    part = meta[0]
    n = 2 * BS
    first = pl.multiple_of(part * n, n)
    mine = start[pl.ds(first, n), :]
    before8 = start[pl.ds(pl.multiple_of(jnp.maximum(first - 8, 0), 8), 8), :]
    after8 = start[pl.ds(pl.multiple_of(jnp.minimum(first + n, 3 * n + n - 8), 8), 8), :]
    before = jnp.where(part == 0, low[7:8, :], before8[7:8, :])
    after = jnp.where(part == 3, high[0:1, :], after8[0:1, :])
    banded = band_of(mine, before, after, ext)
    data = total[2 * BS : 4 * BS, :].T
    for k in range(2):
        gram = unpack(
            total[k * BS : (k + 1) * BS, :BS],
            total[k * BS : (k + 1) * BS, BS:],
            total[4 * BS + k : 4 * BS + k + 1, :BS],
        )
        up, down = split(gram)
        g_high[k] = up
        g_low[k] = down
        rows = slice(k * BS, (k + 1) * BS)
        resid[rows, :] = (
            data[rows]
            - times(mine[rows], up, down)
            - ridge_weight * mine[rows]
            - smooth_weight * banded[rows]
        )
    value = resid[...]
    zero = jnp.zeros((1, R), f32)
    banded = band_of(value, zero, zero, ext)
    for k in range(2):
        rows = slice(k * BS, (k + 1) * BS)
        applied[rows, :] = (
            times(value[rows], g_high[k], g_low[k])
            + ridge_weight * value[rows]
            + smooth_weight * banded[rows]
        )
    edge[...] = jnp.zeros_like(edge)
    edge[0:1, :] = resid[0:1, :]
    edge[1:2, :] = applied[0:1, :]
    edge[2:3, :] = resid[n - 1 : n, :]
    edge[3:4, :] = applied[n - 1 : n, :]


def as_row(values):
    lanes = lax.broadcasted_iota(jnp.int32, (8, BS), 1)
    row = jnp.zeros((8, BS), f32)
    for k, value in enumerate(values):
        row = jnp.where(lanes == k, value, row)
    return row


def total_of(values):
    return jnp.sum(jnp.sum(values, axis=0, keepdims=True), axis=1, keepdims=True)


def largest(values):
    return jnp.max(jnp.max(jnp.abs(values), axis=0, keepdims=True), axis=1, keepdims=True)


def curve_of(rr, ra, aa, aaa):
    first = rr / ra
    rr_next = rr - 2.0 * first * ra + first * first * aa
    ratio = rr_next / rr
    curve = (
        (1.0 + ratio) * (1.0 + ratio) * ra
        - 2.0 * (1.0 + ratio) * first * aa
        + first * first * aaa
    )
    second = rr_next / curve
    return first + second * (1.0 + ratio), second * first, rr_next, curve


def variant_moments(
    meta, start, resid, applied, g_high, g_low, edge_before, edge_after, sent, moments, ext
):
    has_before, has_after = meta[1], meta[2]
    n = 2 * BS
    value = resid[...]
    zero = jnp.zeros((1, R), f32)
    low = jnp.concatenate([edge_before[2:3, :], jnp.zeros((n - 1, R), f32)], axis=0)
    high = jnp.concatenate([jnp.zeros((n - 1, R), f32), edge_after[0:1, :]], axis=0)
    first = applied[...] - smooth_weight * (low + high)
    before = jnp.where(has_before == 1, edge_before[3:4, :] - smooth_weight * value[0:1, :], zero)
    after = jnp.where(has_after == 1, edge_after[1:2, :] - smooth_weight * value[n - 1 : n, :], zero)
    banded = band_of(first, before, after, ext)
    data = jnp.concatenate(
        [times(first[k * BS : (k + 1) * BS], g_high[k], g_low[k]) for k in range(2)], axis=0
    )
    second = data + ridge_weight * first + smooth_weight * banded
    rr, ra = total_of(value * value), total_of(value * first)
    aa, aaa = total_of(first * first), total_of(first * second)
    near, far, rr_next, curve = curve_of(rr, ra, aa, aaa)
    good = (ra > 0.0) & (rr_next > 1e-3 * rr) & (curve > 0.0) & (far > 0.0)
    on_start = jnp.where(good, 1.0, 0.0)
    near = jnp.where(good, near, 0.0)
    far = jnp.where(good, far, -1.0)
    mine = start[pl.ds(pl.multiple_of(meta[0] * n, n), n), :]
    guess = on_start * mine + near * value - far * first
    peak_value, peak_guess = largest(value), largest(guess)
    unit_value = jnp.maximum(peak_value, 1e-30) / 16384.0
    unit_guess = jnp.maximum(peak_guess, 1e-30) / 16384.0
    sent[0] = value / unit_value
    sent[1] = guess / unit_guess
    moments[...] = as_row(
        [rr, ra, aa, aaa, peak_value, largest(first), on_start, near, far, unit_value, unit_guess]
    )


def new_variants(meta, table, start, pieces, new, rounded, scales):
    me, odd, slab = meta[1], meta[2], meta[4]
    sums = jnp.sum(table[...], axis=0, keepdims=True)
    peaks = jnp.max(table[...], axis=0, keepdims=True)
    on_resid, on_applied, _, _ = curve_of(*(sums[:, k : k + 1] for k in range(4)))
    n = 2 * BS
    for k in range(4):
        owner = lax.rem(me - k + 4, 4)
        part = jnp.where(odd == 1, 3 - owner, owner)
        rows = pl.ds(pl.multiple_of(part * n, n), n)
        line = table[pl.ds(slab * 4 + owner, 1), :]
        on_start, near, far, unit_value, unit_guess = (line[:, j : j + 1] for j in range(6, 11))
        share = on_applied / far
        value = (
            (1.0 - share * on_start) * start[rows, :]
            + ((on_resid - share * near) * unit_value) * pieces[k, 0]
            + (share * unit_guess) * pieces[k, 1]
        )
        new[rows, :] = value
        rounded[rows, :] = value.astype(bf16)
    top = jnp.abs(on_resid) * peaks[:, 4:5] + jnp.abs(on_applied) * peaks[:, 5:6] + 1.5
    scale_e = 30000.0 / (2.0 * 6.0 * COLS * BS * top)
    scale_h = 30000.0 / (2.0 * COLS * BS * top * top)
    scales[...] = as_row([scale_e, scale_h, 1.0 / scale_e, 1.0 / scale_h])


def indiv_sums(
    meta, mask_own, mask_far, scales, dense_own, dense_far, rounded_own, rounded_far, pay, grams, diags
):
    core = meta[3]

    @pl.when(core == 0)
    def _():
        scale = scales[0:1, 0:1]
        for r in range(ROWS):
            rows = slice(r * BS, (r + 1) * BS)
            product = jnp.dot(dense_own[rows, :], rounded_own[...], preferred_element_type=f32)
            product += jnp.dot(dense_far[rows, :], rounded_far[...], preferred_element_type=f32)
            pay[r, :BS, :] = scale * product
            pay[r, BS:, :] = jnp.zeros((PAY_I - BS, R), f32)

    @pl.when(core == 1)
    def _():
        scale = scales[0:1, 1:2]
        for k, source in enumerate((rounded_own, rounded_far)):
            for c in range(COLS):
                block = source[c * BS : (c + 1) * BS, :]
                turned = block.astype(f32).T.astype(bf16)
                gram = scale * jnp.dot(turned, block, preferred_element_type=f32)
                mixed, cross, diag = pack(gram)
                at = k * COLS + c
                grams[at, :, :BS] = mixed
                grams[at, :, BS:] = cross
                diags[at : at + 1, :] = diag
        for r in range(ROWS):
            weights = [mask_own[r * COLS + c] for c in range(COLS)]
            weights += [mask_far[r * COLS + c] for c in range(COLS)]
            for piece in range(4):
                rows = slice(piece * 32, (piece + 1) * 32)
                total = weights[0] * grams[0, rows, :]
                for c in range(1, 2 * COLS):
                    total += weights[c] * grams[c, rows, :]
                pay[r, rows, :] = total
            total = weights[0] * diags[0:1, :]
            for c in range(1, 2 * COLS):
                total += weights[c] * diags[c : c + 1, :]
            pay[r, BS:, :] = jnp.zeros((PAY_I - BS, R), f32)
            pay[r, BS : BS + 1, :BS] = total


def exponent_of(peak):
    return jnp.clip(jnp.ceil(jnp.log2(jnp.maximum(peak, 1e-30))), -100.0, 100.0)


def pieces_of(value):
    high = value.astype(bf16).astype(f32)
    rest = (value - high) * 256.0
    middle = rest.astype(bf16).astype(f32)
    return [high, middle, (rest - middle) * 256.0]


def indiv_moments(meta, mine, theirs, start, scales, sent):
    core = meta[3]
    own, far = mine[...], theirs[...]
    data = jnp.where(core == 0, own, far) * scales[0:1, 2:3]
    packed = jnp.where(core == 0, far, own) * scales[0:1, 3:4]
    high, low = split(unpack(packed[:BS, :BS], packed[:BS, BS:], packed[BS : BS + 1, :BS]))
    begin = start[...]
    value = data[:BS, :] - times(begin, high, low) - ridge_weight * begin
    first = times(value, high, low) + ridge_weight * value
    second = times(first, high, low) + ridge_weight * first
    powers = [exponent_of(largest(array)) for array in (value, first, second)]
    value, first, second = (
        array * jnp.exp2(-power) for array, power in zip((value, first, second), powers)
    )
    moments = [
        total_of(value * value),
        total_of(value * first),
        total_of(first * first),
        total_of(first * second),
    ]
    sent[:BS, :] = jnp.where(core == 0, value, first) * 16384.0
    row = as_row([part for moment in moments for part in pieces_of(moment)] + powers)
    sent[BS:, :] = jnp.concatenate([row, row], axis=1)


def chip_moments(lines, moments):
    def moment(k, power):
        parts = [lines[:, 3 * k + j : 3 * k + j + 1] for j in range(3)]
        value = parts[0] + parts[1] * (1.0 / 256.0) + parts[2] * (1.0 / 65536.0)
        return jnp.sum(value * power, axis=0, keepdims=True)

    one, two, three = (jnp.exp2(lines[:, j : j + 1]) for j in (12, 13, 14))
    moments[...] = as_row(
        [
            moment(0, one * one),
            moment(1, one * two),
            moment(2, two * two),
            moment(3, two * three),
        ]
    )


def indiv_shares(meta, lines, own, next1, next2, next3, shares):
    sums = own[0:1, :] + next1[0:1, :] + next2[0:1, :] + next3[0:1, :]
    on_resid, on_applied, _, _ = curve_of(*(sums[:, k : k + 1] for k in range(4)))
    of_resid = on_resid * jnp.exp2(lines[:, 12:13]) * (1.0 / 16384.0)
    of_applied = -on_applied * jnp.exp2(lines[:, 13:14]) * (1.0 / 16384.0)
    core = meta[3]
    lanes = lax.broadcasted_iota(jnp.int32, (ROWS, BS), 1)
    here = jnp.where(core == 0, of_resid, of_applied)
    there = jnp.where(core == 0, of_applied, of_resid)
    shares[...] = jnp.where(lanes == 0, here, there)


def ring(step):
    return [(k, (k + step) % 4) for k in range(4)]


def call(kernel, ins, outs, scratch=(), limit=VMEM_LIMIT):
    return pl.pallas_call(
        kernel,
        out_shape=tuple(jax.ShapeDtypeStruct(shape, dtype) for shape, dtype, _ in outs),
        in_specs=[pl.BlockSpec(memory_space=space) for space in ins],
        out_specs=tuple(pl.BlockSpec(memory_space=space) for _, _, space in outs),
        scratch_shapes=list(scratch),
        compiler_params=pltpu.CompilerParams(vmem_limit_bytes=limit),
    )


def on_device(indiv_factors, variant_factors, dosage_tiles, block_rows, block_cols, live_blocks):
    S, V, H = pltpu.SMEM, pltpu.VMEM, pl.ANY
    live = live_blocks[0, 0]
    me = lax.axis_index("x")
    core = lax.axis_index("c")
    chip = lax.axis_index(CHIP)
    slab = lax.axis_index(GEN)
    part = jnp.where(core == 1, 3 - me, me)
    slabs = 32
    swap = [(0, 1), (1, 0)]
    meta = jnp.stack([live, me, core, core, slab]).astype(jnp.int32)

    own, far, dense, mask = call(
        variant_sums,
        [S, S, S, H, H],
        [
            ((PAY_V, R), f32, V),
            ((3, PAY_V, R), f32, V),
            ((ROWS * BS, COLS * BS), bf16, H),
            ((ROWS * COLS,), f32, S),
        ],
        [
            pltpu.VMEM((NB, BS, BS), bf16),
            pltpu.VMEM((ROWS * BS, R), f32),
            pltpu.VMEM((ROWS * BS, COLS * BS), bf16),
            pltpu.VMEM((R, ROWS * BS), bf16),
            pltpu.VMEM((ROWS, BS, R), bf16),
            pltpu.VMEM((ROWS, BS, R), f32),
            pltpu.VMEM((ROWS, BS), f32),
            pltpu.SemaphoreType.DMA((6,)),
        ],
    )(block_rows, block_cols, meta, dosage_tiles, indiv_factors)
    far = far.astype(f16)
    got = [lax.ppermute(far[k - 1], "x", ring(k)) for k in (1, 2, 3)]
    low = lax.ppermute(variant_factors[-8:], GEN, [(k, k + 1) for k in range(slabs - 1)])
    high = lax.ppermute(variant_factors[:8], GEN, [(k + 1, k) for k in range(slabs - 1)])
    dense_far = lax.ppermute(dense, "c", swap)
    mask_far = lax.ppermute(mask, "c", swap)
    total = own + got[0].astype(f32) + got[1].astype(f32) + got[2].astype(f32)

    def device(position):
        at, place = divmod(position, 4)
        return at * 4 + (3 - place if at % 2 else place)

    line = [device(k) for k in range(4 * slabs)]
    position = slab * 4 + part
    meta_line = jnp.stack(
        [part, (position > 0).astype(jnp.int32), (position < 4 * slabs - 1).astype(jnp.int32)]
    ).astype(jnp.int32)
    square = ((2 * BS, R), f32, V)
    halves = ((2, R, R), bf16, V)
    row = ((8, BS), f32, V)
    ext = pltpu.VMEM((2 * BS + 16, R), f32)
    resid, applied, g_high, g_low, edge = call(
        variant_start,
        [S, V, V, V, V],
        [square, square, halves, halves, ((8, R), f32, V)],
        [ext],
    )(meta_line, total, variant_factors, low, high)
    edge_before = lax.ppermute(edge, ALL, list(zip(line[:-1], line[1:])))
    edge_after = lax.ppermute(edge, ALL, list(zip(line[1:], line[:-1])))
    sent, moments = call(
        variant_moments, [S] + [V] * 7, [((2, 2 * BS, R), f32, V), row], [ext]
    )(meta_line, variant_factors, resid, applied, g_high, g_low, edge_before, edge_after)
    sent = sent.astype(f16)
    pieces = jnp.stack([sent] + [lax.ppermute(sent, "x", ring(k)) for k in (1, 2, 3)])
    table = lax.all_to_all(
        jnp.broadcast_to(moments[None, :1], (4 * slabs, 1, BS)), ALL, 0, 0
    ).reshape(4 * slabs, BS)

    variant_new, rounded, scales = call(
        new_variants,
        [S, V, V, V],
        [((COLS * BS, R), f32, V), ((COLS * BS, R), bf16, V), row],
    )(meta, table, variant_factors, pieces.astype(f32))
    rounded_far = lax.ppermute(rounded, "c", swap)
    (pay,) = call(
        indiv_sums,
        [S, S, S, V, V, V, V, V],
        [((ROWS, PAY_I, R), f32, V)],
        [pltpu.VMEM((ROWS, BS, R), f32), pltpu.VMEM((ROWS, BS), f32)],
    )(meta, mask, mask_far, scales, dense, dense_far, rounded, rounded_far)
    arrived = lax.all_to_all(pay.astype(f16), CHIP, 0, 0)
    mine = jnp.sum(arrived.astype(f32), axis=0)
    theirs = lax.ppermute(mine, "c", swap)
    begin = lax.dynamic_slice_in_dim(indiv_factors, chip * BS, BS, 0)
    (sent,) = call(indiv_moments, [S, V, V, V, V], [((PAY_I, R), f32, V)])(
        meta, mine, theirs, begin, scales
    )
    sent = jnp.broadcast_to(sent.astype(f16)[None], (ROWS, PAY_I, R))
    here = lax.all_to_all(sent, CHIP, 0, 0)
    there = lax.ppermute(here, "c", swap)
    lines = here[:, BS, :BS].astype(f32)
    (moments,) = call(chip_moments, [V], [row])(lines)
    nexts = [lax.ppermute(moments, "x", ring(k)) for k in (1, 2, 3)]
    (shares,) = call(indiv_shares, [S] + [V] * 5, [((ROWS, BS), f32, V)])(
        meta, lines, moments, *nexts
    )
    change = (
        shares[:, 0].reshape(ROWS, 1, 1) * here[:, :BS].astype(f32)
        + shares[:, 1].reshape(ROWS, 1, 1) * there[:, :BS].astype(f32)
    )
    return variant_new, indiv_factors + change.reshape(ROWS * BS, R)


def solution(mesh):
    grid = np.asarray(mesh.devices).reshape(4, 4, 2, 4)
    inner = Mesh(grid, ALL)
    return jax.shard_map(
        on_device,
        mesh=inner,
        in_specs=(
            P("x", None),
            P(GEN, None),
            P(GEN, "x", None, None, None),
            P(GEN, "x", None),
            P(GEN, "x", None),
            P(GEN, "x"),
        ),
        out_specs=(P(GEN, None), P("x", None)),
        check_vma=False,
    )
```

time: 149 us -> 136 us (0.913)
  blocking collectives: 74.3 us -> 43.5 us
  waiting for transfers between devices: 10.5 us -> 28.6 us
  other arithmetic: 10.2 us -> 4.26 us
  Pallas kernels: 16.1 us -> 21 us
  starting transfers between devices: 29.7 us -> 32.1 us
    all_to_all x4 -> x2, blocking collectives: 74.3 us -> 43.5 us  [the longest x1 22.2 us: on_device(): arrived = lax.all_to_all(pay.astype(f16), CHIP, 0, 0)]
    all_to_all x0 -> x1, starting transfers between devices: none -> 11.2 us  [on_device(): lax.all_to_all(jnp.broadcast_to(moments[None, :1], (4 * slabs, 1, BS)), A...]
    all_to_all x0 -> x1, waiting for transfers between devices: none -> 7.05 us  [on_device(): lax.all_to_all(jnp.broadcast_to(moments[None, :1], (4 * slabs, 1, BS)), A...]
    ppermute x11 -> x13, waiting for transfers between devices: 9.16 us -> 16 us  [the longest x3 11.1 us: on_device(): got = [lax.ppermute(far[k - 1], 'x', ring(k)) for k in (1, 2, 3)]]
    pallas_call x6 -> x8, Pallas kernels: 16.1 us -> 21 us  [the longest x1 8.19 us: on_device(): call(variant_sums, [S, S, S, H, H], [((PAY_V, R), f32, V), ((3, PAY_V, R)...]
    ppermute x11 -> x13, starting transfers between devices: 19.7 us -> 15.3 us  [the longest x3 6.26 us: on_device(): lax.ppermute(sent, 'x', ring(k))]
    ppermute x1, waiting for transfers between devices: 0.01 us -> 4.2 us  [on_device(): edge_after = lax.ppermute(edge, ALL, list(zip(line[1:], line[:-1])))]
    ppermute x1, starting transfers between devices: 4.25 us -> 1.47 us  [on_device(): edge_before = lax.ppermute(edge, ALL, list(zip(line[:-1], line[1:])))]
  transfers between devices with their start and end apart: 16 -> 19, of which waited for: 5 -> 10; matrix products, arithmetic and copies ran while one was open for 1% -> 2% of each run, Pallas kernels for 1% -> 4%
where the time goes in v2:
time: 136 us; the launch traced here: 135 us
  blocking collectives  43.5 us (32%)
  starting transfers between devices  32.1 us (24%)
  waiting for transfers between devices  28.6 us (21%)
  Pallas kernels  21 us (15%)
  other arithmetic  4.26 us (3%)
  local copies, waits for them, and re-layouts  4.13 us (3%)
  between operations  1.58 us (1%)
    all_to_all x1, blocking collectives, on_device(): arrived = lax.all_to_all(pay.astype(f16), CHIP, 0, 0)  22.2 us
    all_to_all x1, blocking collectives, on_device(): here = lax.all_to_all(sent, CHIP, 0, 0)  21.3 us
    all_to_all x1, starting transfers between devices, on_device(): lax.all_to_all(jnp.broadcast_to(moments[None, :1], (4 * slabs, 1, BS)), A...  11.2 us
    ppermute x3, waiting for transfers between devices, on_device(): got = [lax.ppermute(far[k - 1], 'x', ring(k)) for k in (1, 2, 3)]  11.1 us
    pallas_call x1, Pallas kernels, on_device(): call(variant_sums, [S, S, S, H, H], [((PAY_V, R), f32, V), ((3, PAY_V, R)...  8.19 us
    all_to_all x1, waiting for transfers between devices, on_device(): lax.all_to_all(jnp.broadcast_to(moments[None, :1], (4 * slabs, 1, BS)), A...  7.05 us
    ppermute x3, starting transfers between devices, on_device(): lax.ppermute(sent, 'x', ring(k))  6.26 us
    pallas_call x1, Pallas kernels, on_device(): call(indiv_sums, [S, S, S, V, V, V, V, V], [((ROWS, PAY_I, R), f32, V)],...  6.23 us
  transfers between devices with their start and end apart: 19, of which 10 were waited for; matrix products, arithmetic and copies ran while one was open for 2% of the time, Pallas kernels for 4%

profile of v2, /device:TPU:0, one launch (start us, length us, event | category | flops | bytes accessed | tf_op | source)
XLA Modules:
  0.0 135.2 jit_solution(2373782082857417522)
XLA Ops:
  1.3 0.1 stack.49.meta
  1.4 1.6 %copy-done.1 = bf16[1,1,64,128,128]{4,3,2,1,0:T(8,128)(2,1)S(1)} copy-done((bf16[1,1,64,128,128]{4,3,2,1,0:T(8,128)(2,1)S(1)}, bf16[1,1,64,128,128]{4,3,2,1,0:T(8,128)(2,1)}, u32[]{:S(2)}) %copy-start.1) | copy-done | bytes 2097176
  3.0 0.7 copy-done.2
  3.6 0.7 copy-done.3
  4.3 8.2 %shard_map.77 = (f32[528,256]{1,0:T(8,128)S(1)}, f32[3,528,256]{2,1,0:T(8,128)S(1)}, bf16[2048,1024]{1,0:T(8,128)(2,1)}, f32[128]{0:T(128)S(1)}) custom-call(s32[1,1,64]{2,1,0:T(1,128)S(1)} %copy-done.2, s32[1,1,64]{2,1,0:T(1,128)S(1)} %copy-done.3, s32[5]{0:T(128)S(1)} %stack.49.meta, bf16[1,1,64,128,128]{4,3,2,1,0:T(8,128)(2,1)S(1)} %copy-done.1, ...), custom_call_target="tpu_custom_call" | custom-call | tf_op jit(solution)/shard_map/pallas_call | solution.py:423
  12.5 0.0 copy-start
  12.5 0.1 collective-permute-start.11
  12.6 0.2 convert_element_type.40
  12.7 0.2 slice_bitcast_fusion.2
  12.9 3.0 %collective-permute-start.2 = (f16[528,256]{1,0:T(8,128)(2,1)S(1)}, f16[528,256]{1,0:T(8,128)(2,1)S(1)}, u32[]{:S(2)}, u32[]{:S(2)}) collective-permute-start(f16[528,256]{1,0:T(8,128)(2,1)S(1)} %get-tuple-element.35), channel_id=1, source_target_pairs={{0,3},{1,0},{2,1},{3,2},{4,7},{5,4},{6,5},{7,6},{8,11},{9,8},{10,9... | collective-permute-start | bytes 811016 | tf_op jit(solution)/shard_map/ppermute | solution.py:444
  15.9 0.9 collective-permute-start.1
  16.8 0.8 collective-permute-start
  17.6 1.5 %collective-permute-start.3 = (f32[8,256]{1,0:T(8,128)S(1)}, f32[8,256]{1,0:T(8,128)S(1)}, u32[]{:S(2)}, u32[]{:S(2)}) collective-permute-start(f32[8,256]{1,0:T(8,128)S(1)} %get-tuple-element.33), channel_id=1, source_target_pairs={{0,4},{4,8},{8,12},{12,16},{16,20},{20,24},{24,28},{28,32},{32,36}... | collective-permute-start | bytes 24584 | tf_op jit(solution)/shard_map/ppermute | solution.py:445
  19.2 0.1 pad_add_fusion.meta
  19.3 8.7 %collective-permute-done.2 = f16[528,256]{1,0:T(8,128)(2,1)S(1)} collective-permute-done((f16[528,256]{1,0:T(8,128)(2,1)S(1)}, f16[528,256]{1,0:T(8,128)(2,1)S(1)}, u32[]{:S(2)}, u32[]{:S(2)}) %collective-permute-start.2) | collective-permute-done | bytes 270368 | tf_op jit(solution)/shard_map/ppermute | solution.py:444
  28.0 1.3 collective-permute-start.4
  29.3 0.0 collective-permute-done.1
  29.3 2.4 %collective-permute-done = f16[528,256]{1,0:T(8,128)(2,1)S(1)} collective-permute-done((f16[528,256]{1,0:T(8,128)(2,1)S(1)}, f16[528,256]{1,0:T(8,128)(2,1)S(1)}, u32[]{:S(2)}, u32[]{:S(2)}) %collective-permute-start) | collective-permute-done | bytes 270368 | tf_op jit(solution)/shard_map/ppermute | solution.py:444
  31.7 0.1 convert_add_fusion.total
  31.8 0.0 collective-permute-done.3.low
  31.8 0.0 collective-permute-done.4.high
  31.9 1.1 shard_map.78
  33.0 1.5 %collective-permute-start.5 = (f32[8,256]{1,0:T(8,128)S(1)}, f32[8,256]{1,0:T(8,128)S(1)}, u32[]{:S(2)}, u32[]{:S(2)}) collective-permute-start(f32[8,256]{1,0:T(8,128)S(1)} %get-tuple-element.22), channel_id=1, source_target_pairs={{0,1},{1,2},{2,3},{3,7},{7,6},{6,5},{5,4},{4,8},{8,9},{9,10},{10,1... | collective-permute-start | bytes 24584 | tf_op jit(solution)/shard_map/ppermute | solution.py:470
  34.5 1.3 collective-permute-start.6
  35.8 0.0 collective-permute-done.5.edge_before
  35.8 4.2 %collective-permute-done.6.edge_after = f32[8,256]{1,0:T(8,128)S(1)} collective-permute-done((f32[8,256]{1,0:T(8,128)S(1)}, f32[8,256]{1,0:T(8,128)S(1)}, u32[]{:S(2)}, u32[]{:S(2)}) %collective-permute-start.6) | collective-permute-done | bytes 8224 | tf_op jit(solution)/shard_map/ppermute | solution.py:471
  40.0 1.1 shard_map.79
  41.2 3.1 %collective-permute-start.9 = (f16[2,256,256]{2,1,0:T(8,128)(2,1)S(1)}, f16[2,256,256]{2,1,0:T(8,128)(2,1)S(1)}, u32[]{:S(2)}, u32[]{:S(2)}) collective-permute-start(f16[2,256,256]{2,1,0:T(8,128)(2,1)S(1)} %convert_element_type.44), channel_id=1, source_target_pairs={{0,3},{1,0},{2,1},{3,2},{4,7},{5,4},{6,5},{7,6},{8,11},{9,8},{10,9... | collective-permute-start | bytes 786440 | tf_op jit(solution)/shard_map/ppermute | solution.py:476
  44.3 1.8 %collective-permute-start.8 = (f16[2,256,256]{2,1,0:T(8,128)(2,1)S(1)}, f16[2,256,256]{2,1,0:T(8,128)(2,1)}, u32[]{:S(2)}, u32[]{:S(2)}) collective-permute-start(f16[2,256,256]{2,1,0:T(8,128)(2,1)S(1)} %convert_element_type.44), channel_id=1, source_target_pairs={{0,2},{1,3},{2,0},{3,1},{4,6},{5,7},{6,4},{7,5},{8,10},{9,11},{10,... | collective-permute-start | bytes 786440 | tf_op jit(solution)/shard_map/ppermute | solution.py:476
  46.1 1.3 collective-permute-start.7
  47.4 0.7 broadcast_in_dim.7
  48.1 11.2 %all-to-all-start = ((f32[128,1,128]{2,1,0:T(1,128)}), f32[128,1,128]{2,1,0:T(1,128)S(1)}, u32[]{:S(2)}, u32[]{:S(2)}) async-start(f32[128,1,128]{2,1,0:T(1,128)} %broadcast_in_dim.7), calls=%async_computation | async-start | bytes 131072 | tf_op jit(solution)/shard_map/all_to_all | solution.py:477
  59.3 0.0 collective-permute-done.9
  59.3 0.0 collective-permute-done.8
  59.3 0.9 collective-permute-done.7
  60.2 1.3 maximum_convert_fusion.pieces
  61.5 7.0 %all-to-all-done = f32[128,1,128]{2,1,0:T(1,128)S(1)} async-done(((f32[128,1,128]{2,1,0:T(1,128)}), f32[128,1,128]{2,1,0:T(1,128)S(1)}, u32[]{:S(2)}, u32[]{:S(2)}) %all-to-all-start) | async-done | bytes 65568 | tf_op jit(solution)/shard_map/all_to_all | solution.py:477
  68.5 2.0 %shard_map.80 = (f32[1024,256]{1,0:T(8,128)}, bf16[1024,256]{1,0:T(8,128)(2,1)S(1)}, f32[8,128]{1,0:T(8,128)S(1)}) custom-call(s32[5]{0:T(128)S(1)} %stack.49.meta, f32[128,128]{1,0:T(8,128)S(1)} %bitcast.29, f32[1024,256]{1,0:T(8,128)S(1)} %copy-done, f32[4,2,256,256]{3,2,1,0:T(8,128)S(1)} %maximum_convert_fusion.pieces), custom_call_target="tpu_custom_call" | custom-call | tf_op jit(solution)/shard_map/pallas_call | solution.py:481
  70.5 0.0 collective-permute-start.12
  70.5 0.5 collective-permute-start.10
  71.0 1.4 %collective-permute-done.10.mask_far = f32[128]{0:T(128)S(1)} collective-permute-done((f32[128]{0:T(128)S(1)}, f32[128]{0:T(128)S(1)}, u32[]{:S(2)}, u32[]{:S(2)}) %collective-permute-start.10) | collective-permute-done | bytes 544 | tf_op jit(solution)/shard_map/ppermute | solution.py:448
  72.4 0.0 collective-permute-done.12.rounded_far
  72.4 0.0 collective-permute-done.11.dense_far
  72.4 6.2 %shard_map.81 = f32[16,136,256]{2,1,0:T(8,128)S(1)} custom-call(s32[5]{0:T(128)S(1)} %stack.49.meta, f32[128]{0:T(128)S(1)} %get-tuple-element.26.mask_own, f32[128]{0:T(128)S(1)} %collective-permute-done.10.mask_far, f32[8,128]{1,0:T(8,128)S(1)} %get-tuple-element.27.scales, bf16[2048,1024]{1,0:T(8,128)(2,1)} %get-tuple-element.28.dense_own, ...), custom_call_target="tpu_custom_call" | custom-call | tf_op jit(solution)/shard_map/pallas_call | solution.py:487
  78.7 0.2 convert_element_type.46
  78.8 0.0 copy-start.4
  78.8 22.2 %all_to_all.15 = f16[16,136,256]{2,1,0:T(8,128)(2,1)S(1)} all-to-all(f16[16,136,256]{2,1,0:T(8,128)(2,1)S(1)} %convert_element_type.46), channel_id=1, replica_groups=mesh['z'=4,'y'=4,'c'=2,'x'=4] {'z','y'}, dimensions={0} | all-to-all | bytes 2228224 | tf_op jit(solution)/shard_map/all_to_all | solution.py:493
  101.1 0.2 convert_reduce_fusion.mine
  101.2 0.1 collective-permute-start.13
  101.4 1.3 collective-permute-done.13.theirs
  102.7 1.4 %shard_map.82 = f32[136,256]{1,0:T(8,128)S(1)} custom-call(s32[5]{0:T(128)S(1)} %stack.49.meta, f32[136,256]{1,0:T(8,128)S(1)} %convert_reduce_fusion.mine, f32[136,256]{1,0:T(8,128)S(1)} %collective-permute-done.13.theirs, f32[128,256]{1,0:T(8,128)S(1)} %constant_dynamic-slice_fusion.start, f32[8,128]{1,0:T(8,128)S(1)} %get-tuple-element.27.scales), custom_call_target="tpu_custom_call" | custom-call | tf_op jit(solution)/shard_map/pallas_call | solution.py:497
  104.1 0.1 broadcast_in_dim.16
  104.2 21.3 %all_to_all.16 = f16[16,136,256]{2,1,0:T(8,128)(2,1)S(1)} all-to-all(f16[16,136,256]{2,1,0:T(8,128)(2,1)S(1)} %broadcast_in_dim.16), channel_id=1, replica_groups=mesh['z'=4,'y'=4,'c'=2,'x'=4] {'z','y'}, dimensions={0} | all-to-all | bytes 2228224 | tf_op jit(solution)/shard_map/all_to_all | solution.py:501
  125.6 0.2 shard_map.83.own
  125.8 0.4 collective-permute-start.14
  126.2 2.3 %collective-permute-start.15 = (f32[8,128]{1,0:T(8,128)S(1)}, f32[8,128]{1,0:T(8,128)S(1)}, u32[]{:S(2)}, u32[]{:S(2)}) collective-permute-start(f32[8,128]{1,0:T(8,128)S(1)} %shard_map.83.own), channel_id=1, source_target_pairs={{0,2},{1,3},{2,0},{3,1},{4,6},{5,7},{6,4},{7,5},{8,10},{9,11},{10,... | collective-permute-start | bytes 12296 | tf_op jit(solution)/shard_map/ppermute | solution.py:505
  128.5 1.0 collective-permute-start.16
  129.5 1.1 collective-permute-done.14.next1
  130.6 0.7 collective-permute-done.15.next2
  131.3 0.8 collective-permute-done.16.next3
  132.1 0.7 shard_map.84
  132.8 0.2 slice_reduce_fusion.1
  133.0 0.5 multiply_add_fusion
  133.5 1.8 %bitcast_add_fusion = f32[2048,256]{1,0:T(8,128)} fusion(f32[2048,256]{1,0:T(8,128)S(1)} %copy-done.4, f32[16,128,256]{2,1,0:T(8,128)S(1)} %multiply_add_fusion), kind=kLoop, calls=%fused_computation.1 | loop fusion | flops 524288 | bytes 6291456 | tf_op jit(solution)/shard_map/add | solution.py:513
  (15 shorter events, 0.1 us)
Async XLA Ops:
  1.4 1.6 %copy-start.1 = (bf16[1,1,64,128,128]{4,3,2,1,0:T(8,128)(2,1)S(1)}, bf16[1,1,64,128,128]{4,3,2,1,0:T(8,128)(2,1)}, u32[]{:S(2)}) copy-start(bf16[1,1,64,128,128]{4,3,2,1,0:T(8,128)(2,1)} %tiles_hbm.1) | copy-start | bytes 6291460
  3.0 0.7 copy-start.2
  3.6 0.7 copy-start.3
  12.5 5.2 %copy-start = (f32[1024,256]{1,0:T(8,128)S(1)}, f32[1024,256]{1,0:T(8,128)}, u32[]{:S(2)}) copy-start(f32[1024,256]{1,0:T(8,128)} %start.5) | copy-start | bytes 3145732
  12.5 59.9 %collective-permute-start.11 = (bf16[2048,1024]{1,0:T(8,128)(2,1)}, bf16[2048,1024]{1,0:T(8,128)(2,1)}, u32[]{:S(2)}, u32[]{:S(2)}) collective-permute-start(bf16[2048,1024]{1,0:T(8,128)(2,1)} %get-tuple-element.28.dense_own), channel_id=1, source_target_pairs={{0,4},{4,0},{1,5},{5,1},{2,6},{6,2},{3,7},{7,3},{8,12},{12,8},{9,1... | collective-permute-start | bytes 12582920 | tf_op jit(solution)/shard_map/ppermute | solution.py:447
  12.9 15.1 %collective-permute-start.2 = (f16[528,256]{1,0:T(8,128)(2,1)S(1)}, f16[528,256]{1,0:T(8,128)(2,1)S(1)}, u32[]{:S(2)}, u32[]{:S(2)}) collective-permute-start(f16[528,256]{1,0:T(8,128)(2,1)S(1)} %get-tuple-element.35), channel_id=1, source_target_pairs={{0,3},{1,0},{2,1},{3,2},{4,7},{5,4},{6,5},{7,6},{8,11},{9,8},{10,9... | collective-permute-start | bytes 811016 | tf_op jit(solution)/shard_map/ppermute | solution.py:444
  15.9 13.4 %collective-permute-start.1 = (f16[528,256]{1,0:T(8,128)(2,1)S(1)}, f16[528,256]{1,0:T(8,128)(2,1)S(1)}, u32[]{:S(2)}, u32[]{:S(2)}) collective-permute-start(f16[528,256]{1,0:T(8,128)(2,1)S(1)} %get-tuple-element.36), channel_id=1, source_target_pairs={{0,2},{1,3},{2,0},{3,1},{4,6},{5,7},{6,4},{7,5},{8,10},{9,11},{10,... | collective-permute-start | bytes 811016 | tf_op jit(solution)/shard_map/ppermute | solution.py:444
  16.8 14.9 %collective-permute-start = (f16[528,256]{1,0:T(8,128)(2,1)S(1)}, f16[528,256]{1,0:T(8,128)(2,1)S(1)}, u32[]{:S(2)}, u32[]{:S(2)}) collective-permute-start(f16[528,256]{1,0:T(8,128)(2,1)S(1)} %get-tuple-element.34), channel_id=1, source_target_pairs={{0,1},{1,2},{2,3},{3,0},{4,5},{5,6},{6,7},{7,4},{8,9},{9,10},{10,1... | collective-permute-start | bytes 811016 | tf_op jit(solution)/shard_map/ppermute | solution.py:444
  17.6 14.2 %collective-permute-start.3 = (f32[8,256]{1,0:T(8,128)S(1)}, f32[8,256]{1,0:T(8,128)S(1)}, u32[]{:S(2)}, u32[]{:S(2)}) collective-permute-start(f32[8,256]{1,0:T(8,128)S(1)} %get-tuple-element.33), channel_id=1, source_target_pairs={{0,4},{4,8},{8,12},{12,16},{16,20},{20,24},{24,28},{28,32},{32,36}... | collective-permute-start | bytes 24584 | tf_op jit(solution)/shard_map/ppermute | solution.py:445
  28.0 3.8 %collective-permute-start.4 = (f32[8,256]{1,0:T(8,128)S(1)}, f32[8,256]{1,0:T(8,128)S(1)}, u32[]{:S(2)}, u32[]{:S(2)}) collective-permute-start(f32[8,256]{1,0:T(8,128)S(1)} %get-tuple-element.32), channel_id=1, source_target_pairs={{4,0},{8,4},{12,8},{16,12},{20,16},{24,20},{28,24},{32,28},{36,32}... | collective-permute-start | bytes 24584 | tf_op jit(solution)/shard_map/ppermute | solution.py:446
  33.0 2.8 %collective-permute-start.5 = (f32[8,256]{1,0:T(8,128)S(1)}, f32[8,256]{1,0:T(8,128)S(1)}, u32[]{:S(2)}, u32[]{:S(2)}) collective-permute-start(f32[8,256]{1,0:T(8,128)S(1)} %get-tuple-element.22), channel_id=1, source_target_pairs={{0,1},{1,2},{2,3},{3,7},{7,6},{6,5},{5,4},{4,8},{8,9},{9,10},{10,1... | collective-permute-start | bytes 24584 | tf_op jit(solution)/shard_map/ppermute | solution.py:470
  34.5 5.5 %collective-permute-start.6 = (f32[8,256]{1,0:T(8,128)S(1)}, f32[8,256]{1,0:T(8,128)S(1)}, u32[]{:S(2)}, u32[]{:S(2)}) collective-permute-start(f32[8,256]{1,0:T(8,128)S(1)} %get-tuple-element.22), channel_id=1, source_target_pairs={{1,0},{2,1},{3,2},{7,3},{6,7},{5,6},{4,5},{8,4},{9,8},{10,9},{11,1... | collective-permute-start | bytes 24584 | tf_op jit(solution)/shard_map/ppermute | solution.py:471
  41.2 18.1 %collective-permute-start.9 = (f16[2,256,256]{2,1,0:T(8,128)(2,1)S(1)}, f16[2,256,256]{2,1,0:T(8,128)(2,1)S(1)}, u32[]{:S(2)}, u32[]{:S(2)}) collective-permute-start(f16[2,256,256]{2,1,0:T(8,128)(2,1)S(1)} %convert_element_type.44), channel_id=1, source_target_pairs={{0,3},{1,0},{2,1},{3,2},{4,7},{5,4},{6,5},{7,6},{8,11},{9,8},{10,9... | collective-permute-start | bytes 786440 | tf_op jit(solution)/shard_map/ppermute | solution.py:476
  44.3 15.0 %collective-permute-start.8 = (f16[2,256,256]{2,1,0:T(8,128)(2,1)S(1)}, f16[2,256,256]{2,1,0:T(8,128)(2,1)}, u32[]{:S(2)}, u32[]{:S(2)}) collective-permute-start(f16[2,256,256]{2,1,0:T(8,128)(2,1)S(1)} %convert_element_type.44), channel_id=1, source_target_pairs={{0,2},{1,3},{2,0},{3,1},{4,6},{5,7},{6,4},{7,5},{8,10},{9,11},{10,... | collective-permute-start | bytes 786440 | tf_op jit(solution)/shard_map/ppermute | solution.py:476
  46.1 14.1 %collective-permute-start.7 = (f16[2,256,256]{2,1,0:T(8,128)(2,1)S(1)}, f16[2,256,256]{2,1,0:T(8,128)(2,1)}, u32[]{:S(2)}, u32[]{:S(2)}) collective-permute-start(f16[2,256,256]{2,1,0:T(8,128)(2,1)S(1)} %convert_element_type.44), channel_id=1, source_target_pairs={{0,1},{1,2},{2,3},{3,0},{4,5},{5,6},{6,7},{7,4},{8,9},{9,10},{10,1... | collective-permute-start | bytes 786440 | tf_op jit(solution)/shard_map/ppermute | solution.py:476
  48.1 20.4 %all-to-all-start = ((f32[128,1,128]{2,1,0:T(1,128)}), f32[128,1,128]{2,1,0:T(1,128)S(1)}, u32[]{:S(2)}, u32[]{:S(2)}) async-start(f32[128,1,128]{2,1,0:T(1,128)} %broadcast_in_dim.7), calls=%async_computation | async-start | bytes 131072 | tf_op jit(solution)/shard_map/all_to_all | solution.py:477
  70.5 1.9 %collective-permute-start.12 = (bf16[1024,256]{1,0:T(8,128)(2,1)S(1)}, bf16[1024,256]{1,0:T(8,128)(2,1)S(1)}, u32[]{:S(2)}, u32[]{:S(2)}) collective-permute-start(bf16[1024,256]{1,0:T(8,128)(2,1)S(1)} %get-tuple-element.29.rounded_own), channel_id=1, source_target_pairs={{0,4},{4,0},{1,5},{5,1},{2,6},{6,2},{3,7},{7,3},{8,12},{12,8},{9,1... | collective-permute-start | bytes 1572872 | tf_op jit(solution)/shard_map/ppermute | solution.py:486
  70.5 1.9 %collective-permute-start.10 = (f32[128]{0:T(128)S(1)}, f32[128]{0:T(128)S(1)}, u32[]{:S(2)}, u32[]{:S(2)}) collective-permute-start(f32[128]{0:T(128)S(1)} %get-tuple-element.26.mask_own), channel_id=1, source_target_pairs={{0,4},{4,0},{1,5},{5,1},{2,6},{6,2},{3,7},{7,3},{8,12},{12,8},{9,1... | collective-permute-start | bytes 1544 | tf_op jit(solution)/shard_map/ppermute | solution.py:448
  78.8 22.5 %copy-start.4 = (f32[2048,256]{1,0:T(8,128)S(1)}, f32[2048,256]{1,0:T(8,128)}, u32[]{:S(2)}) copy-start(f32[2048,256]{1,0:T(8,128)} %factors_hbm.1) | copy-start | bytes 6291460
  101.2 1.4 %collective-permute-start.13 = (f32[136,256]{1,0:T(8,128)S(1)}, f32[136,256]{1,0:T(8,128)S(1)}, u32[]{:S(2)}, u32[]{:S(2)}) collective-permute-start(f32[136,256]{1,0:T(8,128)S(1)} %convert_reduce_fusion.mine), channel_id=1, source_target_pairs={{0,4},{4,0},{1,5},{5,1},{2,6},{6,2},{3,7},{7,3},{8,12},{12,8},{9,1... | collective-permute-start | bytes 417800 | tf_op jit(solution)/shard_map/ppermute | solution.py:495
  125.5 7.5 %collective-permute-start.17 = (f16[16,136,256]{2,1,0:T(8,128)(2,1)S(1)}, f16[16,136,256]{2,1,0:T(8,128)(2,1)S(1)}, u32[]{:S(2)}, u32[]{:S(2)}) collective-permute-start(f16[16,136,256]{2,1,0:T(8,128)(2,1)S(1)} %all_to_all.16), channel_id=1, source_target_pairs={{0,4},{4,0},{1,5},{5,1},{2,6},{6,2},{3,7},{7,3},{8,12},{12,8},{9,1... | collective-permute-start | bytes 3342344 | tf_op jit(solution)/shard_map/ppermute | solution.py:502
  125.8 4.8 %collective-permute-start.14 = (f32[8,128]{1,0:T(8,128)S(1)}, f32[8,128]{1,0:T(8,128)S(1)}, u32[]{:S(2)}, u32[]{:S(2)}) collective-permute-start(f32[8,128]{1,0:T(8,128)S(1)} %shard_map.83.own), channel_id=1, source_target_pairs={{0,1},{1,2},{2,3},{3,0},{4,5},{5,6},{6,7},{7,4},{8,9},{9,10},{10,1... | collective-permute-start | bytes 12296 | tf_op jit(solution)/shard_map/ppermute | solution.py:505
  126.2 5.1 %collective-permute-start.15 = (f32[8,128]{1,0:T(8,128)S(1)}, f32[8,128]{1,0:T(8,128)S(1)}, u32[]{:S(2)}, u32[]{:S(2)}) collective-permute-start(f32[8,128]{1,0:T(8,128)S(1)} %shard_map.83.own), channel_id=1, source_target_pairs={{0,2},{1,3},{2,0},{3,1},{4,6},{5,7},{6,4},{7,5},{8,10},{9,11},{10,... | collective-permute-start | bytes 12296 | tf_op jit(solution)/shard_map/ppermute | solution.py:505
  128.5 3.6 %collective-permute-start.16 = (f32[8,128]{1,0:T(8,128)S(1)}, f32[8,128]{1,0:T(8,128)S(1)}, u32[]{:S(2)}, u32[]{:S(2)}) collective-permute-start(f32[8,128]{1,0:T(8,128)S(1)} %shard_map.83.own), channel_id=1, source_target_pairs={{0,3},{1,0},{2,1},{3,2},{4,7},{5,4},{6,5},{7,6},{8,11},{9,8},{10,9... | collective-permute-start | bytes 12296 | tf_op jit(solution)/shard_map/ppermute | solution.py:505

commit v3 on v2

--- a/solution.py
+++ b/solution.py
@@ -20,7 +20,7 @@
 CHIP = ("z", "y")
 PAY_V = 2 * BS + 2 * BS + 16
 PAY_I = BS + 8
-VMEM_LIMIT = 48 * 1024 * 1024
+VMEM_LIMIT = 16 * 1024 * 1024
 
 
 def row_col():
@@ -60,7 +60,7 @@
     )
 
 
-def set_mask(row_ids, col_ids, live, mask):
+def set_mask(ids, mask):
     def clear(k, carry):
         mask[k] = 0.0
         return carry
@@ -68,17 +68,27 @@
     lax.fori_loop(0, ROWS * COLS, clear, 0)
 
     def mark(s, carry):
-        mask[row_ids[0, 0, s] * COLS + col_ids[0, 0, s]] = 1.0
+        mask[ids[s] * COLS + ids[NB + s]] = 1.0
         return carry
 
-    lax.fori_loop(0, live, mark, 0)
+    lax.fori_loop(0, ids[2 * NB], mark, 0)
+
+
+def fill(ids, tiles, dense):
+    def scatter(s, carry):
+        rows = pl.ds(pl.multiple_of(ids[s] * BS, BS), BS)
+        cols = pl.ds(pl.multiple_of(ids[NB + s] * BS, BS), BS)
+        dense[rows, cols] = tiles[s]
+        return carry
+
+    lax.fori_loop(0, ids[2 * NB], scatter, 0)
 
 
 def variant_sums(
-    row_ids, col_ids, meta, tiles_hbm, factors_hbm, own, far, dense_hbm, mask,
+    ids, meta, tiles_hbm, factors_hbm, own, far, mask,
     tiles, factors, dense, turned, rounded, grams, diags, sems,
 ):
-    live, me, odd = meta[0], meta[1], meta[2]
+    me, odd = meta[0], meta[1]
     quarter = ROWS * BS // 4
     loads = [
         pltpu.make_async_copy(
@@ -93,7 +103,7 @@
         load.start()
     load_tiles.start()
     dense[...] = jnp.zeros_like(dense)
-    set_mask(row_ids, col_ids, live, mask)
+    set_mask(ids, mask)
     for r in range(ROWS):
         if r % 4 == 0:
             loads[r // 4].wait()
@@ -106,16 +116,7 @@
         grams[r, :, BS:] = cross
         diags[r : r + 1, :] = diag
     load_tiles.wait()
-
-    def scatter(s, carry):
-        rows = pl.ds(pl.multiple_of(row_ids[0, 0, s] * BS, BS), BS)
-        cols = pl.ds(pl.multiple_of(col_ids[0, 0, s] * BS, BS), BS)
-        dense[rows, cols] = tiles[s]
-        return carry
-
-    lax.fori_loop(0, live, scatter, 0)
-    keep = pltpu.make_async_copy(dense, dense_hbm, sems.at[5])
-    keep.start()
+    fill(ids, tiles, dense)
     zero = jnp.zeros((16, R), f32)
     for k in range(4):
         at = lax.rem(me + k, 4)
@@ -138,7 +139,6 @@
             for r in range(1, ROWS):
                 total += weights[r] * diags[r : r + 1, :]
             out[4 * BS + j : 4 * BS + j + 1, :BS] = total
-    keep.wait()
 
 
 def band_of(values, before, after, ext):
@@ -258,15 +258,25 @@
     )
 
 
-def new_variants(meta, table, start, pieces, new, rounded, scales):
-    me, odd, slab = meta[1], meta[2], meta[4]
+def new_variants(
+    meta, ids, table, start, pieces, tiles_hbm, new_hbm, rounded, scales, dense, new, tiles, sems
+):
+    me, core, slab = meta[0], meta[1], meta[2]
+    load = pltpu.make_async_copy(tiles_hbm.at[0, 0], tiles, sems.at[4])
+    load.start()
+
+    @pl.when(core == 1)
+    def _():
+        dense[...] = jnp.zeros_like(dense)
+
     sums = jnp.sum(table[...], axis=0, keepdims=True)
     peaks = jnp.max(table[...], axis=0, keepdims=True)
     on_resid, on_applied, _, _ = curve_of(*(sums[:, k : k + 1] for k in range(4)))
     n = 2 * BS
+    keeps = []
     for k in range(4):
         owner = lax.rem(me - k + 4, 4)
-        part = jnp.where(odd == 1, 3 - owner, owner)
+        part = jnp.where(core == 1, 3 - owner, owner)
         rows = pl.ds(pl.multiple_of(part * n, n), n)
         line = table[pl.ds(slab * 4 + owner, 1), :]
         on_start, near, far, unit_value, unit_guess = (line[:, j : j + 1] for j in range(6, 11))
@@ -278,54 +288,85 @@
         )
         new[rows, :] = value
         rounded[rows, :] = value.astype(bf16)
+        keep = pltpu.make_async_copy(new.at[rows, :], new_hbm.at[rows, :], sems.at[k])
+        keep.start()
+        keeps.append(keep)
     top = jnp.abs(on_resid) * peaks[:, 4:5] + jnp.abs(on_applied) * peaks[:, 5:6] + 1.5
     scale_e = 30000.0 / (2.0 * 6.0 * COLS * BS * top)
     scale_h = 30000.0 / (2.0 * COLS * BS * top * top)
     scales[...] = as_row([scale_e, scale_h, 1.0 / scale_e, 1.0 / scale_h])
-
-
-def indiv_sums(
-    meta, mask_own, mask_far, scales, dense_own, dense_far, rounded_own, rounded_far, pay, grams, diags
-):
-    core = meta[3]
-
-    @pl.when(core == 0)
-    def _():
-        scale = scales[0:1, 0:1]
-        for r in range(ROWS):
-            rows = slice(r * BS, (r + 1) * BS)
-            product = jnp.dot(dense_own[rows, :], rounded_own[...], preferred_element_type=f32)
-            product += jnp.dot(dense_far[rows, :], rounded_far[...], preferred_element_type=f32)
-            pay[r, :BS, :] = scale * product
-            pay[r, BS:, :] = jnp.zeros((PAY_I - BS, R), f32)
+    load.wait()
 
     @pl.when(core == 1)
     def _():
-        scale = scales[0:1, 1:2]
-        for k, source in enumerate((rounded_own, rounded_far)):
-            for c in range(COLS):
-                block = source[c * BS : (c + 1) * BS, :]
-                turned = block.astype(f32).T.astype(bf16)
-                gram = scale * jnp.dot(turned, block, preferred_element_type=f32)
-                mixed, cross, diag = pack(gram)
-                at = k * COLS + c
-                grams[at, :, :BS] = mixed
-                grams[at, :, BS:] = cross
-                diags[at : at + 1, :] = diag
-        for r in range(ROWS):
-            weights = [mask_own[r * COLS + c] for c in range(COLS)]
-            weights += [mask_far[r * COLS + c] for c in range(COLS)]
-            for piece in range(4):
-                rows = slice(piece * 32, (piece + 1) * 32)
-                total = weights[0] * grams[0, rows, :]
-                for c in range(1, 2 * COLS):
-                    total += weights[c] * grams[c, rows, :]
-                pay[r, rows, :] = total
-            total = weights[0] * diags[0:1, :]
-            for c in range(1, 2 * COLS):
-                total += weights[c] * diags[c : c + 1, :]
-            pay[r, BS:, :] = jnp.zeros((PAY_I - BS, R), f32)
-            pay[r, BS : BS + 1, :BS] = total
+        fill(ids, tiles, dense)
+
+    for keep in keeps:
+        keep.wait()
+
+
+def tile_sums(scale, dense, rounded, pay):
+    for r in range(ROWS):
+        product = jnp.dot(
+            dense[r * BS : (r + 1) * BS, :], rounded[...], preferred_element_type=f32
+        )
+        pay[r, :BS, :] = scale * product
+        pay[r, BS:, :] = jnp.zeros((PAY_I - BS, R), f32)
+
+
+def gram_sums(scale, mask, rounded, pay, grams, diags):
+    for c in range(COLS):
+        block = rounded[c * BS : (c + 1) * BS, :]
+        turned = block.astype(f32).T.astype(bf16)
+        gram = scale * jnp.dot(turned, block, preferred_element_type=f32)
+        mixed, cross, diag = pack(gram)
+        grams[c, :, :BS] = mixed
+        grams[c, :, BS:] = cross
+        diags[c : c + 1, :] = diag
+    lines = lax.broadcasted_iota(jnp.int32, (PAY_I - BS, R), 0)
+    for r in range(ROWS):
+        weights = [mask[r * COLS + c] for c in range(COLS)]
+        for piece in range(4):
+            rows = slice(piece * 32, (piece + 1) * 32)
+            total = weights[0] * grams[0, rows, :]
+            for c in range(1, COLS):
+                total += weights[c] * grams[c, rows, :]
+            pay[r, rows, :] = total
+        total = weights[0] * diags[0:1, :]
+        for c in range(1, COLS):
+            total += weights[c] * diags[c : c + 1, :]
+        row = jnp.concatenate([total, jnp.zeros((1, BS), f32)], axis=1)
+        pay[r, BS:, :] = jnp.where(lines == 0, row, 0.0)
+
+
+def sums_to_send(meta, mask, scales, dense, rounded, pay, grams, diags):
+    @pl.when(meta[1] == 1)
+    def _():
+        tile_sums(scales[0:1, 0:1], dense, rounded, pay)
+
+    @pl.when(meta[1] == 0)
+    def _():
+        gram_sums(scales[0:1, 1:2], mask, rounded, pay, grams, diags)
+
+
+def sums_to_keep(meta, ids, mask, scales, rounded, tiles_hbm, pay, dense, tiles, grams, diags, sem):
+    load = pltpu.make_async_copy(tiles_hbm.at[0, 0], tiles, sem)
+    load.start()
+
+    @pl.when(meta[1] == 0)
+    def _():
+        dense[...] = jnp.zeros_like(dense)
+
+    load.wait()
+
+    @pl.when(meta[1] == 0)
+    def _():
+        fill(ids, tiles, dense)
+        tile_sums(scales[0:1, 0:1], dense, rounded, pay)
+
+    @pl.when(meta[1] == 1)
+    def _():
+        gram_sums(scales[0:1, 1:2], mask, rounded, pay, grams, diags)
 
 
 def exponent_of(peak):
@@ -340,7 +381,7 @@
 
 
 def indiv_moments(meta, mine, theirs, start, scales, sent):
-    core = meta[3]
+    core = meta[1]
     own, far = mine[...], theirs[...]
     data = jnp.where(core == 0, own, far) * scales[0:1, 2:3]
     packed = jnp.where(core == 0, far, own) * scales[0:1, 3:4]
@@ -386,7 +427,7 @@
     on_resid, on_applied, _, _ = curve_of(*(sums[:, k : k + 1] for k in range(4)))
     of_resid = on_resid * jnp.exp2(lines[:, 12:13]) * (1.0 / 16384.0)
     of_applied = -on_applied * jnp.exp2(lines[:, 13:14]) * (1.0 / 16384.0)
-    core = meta[3]
+    core = meta[1]
     lanes = lax.broadcasted_iota(jnp.int32, (ROWS, BS), 1)
     here = jnp.where(core == 0, of_resid, of_applied)
     there = jnp.where(core == 0, of_applied, of_resid)
@@ -397,20 +438,32 @@
     return [(k, (k + step) % 4) for k in range(4)]
 
 
-def call(kernel, ins, outs, scratch=(), limit=VMEM_LIMIT):
-    return pl.pallas_call(
-        kernel,
-        out_shape=tuple(jax.ShapeDtypeStruct(shape, dtype) for shape, dtype, _ in outs),
-        in_specs=[pl.BlockSpec(memory_space=space) for space in ins],
-        out_specs=tuple(pl.BlockSpec(memory_space=space) for _, _, space in outs),
-        scratch_shapes=list(scratch),
-        compiler_params=pltpu.CompilerParams(vmem_limit_bytes=limit),
-    )
+def call(kernel, ins, outs, scratch=(), nbytes=1 << 20):
+    def placed(shape, dtype, space):
+        if space == pltpu.SMEM:
+            return jax.ShapeDtypeStruct(shape, dtype)
+        return space(shape, dtype)
+
+    def run(*operands):
+        operands = [
+            pltpu.with_memory_space_constraint(x, pltpu.HBM) if space == pltpu.HBM else x
+            for x, space in zip(operands, ins)
+        ]
+        return pl.pallas_call(
+            kernel,
+            out_shape=tuple(placed(*out) for out in outs),
+            in_specs=[pl.BlockSpec(memory_space=space) for space in ins],
+            out_specs=tuple(pl.BlockSpec(memory_space=out[2]) for out in outs),
+            scratch_shapes=list(scratch),
+            compiler_params=pltpu.CompilerParams(vmem_limit_bytes=VMEM_LIMIT),
+            cost_estimate=pl.CostEstimate(flops=0, bytes_accessed=nbytes, transcendentals=0),
+        )(*operands)
+
+    return run
 
 
 def on_device(indiv_factors, variant_factors, dosage_tiles, block_rows, block_cols, live_blocks):
-    S, V, H = pltpu.SMEM, pltpu.VMEM, pl.ANY
-    live = live_blocks[0, 0]
+    S, V, H = pltpu.SMEM, pltpu.VMEM, pltpu.HBM
     me = lax.axis_index("x")
     core = lax.axis_index("c")
     chip = lax.axis_index(CHIP)
@@ -418,36 +471,32 @@
     part = jnp.where(core == 1, 3 - me, me)
     slabs = 32
     swap = [(0, 1), (1, 0)]
-    meta = jnp.stack([live, me, core, core, slab]).astype(jnp.int32)
-
-    own, far, dense, mask = call(
+    meta = jnp.stack([me, core, slab]).astype(jnp.int32)
+    ids = jnp.concatenate([block_rows[0, 0], block_cols[0, 0], live_blocks[0]])
+
+    big = pltpu.VMEM((NB, BS, BS), bf16)
+    flags = ((ROWS * COLS,), f32, S)
+    own, far, mask = call(
         variant_sums,
-        [S, S, S, H, H],
+        [S, S, H, H],
+        [((PAY_V, R), f32, V), ((3, PAY_V, R), f32, V), flags],
         [
-            ((PAY_V, R), f32, V),
-            ((3, PAY_V, R), f32, V),
-            ((ROWS * BS, COLS * BS), bf16, H),
-            ((ROWS * COLS,), f32, S),
-        ],
-        [
-            pltpu.VMEM((NB, BS, BS), bf16),
+            big,
             pltpu.VMEM((ROWS * BS, R), f32),
             pltpu.VMEM((ROWS * BS, COLS * BS), bf16),
             pltpu.VMEM((R, ROWS * BS), bf16),
             pltpu.VMEM((ROWS, BS, R), bf16),
             pltpu.VMEM((ROWS, BS, R), f32),
             pltpu.VMEM((ROWS, BS), f32),
-            pltpu.SemaphoreType.DMA((6,)),
+            pltpu.SemaphoreType.DMA((5,)),
         ],
-    )(block_rows, block_cols, meta, dosage_tiles, indiv_factors)
+        20 << 20,
+    )(ids, meta, dosage_tiles, indiv_factors)
     far = far.astype(f16)
     got = [lax.ppermute(far[k - 1], "x", ring(k)) for k in (1, 2, 3)]
     low = lax.ppermute(variant_factors[-8:], GEN, [(k, k + 1) for k in range(slabs - 1)])
     high = lax.ppermute(variant_factors[:8], GEN, [(k + 1, k) for k in range(slabs - 1)])
-    dense_far = lax.ppermute(dense, "c", swap)
-    mask_far = lax.ppermute(mask, "c", swap)
     total = own + got[0].astype(f32) + got[1].astype(f32) + got[2].astype(f32)
-
     def device(position):
         at, place = divmod(position, 4)
         return at * 4 + (3 - place if at % 2 else place)
@@ -469,28 +518,38 @@
     )(meta_line, total, variant_factors, low, high)
     edge_before = lax.ppermute(edge, ALL, list(zip(line[:-1], line[1:])))
     edge_after = lax.ppermute(edge, ALL, list(zip(line[1:], line[:-1])))
-    sent, moments = call(
-        variant_moments, [S] + [V] * 7, [((2, 2 * BS, R), f32, V), row], [ext]
-    )(meta_line, variant_factors, resid, applied, g_high, g_low, edge_before, edge_after)
+    sent, moments = call(variant_moments, [S] + [V] * 7, [((2, 2 * BS, R), f32, V), row], [ext])(
+        meta_line, variant_factors, resid, applied, g_high, g_low, edge_before, edge_after
+    )
     sent = sent.astype(f16)
     pieces = jnp.stack([sent] + [lax.ppermute(sent, "x", ring(k)) for k in (1, 2, 3)])
+    pieces = pieces.astype(f32)
     table = lax.all_to_all(
         jnp.broadcast_to(moments[None, :1], (4 * slabs, 1, BS)), ALL, 0, 0
     ).reshape(4 * slabs, BS)
 
-    variant_new, rounded, scales = call(
+    whole = ((ROWS * BS, COLS * BS), bf16, V)
+    variant_new, rounded, scales, dense = call(
         new_variants,
-        [S, V, V, V],
-        [((COLS * BS, R), f32, V), ((COLS * BS, R), bf16, V), row],
-    )(meta, table, variant_factors, pieces.astype(f32))
-    rounded_far = lax.ppermute(rounded, "c", swap)
+        [S, S, V, V, V, H],
+        [((COLS * BS, R), f32, H), ((COLS * BS, R), bf16, V), row, whole],
+        [pltpu.VMEM((COLS * BS, R), f32), big, pltpu.SemaphoreType.DMA((5,))],
+    )(meta, ids, table, variant_factors, pieces, dosage_tiles)
+    sums = ((ROWS, PAY_I, R), f32, V)
+    scratch = [pltpu.VMEM((COLS, BS, R), f32), pltpu.VMEM((COLS, BS), f32)]
+    (pay,) = call(sums_to_send, [S, S, V, V, V], [sums], scratch)(
+        meta, mask, scales, dense, rounded
+    )
+    from_other = lax.ppermute(pay.astype(f16), "c", swap)
     (pay,) = call(
-        indiv_sums,
-        [S, S, S, V, V, V, V, V],
-        [((ROWS, PAY_I, R), f32, V)],
-        [pltpu.VMEM((ROWS, BS, R), f32), pltpu.VMEM((ROWS, BS), f32)],
-    )(meta, mask, mask_far, scales, dense, dense_far, rounded, rounded_far)
-    arrived = lax.all_to_all(pay.astype(f16), CHIP, 0, 0)
+        sums_to_keep,
+        [S, S, S, V, V, H],
+        [sums],
+        [pltpu.VMEM((ROWS * BS, COLS * BS), bf16), big, *scratch, pltpu.SemaphoreType.DMA],
+        8 << 20,
+    )(meta, ids, mask, scales, rounded, dosage_tiles)
+    of_chip = (pay + from_other.astype(f32)).astype(f16)
+    arrived = lax.all_to_all(of_chip, CHIP, 0, 0)
     mine = jnp.sum(arrived.astype(f32), axis=0)
     theirs = lax.ppermute(mine, "c", swap)
     begin = lax.dynamic_slice_in_dim(indiv_factors, chip * BS, BS, 0)

time: 136 us -> 127 us (0.934)
  waiting for transfers between devices: 28.6 us -> 23.8 us
  local copies, waits for them, and re-layouts: 4.13 us -> 1.15 us
  Pallas kernels: 21 us -> 19.3 us
    ppermute x3, waiting for transfers between devices: 11.1 us -> 7.73 us  [on_device(): got = [lax.ppermute(far[k - 1], 'x', ring(k)) for k in (1, 2, 3)]]
    unnamed x10 -> x4, local copies, waits for them, and re-layouts: 2.91 us -> 0.01 us
    pallas_call x8 -> x9, Pallas kernels: 21 us -> 19.3 us  [run(): pl.pallas_call(kernel, out_shape=tuple((placed(*out) for out in outs)), i...]
    ppermute x1, starting transfers between devices: 1.47 us -> 3.13 us  [on_device(): edge_before = lax.ppermute(edge, ALL, list(zip(line[:-1], line[1:])))]
    ppermute x3 -> x1, waiting for transfers between devices: 1.4 us -> 0.01 us  [on_device(): from_other = lax.ppermute(pay.astype(f16), 'c', swap)]
  transfers between devices with their start and end apart: 19 -> 17, of which waited for: 10 -> 9; matrix products, arithmetic and copies ran while one was open for 2% -> 2% of each run, Pallas kernels for 4% -> 4%
where the time goes in v3:
time: 127 us
  blocking collectives  43.2 us (34%)
  starting transfers between devices  32.2 us (25%)
  waiting for transfers between devices  23.8 us (19%)
  Pallas kernels  19.3 us (15%)
  other arithmetic  5.51 us (4%)
  between operations  1.59 us (1%)
    all_to_all x1, blocking collectives, on_device(): arrived = lax.all_to_all(of_chip, CHIP, 0, 0)  21.8 us
    all_to_all x1, blocking collectives, on_device(): here = lax.all_to_all(sent, CHIP, 0, 0)  21.3 us
    pallas_call x9, Pallas kernels, run(): pl.pallas_call(kernel, out_shape=tuple((placed(*out) for out in outs)), i...  19.3 us
    all_to_all x1, starting transfers between devices, on_device(): lax.all_to_all(jnp.broadcast_to(moments[None, :1], (4 * slabs, 1, BS)), A...  10.1 us
    all_to_all x1, waiting for transfers between devices, on_device(): lax.all_to_all(jnp.broadcast_to(moments[None, :1], (4 * slabs, 1, BS)), A...  7.84 us
    ppermute x3, waiting for transfers between devices, on_device(): got = [lax.ppermute(far[k - 1], 'x', ring(k)) for k in (1, 2, 3)]  7.73 us
    ppermute x3, starting transfers between devices, on_device(): got = [lax.ppermute(far[k - 1], 'x', ring(k)) for k in (1, 2, 3)]  5.96 us
    ppermute x3, starting transfers between devices, on_device(): lax.ppermute(sent, 'x', ring(k))  5.09 us
  transfers between devices with their start and end apart: 17, of which 9 were waited for; matrix products, arithmetic and copies ran while one was open for 2% of the time, Pallas kernels for 4%

profile of v3, /device:TPU:0, one launch (start us, length us, event | category | flops | bytes accessed | tf_op | source)
XLA Modules:
  0.0 126.8 jit_solution(3000748155337552952)
XLA Ops:
  1.3 0.1 pad_add_fusion.1.meta
  1.4 0.7 pad_add_fusion.ids
  2.1 6.2 %shard_map.77 = (f32[528,256]{1,0:T(8,128)S(1)}, f32[3,528,256]{2,1,0:T(8,128)S(1)}, f32[128]{0:T(128)S(1)}) custom-call(s32[129]{0:T(256)S(1)} %pad_add_fusion.ids, s32[3]{0:T(128)S(1)} %pad_add_fusion.1.meta, bf16[1,1,64,128,128]{4,3,2,1,0:T(8,128)(2,1)} %tiles_hbm.5, f32[2048,256]{1,0:T(8,128)} %factors_hbm.1), custom_call_target="tpu_custom_call" | custom-call | bytes 20971520 | tf_op jit(solution)/shard_map/pallas_call | solution.py:452
  8.3 0.0 copy-start
  8.3 0.2 convert_element_type.46
  8.5 0.2 slice_bitcast_fusion.2
  8.6 1.8 %collective-permute-start = (f16[528,256]{1,0:T(8,128)(2,1)S(1)}, f16[528,256]{1,0:T(8,128)(2,1)S(1)}, u32[]{:S(2)}, u32[]{:S(2)}) collective-permute-start(f16[528,256]{1,0:T(8,128)(2,1)S(1)} %get-tuple-element.34), channel_id=1, source_target_pairs={{0,1},{1,2},{2,3},{3,0},{4,5},{5,6},{6,7},{7,4},{8,9},{9,10},{10,1... | collective-permute-start | bytes 811016 | tf_op jit(solution)/shard_map/ppermute | solution.py:496
  10.4 2.8 %collective-permute-start.1 = (f16[528,256]{1,0:T(8,128)(2,1)S(1)}, f16[528,256]{1,0:T(8,128)(2,1)S(1)}, u32[]{:S(2)}, u32[]{:S(2)}) collective-permute-start(f16[528,256]{1,0:T(8,128)(2,1)S(1)} %get-tuple-element.36), channel_id=1, source_target_pairs={{0,2},{1,3},{2,0},{3,1},{4,6},{5,7},{6,4},{7,5},{8,10},{9,11},{10,... | collective-permute-start | bytes 811016 | tf_op jit(solution)/shard_map/ppermute | solution.py:496
  13.2 1.3 %collective-permute-start.2 = (f16[528,256]{1,0:T(8,128)(2,1)S(1)}, f16[528,256]{1,0:T(8,128)(2,1)S(1)}, u32[]{:S(2)}, u32[]{:S(2)}) collective-permute-start(f16[528,256]{1,0:T(8,128)(2,1)S(1)} %get-tuple-element.35), channel_id=1, source_target_pairs={{0,3},{1,0},{2,1},{3,2},{4,7},{5,4},{6,5},{7,6},{8,11},{9,8},{10,9... | collective-permute-start | bytes 811016 | tf_op jit(solution)/shard_map/ppermute | solution.py:496
  14.6 0.0 copy-done
  14.6 1.3 %collective-permute-start.3 = (f32[8,256]{1,0:T(8,128)S(1)}, f32[8,256]{1,0:T(8,128)S(1)}, u32[]{:S(2)}, u32[]{:S(2)}) collective-permute-start(f32[8,256]{1,0:T(8,128)S(1)} %get-tuple-element.33), channel_id=1, source_target_pairs={{0,4},{4,8},{8,12},{12,16},{16,20},{20,24},{24,28},{28,32},{32,36}... | collective-permute-start | bytes 24584 | tf_op jit(solution)/shard_map/ppermute | solution.py:497
  15.9 1.3 %collective-permute-start.4 = (f32[8,256]{1,0:T(8,128)S(1)}, f32[8,256]{1,0:T(8,128)S(1)}, u32[]{:S(2)}, u32[]{:S(2)}) collective-permute-start(f32[8,256]{1,0:T(8,128)S(1)} %get-tuple-element.32), channel_id=1, source_target_pairs={{4,0},{8,4},{12,8},{16,12},{20,16},{24,20},{28,24},{32,28},{36,32}... | collective-permute-start | bytes 24584 | tf_op jit(solution)/shard_map/ppermute | solution.py:498
  17.2 0.1 pad_add_fusion.2.meta
  17.3 1.0 collective-permute-done
  18.3 6.7 %collective-permute-done.1 = f16[528,256]{1,0:T(8,128)(2,1)S(1)} collective-permute-done((f16[528,256]{1,0:T(8,128)(2,1)S(1)}, f16[528,256]{1,0:T(8,128)(2,1)S(1)}, u32[]{:S(2)}, u32[]{:S(2)}) %collective-permute-start.1) | collective-permute-done | bytes 270368 | tf_op jit(solution)/shard_map/ppermute | solution.py:496
  25.0 0.0 collective-permute-done.2
  25.0 0.1 convert_add_fusion.total
  25.2 0.0 collective-permute-done.3.low
  25.2 0.0 collective-permute-done.4.high
  25.2 1.1 shard_map.78
  26.3 3.1 %collective-permute-start.5 = (f32[8,256]{1,0:T(8,128)S(1)}, f32[8,256]{1,0:T(8,128)S(1)}, u32[]{:S(2)}, u32[]{:S(2)}) collective-permute-start(f32[8,256]{1,0:T(8,128)S(1)} %get-tuple-element.22), channel_id=1, source_target_pairs={{0,1},{1,2},{2,3},{3,7},{7,6},{6,5},{5,4},{4,8},{8,9},{9,10},{10,1... | collective-permute-start | bytes 24584 | tf_op jit(solution)/shard_map/ppermute | solution.py:519
  29.4 1.3 %collective-permute-start.6 = (f32[8,256]{1,0:T(8,128)S(1)}, f32[8,256]{1,0:T(8,128)S(1)}, u32[]{:S(2)}, u32[]{:S(2)}) collective-permute-start(f32[8,256]{1,0:T(8,128)S(1)} %get-tuple-element.22), channel_id=1, source_target_pairs={{1,0},{2,1},{3,2},{7,3},{6,7},{5,6},{4,5},{8,4},{9,8},{10,9},{11,1... | collective-permute-start | bytes 24584 | tf_op jit(solution)/shard_map/ppermute | solution.py:520
  30.7 0.0 collective-permute-done.5.edge_before
  30.8 4.2 %collective-permute-done.6.edge_after = f32[8,256]{1,0:T(8,128)S(1)} collective-permute-done((f32[8,256]{1,0:T(8,128)S(1)}, f32[8,256]{1,0:T(8,128)S(1)}, u32[]{:S(2)}, u32[]{:S(2)}) %collective-permute-start.6) | collective-permute-done | bytes 8224 | tf_op jit(solution)/shard_map/ppermute | solution.py:520
  35.0 1.1 shard_map.79
  36.2 1.5 %collective-permute-start.7 = (f16[2,256,256]{2,1,0:T(8,128)(2,1)S(1)}, f16[2,256,256]{2,1,0:T(8,128)(2,1)S(1)}, u32[]{:S(2)}, u32[]{:S(2)}) collective-permute-start(f16[2,256,256]{2,1,0:T(8,128)(2,1)S(1)} %convert_element_type.50), channel_id=1, source_target_pairs={{0,1},{1,2},{2,3},{3,0},{4,5},{5,6},{6,7},{7,4},{8,9},{9,10},{10,1... | collective-permute-start | bytes 786440 | tf_op jit(solution)/shard_map/ppermute | solution.py:525
  37.6 1.1 collective-permute-start.8
  38.7 2.5 %collective-permute-start.9 = (f16[2,256,256]{2,1,0:T(8,128)(2,1)S(1)}, f16[2,256,256]{2,1,0:T(8,128)(2,1)}, u32[]{:S(2)}, u32[]{:S(2)}) collective-permute-start(f16[2,256,256]{2,1,0:T(8,128)(2,1)S(1)} %convert_element_type.50), channel_id=1, source_target_pairs={{0,3},{1,0},{2,1},{3,2},{4,7},{5,4},{6,5},{7,6},{8,11},{9,8},{10,9... | collective-permute-start | bytes 786440 | tf_op jit(solution)/shard_map/ppermute | solution.py:525
  41.3 0.7 broadcast_in_dim.7
  41.9 10.1 %all-to-all-start = ((f32[128,1,128]{2,1,0:T(1,128)}), f32[128,1,128]{2,1,0:T(1,128)S(1)}, u32[]{:S(2)}, u32[]{:S(2)}) async-start(f32[128,1,128]{2,1,0:T(1,128)} %broadcast_in_dim.7), calls=%async_computation | async-start | bytes 131072 | tf_op jit(solution)/shard_map/all_to_all | solution.py:527
  52.0 0.0 collective-permute-done.7
  52.0 0.0 collective-permute-done.8
  52.1 0.1 collective-permute-done.9
  52.1 1.3 maximum_convert_fusion.pieces
  53.4 7.8 %all-to-all-done = f32[128,1,128]{2,1,0:T(1,128)S(1)} async-done(((f32[128,1,128]{2,1,0:T(1,128)}), f32[128,1,128]{2,1,0:T(1,128)S(1)}, u32[]{:S(2)}, u32[]{:S(2)}) %all-to-all-start) | async-done | bytes 65568 | tf_op jit(solution)/shard_map/all_to_all | solution.py:527
  61.2 2.6 %shard_map.80 = (f32[1024,256]{1,0:T(8,128)}, bf16[1024,256]{1,0:T(8,128)(2,1)S(1)}, f32[8,128]{1,0:T(8,128)S(1)}, bf16[2048,1024]{1,0:T(8,128)(2,1)S(1)}) custom-call(s32[3]{0:T(128)S(1)} %pad_add_fusion.1.meta, s32[129]{0:T(256)S(1)} %pad_add_fusion.ids, f32[128,128]{1,0:T(8,128)S(1)} %bitcast.31, f32[1024,256]{1,0:T(8,128)S(1)} %copy-done, ...), custom_call_target="tpu_custom_call" | custom-call | bytes 1048576 | tf_op jit(solution)/shard_map/pallas_call | solution.py:452
  63.8 2.4 %shard_map.82 = f32[16,136,256]{2,1,0:T(8,128)S(1)} custom-call(s32[3]{0:T(128)S(1)} %pad_add_fusion.1.meta, f32[128]{0:T(128)S(1)} %get-tuple-element.26.mask, f32[8,128]{1,0:T(8,128)S(1)} %get-tuple-element.27.scales, bf16[2048,1024]{1,0:T(8,128)(2,1)S(1)} %get-tuple-element.29.dense, bf16[1024,256]{1,0:T(8,128)(2,1)S(1)} %get-tuple-element.28.rounded), custom_call_target="tpu_custom_call" | custom-call | bytes 1048576 | tf_op jit(solution)/shard_map/pallas_call | solution.py:452
  66.2 0.2 convert_element_type.52
  66.4 0.1 collective-permute-start.10
  66.5 3.6 %shard_map.81 = f32[16,136,256]{2,1,0:T(8,128)S(1)} custom-call(s32[3]{0:T(128)S(1)} %pad_add_fusion.1.meta, s32[129]{0:T(256)S(1)} %pad_add_fusion.ids, f32[128]{0:T(128)S(1)} %get-tuple-element.26.mask, f32[8,128]{1,0:T(8,128)S(1)} %get-tuple-element.27.scales, bf16[1024,256]{1,0:T(8,128)(2,1)S(1)} %get-tuple-element.28.rounded, ...), custom_call_target="tpu_custom_call" | custom-call | bytes 8388608 | tf_op jit(solution)/shard_map/pallas_call | solution.py:452
  70.1 0.0 collective-permute-done.10
  70.1 0.4 add_convert_fusion
  70.5 0.0 copy-start.1
  70.5 21.8 %all_to_all.15 = f16[16,136,256]{2,1,0:T(8,128)(2,1)S(1)} all-to-all(f16[16,136,256]{2,1,0:T(8,128)(2,1)S(1)} %add_convert_fusion), channel_id=1, replica_groups=mesh['z'=4,'y'=4,'c'=2,'x'=4] {'z','y'}, dimensions={0} | all-to-all | bytes 2228224 | tf_op jit(solution)/shard_map/all_to_all | solution.py:552
  92.4 0.2 convert_reduce_fusion.mine
  92.5 0.1 collective-permute-start.11
  92.6 0.0 copy-done.1
  92.7 1.3 %collective-permute-done.11.theirs = f32[136,256]{1,0:T(8,128)S(1)} collective-permute-done((f32[136,256]{1,0:T(8,128)S(1)}, f32[136,256]{1,0:T(8,128)S(1)}, u32[]{:S(2)}, u32[]{:S(2)}) %collective-permute-start.11) | collective-permute-done | bytes 139296 | tf_op jit(solution)/shard_map/ppermute | solution.py:554
  94.0 1.4 %shard_map.83 = f32[136,256]{1,0:T(8,128)S(1)} custom-call(s32[3]{0:T(128)S(1)} %pad_add_fusion.1.meta, f32[136,256]{1,0:T(8,128)S(1)} %convert_reduce_fusion.mine, f32[136,256]{1,0:T(8,128)S(1)} %collective-permute-done.11.theirs, f32[128,256]{1,0:T(8,128)S(1)} %constant_dynamic-slice_fusion.start, f32[8,128]{1,0:T(8,128)S(1)} %get-tuple-element.27.scales), custom_call_target="tpu_custom_call" | custom-call | bytes 1048576 | tf_op jit(solution)/shard_map/pallas_call | solution.py:452
  95.4 0.1 broadcast_in_dim.16
  95.5 21.3 %all_to_all.16 = f16[16,136,256]{2,1,0:T(8,128)(2,1)S(1)} all-to-all(f16[16,136,256]{2,1,0:T(8,128)(2,1)S(1)} %broadcast_in_dim.16), channel_id=1, replica_groups=mesh['z'=4,'y'=4,'c'=2,'x'=4] {'z','y'}, dimensions={0} | all-to-all | bytes 2228224 | tf_op jit(solution)/shard_map/all_to_all | solution.py:560
  116.8 0.0 collective-permute-start.15
  116.9 0.2 shard_map.84.own
  117.1 0.6 collective-permute-start.12
  117.7 2.3 %collective-permute-start.13 = (f32[8,128]{1,0:T(8,128)S(1)}, f32[8,128]{1,0:T(8,128)S(1)}, u32[]{:S(2)}, u32[]{:S(2)}) collective-permute-start(f32[8,128]{1,0:T(8,128)S(1)} %shard_map.84.own), channel_id=1, source_target_pairs={{0,2},{1,3},{2,0},{3,1},{4,6},{5,7},{6,4},{7,5},{8,10},{9,11},{10,... | collective-permute-start | bytes 12296 | tf_op jit(solution)/shard_map/ppermute | solution.py:564
  120.0 1.0 collective-permute-start.14
  121.0 0.9 collective-permute-done.12.next1
  121.9 0.9 collective-permute-done.13.next2
  122.8 0.8 collective-permute-done.14.next3
  123.6 0.7 shard_map.85
  124.3 0.2 slice_reduce_fusion.1
  124.5 0.0 collective-permute-done.15
  124.5 0.5 multiply_add_fusion
  125.0 1.8 %bitcast_add_fusion = f32[2048,256]{1,0:T(8,128)} fusion(f32[2048,256]{1,0:T(8,128)S(1)} %copy-done.1, f32[16,128,256]{2,1,0:T(8,128)S(1)} %multiply_add_fusion), kind=kLoop, calls=%fused_computation.2 | loop fusion | flops 524288 | bytes 6291456 | tf_op jit(solution)/shard_map/add | solution.py:572
  (8 shorter events, 0.1 us)
Async XLA Ops:
  8.3 6.3 %copy-start = (f32[1024,256]{1,0:T(8,128)S(1)}, f32[1024,256]{1,0:T(8,128)}, u32[]{:S(2)}) copy-start(f32[1024,256]{1,0:T(8,128)} %start.5) | copy-start | bytes 3145732
  8.6 9.6 %collective-permute-start = (f16[528,256]{1,0:T(8,128)(2,1)S(1)}, f16[528,256]{1,0:T(8,128)(2,1)S(1)}, u32[]{:S(2)}, u32[]{:S(2)}) collective-permute-start(f16[528,256]{1,0:T(8,128)(2,1)S(1)} %get-tuple-element.34), channel_id=1, source_target_pairs={{0,1},{1,2},{2,3},{3,0},{4,5},{5,6},{6,7},{7,4},{8,9},{9,10},{10,1... | collective-permute-start | bytes 811016 | tf_op jit(solution)/shard_map/ppermute | solution.py:496
  10.4 14.6 %collective-permute-start.1 = (f16[528,256]{1,0:T(8,128)(2,1)S(1)}, f16[528,256]{1,0:T(8,128)(2,1)S(1)}, u32[]{:S(2)}, u32[]{:S(2)}) collective-permute-start(f16[528,256]{1,0:T(8,128)(2,1)S(1)} %get-tuple-element.36), channel_id=1, source_target_pairs={{0,2},{1,3},{2,0},{3,1},{4,6},{5,7},{6,4},{7,5},{8,10},{9,11},{10,... | collective-permute-start | bytes 811016 | tf_op jit(solution)/shard_map/ppermute | solution.py:496
  13.2 11.8 %collective-permute-start.2 = (f16[528,256]{1,0:T(8,128)(2,1)S(1)}, f16[528,256]{1,0:T(8,128)(2,1)S(1)}, u32[]{:S(2)}, u32[]{:S(2)}) collective-permute-start(f16[528,256]{1,0:T(8,128)(2,1)S(1)} %get-tuple-element.35), channel_id=1, source_target_pairs={{0,3},{1,0},{2,1},{3,2},{4,7},{5,4},{6,5},{7,6},{8,11},{9,8},{10,9... | collective-permute-start | bytes 811016 | tf_op jit(solution)/shard_map/ppermute | solution.py:496
  14.6 10.6 %collective-permute-start.3 = (f32[8,256]{1,0:T(8,128)S(1)}, f32[8,256]{1,0:T(8,128)S(1)}, u32[]{:S(2)}, u32[]{:S(2)}) collective-permute-start(f32[8,256]{1,0:T(8,128)S(1)} %get-tuple-element.33), channel_id=1, source_target_pairs={{0,4},{4,8},{8,12},{12,16},{16,20},{20,24},{24,28},{28,32},{32,36}... | collective-permute-start | bytes 24584 | tf_op jit(solution)/shard_map/ppermute | solution.py:497
  15.9 9.3 %collective-permute-start.4 = (f32[8,256]{1,0:T(8,128)S(1)}, f32[8,256]{1,0:T(8,128)S(1)}, u32[]{:S(2)}, u32[]{:S(2)}) collective-permute-start(f32[8,256]{1,0:T(8,128)S(1)} %get-tuple-element.32), channel_id=1, source_target_pairs={{4,0},{8,4},{12,8},{16,12},{20,16},{24,20},{28,24},{32,28},{36,32}... | collective-permute-start | bytes 24584 | tf_op jit(solution)/shard_map/ppermute | solution.py:498
  26.3 4.5 %collective-permute-start.5 = (f32[8,256]{1,0:T(8,128)S(1)}, f32[8,256]{1,0:T(8,128)S(1)}, u32[]{:S(2)}, u32[]{:S(2)}) collective-permute-start(f32[8,256]{1,0:T(8,128)S(1)} %get-tuple-element.22), channel_id=1, source_target_pairs={{0,1},{1,2},{2,3},{3,7},{7,6},{6,5},{5,4},{4,8},{8,9},{9,10},{10,1... | collective-permute-start | bytes 24584 | tf_op jit(solution)/shard_map/ppermute | solution.py:519
  29.4 5.5 %collective-permute-start.6 = (f32[8,256]{1,0:T(8,128)S(1)}, f32[8,256]{1,0:T(8,128)S(1)}, u32[]{:S(2)}, u32[]{:S(2)}) collective-permute-start(f32[8,256]{1,0:T(8,128)S(1)} %get-tuple-element.22), channel_id=1, source_target_pairs={{1,0},{2,1},{3,2},{7,3},{6,7},{5,6},{4,5},{8,4},{9,8},{10,9},{11,1... | collective-permute-start | bytes 24584 | tf_op jit(solution)/shard_map/ppermute | solution.py:520
  36.2 15.9 %collective-permute-start.7 = (f16[2,256,256]{2,1,0:T(8,128)(2,1)S(1)}, f16[2,256,256]{2,1,0:T(8,128)(2,1)S(1)}, u32[]{:S(2)}, u32[]{:S(2)}) collective-permute-start(f16[2,256,256]{2,1,0:T(8,128)(2,1)S(1)} %convert_element_type.50), channel_id=1, source_target_pairs={{0,1},{1,2},{2,3},{3,0},{4,5},{5,6},{6,7},{7,4},{8,9},{9,10},{10,1... | collective-permute-start | bytes 786440 | tf_op jit(solution)/shard_map/ppermute | solution.py:525
  37.6 14.4 %collective-permute-start.8 = (f16[2,256,256]{2,1,0:T(8,128)(2,1)S(1)}, f16[2,256,256]{2,1,0:T(8,128)(2,1)}, u32[]{:S(2)}, u32[]{:S(2)}) collective-permute-start(f16[2,256,256]{2,1,0:T(8,128)(2,1)S(1)} %convert_element_type.50), channel_id=1, source_target_pairs={{0,2},{1,3},{2,0},{3,1},{4,6},{5,7},{6,4},{7,5},{8,10},{9,11},{10,... | collective-permute-start | bytes 786440 | tf_op jit(solution)/shard_map/ppermute | solution.py:525
  38.7 13.4 %collective-permute-start.9 = (f16[2,256,256]{2,1,0:T(8,128)(2,1)S(1)}, f16[2,256,256]{2,1,0:T(8,128)(2,1)}, u32[]{:S(2)}, u32[]{:S(2)}) collective-permute-start(f16[2,256,256]{2,1,0:T(8,128)(2,1)S(1)} %convert_element_type.50), channel_id=1, source_target_pairs={{0,3},{1,0},{2,1},{3,2},{4,7},{5,4},{6,5},{7,6},{8,11},{9,8},{10,9... | collective-permute-start | bytes 786440 | tf_op jit(solution)/shard_map/ppermute | solution.py:525
  41.9 19.3 %all-to-all-start = ((f32[128,1,128]{2,1,0:T(1,128)}), f32[128,1,128]{2,1,0:T(1,128)S(1)}, u32[]{:S(2)}, u32[]{:S(2)}) async-start(f32[128,1,128]{2,1,0:T(1,128)} %broadcast_in_dim.7), calls=%async_computation | async-start | bytes 131072 | tf_op jit(solution)/shard_map/all_to_all | solution.py:527
  66.4 3.8 %collective-permute-start.10 = (f16[16,136,256]{2,1,0:T(8,128)(2,1)S(1)}, f16[16,136,256]{2,1,0:T(8,128)(2,1)S(1)}, u32[]{:S(2)}, u32[]{:S(2)}) collective-permute-start(f16[16,136,256]{2,1,0:T(8,128)(2,1)S(1)} %convert_element_type.52), channel_id=1, source_target_pairs={{0,4},{4,0},{1,5},{5,1},{2,6},{6,2},{3,7},{7,3},{8,12},{12,8},{9,1... | collective-permute-start | bytes 3342344 | tf_op jit(solution)/shard_map/ppermute | solution.py:543
  70.5 22.1 %copy-start.1 = (f32[2048,256]{1,0:T(8,128)S(1)}, f32[2048,256]{1,0:T(8,128)}, u32[]{:S(2)}) copy-start(f32[2048,256]{1,0:T(8,128)} %factors_hbm.1) | copy-start | bytes 6291460
  92.5 1.4 %collective-permute-start.11 = (f32[136,256]{1,0:T(8,128)S(1)}, f32[136,256]{1,0:T(8,128)S(1)}, u32[]{:S(2)}, u32[]{:S(2)}) collective-permute-start(f32[136,256]{1,0:T(8,128)S(1)} %convert_reduce_fusion.mine), channel_id=1, source_target_pairs={{0,4},{4,0},{1,5},{5,1},{2,6},{6,2},{3,7},{7,3},{8,12},{12,8},{9,1... | collective-permute-start | bytes 417800 | tf_op jit(solution)/shard_map/ppermute | solution.py:554
  116.8 7.7 %collective-permute-start.15 = (f16[16,136,256]{2,1,0:T(8,128)(2,1)S(1)}, f16[16,136,256]{2,1,0:T(8,128)(2,1)S(1)}, u32[]{:S(2)}, u32[]{:S(2)}) collective-permute-start(f16[16,136,256]{2,1,0:T(8,128)(2,1)S(1)} %all_to_all.16), channel_id=1, source_target_pairs={{0,4},{4,0},{1,5},{5,1},{2,6},{6,2},{3,7},{7,3},{8,12},{12,8},{9,1... | collective-permute-start | bytes 3342344 | tf_op jit(solution)/shard_map/ppermute | solution.py:561
  117.1 4.8 %collective-permute-start.12 = (f32[8,128]{1,0:T(8,128)S(1)}, f32[8,128]{1,0:T(8,128)S(1)}, u32[]{:S(2)}, u32[]{:S(2)}) collective-permute-start(f32[8,128]{1,0:T(8,128)S(1)} %shard_map.84.own), channel_id=1, source_target_pairs={{0,1},{1,2},{2,3},{3,0},{4,5},{5,6},{6,7},{7,4},{8,9},{9,10},{10,1... | collective-permute-start | bytes 12296 | tf_op jit(solution)/shard_map/ppermute | solution.py:564
  117.7 5.1 %collective-permute-start.13 = (f32[8,128]{1,0:T(8,128)S(1)}, f32[8,128]{1,0:T(8,128)S(1)}, u32[]{:S(2)}, u32[]{:S(2)}) collective-permute-start(f32[8,128]{1,0:T(8,128)S(1)} %shard_map.84.own), channel_id=1, source_target_pairs={{0,2},{1,3},{2,0},{3,1},{4,6},{5,7},{6,4},{7,5},{8,10},{9,11},{10,... | collective-permute-start | bytes 12296 | tf_op jit(solution)/shard_map/ppermute | solution.py:564
  120.0 3.6 %collective-permute-start.14 = (f32[8,128]{1,0:T(8,128)S(1)}, f32[8,128]{1,0:T(8,128)S(1)}, u32[]{:S(2)}, u32[]{:S(2)}) collective-permute-start(f32[8,128]{1,0:T(8,128)S(1)} %shard_map.84.own), channel_id=1, source_target_pairs={{0,3},{1,0},{2,1},{3,2},{4,7},{5,4},{6,5},{7,6},{8,11},{9,8},{10,9... | collective-permute-start | bytes 12296 | tf_op jit(solution)/shard_map/ppermute | solution.py:564

commit v4 on v3

--- a/solution.py
+++ b/solution.py
@@ -18,7 +18,7 @@
 ALL = ("z", "y", "c", "x")
 GEN = ("z", "y", "c")
 CHIP = ("z", "y")
-PAY_V = 2 * BS + 2 * BS + 16
+PAY_V = 2 * BS + 2 * BS + 8
 PAY_I = BS + 8
 VMEM_LIMIT = 16 * 1024 * 1024
 
@@ -60,35 +60,36 @@
     )
 
 
-def set_mask(ids, mask):
-    def clear(k, carry):
-        mask[k] = 0.0
+def scatter(row_of, col_of, live, tiles, dense, mask=None):
+    def four(step, carry):
+        for k in range(4):
+            s = jnp.minimum(step * 4 + k, live - 1)
+            row, col = row_of(s), col_of(s)
+            rows = pl.ds(pl.multiple_of(row * BS, BS), BS)
+            cols = pl.ds(pl.multiple_of(col * BS, BS), BS)
+            dense[rows, cols] = tiles[s]
+            if mask is not None:
+                mask[row * COLS + col] = 1.0
         return carry
 
-    lax.fori_loop(0, ROWS * COLS, clear, 0)
-
-    def mark(s, carry):
-        mask[ids[s] * COLS + ids[NB + s]] = 1.0
-        return carry
-
-    lax.fori_loop(0, ids[2 * NB], mark, 0)
+    lax.fori_loop(0, (live + 3) // 4, four, 0)
 
 
 def fill(ids, tiles, dense):
-    def scatter(s, carry):
-        rows = pl.ds(pl.multiple_of(ids[s] * BS, BS), BS)
-        cols = pl.ds(pl.multiple_of(ids[NB + s] * BS, BS), BS)
-        dense[rows, cols] = tiles[s]
-        return carry
-
-    lax.fori_loop(0, ids[2 * NB], scatter, 0)
+    scatter(lambda s: ids[s], lambda s: ids[NB + s], ids[2 * NB], tiles, dense)
 
 
 def variant_sums(
-    ids, meta, tiles_hbm, factors_hbm, own, far, mask,
-    tiles, factors, dense, turned, rounded, grams, diags, sems,
+    meta, live, rows_hbm, cols_hbm, tiles_hbm, factors_hbm, own, far, mask,
+    tiles, factors, dense, turned, rounded, grams, diags, ids, sems,
 ):
     me, odd = meta[0], meta[1]
+    plan = [
+        pltpu.make_async_copy(rows_hbm.at[0], ids.at[0], sems.at[5]),
+        pltpu.make_async_copy(cols_hbm.at[0], ids.at[1], sems.at[6]),
+    ]
+    for load in plan:
+        load.start()
     quarter = ROWS * BS // 4
     loads = [
         pltpu.make_async_copy(
@@ -103,7 +104,8 @@
         load.start()
     load_tiles.start()
     dense[...] = jnp.zeros_like(dense)
-    set_mask(ids, mask)
+    for cell in range(ROWS * COLS):
+        mask[cell] = 0.0
     for r in range(ROWS):
         if r % 4 == 0:
             loads[r // 4].wait()
@@ -115,9 +117,11 @@
         grams[r, :, :BS] = mixed
         grams[r, :, BS:] = cross
         diags[r : r + 1, :] = diag
+    for load in plan:
+        load.wait()
     load_tiles.wait()
-    fill(ids, tiles, dense)
-    zero = jnp.zeros((16, R), f32)
+    scatter(lambda s: ids[0, 0, s], lambda s: ids[1, 0, s], live[0, 0], tiles, dense, mask)
+    zero = jnp.zeros((8, R), f32)
     for k in range(4):
         at = lax.rem(me + k, 4)
         part = jnp.where(odd == 1, 3 - at, at)
@@ -253,9 +257,10 @@
     unit_guess = jnp.maximum(peak_guess, 1e-30) / 16384.0
     sent[0] = value / unit_value
     sent[1] = guess / unit_guess
-    moments[...] = as_row(
+    line = as_row(
         [rr, ra, aa, aaa, peak_value, largest(first), on_start, near, far, unit_value, unit_guess]
     )
+    moments[...] = jnp.concatenate([line] * (moments.shape[0] // 8), axis=0)
 
 
 def new_variants(
@@ -349,19 +354,11 @@
         gram_sums(scales[0:1, 1:2], mask, rounded, pay, grams, diags)
 
 
-def sums_to_keep(meta, ids, mask, scales, rounded, tiles_hbm, pay, dense, tiles, grams, diags, sem):
-    load = pltpu.make_async_copy(tiles_hbm.at[0, 0], tiles, sem)
-    load.start()
-
+def sums_to_keep(meta, ids, mask, scales, rounded, tiles, pay, dense, grams, diags):
     @pl.when(meta[1] == 0)
     def _():
         dense[...] = jnp.zeros_like(dense)
-
-    load.wait()
-
-    @pl.when(meta[1] == 0)
-    def _():
-        fill(ids, tiles, dense)
+        fill(ids, tiles.at[0, 0], dense)
         tile_sums(scales[0:1, 0:1], dense, rounded, pay)
 
     @pl.when(meta[1] == 1)
@@ -478,7 +475,7 @@
     flags = ((ROWS * COLS,), f32, S)
     own, far, mask = call(
         variant_sums,
-        [S, S, H, H],
+        [S, S, H, H, H, H],
         [((PAY_V, R), f32, V), ((3, PAY_V, R), f32, V), flags],
         [
             big,
@@ -488,10 +485,11 @@
             pltpu.VMEM((ROWS, BS, R), bf16),
             pltpu.VMEM((ROWS, BS, R), f32),
             pltpu.VMEM((ROWS, BS), f32),
-            pltpu.SemaphoreType.DMA((5,)),
+            pltpu.SMEM((2, 1, NB), jnp.int32),
+            pltpu.SemaphoreType.DMA((7,)),
         ],
         20 << 20,
-    )(ids, meta, dosage_tiles, indiv_factors)
+    )(meta, live_blocks, block_rows, block_cols, dosage_tiles, indiv_factors)
     far = far.astype(f16)
     got = [lax.ppermute(far[k - 1], "x", ring(k)) for k in (1, 2, 3)]
     low = lax.ppermute(variant_factors[-8:], GEN, [(k, k + 1) for k in range(slabs - 1)])
@@ -518,14 +516,14 @@
     )(meta_line, total, variant_factors, low, high)
     edge_before = lax.ppermute(edge, ALL, list(zip(line[:-1], line[1:])))
     edge_after = lax.ppermute(edge, ALL, list(zip(line[1:], line[:-1])))
-    sent, moments = call(variant_moments, [S] + [V] * 7, [((2, 2 * BS, R), f32, V), row], [ext])(
+    sent, moments = call(variant_moments, [S] + [V] * 7, [((2, 2 * BS, R), f32, V), ((4 * slabs, BS), f32, V)], [ext])(
         meta_line, variant_factors, resid, applied, g_high, g_low, edge_before, edge_after
     )
     sent = sent.astype(f16)
     pieces = jnp.stack([sent] + [lax.ppermute(sent, "x", ring(k)) for k in (1, 2, 3)])
     pieces = pieces.astype(f32)
     table = lax.all_to_all(
-        jnp.broadcast_to(moments[None, :1], (4 * slabs, 1, BS)), ALL, 0, 0
+        moments.reshape(4 * slabs, 1, BS), ALL, 0, 0
     ).reshape(4 * slabs, BS)
 
     whole = ((ROWS * BS, COLS * BS), bf16, V)
@@ -543,9 +541,9 @@
     from_other = lax.ppermute(pay.astype(f16), "c", swap)
     (pay,) = call(
         sums_to_keep,
-        [S, S, S, V, V, H],
+        [S, S, S, V, V, V],
         [sums],
-        [pltpu.VMEM((ROWS * BS, COLS * BS), bf16), big, *scratch, pltpu.SemaphoreType.DMA],
+        [pltpu.VMEM((ROWS * BS, COLS * BS), bf16), *scratch],
         8 << 20,
     )(meta, ids, mask, scales, rounded, dosage_tiles)
     of_chip = (pay + from_other.astype(f32)).astype(f16)
@@ -569,7 +567,8 @@
         shares[:, 0].reshape(ROWS, 1, 1) * here[:, :BS].astype(f32)
         + shares[:, 1].reshape(ROWS, 1, 1) * there[:, :BS].astype(f32)
     )
-    return variant_new, indiv_factors + change.reshape(ROWS * BS, R)
+    indiv_new = indiv_factors.reshape(ROWS, BS, R) + change
+    return variant_new, indiv_new.reshape(ROWS * BS, R)
 
 
 def solution(mesh):

time: 127 us -> 125 us (0.984)
    ppermute x3, waiting for transfers between devices: 0.06 us -> 1.76 us  [on_device(): lax.ppermute(sent, 'x', ring(k))]
    all_to_all x1, waiting for transfers between devices: 7.84 us -> 6.16 us  [on_device(): lax.all_to_all(moments.reshape(4 * slabs, 1, BS), ALL, 0, 0)]
    unnamed x4 -> x10, local copies, waits for them, and re-layouts: 0.01 us -> 1.33 us
  transfers between devices with their start and end apart: 17 -> 17, of which waited for: 9 -> 10; matrix products, arithmetic and copies ran while one was open for 2% -> 1% of each run, Pallas kernels for 4% -> 3%
where the time goes in v4:
time: 125 us; the launch traced here: 124 us
  blocking collectives  42.4 us (34%)
  starting transfers between devices  31.5 us (25%)
  waiting for transfers between devices  24.2 us (19%)
  Pallas kernels  18.6 us (15%)
  other arithmetic  4.43 us (4%)
  local copies, waits for them, and re-layouts  1.8 us (1%)
  between operations  1.59 us (1%)
    all_to_all x1, blocking collectives, on_device(): here = lax.all_to_all(sent, CHIP, 0, 0)  21.3 us
    all_to_all x1, blocking collectives, on_device(): arrived = lax.all_to_all(of_chip, CHIP, 0, 0)  21.1 us
    pallas_call x9, Pallas kernels, run(): pl.pallas_call(kernel, out_shape=tuple((placed(*out) for out in outs)), i...  18.6 us
    all_to_all x1, starting transfers between devices, on_device(): lax.all_to_all(moments.reshape(4 * slabs, 1, BS), ALL, 0, 0)  9.43 us
    ppermute x3, waiting for transfers between devices, on_device(): got = [lax.ppermute(far[k - 1], 'x', ring(k)) for k in (1, 2, 3)]  7.64 us
    all_to_all x1, waiting for transfers between devices, on_device(): lax.all_to_all(moments.reshape(4 * slabs, 1, BS), ALL, 0, 0)  6.16 us
    ppermute x3, starting transfers between devices, on_device(): got = [lax.ppermute(far[k - 1], 'x', ring(k)) for k in (1, 2, 3)]  5.9 us
    ppermute x3, starting transfers between devices, on_device(): lax.ppermute(sent, 'x', ring(k))  5.09 us
  transfers between devices with their start and end apart: 17, of which 10 were waited for; matrix products, arithmetic and copies ran while one was open for 1% of the time, Pallas kernels for 3%

profile of v4, /device:TPU:0, one launch (start us, length us, event | category | flops | bytes accessed | tf_op | source)
XLA Modules:
  0.0 124.5 jit_solution(2494482609218874153)
XLA Ops:
  1.3 0.1 pad_add_fusion.1.meta
  1.4 6.1 %shard_map.77 = (f32[520,256]{1,0:T(8,128)S(1)}, f32[3,520,256]{2,1,0:T(8,128)S(1)}, f32[128]{0:T(128)S(1)}) custom-call(s32[3]{0:T(128)S(1)} %pad_add_fusion.1.meta, s32[1,1]{1,0:T(1,128)} %copy.16.live, s32[1,1,64]{2,1,0:T(1,128)} %rows_hbm.1, s32[1,1,64]{2,1,0:T(1,128)} %cols_hbm.1, bf16[1,1,64,128,128]{4,3,2,1,0:T(8,128)(2,1)} %tiles.1, ...), custom_call_target="tpu_custom_call" | custom-call | bytes 20971520 | tf_op jit(solution)/shard_map/pallas_call | solution.py:449
  7.5 0.0 copy-start.1
  7.5 0.2 convert_element_type.46
  7.7 0.2 slice_bitcast_fusion.2
  7.8 1.8 %collective-permute-start = (f16[520,256]{1,0:T(8,128)(2,1)S(1)}, f16[520,256]{1,0:T(8,128)(2,1)S(1)}, u32[]{:S(2)}, u32[]{:S(2)}) collective-permute-start(f16[520,256]{1,0:T(8,128)(2,1)S(1)} %get-tuple-element.34), channel_id=1, source_target_pairs={{0,1},{1,2},{2,3},{3,0},{4,5},{5,6},{6,7},{7,4},{8,9},{9,10},{10,1... | collective-permute-start | bytes 798728 | tf_op jit(solution)/shard_map/ppermute | solution.py:494
  9.6 2.6 %collective-permute-start.1 = (f16[520,256]{1,0:T(8,128)(2,1)S(1)}, f16[520,256]{1,0:T(8,128)(2,1)S(1)}, u32[]{:S(2)}, u32[]{:S(2)}) collective-permute-start(f16[520,256]{1,0:T(8,128)(2,1)S(1)} %get-tuple-element.36), channel_id=1, source_target_pairs={{0,2},{1,3},{2,0},{3,1},{4,6},{5,7},{6,4},{7,5},{8,10},{9,11},{10,... | collective-permute-start | bytes 798728 | tf_op jit(solution)/shard_map/ppermute | solution.py:494
  12.3 1.5 %collective-permute-start.2 = (f16[520,256]{1,0:T(8,128)(2,1)S(1)}, f16[520,256]{1,0:T(8,128)(2,1)S(1)}, u32[]{:S(2)}, u32[]{:S(2)}) collective-permute-start(f16[520,256]{1,0:T(8,128)(2,1)S(1)} %get-tuple-element.35), channel_id=1, source_target_pairs={{0,3},{1,0},{2,1},{3,2},{4,7},{5,4},{6,5},{7,6},{8,11},{9,8},{10,9... | collective-permute-start | bytes 798728 | tf_op jit(solution)/shard_map/ppermute | solution.py:494
  13.7 1.3 %collective-permute-start.3 = (f32[8,256]{1,0:T(8,128)S(1)}, f32[8,256]{1,0:T(8,128)S(1)}, u32[]{:S(2)}, u32[]{:S(2)}) collective-permute-start(f32[8,256]{1,0:T(8,128)S(1)} %get-tuple-element.33), channel_id=1, source_target_pairs={{0,4},{4,8},{8,12},{12,16},{16,20},{20,24},{24,28},{28,32},{32,36}... | collective-permute-start | bytes 24584 | tf_op jit(solution)/shard_map/ppermute | solution.py:495
  15.0 1.3 %collective-permute-start.4 = (f32[8,256]{1,0:T(8,128)S(1)}, f32[8,256]{1,0:T(8,128)S(1)}, u32[]{:S(2)}, u32[]{:S(2)}) collective-permute-start(f32[8,256]{1,0:T(8,128)S(1)} %get-tuple-element.32), channel_id=1, source_target_pairs={{4,0},{8,4},{12,8},{16,12},{20,16},{24,20},{28,24},{32,28},{36,32}... | collective-permute-start | bytes 24584 | tf_op jit(solution)/shard_map/ppermute | solution.py:496
  16.4 0.1 pad_add_fusion.2.meta
  16.4 0.8 collective-permute-done
  17.2 6.9 %collective-permute-done.1 = f16[520,256]{1,0:T(8,128)(2,1)S(1)} collective-permute-done((f16[520,256]{1,0:T(8,128)(2,1)S(1)}, f16[520,256]{1,0:T(8,128)(2,1)S(1)}, u32[]{:S(2)}, u32[]{:S(2)}) %collective-permute-start.1) | collective-permute-done | bytes 266272 | tf_op jit(solution)/shard_map/ppermute | solution.py:494
  24.1 0.0 collective-permute-done.2
  24.1 0.2 convert_add_fusion.total
  24.2 0.0 copy-start.3
  24.2 0.0 copy-start.4
  24.3 0.0 collective-permute-done.3.low
  24.3 0.0 collective-permute-done.4.high
  24.3 1.1 shard_map.78
  25.4 3.1 %collective-permute-start.5 = (f32[8,256]{1,0:T(8,128)S(1)}, f32[8,256]{1,0:T(8,128)S(1)}, u32[]{:S(2)}, u32[]{:S(2)}) collective-permute-start(f32[8,256]{1,0:T(8,128)S(1)} %get-tuple-element.22), channel_id=1, source_target_pairs={{0,1},{1,2},{2,3},{3,7},{7,6},{6,5},{5,4},{4,8},{8,9},{9,10},{10,1... | collective-permute-start | bytes 24584 | tf_op jit(solution)/shard_map/ppermute | solution.py:517
  28.5 1.3 %collective-permute-start.6 = (f32[8,256]{1,0:T(8,128)S(1)}, f32[8,256]{1,0:T(8,128)S(1)}, u32[]{:S(2)}, u32[]{:S(2)}) collective-permute-start(f32[8,256]{1,0:T(8,128)S(1)} %get-tuple-element.22), channel_id=1, source_target_pairs={{1,0},{2,1},{3,2},{7,3},{6,7},{5,6},{4,5},{8,4},{9,8},{10,9},{11,1... | collective-permute-start | bytes 24584 | tf_op jit(solution)/shard_map/ppermute | solution.py:518
  29.8 0.0 collective-permute-done.5.edge_before
  29.9 4.2 %collective-permute-done.6.edge_after = f32[8,256]{1,0:T(8,128)S(1)} collective-permute-done((f32[8,256]{1,0:T(8,128)S(1)}, f32[8,256]{1,0:T(8,128)S(1)}, u32[]{:S(2)}, u32[]{:S(2)}) %collective-permute-start.6) | collective-permute-done | bytes 8224 | tf_op jit(solution)/shard_map/ppermute | solution.py:518
  34.1 1.7 %shard_map.79 = (f32[2,256,256]{2,1,0:T(8,128)S(1)}, f32[128,128]{1,0:T(8,128)}) custom-call(s32[3]{0:T(128)S(1)} %pad_add_fusion.2.meta, f32[1024,256]{1,0:T(8,128)S(1)} %copy-done.1, f32[256,256]{1,0:T(8,128)S(1)} %get-tuple-element.18.resid, f32[256,256]{1,0:T(8,128)S(1)} %get-tuple-element.19.applied, bf16[2,256,256]{2,1,0:T(8,128)(2,1)S(1)} %get-tuple-element.20.g_high, ...), custom_call_target="tpu_custom_call" | custom-call | bytes 1048576 | tf_op jit(solution)/shard_map/pallas_call | solution.py:449
  35.9 1.5 %collective-permute-start.7 = (f16[2,256,256]{2,1,0:T(8,128)(2,1)S(1)}, f16[2,256,256]{2,1,0:T(8,128)(2,1)S(1)}, u32[]{:S(2)}, u32[]{:S(2)}) collective-permute-start(f16[2,256,256]{2,1,0:T(8,128)(2,1)S(1)} %convert_element_type.50), channel_id=1, source_target_pairs={{0,1},{1,2},{2,3},{3,0},{4,5},{5,6},{6,7},{7,4},{8,9},{9,10},{10,1... | collective-permute-start | bytes 786440 | tf_op jit(solution)/shard_map/ppermute | solution.py:523
  37.3 1.1 collective-permute-start.8
  38.4 2.5 %collective-permute-start.9 = (f16[2,256,256]{2,1,0:T(8,128)(2,1)S(1)}, f16[2,256,256]{2,1,0:T(8,128)(2,1)}, u32[]{:S(2)}, u32[]{:S(2)}) collective-permute-start(f16[2,256,256]{2,1,0:T(8,128)(2,1)S(1)} %convert_element_type.50), channel_id=1, source_target_pairs={{0,3},{1,0},{2,1},{3,2},{4,7},{5,4},{6,5},{7,6},{8,11},{9,8},{10,9... | collective-permute-start | bytes 786440 | tf_op jit(solution)/shard_map/ppermute | solution.py:523
  41.0 0.1 pad_add_fusion.ids
  41.0 9.4 %all-to-all-start = ((f32[128,1,128]{2,1,0:T(1,128)}), f32[128,1,128]{2,1,0:T(1,128)S(1)}, u32[]{:S(2)}, u32[]{:S(2)}) async-start(f32[128,1,128]{2,1,0:T(1,128)} %bitcast.13), calls=%async_computation | async-start | bytes 131072 | tf_op jit(solution)/shard_map/all_to_all | solution.py:525
  50.5 0.8 collective-permute-done.7
  51.3 0.0 collective-permute-done.8
  51.3 0.9 collective-permute-done.9
  52.3 1.3 %maximum_convert_fusion.pieces = f32[4,2,256,256]{3,2,1,0:T(8,128)S(1)} fusion(f16[1,2,256,256]{3,2,1,0:T(8,128)(2,1)} %bitcast.18, f16[1,2,256,256]{3,2,1,0:T(8,128)(2,1)} %bitcast.17, f16[1,2,256,256]{3,2,1,0:T(8,128)(2,1)S(1)} %bitcast.35, f16[1,2,256,256]{3,2,1,0:T(8,128)(2,1)S(1)} %convert_bitcast_fusion), kind=kLoop, calls=%fused_computation.3 | loop fusion | flops 2097152 | bytes 3145728 | tf_op jit(solution)/shard_map/convert_element_type | solution.py:524
  53.5 6.2 %all-to-all-done = f32[128,1,128]{2,1,0:T(1,128)S(1)} async-done(((f32[128,1,128]{2,1,0:T(1,128)}), f32[128,1,128]{2,1,0:T(1,128)S(1)}, u32[]{:S(2)}, u32[]{:S(2)}) %all-to-all-start) | async-done | bytes 65568 | tf_op jit(solution)/shard_map/all_to_all | solution.py:525
  59.7 2.6 %shard_map.80 = (f32[1024,256]{1,0:T(8,128)}, bf16[1024,256]{1,0:T(8,128)(2,1)S(1)}, f32[8,128]{1,0:T(8,128)S(1)}, bf16[2048,1024]{1,0:T(8,128)(2,1)S(1)}) custom-call(s32[3]{0:T(128)S(1)} %pad_add_fusion.1.meta, s32[129]{0:T(256)S(1)} %pad_add_fusion.ids, f32[128,128]{1,0:T(8,128)S(1)} %bitcast.32, f32[1024,256]{1,0:T(8,128)S(1)} %copy-done.1, ...), custom_call_target="tpu_custom_call" | custom-call | bytes 1048576 | tf_op jit(solution)/shard_map/pallas_call | solution.py:449
  62.3 2.4 %shard_map.82 = f32[16,136,256]{2,1,0:T(8,128)S(1)} custom-call(s32[3]{0:T(128)S(1)} %pad_add_fusion.1.meta, f32[128]{0:T(128)S(1)} %get-tuple-element.26.mask, f32[8,128]{1,0:T(8,128)S(1)} %get-tuple-element.27.scales, bf16[2048,1024]{1,0:T(8,128)(2,1)S(1)} %get-tuple-element.29.dense, bf16[1024,256]{1,0:T(8,128)(2,1)S(1)} %get-tuple-element.28.rounded), custom_call_target="tpu_custom_call" | custom-call | bytes 1048576 | tf_op jit(solution)/shard_map/pallas_call | solution.py:449
  64.6 0.0 copy-start
  64.7 0.2 convert_element_type.52
  64.8 0.1 collective-permute-start.10
  64.9 1.3 %copy-done = bf16[1,1,64,128,128]{4,3,2,1,0:T(8,128)(2,1)S(1)} copy-done((bf16[1,1,64,128,128]{4,3,2,1,0:T(8,128)(2,1)S(1)}, bf16[1,1,64,128,128]{4,3,2,1,0:T(8,128)(2,1)}, u32[]{:S(2)}) %copy-start) | copy-done | bytes 2097176
  66.2 2.3 %shard_map.81 = f32[16,136,256]{2,1,0:T(8,128)S(1)} custom-call(s32[3]{0:T(128)S(1)} %pad_add_fusion.1.meta, s32[129]{0:T(256)S(1)} %pad_add_fusion.ids, f32[128]{0:T(128)S(1)} %get-tuple-element.26.mask, f32[8,128]{1,0:T(8,128)S(1)} %get-tuple-element.27.scales, bf16[1024,256]{1,0:T(8,128)(2,1)S(1)} %get-tuple-element.28.rounded, ...), custom_call_target="tpu_custom_call" | custom-call | bytes 8388608 | tf_op jit(solution)/shard_map/pallas_call | solution.py:449
  68.6 0.0 collective-permute-done.10
  68.6 0.3 add_convert_fusion
  68.9 0.0 copy-start.2
  68.9 21.1 %all_to_all.15 = f16[16,136,256]{2,1,0:T(8,128)(2,1)S(1)} all-to-all(f16[16,136,256]{2,1,0:T(8,128)(2,1)S(1)} %add_convert_fusion), channel_id=1, replica_groups=mesh['z'=4,'y'=4,'c'=2,'x'=4] {'z','y'}, dimensions={0} | all-to-all | bytes 2228224 | tf_op jit(solution)/shard_map/all_to_all | solution.py:550
  90.0 0.2 convert_reduce_fusion.mine
  90.1 0.1 collective-permute-start.11
  90.3 1.3 %collective-permute-done.11.theirs = f32[136,256]{1,0:T(8,128)S(1)} collective-permute-done((f32[136,256]{1,0:T(8,128)S(1)}, f32[136,256]{1,0:T(8,128)S(1)}, u32[]{:S(2)}, u32[]{:S(2)}) %collective-permute-start.11) | collective-permute-done | bytes 139296 | tf_op jit(solution)/shard_map/ppermute | solution.py:552
  91.6 1.4 %shard_map.83 = f32[136,256]{1,0:T(8,128)S(1)} custom-call(s32[3]{0:T(128)S(1)} %pad_add_fusion.1.meta, f32[136,256]{1,0:T(8,128)S(1)} %convert_reduce_fusion.mine, f32[136,256]{1,0:T(8,128)S(1)} %collective-permute-done.11.theirs, f32[128,256]{1,0:T(8,128)S(1)} %constant_dynamic-slice_fusion.start, f32[8,128]{1,0:T(8,128)S(1)} %get-tuple-element.27.scales), custom_call_target="tpu_custom_call" | custom-call | bytes 1048576 | tf_op jit(solution)/shard_map/pallas_call | solution.py:449
  93.0 0.1 broadcast_in_dim.2
  93.1 21.3 %all_to_all.16 = f16[16,136,256]{2,1,0:T(8,128)(2,1)S(1)} all-to-all(f16[16,136,256]{2,1,0:T(8,128)(2,1)S(1)} %broadcast_in_dim.2), channel_id=1, replica_groups=mesh['z'=4,'y'=4,'c'=2,'x'=4] {'z','y'}, dimensions={0} | all-to-all | bytes 2228224 | tf_op jit(solution)/shard_map/all_to_all | solution.py:558
  114.5 0.0 collective-permute-start.15
  114.5 0.2 shard_map.84.own
  114.7 0.6 collective-permute-start.12
  115.3 2.8 %collective-permute-start.13 = (f32[8,128]{1,0:T(8,128)S(1)}, f32[8,128]{1,0:T(8,128)S(1)}, u32[]{:S(2)}, u32[]{:S(2)}) collective-permute-start(f32[8,128]{1,0:T(8,128)S(1)} %shard_map.84.own), channel_id=1, source_target_pairs={{0,2},{1,3},{2,0},{3,1},{4,6},{5,7},{6,4},{7,5},{8,10},{9,11},{10,... | collective-permute-start | bytes 12296 | tf_op jit(solution)/shard_map/ppermute | solution.py:562
  118.1 0.5 collective-permute-start.14
  118.6 0.9 collective-permute-done.12.next1
  119.5 0.9 collective-permute-done.13.next2
  120.4 1.3 %collective-permute-done.14.next3 = f32[8,128]{1,0:T(8,128)S(1)} collective-permute-done((f32[8,128]{1,0:T(8,128)S(1)}, f32[8,128]{1,0:T(8,128)S(1)}, u32[]{:S(2)}, u32[]{:S(2)}) %collective-permute-start.14) | collective-permute-done | bytes 4128 | tf_op jit(solution)/shard_map/ppermute | solution.py:562
  121.7 0.7 shard_map.85
  122.4 0.2 slice_reduce_fusion.1
  122.6 0.0 collective-permute-done.15
  122.6 1.9 %add_add_fusion = f32[16,128,256]{2,1,0:T(8,128)} fusion(f32[16,128,256]{2,1,0:T(8,128)S(1)} %bitcast.33, f16[16,136,256]{2,1,0:T(8,128)(2,1)S(1)} %collective-permute-done.15, f16[16,136,256]{2,1,0:T(8,128)(2,1)S(1)} %all_to_all.16, f32[16]{0:T(128)S(1)} %get-tuple-element.31, f32[16]{0:T(128)S(1)} %get-tuple-element.30), kind=kLoop, calls=%fused_computation.2 | loop fusion | flops 3145728 | bytes 6291584 | tf_op jit(solution)/shard_map/add | solution.py:570
  (11 shorter events, 0.1 us)
Async XLA Ops:
  7.5 6.3 %copy-start.1 = (f32[1024,256]{1,0:T(8,128)S(1)}, f32[1024,256]{1,0:T(8,128)}, u32[]{:S(2)}) copy-start(f32[1024,256]{1,0:T(8,128)} %start.5) | copy-start | bytes 3145732
  7.8 9.3 %collective-permute-start = (f16[520,256]{1,0:T(8,128)(2,1)S(1)}, f16[520,256]{1,0:T(8,128)(2,1)S(1)}, u32[]{:S(2)}, u32[]{:S(2)}) collective-permute-start(f16[520,256]{1,0:T(8,128)(2,1)S(1)} %get-tuple-element.34), channel_id=1, source_target_pairs={{0,1},{1,2},{2,3},{3,0},{4,5},{5,6},{6,7},{7,4},{8,9},{9,10},{10,1... | collective-permute-start | bytes 798728 | tf_op jit(solution)/shard_map/ppermute | solution.py:494
  9.6 14.4 %collective-permute-start.1 = (f16[520,256]{1,0:T(8,128)(2,1)S(1)}, f16[520,256]{1,0:T(8,128)(2,1)S(1)}, u32[]{:S(2)}, u32[]{:S(2)}) collective-permute-start(f16[520,256]{1,0:T(8,128)(2,1)S(1)} %get-tuple-element.36), channel_id=1, source_target_pairs={{0,2},{1,3},{2,0},{3,1},{4,6},{5,7},{6,4},{7,5},{8,10},{9,11},{10,... | collective-permute-start | bytes 798728 | tf_op jit(solution)/shard_map/ppermute | solution.py:494
  12.3 11.8 %collective-permute-start.2 = (f16[520,256]{1,0:T(8,128)(2,1)S(1)}, f16[520,256]{1,0:T(8,128)(2,1)S(1)}, u32[]{:S(2)}, u32[]{:S(2)}) collective-permute-start(f16[520,256]{1,0:T(8,128)(2,1)S(1)} %get-tuple-element.35), channel_id=1, source_target_pairs={{0,3},{1,0},{2,1},{3,2},{4,7},{5,4},{6,5},{7,6},{8,11},{9,8},{10,9... | collective-permute-start | bytes 798728 | tf_op jit(solution)/shard_map/ppermute | solution.py:494
  13.7 10.5 %collective-permute-start.3 = (f32[8,256]{1,0:T(8,128)S(1)}, f32[8,256]{1,0:T(8,128)S(1)}, u32[]{:S(2)}, u32[]{:S(2)}) collective-permute-start(f32[8,256]{1,0:T(8,128)S(1)} %get-tuple-element.33), channel_id=1, source_target_pairs={{0,4},{4,8},{8,12},{12,16},{16,20},{20,24},{24,28},{28,32},{32,36}... | collective-permute-start | bytes 24584 | tf_op jit(solution)/shard_map/ppermute | solution.py:495
  15.0 9.2 %collective-permute-start.4 = (f32[8,256]{1,0:T(8,128)S(1)}, f32[8,256]{1,0:T(8,128)S(1)}, u32[]{:S(2)}, u32[]{:S(2)}) collective-permute-start(f32[8,256]{1,0:T(8,128)S(1)} %get-tuple-element.32), channel_id=1, source_target_pairs={{4,0},{8,4},{12,8},{16,12},{20,16},{24,20},{28,24},{32,28},{36,32}... | collective-permute-start | bytes 24584 | tf_op jit(solution)/shard_map/ppermute | solution.py:496
  24.2 16.7 %copy-start.3 = (s32[1,1,64]{2,1,0:T(1,128)S(1)}, s32[1,1,64]{2,1,0:T(1,128)}, u32[]{:S(2)}) copy-start(s32[1,1,64]{2,1,0:T(1,128)} %cols_hbm.1) | copy-start | bytes 772
  24.2 16.7 %copy-start.4 = (s32[1,1,64]{2,1,0:T(1,128)S(1)}, s32[1,1,64]{2,1,0:T(1,128)}, u32[]{:S(2)}) copy-start(s32[1,1,64]{2,1,0:T(1,128)} %rows_hbm.1) | copy-start | bytes 772
  25.4 4.5 %collective-permute-start.5 = (f32[8,256]{1,0:T(8,128)S(1)}, f32[8,256]{1,0:T(8,128)S(1)}, u32[]{:S(2)}, u32[]{:S(2)}) collective-permute-start(f32[8,256]{1,0:T(8,128)S(1)} %get-tuple-element.22), channel_id=1, source_target_pairs={{0,1},{1,2},{2,3},{3,7},{7,6},{6,5},{5,4},{4,8},{8,9},{9,10},{10,1... | collective-permute-start | bytes 24584 | tf_op jit(solution)/shard_map/ppermute | solution.py:517
  28.5 5.5 %collective-permute-start.6 = (f32[8,256]{1,0:T(8,128)S(1)}, f32[8,256]{1,0:T(8,128)S(1)}, u32[]{:S(2)}, u32[]{:S(2)}) collective-permute-start(f32[8,256]{1,0:T(8,128)S(1)} %get-tuple-element.22), channel_id=1, source_target_pairs={{1,0},{2,1},{3,2},{7,3},{6,7},{5,6},{4,5},{8,4},{9,8},{10,9},{11,1... | collective-permute-start | bytes 24584 | tf_op jit(solution)/shard_map/ppermute | solution.py:518
  35.9 15.5 %collective-permute-start.7 = (f16[2,256,256]{2,1,0:T(8,128)(2,1)S(1)}, f16[2,256,256]{2,1,0:T(8,128)(2,1)S(1)}, u32[]{:S(2)}, u32[]{:S(2)}) collective-permute-start(f16[2,256,256]{2,1,0:T(8,128)(2,1)S(1)} %convert_element_type.50), channel_id=1, source_target_pairs={{0,1},{1,2},{2,3},{3,0},{4,5},{5,6},{6,7},{7,4},{8,9},{9,10},{10,1... | collective-permute-start | bytes 786440 | tf_op jit(solution)/shard_map/ppermute | solution.py:523
  37.3 14.0 %collective-permute-start.8 = (f16[2,256,256]{2,1,0:T(8,128)(2,1)S(1)}, f16[2,256,256]{2,1,0:T(8,128)(2,1)}, u32[]{:S(2)}, u32[]{:S(2)}) collective-permute-start(f16[2,256,256]{2,1,0:T(8,128)(2,1)S(1)} %convert_element_type.50), channel_id=1, source_target_pairs={{0,2},{1,3},{2,0},{3,1},{4,6},{5,7},{6,4},{7,5},{8,10},{9,11},{10,... | collective-permute-start | bytes 786440 | tf_op jit(solution)/shard_map/ppermute | solution.py:523
  38.4 13.9 %collective-permute-start.9 = (f16[2,256,256]{2,1,0:T(8,128)(2,1)S(1)}, f16[2,256,256]{2,1,0:T(8,128)(2,1)}, u32[]{:S(2)}, u32[]{:S(2)}) collective-permute-start(f16[2,256,256]{2,1,0:T(8,128)(2,1)S(1)} %convert_element_type.50), channel_id=1, source_target_pairs={{0,3},{1,0},{2,1},{3,2},{4,7},{5,4},{6,5},{7,6},{8,11},{9,8},{10,9... | collective-permute-start | bytes 786440 | tf_op jit(solution)/shard_map/ppermute | solution.py:523
  41.0 18.7 %all-to-all-start = ((f32[128,1,128]{2,1,0:T(1,128)}), f32[128,1,128]{2,1,0:T(1,128)S(1)}, u32[]{:S(2)}, u32[]{:S(2)}) async-start(f32[128,1,128]{2,1,0:T(1,128)} %bitcast.13), calls=%async_computation | async-start | bytes 131072 | tf_op jit(solution)/shard_map/all_to_all | solution.py:525
  64.6 1.6 %copy-start = (bf16[1,1,64,128,128]{4,3,2,1,0:T(8,128)(2,1)S(1)}, bf16[1,1,64,128,128]{4,3,2,1,0:T(8,128)(2,1)}, u32[]{:S(2)}) copy-start(bf16[1,1,64,128,128]{4,3,2,1,0:T(8,128)(2,1)} %tiles.1) | copy-start | bytes 6291460
  64.8 3.7 %collective-permute-start.10 = (f16[16,136,256]{2,1,0:T(8,128)(2,1)S(1)}, f16[16,136,256]{2,1,0:T(8,128)(2,1)S(1)}, u32[]{:S(2)}, u32[]{:S(2)}) collective-permute-start(f16[16,136,256]{2,1,0:T(8,128)(2,1)S(1)} %convert_element_type.52), channel_id=1, source_target_pairs={{0,4},{4,0},{1,5},{5,1},{2,6},{6,2},{3,7},{7,3},{8,12},{12,8},{9,1... | collective-permute-start | bytes 3342344 | tf_op jit(solution)/shard_map/ppermute | solution.py:541
  68.9 21.3 %copy-start.2 = (f32[2048,256]{1,0:T(8,128)S(1)}, f32[2048,256]{1,0:T(8,128)}, u32[]{:S(2)}) copy-start(f32[2048,256]{1,0:T(8,128)} %factors_hbm.1) | copy-start | bytes 6291460
  90.1 1.4 %collective-permute-start.11 = (f32[136,256]{1,0:T(8,128)S(1)}, f32[136,256]{1,0:T(8,128)S(1)}, u32[]{:S(2)}, u32[]{:S(2)}) collective-permute-start(f32[136,256]{1,0:T(8,128)S(1)} %convert_reduce_fusion.mine), channel_id=1, source_target_pairs={{0,4},{4,0},{1,5},{5,1},{2,6},{6,2},{3,7},{7,3},{8,12},{12,8},{9,1... | collective-permute-start | bytes 417800 | tf_op jit(solution)/shard_map/ppermute | solution.py:552
  114.5 8.1 %collective-permute-start.15 = (f16[16,136,256]{2,1,0:T(8,128)(2,1)S(1)}, f16[16,136,256]{2,1,0:T(8,128)(2,1)S(1)}, u32[]{:S(2)}, u32[]{:S(2)}) collective-permute-start(f16[16,136,256]{2,1,0:T(8,128)(2,1)S(1)} %all_to_all.16), channel_id=1, source_target_pairs={{0,4},{4,0},{1,5},{5,1},{2,6},{6,2},{3,7},{7,3},{8,12},{12,8},{9,1... | collective-permute-start | bytes 3342344 | tf_op jit(solution)/shard_map/ppermute | solution.py:559
  114.7 4.8 %collective-permute-start.12 = (f32[8,128]{1,0:T(8,128)S(1)}, f32[8,128]{1,0:T(8,128)S(1)}, u32[]{:S(2)}, u32[]{:S(2)}) collective-permute-start(f32[8,128]{1,0:T(8,128)S(1)} %shard_map.84.own), channel_id=1, source_target_pairs={{0,1},{1,2},{2,3},{3,0},{4,5},{5,6},{6,7},{7,4},{8,9},{9,10},{10,1... | collective-permute-start | bytes 12296 | tf_op jit(solution)/shard_map/ppermute | solution.py:562
  115.3 5.1 %collective-permute-start.13 = (f32[8,128]{1,0:T(8,128)S(1)}, f32[8,128]{1,0:T(8,128)S(1)}, u32[]{:S(2)}, u32[]{:S(2)}) collective-permute-start(f32[8,128]{1,0:T(8,128)S(1)} %shard_map.84.own), channel_id=1, source_target_pairs={{0,2},{1,3},{2,0},{3,1},{4,6},{5,7},{6,4},{7,5},{8,10},{9,11},{10,... | collective-permute-start | bytes 12296 | tf_op jit(solution)/shard_map/ppermute | solution.py:562
  118.1 3.6 %collective-permute-start.14 = (f32[8,128]{1,0:T(8,128)S(1)}, f32[8,128]{1,0:T(8,128)S(1)}, u32[]{:S(2)}, u32[]{:S(2)}) collective-permute-start(f32[8,128]{1,0:T(8,128)S(1)} %shard_map.84.own), channel_id=1, source_target_pairs={{0,3},{1,0},{2,1},{3,2},{4,7},{5,4},{6,5},{7,6},{8,11},{9,8},{10,9... | collective-permute-start | bytes 12296 | tf_op jit(solution)/shard_map/ppermute | solution.py:562

commit v5 on v4

--- a/solution.py
+++ b/solution.py
@@ -80,14 +80,22 @@
 
 
 def variant_sums(
-    meta, live, rows_hbm, cols_hbm, tiles_hbm, factors_hbm, own, far, mask,
-    tiles, factors, dense, turned, rounded, grams, diags, ids, sems,
+    meta, live, rows_hbm, cols_hbm, tiles_hbm, factors_hbm, start_hbm,
+    own, far, mask, upward, downward,
+    tiles, factors, dense, turned, rounded, grams, diags, ids, sides, rims, sems,
 ):
-    me, odd = meta[0], meta[1]
+    me = meta[0]
     plan = [
         pltpu.make_async_copy(rows_hbm.at[0], ids.at[0], sems.at[5]),
         pltpu.make_async_copy(cols_hbm.at[0], ids.at[1], sems.at[6]),
     ]
+    for c in range(COLS):
+        first = c * BS if c % 2 == 0 else (c + 1) * BS - 8
+        plan.append(
+            pltpu.make_async_copy(
+                start_hbm.at[pl.ds(first, 8), :], sides.at[pl.ds(8 * c, 8), :], sems.at[7 + c]
+            )
+        )
     for load in plan:
         load.start()
     quarter = ROWS * BS // 4
@@ -110,9 +118,13 @@
         if r % 4 == 0:
             loads[r // 4].wait()
         block = factors[r * BS : (r + 1) * BS, :]
-        rounded[r] = block.astype(bf16)
+        rounded[r * BS : (r + 1) * BS, :] = block.astype(bf16)
         turned[:, r * BS : (r + 1) * BS] = block.T.astype(bf16)
-        gram = jnp.dot(turned[:, r * BS : (r + 1) * BS], rounded[r], preferred_element_type=f32)
+        gram = jnp.dot(
+            turned[:, r * BS : (r + 1) * BS],
+            rounded[r * BS : (r + 1) * BS, :],
+            preferred_element_type=f32,
+        )
         mixed, cross, diag = pack(gram)
         grams[r, :, :BS] = mixed
         grams[r, :, BS:] = cross
@@ -123,13 +135,13 @@
     scatter(lambda s: ids[0, 0, s], lambda s: ids[1, 0, s], live[0, 0], tiles, dense, mask)
     zero = jnp.zeros((8, R), f32)
     for k in range(4):
-        at = lax.rem(me + k, 4)
-        part = jnp.where(odd == 1, 3 - at, at)
+        part = lax.rem(me + k, 4)
         out = own if k == 0 else far.at[k - 1]
         cols = pl.ds(pl.multiple_of(part * 2 * BS, 2 * BS), 2 * BS)
-        out[2 * BS : 4 * BS, :] = jnp.dot(
-            turned[...], dense[:, cols], preferred_element_type=f32
-        )
+        data = jnp.dot(turned[...], dense[:, cols], preferred_element_type=f32)
+        out[2 * BS : 4 * BS, :] = data
+        rims[pl.ds(2 * part, 1), :] = data[:, :BS].T[0:1, :]
+        rims[pl.ds(2 * part + 1, 1), :] = data[:, BS:].T[BS - 1 : BS, :]
         out[4 * BS :, :] = zero
         for j in range(2):
             weights = [mask[r * COLS + part * 2 + j] for r in range(ROWS)]
@@ -143,6 +155,32 @@
             for r in range(1, ROWS):
                 total += weights[r] * diags[r : r + 1, :]
             out[4 * BS + j : 4 * BS + j + 1, :BS] = total
+    edges = [sides[8 * c + (0 if c % 2 == 0 else 7) : 8 * c + (1 if c % 2 == 0 else 8), :] for c in range(COLS)]
+    met = jnp.dot(
+        jnp.concatenate(edges, axis=0).astype(bf16), turned[...], preferred_element_type=f32
+    )
+    lines = lax.broadcasted_iota(jnp.int32, (COLS, BS), 0)
+    live_cells = []
+    for r in range(ROWS):
+        cells = jnp.zeros((COLS, BS), f32)
+        for c in range(COLS):
+            cells = jnp.where(lines == c, mask[r * COLS + c], cells)
+        live_cells.append(cells)
+    high, low = split(met * jnp.concatenate(live_cells, axis=1))
+    rims[...] -= jnp.dot(high, rounded[...], preferred_element_type=f32) + jnp.dot(
+        low, rounded[...], preferred_element_type=f32
+    )
+    for k in range(4):
+        part = lax.rem(me + k, 4)
+        out = own if k == 0 else far.at[k - 1]
+        out[4 * BS + 2 : 4 * BS + 3, :] = rims[pl.ds(jnp.maximum(2 * part - 1, 0), 1), :]
+        out[4 * BS + 3 : 4 * BS + 4, :] = rims[pl.ds(jnp.minimum(2 * part + 2, COLS - 1), 1), :]
+    upward[...] = jnp.concatenate(
+        [sides[8 * COLS - 2 : 8 * COLS, :], rims[COLS - 1 : COLS, :], jnp.zeros((5, R), f32)], axis=0
+    )
+    downward[...] = jnp.concatenate(
+        [sides[0:2, :], rims[0:1, :], jnp.zeros((5, R), f32)], axis=0
+    )
 
 
 def band_of(values, before, after, ext):
@@ -151,50 +189,6 @@
     ext[8 : 8 + n, :] = values
     ext[8 + n : 9 + n, :] = after
     return 2.0 * values - ext[7 : 7 + n, :] - ext[9 : 9 + n, :]
-
-
-def variant_start(meta, total, start, low, high, resid, applied, g_high, g_low, edge, ext):
-    part = meta[0]
-    n = 2 * BS
-    first = pl.multiple_of(part * n, n)
-    mine = start[pl.ds(first, n), :]
-    before8 = start[pl.ds(pl.multiple_of(jnp.maximum(first - 8, 0), 8), 8), :]
-    after8 = start[pl.ds(pl.multiple_of(jnp.minimum(first + n, 3 * n + n - 8), 8), 8), :]
-    before = jnp.where(part == 0, low[7:8, :], before8[7:8, :])
-    after = jnp.where(part == 3, high[0:1, :], after8[0:1, :])
-    banded = band_of(mine, before, after, ext)
-    data = total[2 * BS : 4 * BS, :].T
-    for k in range(2):
-        gram = unpack(
-            total[k * BS : (k + 1) * BS, :BS],
-            total[k * BS : (k + 1) * BS, BS:],
-            total[4 * BS + k : 4 * BS + k + 1, :BS],
-        )
-        up, down = split(gram)
-        g_high[k] = up
-        g_low[k] = down
-        rows = slice(k * BS, (k + 1) * BS)
-        resid[rows, :] = (
-            data[rows]
-            - times(mine[rows], up, down)
-            - ridge_weight * mine[rows]
-            - smooth_weight * banded[rows]
-        )
-    value = resid[...]
-    zero = jnp.zeros((1, R), f32)
-    banded = band_of(value, zero, zero, ext)
-    for k in range(2):
-        rows = slice(k * BS, (k + 1) * BS)
-        applied[rows, :] = (
-            times(value[rows], g_high[k], g_low[k])
-            + ridge_weight * value[rows]
-            + smooth_weight * banded[rows]
-        )
-    edge[...] = jnp.zeros_like(edge)
-    edge[0:1, :] = resid[0:1, :]
-    edge[1:2, :] = applied[0:1, :]
-    edge[2:3, :] = resid[n - 1 : n, :]
-    edge[3:4, :] = applied[n - 1 : n, :]
 
 
 def as_row(values):
@@ -227,22 +221,53 @@
 
 
 def variant_moments(
-    meta, start, resid, applied, g_high, g_low, edge_before, edge_after, sent, moments, ext
+    meta, total, start, near0, near1, near2, near3, sent, table, g_high, g_low, ext
 ):
-    has_before, has_after = meta[1], meta[2]
+    part, has_before, has_after = meta[0], meta[1], meta[2]
     n = 2 * BS
-    value = resid[...]
+    first_row = pl.multiple_of(part * n, n)
+    mine = start[pl.ds(first_row, n), :]
+    before8 = start[pl.ds(pl.multiple_of(jnp.maximum(first_row - 8, 0), 8), 8), :]
+    after8 = start[pl.ds(pl.multiple_of(jnp.minimum(first_row + n, 4 * n - 8), 8), 8), :]
+    at_low, at_high = part == 0, part == 3
+    before = jnp.where(at_low, near0[1:2, :], before8[7:8, :])
+    before2 = jnp.where(at_low, near0[0:1, :], before8[6:7, :])
+    after = jnp.where(at_high, near0[8:9, :], after8[0:1, :])
+    after2 = jnp.where(at_high, near0[9:10, :], after8[1:2, :])
+    banded = band_of(mine, before, after, ext)
+    data = total[2 * BS : 4 * BS, :].T
+    pieces = []
+    for k in range(2):
+        gram = unpack(
+            total[k * BS : (k + 1) * BS, :BS],
+            total[k * BS : (k + 1) * BS, BS:],
+            total[4 * BS + k : 4 * BS + k + 1, :BS],
+        )
+        g_high[k], g_low[k] = split(gram)
+        rows = slice(k * BS, (k + 1) * BS)
+        pieces.append(
+            data[rows]
+            - times(mine[rows], g_high[k], g_low[k])
+            - ridge_weight * mine[rows]
+            - smooth_weight * banded[rows]
+        )
+    value = jnp.concatenate(pieces, axis=0)
+    low = near0[2:3, :] + near1[2:3, :] + near2[2:3, :] + near3[2:3, :]
+    high = near0[10:11, :] + near1[10:11, :] + near2[10:11, :] + near3[10:11, :]
+    low = jnp.where(at_low, low, total[4 * BS + 2 : 4 * BS + 3, :])
+    high = jnp.where(at_high, high, total[4 * BS + 3 : 4 * BS + 4, :])
+    low = low - ridge_weight * before - smooth_weight * (2.0 * before - before2 - mine[0:1, :])
+    high = high - ridge_weight * after - smooth_weight * (2.0 * after - after2 - mine[n - 1 : n, :])
     zero = jnp.zeros((1, R), f32)
-    low = jnp.concatenate([edge_before[2:3, :], jnp.zeros((n - 1, R), f32)], axis=0)
-    high = jnp.concatenate([jnp.zeros((n - 1, R), f32), edge_after[0:1, :]], axis=0)
-    first = applied[...] - smooth_weight * (low + high)
-    before = jnp.where(has_before == 1, edge_before[3:4, :] - smooth_weight * value[0:1, :], zero)
-    after = jnp.where(has_after == 1, edge_after[1:2, :] - smooth_weight * value[n - 1 : n, :], zero)
-    banded = band_of(first, before, after, ext)
-    data = jnp.concatenate(
-        [times(first[k * BS : (k + 1) * BS], g_high[k], g_low[k]) for k in range(2)], axis=0
-    )
-    second = data + ridge_weight * first + smooth_weight * banded
+    low = jnp.where(has_before == 1, low, zero)
+    high = jnp.where(has_after == 1, high, zero)
+
+    def operator(values, banded):
+        data = [times(values[k * BS : (k + 1) * BS], g_high[k], g_low[k]) for k in range(2)]
+        return jnp.concatenate(data, axis=0) + ridge_weight * values + smooth_weight * banded
+
+    first = operator(value, band_of(value, low, high, ext))
+    second = operator(first, band_of(first, zero, zero, ext))
     rr, ra = total_of(value * value), total_of(value * first)
     aa, aaa = total_of(first * first), total_of(first * second)
     near, far, rr_next, curve = curve_of(rr, ra, aa, aaa)
@@ -250,7 +275,6 @@
     on_start = jnp.where(good, 1.0, 0.0)
     near = jnp.where(good, near, 0.0)
     far = jnp.where(good, far, -1.0)
-    mine = start[pl.ds(pl.multiple_of(meta[0] * n, n), n), :]
     guess = on_start * mine + near * value - far * first
     peak_value, peak_guess = largest(value), largest(guess)
     unit_value = jnp.maximum(peak_value, 1e-30) / 16384.0
@@ -260,7 +284,19 @@
     line = as_row(
         [rr, ra, aa, aaa, peak_value, largest(first), on_start, near, far, unit_value, unit_guess]
     )
-    moments[...] = jnp.concatenate([line] * (moments.shape[0] // 8), axis=0)
+    five = jnp.concatenate(
+        [
+            line[0:1, :],
+            first[0:1, :BS],
+            first[0:1, BS:],
+            first[n - 1 : n, :BS],
+            first[n - 1 : n, BS:],
+        ],
+        axis=0,
+    )
+    forty = jnp.concatenate([five] * 8, axis=0)
+    for k in range(table.shape[0] // 40):
+        table[40 * k : 40 * (k + 1), :] = forty
 
 
 def new_variants(
@@ -274,16 +310,22 @@
     def _():
         dense[...] = jnp.zeros_like(dense)
 
-    sums = jnp.sum(table[...], axis=0, keepdims=True)
-    peaks = jnp.max(table[...], axis=0, keepdims=True)
-    on_resid, on_applied, _, _ = curve_of(*(sums[:, k : k + 1] for k in range(4)))
+    parts = table.shape[0] // 5
+    lines = table[pl.ds(0, parts, stride=5), :]
+    sums = jnp.sum(lines, axis=0, keepdims=True)
+    peaks = jnp.max(lines, axis=0, keepdims=True)
+    across = sum(
+        table[pl.ds(3 + half, parts - 1, stride=5), :] * table[pl.ds(6 + half, parts - 1, stride=5), :]
+        for half in range(2)
+    )
+    rr, ra, aa, aaa = (sums[:, k : k + 1] for k in range(4))
+    on_resid, on_applied, _, _ = curve_of(rr, ra, aa, aaa - 2.0 * smooth_weight * total_of(across))
     n = 2 * BS
     keeps = []
     for k in range(4):
         owner = lax.rem(me - k + 4, 4)
-        part = jnp.where(core == 1, 3 - owner, owner)
-        rows = pl.ds(pl.multiple_of(part * n, n), n)
-        line = table[pl.ds(slab * 4 + owner, 1), :]
+        rows = pl.ds(pl.multiple_of(owner * n, n), n)
+        line = table[pl.ds((slab * 4 + owner) * 5, 1), :]
         on_start, near, far, unit_value, unit_guess = (line[:, j : j + 1] for j in range(6, 11))
         share = on_applied / far
         value = (
@@ -465,7 +507,6 @@
     core = lax.axis_index("c")
     chip = lax.axis_index(CHIP)
     slab = lax.axis_index(GEN)
-    part = jnp.where(core == 1, 3 - me, me)
     slabs = 32
     swap = [(0, 1), (1, 0)]
     meta = jnp.stack([me, core, slab]).astype(jnp.int32)
@@ -473,58 +514,52 @@
 
     big = pltpu.VMEM((NB, BS, BS), bf16)
     flags = ((ROWS * COLS,), f32, S)
-    own, far, mask = call(
+    edge = ((8, R), f32, V)
+    own, far, mask, upward, downward = call(
         variant_sums,
-        [S, S, H, H, H, H],
-        [((PAY_V, R), f32, V), ((3, PAY_V, R), f32, V), flags],
+        [S, S, H, H, H, H, H],
+        [((PAY_V, R), f32, V), ((3, PAY_V, R), f32, V), flags, edge, edge],
         [
             big,
             pltpu.VMEM((ROWS * BS, R), f32),
             pltpu.VMEM((ROWS * BS, COLS * BS), bf16),
             pltpu.VMEM((R, ROWS * BS), bf16),
-            pltpu.VMEM((ROWS, BS, R), bf16),
+            pltpu.VMEM((ROWS * BS, R), bf16),
             pltpu.VMEM((ROWS, BS, R), f32),
             pltpu.VMEM((ROWS, BS), f32),
             pltpu.SMEM((2, 1, NB), jnp.int32),
-            pltpu.SemaphoreType.DMA((7,)),
+            pltpu.VMEM((8 * COLS, R), f32),
+            pltpu.VMEM((COLS, R), f32),
+            pltpu.SemaphoreType.DMA((7 + COLS,)),
         ],
         20 << 20,
-    )(meta, live_blocks, block_rows, block_cols, dosage_tiles, indiv_factors)
+    )(meta, live_blocks, block_rows, block_cols, dosage_tiles, indiv_factors, variant_factors)
     far = far.astype(f16)
     got = [lax.ppermute(far[k - 1], "x", ring(k)) for k in (1, 2, 3)]
-    low = lax.ppermute(variant_factors[-8:], GEN, [(k, k + 1) for k in range(slabs - 1)])
-    high = lax.ppermute(variant_factors[:8], GEN, [(k + 1, k) for k in range(slabs - 1)])
+    low = lax.ppermute(upward, GEN, [(k, k + 1) for k in range(slabs - 1)])
+    high = lax.ppermute(downward, GEN, [(k + 1, k) for k in range(slabs - 1)])
     total = own + got[0].astype(f32) + got[1].astype(f32) + got[2].astype(f32)
-    def device(position):
-        at, place = divmod(position, 4)
-        return at * 4 + (3 - place if at % 2 else place)
-
-    line = [device(k) for k in range(4 * slabs)]
-    position = slab * 4 + part
-    meta_line = jnp.stack(
-        [part, (position > 0).astype(jnp.int32), (position < 4 * slabs - 1).astype(jnp.int32)]
-    ).astype(jnp.int32)
-    square = ((2 * BS, R), f32, V)
-    halves = ((2, R, R), bf16, V)
+    near = jnp.concatenate([low, high], axis=0)
+    nears = [near] + [lax.ppermute(near, "x", ring(k)) for k in (1, 2, 3)]
+    position = slab * 4 + me
+    meta_line = jnp.stack([me, position > 0, position < 4 * slabs - 1]).astype(jnp.int32)
     row = ((8, BS), f32, V)
-    ext = pltpu.VMEM((2 * BS + 16, R), f32)
-    resid, applied, g_high, g_low, edge = call(
-        variant_start,
-        [S, V, V, V, V],
-        [square, square, halves, halves, ((8, R), f32, V)],
-        [ext],
-    )(meta_line, total, variant_factors, low, high)
-    edge_before = lax.ppermute(edge, ALL, list(zip(line[:-1], line[1:])))
-    edge_after = lax.ppermute(edge, ALL, list(zip(line[1:], line[:-1])))
-    sent, moments = call(variant_moments, [S] + [V] * 7, [((2, 2 * BS, R), f32, V), ((4 * slabs, BS), f32, V)], [ext])(
-        meta_line, variant_factors, resid, applied, g_high, g_low, edge_before, edge_after
-    )
+    sent, table = call(
+        variant_moments,
+        [S] + [V] * 6,
+        [((2, 2 * BS, R), f32, V), ((4 * slabs * 5, BS), f32, V)],
+        [
+            pltpu.VMEM((2, R, R), bf16),
+            pltpu.VMEM((2, R, R), bf16),
+            pltpu.VMEM((2 * BS + 16, R), f32),
+        ],
+    )(meta_line, total, variant_factors, *nears)
     sent = sent.astype(f16)
     pieces = jnp.stack([sent] + [lax.ppermute(sent, "x", ring(k)) for k in (1, 2, 3)])
     pieces = pieces.astype(f32)
     table = lax.all_to_all(
-        moments.reshape(4 * slabs, 1, BS), ALL, 0, 0
-    ).reshape(4 * slabs, BS)
+        table.reshape(4 * slabs * 5, 1, BS), ALL, 0, 0, tiled=True
+    ).reshape(4 * slabs * 5, BS)
 
     whole = ((ROWS * BS, COLS * BS), bf16, V)
     variant_new, rounded, scales, dense = call(

time: 125 us -> 122 us (0.976)
  waiting for transfers between devices: 24.2 us -> 21.2 us
    ppermute x3, waiting for transfers between devices: 7.64 us -> 0.46 us  [on_device(): got = [lax.ppermute(far[k - 1], 'x', ring(k)) for k in (1, 2, 3)]]
    all_to_all x1, waiting for transfers between devices: 6.16 us -> 8.17 us  [on_device(): lax.all_to_all(table.reshape(4 * slabs * 5, 1, BS), ALL, 0, 0, tiled=True)]
    ppermute x4 -> x5, waiting for transfers between devices: 4.25 us -> 5.99 us  [the longest x1 3.86 us: on_device(): high = lax.ppermute(downward, GEN, [(k + 1, k) for k in range(slabs - 1)])]
    ppermute x4 -> x5, starting transfers between devices: 7 us -> 5.81 us  [the longest x3 3.24 us: on_device(): nears = [near] + [lax.ppermute(near, 'x', ring(k)) for k in (1, 2, 3)]]
    pallas_call x9 -> x8, Pallas kernels: 18.6 us -> 18.9 us  [run(): pl.pallas_call(kernel, out_shape=tuple((placed(*out) for out in outs)), i...]
  transfers between devices with their start and end apart: 17 -> 18, of which waited for: 10 -> 12; matrix products, arithmetic and copies ran while one was open for 1% -> 2% of each run, Pallas kernels for 3% -> 3%
where the time goes in v5:
time: 122 us; the launch traced here: 121 us
  blocking collectives  42.2 us (35%)
  starting transfers between devices  31.1 us (25%)
  waiting for transfers between devices  21.2 us (17%)
  Pallas kernels  18.9 us (15%)
  other arithmetic  4.49 us (4%)
  local copies, waits for them, and re-layouts  1.8 us (1%)
  between operations  1.54 us (1%)
    all_to_all x1, blocking collectives, on_device(): here = lax.all_to_all(sent, CHIP, 0, 0)  21.4 us
    all_to_all x1, blocking collectives, on_device(): arrived = lax.all_to_all(of_chip, CHIP, 0, 0)  20.8 us
    pallas_call x8, Pallas kernels, run(): pl.pallas_call(kernel, out_shape=tuple((placed(*out) for out in outs)), i...  18.9 us
    all_to_all x1, starting transfers between devices, on_device(): lax.all_to_all(table.reshape(4 * slabs * 5, 1, BS), ALL, 0, 0, tiled=True)  10.5 us
    all_to_all x1, waiting for transfers between devices, on_device(): lax.all_to_all(table.reshape(4 * slabs * 5, 1, BS), ALL, 0, 0, tiled=True)  8.17 us
    ppermute x3, starting transfers between devices, on_device(): got = [lax.ppermute(far[k - 1], 'x', ring(k)) for k in (1, 2, 3)]  6.03 us
    ppermute x3, starting transfers between devices, on_device(): lax.ppermute(sent, 'x', ring(k))  4.7 us
    ppermute x3, starting transfers between devices, on_device(): nexts = [lax.ppermute(moments, 'x', ring(k)) for k in (1, 2, 3)]  3.92 us
  transfers between devices with their start and end apart: 18, of which 12 were waited for; matrix products, arithmetic and copies ran while one was open for 2% of the time, Pallas kernels for 3%

profile of v5, /device:TPU:0, one launch (start us, length us, event | category | flops | bytes accessed | tf_op | source)
XLA Modules:
  0.0 121.3 jit_solution(686830692254003968)
XLA Ops:
  1.3 0.1 pad_add_fusion.1.meta
  1.4 7.0 %shard_map.77 = (f32[520,256]{1,0:T(8,128)S(1)}, f32[3,520,256]{2,1,0:T(8,128)S(1)}, f32[128]{0:T(128)S(1)}, f32[8,256]{1,0:T(8,128)S(1)}, f32[8,256]{1,0:T(8,128)S(1)}) custom-call(s32[3]{0:T(128)S(1)} %pad_add_fusion.1.meta, s32[1,1]{1,0:T(1,128)} %copy.17.live, s32[1,1,64]{2,1,0:T(1,128)} %rows_hbm.1, s32[1,1,64]{2,1,0:T(1,128)} %cols_hbm.1, ...), custom_call_target="tpu_custom_call" | custom-call | bytes 20971520 | tf_op jit(solution)/shard_map/pallas_call | solution.py:491
  8.4 0.2 convert_element_type.46
  8.6 0.0 copy-start.1
  8.6 0.2 slice_bitcast_fusion.2
  8.8 1.7 %collective-permute-start = (f16[520,256]{1,0:T(8,128)(2,1)S(1)}, f16[520,256]{1,0:T(8,128)(2,1)S(1)}, u32[]{:S(2)}, u32[]{:S(2)}) collective-permute-start(f16[520,256]{1,0:T(8,128)(2,1)S(1)} %get-tuple-element.26), channel_id=1, source_target_pairs={{0,1},{1,2},{2,3},{3,0},{4,5},{5,6},{6,7},{7,4},{8,9},{9,10},{10,1... | collective-permute-start | bytes 798728 | tf_op jit(solution)/shard_map/ppermute | solution.py:538
  10.5 2.9 %collective-permute-start.1 = (f16[520,256]{1,0:T(8,128)(2,1)S(1)}, f16[520,256]{1,0:T(8,128)(2,1)S(1)}, u32[]{:S(2)}, u32[]{:S(2)}) collective-permute-start(f16[520,256]{1,0:T(8,128)(2,1)S(1)} %get-tuple-element.28), channel_id=1, source_target_pairs={{0,2},{1,3},{2,0},{3,1},{4,6},{5,7},{6,4},{7,5},{8,10},{9,11},{10,... | collective-permute-start | bytes 798728 | tf_op jit(solution)/shard_map/ppermute | solution.py:538
  13.4 1.4 %collective-permute-start.2 = (f16[520,256]{1,0:T(8,128)(2,1)S(1)}, f16[520,256]{1,0:T(8,128)(2,1)S(1)}, u32[]{:S(2)}, u32[]{:S(2)}) collective-permute-start(f16[520,256]{1,0:T(8,128)(2,1)S(1)} %get-tuple-element.27), channel_id=1, source_target_pairs={{0,3},{1,0},{2,1},{3,2},{4,7},{5,4},{6,5},{7,6},{8,11},{9,8},{10,9... | collective-permute-start | bytes 798728 | tf_op jit(solution)/shard_map/ppermute | solution.py:538
  14.8 1.3 %collective-permute-start.3 = (f32[8,256]{1,0:T(8,128)S(1)}, f32[8,256]{1,0:T(8,128)S(1)}, u32[]{:S(2)}, u32[]{:S(2)}) collective-permute-start(f32[8,256]{1,0:T(8,128)S(1)} %get-tuple-element.15), channel_id=1, source_target_pairs={{0,4},{4,8},{8,12},{12,16},{16,20},{20,24},{24,28},{28,32},{32,36}... | collective-permute-start | bytes 24584 | tf_op jit(solution)/shard_map/ppermute | solution.py:539
  16.1 1.3 %collective-permute-start.4 = (f32[8,256]{1,0:T(8,128)S(1)}, f32[8,256]{1,0:T(8,128)S(1)}, u32[]{:S(2)}, u32[]{:S(2)}) collective-permute-start(f32[8,256]{1,0:T(8,128)S(1)} %get-tuple-element.16), channel_id=1, source_target_pairs={{4,0},{8,4},{12,8},{16,12},{20,16},{24,20},{28,24},{32,28},{36,32}... | collective-permute-start | bytes 24584 | tf_op jit(solution)/shard_map/ppermute | solution.py:540
  17.4 0.1 pad_add_fusion.2.meta
  17.5 0.0 collective-permute-done.3
  17.5 3.9 %collective-permute-done.4 = f32[8,256]{1,0:T(8,128)S(1)} collective-permute-done((f32[8,256]{1,0:T(8,128)S(1)}, f32[8,256]{1,0:T(8,128)S(1)}, u32[]{:S(2)}, u32[]{:S(2)}) %collective-permute-start.4) | collective-permute-done | bytes 8224 | tf_op jit(solution)/shard_map/ppermute | solution.py:540
  21.3 0.0 collective-permute-start.5
  21.3 1.5 %collective-permute-start.6 = (f32[16,256]{1,0:T(8,128)S(1)}, f32[16,256]{1,0:T(8,128)S(1)}, u32[]{:S(2)}, u32[]{:S(2)}) collective-permute-start(f32[16,256]{1,0:T(8,128)S(1)} %constant_dynamic-update-slice_fusion.near0), channel_id=1, source_target_pairs={{0,2},{1,3},{2,0},{3,1},{4,6},{5,7},{6,4},{7,5},{8,10},{9,11},{10,... | collective-permute-start | bytes 49160 | tf_op jit(solution)/shard_map/ppermute | solution.py:543
  22.8 0.0 collective-permute-done
  22.8 1.8 %collective-permute-start.7 = (f32[16,256]{1,0:T(8,128)S(1)}, f32[16,256]{1,0:T(8,128)S(1)}, u32[]{:S(2)}, u32[]{:S(2)}) collective-permute-start(f32[16,256]{1,0:T(8,128)S(1)} %constant_dynamic-update-slice_fusion.near0), channel_id=1, source_target_pairs={{0,3},{1,0},{2,1},{3,2},{4,7},{5,4},{6,5},{7,6},{8,11},{9,8},{10,9... | collective-permute-start | bytes 49160 | tf_op jit(solution)/shard_map/ppermute | solution.py:543
  24.6 0.5 collective-permute-done.1
  25.0 0.0 collective-permute-done.2
  25.0 0.1 convert_add_fusion.total
  25.2 1.1 collective-permute-done.5.near1
  26.3 0.3 collective-permute-done.6.near2
  26.6 0.7 collective-permute-done.7.near3
  27.3 0.0 copy-done.1
  27.3 2.3 %shard_map.78 = (f32[2,256,256]{2,1,0:T(8,128)S(1)}, f32[640,128]{1,0:T(8,128)}) custom-call(s32[3]{0:T(128)S(1)} %pad_add_fusion.2.meta, f32[520,256]{1,0:T(8,128)S(1)} %convert_add_fusion.total, f32[1024,256]{1,0:T(8,128)S(1)} %copy-done.1, f32[16,256]{1,0:T(8,128)S(1)} %constant_dynamic-update-slice_fusion.near0, ...), custom_call_target="tpu_custom_call" | custom-call | bytes 1048576 | tf_op jit(solution)/shard_map/pallas_call | solution.py:491
  29.6 1.9 %collective-permute-start.8 = (f16[2,256,256]{2,1,0:T(8,128)(2,1)S(1)}, f16[2,256,256]{2,1,0:T(8,128)(2,1)}, u32[]{:S(2)}, u32[]{:S(2)}) collective-permute-start(f16[2,256,256]{2,1,0:T(8,128)(2,1)S(1)} %convert_element_type.50), channel_id=1, source_target_pairs={{0,1},{1,2},{2,3},{3,0},{4,5},{5,6},{6,7},{7,4},{8,9},{9,10},{10,1... | collective-permute-start | bytes 786440 | tf_op jit(solution)/shard_map/ppermute | solution.py:558
  31.6 2.1 %collective-permute-start.9 = (f16[2,256,256]{2,1,0:T(8,128)(2,1)S(1)}, f16[2,256,256]{2,1,0:T(8,128)(2,1)}, u32[]{:S(2)}, u32[]{:S(2)}) collective-permute-start(f16[2,256,256]{2,1,0:T(8,128)(2,1)S(1)} %convert_element_type.50), channel_id=1, source_target_pairs={{0,2},{1,3},{2,0},{3,1},{4,6},{5,7},{6,4},{7,5},{8,10},{9,11},{10,... | collective-permute-start | bytes 786440 | tf_op jit(solution)/shard_map/ppermute | solution.py:558
  33.7 0.7 collective-permute-start.10
  34.3 0.1 pad_add_fusion.ids
  34.4 10.5 %all-to-all-start = ((f32[640,1,128]{2,1,0:T(1,128)}), f32[640,1,128]{2,1,0:T(1,128)S(1)}, u32[]{:S(2)}, u32[]{:S(2)}) async-start(f32[640,1,128]{2,1,0:T(1,128)} %bitcast.12), calls=%async_computation | async-start | bytes 655360 | tf_op jit(solution)/shard_map/all_to_all | solution.py:560
  45.0 0.0 collective-permute-done.8
  45.0 1.3 %collective-permute-done.9 = f16[2,256,256]{2,1,0:T(8,128)(2,1)} collective-permute-done((f16[2,256,256]{2,1,0:T(8,128)(2,1)S(1)}, f16[2,256,256]{2,1,0:T(8,128)(2,1)}, u32[]{:S(2)}, u32[]{:S(2)}) %collective-permute-start.9) | collective-permute-done | bytes 262176 | tf_op jit(solution)/shard_map/ppermute | solution.py:558
  46.3 0.4 collective-permute-done.10
  46.7 1.3 %maximum_convert_fusion.pieces = f32[4,2,256,256]{3,2,1,0:T(8,128)S(1)} fusion(f16[1,2,256,256]{3,2,1,0:T(8,128)(2,1)} %bitcast.17, f16[1,2,256,256]{3,2,1,0:T(8,128)(2,1)} %bitcast.16, f16[1,2,256,256]{3,2,1,0:T(8,128)(2,1)} %bitcast.15, f16[1,2,256,256]{3,2,1,0:T(8,128)(2,1)S(1)} %convert_bitcast_fusion), kind=kLoop, calls=%fused_computation.3 | loop fusion | flops 2097152 | bytes 3145728 | tf_op jit(solution)/shard_map/convert_element_type | solution.py:559
  48.1 8.2 %all-to-all-done = f32[640,1,128]{2,1,0:T(1,128)S(1)} async-done(((f32[640,1,128]{2,1,0:T(1,128)}), f32[640,1,128]{2,1,0:T(1,128)S(1)}, u32[]{:S(2)}, u32[]{:S(2)}) %all-to-all-start) | async-done | bytes 327712 | tf_op jit(solution)/shard_map/all_to_all | solution.py:560
  56.2 2.6 %shard_map.79 = (f32[1024,256]{1,0:T(8,128)}, bf16[1024,256]{1,0:T(8,128)(2,1)S(1)}, f32[8,128]{1,0:T(8,128)S(1)}, bf16[2048,1024]{1,0:T(8,128)(2,1)S(1)}) custom-call(s32[3]{0:T(128)S(1)} %pad_add_fusion.1.meta, s32[129]{0:T(256)S(1)} %pad_add_fusion.ids, f32[640,128]{1,0:T(8,128)S(1)} %bitcast.31, f32[1024,256]{1,0:T(8,128)S(1)} %copy-done.1, ...), custom_call_target="tpu_custom_call" | custom-call | bytes 1048576 | tf_op jit(solution)/shard_map/pallas_call | solution.py:491
  58.8 2.4 %shard_map.81 = f32[16,136,256]{2,1,0:T(8,128)S(1)} custom-call(s32[3]{0:T(128)S(1)} %pad_add_fusion.1.meta, f32[128]{0:T(128)S(1)} %get-tuple-element.20.mask, f32[8,128]{1,0:T(8,128)S(1)} %get-tuple-element.21.scales, bf16[2048,1024]{1,0:T(8,128)(2,1)S(1)} %get-tuple-element.23.dense, bf16[1024,256]{1,0:T(8,128)(2,1)S(1)} %get-tuple-element.22.rounded), custom_call_target="tpu_custom_call" | custom-call | bytes 1048576 | tf_op jit(solution)/shard_map/pallas_call | solution.py:491
  61.2 0.0 copy-start
  61.2 0.2 convert_element_type.52
  61.4 0.1 collective-permute-start.11
  61.5 1.3 %copy-done = bf16[1,1,64,128,128]{4,3,2,1,0:T(8,128)(2,1)S(1)} copy-done((bf16[1,1,64,128,128]{4,3,2,1,0:T(8,128)(2,1)S(1)}, bf16[1,1,64,128,128]{4,3,2,1,0:T(8,128)(2,1)}, u32[]{:S(2)}) %copy-start) | copy-done | bytes 2097176
  62.8 2.3 %shard_map.80 = f32[16,136,256]{2,1,0:T(8,128)S(1)} custom-call(s32[3]{0:T(128)S(1)} %pad_add_fusion.1.meta, s32[129]{0:T(256)S(1)} %pad_add_fusion.ids, f32[128]{0:T(128)S(1)} %get-tuple-element.20.mask, f32[8,128]{1,0:T(8,128)S(1)} %get-tuple-element.21.scales, bf16[1024,256]{1,0:T(8,128)(2,1)S(1)} %get-tuple-element.22.rounded, ...), custom_call_target="tpu_custom_call" | custom-call | bytes 8388608 | tf_op jit(solution)/shard_map/pallas_call | solution.py:491
  65.1 0.0 collective-permute-done.11
  65.1 0.3 add_convert_fusion
  65.4 0.0 copy-start.2
  65.4 20.8 %all_to_all.15 = f16[16,136,256]{2,1,0:T(8,128)(2,1)S(1)} all-to-all(f16[16,136,256]{2,1,0:T(8,128)(2,1)S(1)} %add_convert_fusion), channel_id=1, replica_groups=mesh['z'=4,'y'=4,'c'=2,'x'=4] {'z','y'}, dimensions={0} | all-to-all | bytes 2228224 | tf_op jit(solution)/shard_map/all_to_all | solution.py:585
  86.2 0.2 convert_reduce_fusion.mine
  86.3 0.1 collective-permute-start.12
  86.4 1.3 %collective-permute-done.12.theirs = f32[136,256]{1,0:T(8,128)S(1)} collective-permute-done((f32[136,256]{1,0:T(8,128)S(1)}, f32[136,256]{1,0:T(8,128)S(1)}, u32[]{:S(2)}, u32[]{:S(2)}) %collective-permute-start.12) | collective-permute-done | bytes 139296 | tf_op jit(solution)/shard_map/ppermute | solution.py:587
  87.7 1.4 %shard_map.82 = f32[136,256]{1,0:T(8,128)S(1)} custom-call(s32[3]{0:T(128)S(1)} %pad_add_fusion.1.meta, f32[136,256]{1,0:T(8,128)S(1)} %convert_reduce_fusion.mine, f32[136,256]{1,0:T(8,128)S(1)} %collective-permute-done.12.theirs, f32[128,256]{1,0:T(8,128)S(1)} %constant_dynamic-slice_fusion.start, f32[8,128]{1,0:T(8,128)S(1)} %get-tuple-element.21.scales), custom_call_target="tpu_custom_call" | custom-call | bytes 1048576 | tf_op jit(solution)/shard_map/pallas_call | solution.py:491
  89.2 0.1 broadcast_in_dim.2
  89.3 21.4 %all_to_all.16 = f16[16,136,256]{2,1,0:T(8,128)(2,1)S(1)} all-to-all(f16[16,136,256]{2,1,0:T(8,128)(2,1)S(1)} %broadcast_in_dim.2), channel_id=1, replica_groups=mesh['z'=4,'y'=4,'c'=2,'x'=4] {'z','y'}, dimensions={0} | all-to-all | bytes 2228224 | tf_op jit(solution)/shard_map/all_to_all | solution.py:593
  110.7 0.0 collective-permute-start.16
  110.8 0.2 shard_map.83.own
  111.0 1.1 collective-permute-start.13
  112.1 2.7 %collective-permute-start.14 = (f32[8,128]{1,0:T(8,128)S(1)}, f32[8,128]{1,0:T(8,128)S(1)}, u32[]{:S(2)}, u32[]{:S(2)}) collective-permute-start(f32[8,128]{1,0:T(8,128)S(1)} %shard_map.83.own), channel_id=1, source_target_pairs={{0,2},{1,3},{2,0},{3,1},{4,6},{5,7},{6,4},{7,5},{8,10},{9,11},{10,... | collective-permute-start | bytes 12296 | tf_op jit(solution)/shard_map/ppermute | solution.py:597
  114.9 0.1 collective-permute-start.15
  114.9 0.9 collective-permute-done.13.next1
  115.8 1.4 %collective-permute-done.14.next2 = f32[8,128]{1,0:T(8,128)S(1)} collective-permute-done((f32[8,128]{1,0:T(8,128)S(1)}, f32[8,128]{1,0:T(8,128)S(1)}, u32[]{:S(2)}, u32[]{:S(2)}) %collective-permute-start.14) | collective-permute-done | bytes 4128 | tf_op jit(solution)/shard_map/ppermute | solution.py:597
  117.3 1.2 collective-permute-done.15.next3
  118.5 0.7 shard_map.84
  119.2 0.2 slice_reduce_fusion.1
  119.4 0.0 collective-permute-done.16
  119.4 1.9 %add_add_fusion = f32[16,128,256]{2,1,0:T(8,128)} fusion(f32[16,128,256]{2,1,0:T(8,128)S(1)} %bitcast.32, f16[16,136,256]{2,1,0:T(8,128)(2,1)S(1)} %collective-permute-done.16, f16[16,136,256]{2,1,0:T(8,128)(2,1)S(1)} %all_to_all.16, f32[16]{0:T(128)S(1)} %get-tuple-element.25, f32[16]{0:T(128)S(1)} %get-tuple-element.24), kind=kLoop, calls=%fused_computation.2 | loop fusion | flops 3145728 | bytes 6291584 | tf_op jit(solution)/shard_map/add | solution.py:605
  (13 shorter events, 0.1 us)
Async XLA Ops:
  8.6 18.8 %copy-start.1 = (f32[1024,256]{1,0:T(8,128)S(1)}, f32[1024,256]{1,0:T(8,128)}, u32[]{:S(2)}) copy-start(f32[1024,256]{1,0:T(8,128)} %start.3) | copy-start | bytes 3145732
  8.8 14.0 %collective-permute-start = (f16[520,256]{1,0:T(8,128)(2,1)S(1)}, f16[520,256]{1,0:T(8,128)(2,1)S(1)}, u32[]{:S(2)}, u32[]{:S(2)}) collective-permute-start(f16[520,256]{1,0:T(8,128)(2,1)S(1)} %get-tuple-element.26), channel_id=1, source_target_pairs={{0,1},{1,2},{2,3},{3,0},{4,5},{5,6},{6,7},{7,4},{8,9},{9,10},{10,1... | collective-permute-start | bytes 798728 | tf_op jit(solution)/shard_map/ppermute | solution.py:538
  10.5 14.5 %collective-permute-start.1 = (f16[520,256]{1,0:T(8,128)(2,1)S(1)}, f16[520,256]{1,0:T(8,128)(2,1)S(1)}, u32[]{:S(2)}, u32[]{:S(2)}) collective-permute-start(f16[520,256]{1,0:T(8,128)(2,1)S(1)} %get-tuple-element.28), channel_id=1, source_target_pairs={{0,2},{1,3},{2,0},{3,1},{4,6},{5,7},{6,4},{7,5},{8,10},{9,11},{10,... | collective-permute-start | bytes 798728 | tf_op jit(solution)/shard_map/ppermute | solution.py:538
  13.4 11.7 %collective-permute-start.2 = (f16[520,256]{1,0:T(8,128)(2,1)S(1)}, f16[520,256]{1,0:T(8,128)(2,1)S(1)}, u32[]{:S(2)}, u32[]{:S(2)}) collective-permute-start(f16[520,256]{1,0:T(8,128)(2,1)S(1)} %get-tuple-element.27), channel_id=1, source_target_pairs={{0,3},{1,0},{2,1},{3,2},{4,7},{5,4},{6,5},{7,6},{8,11},{9,8},{10,9... | collective-permute-start | bytes 798728 | tf_op jit(solution)/shard_map/ppermute | solution.py:538
  14.8 2.7 %collective-permute-start.3 = (f32[8,256]{1,0:T(8,128)S(1)}, f32[8,256]{1,0:T(8,128)S(1)}, u32[]{:S(2)}, u32[]{:S(2)}) collective-permute-start(f32[8,256]{1,0:T(8,128)S(1)} %get-tuple-element.15), channel_id=1, source_target_pairs={{0,4},{4,8},{8,12},{12,16},{16,20},{20,24},{24,28},{28,32},{32,36}... | collective-permute-start | bytes 24584 | tf_op jit(solution)/shard_map/ppermute | solution.py:539
  16.1 5.3 %collective-permute-start.4 = (f32[8,256]{1,0:T(8,128)S(1)}, f32[8,256]{1,0:T(8,128)S(1)}, u32[]{:S(2)}, u32[]{:S(2)}) collective-permute-start(f32[8,256]{1,0:T(8,128)S(1)} %get-tuple-element.16), channel_id=1, source_target_pairs={{4,0},{8,4},{12,8},{16,12},{20,16},{24,20},{28,24},{32,28},{36,32}... | collective-permute-start | bytes 24584 | tf_op jit(solution)/shard_map/ppermute | solution.py:540
  21.3 4.9 %collective-permute-start.5 = (f32[16,256]{1,0:T(8,128)S(1)}, f32[16,256]{1,0:T(8,128)S(1)}, u32[]{:S(2)}, u32[]{:S(2)}) collective-permute-start(f32[16,256]{1,0:T(8,128)S(1)} %constant_dynamic-update-slice_fusion.near0), channel_id=1, source_target_pairs={{0,1},{1,2},{2,3},{3,0},{4,5},{5,6},{6,7},{7,4},{8,9},{9,10},{10,1... | collective-permute-start | bytes 49160 | tf_op jit(solution)/shard_map/ppermute | solution.py:543
  21.3 5.2 %collective-permute-start.6 = (f32[16,256]{1,0:T(8,128)S(1)}, f32[16,256]{1,0:T(8,128)S(1)}, u32[]{:S(2)}, u32[]{:S(2)}) collective-permute-start(f32[16,256]{1,0:T(8,128)S(1)} %constant_dynamic-update-slice_fusion.near0), channel_id=1, source_target_pairs={{0,2},{1,3},{2,0},{3,1},{4,6},{5,7},{6,4},{7,5},{8,10},{9,11},{10,... | collective-permute-start | bytes 49160 | tf_op jit(solution)/shard_map/ppermute | solution.py:543
  22.8 4.5 %collective-permute-start.7 = (f32[16,256]{1,0:T(8,128)S(1)}, f32[16,256]{1,0:T(8,128)S(1)}, u32[]{:S(2)}, u32[]{:S(2)}) collective-permute-start(f32[16,256]{1,0:T(8,128)S(1)} %constant_dynamic-update-slice_fusion.near0), channel_id=1, source_target_pairs={{0,3},{1,0},{2,1},{3,2},{4,7},{5,4},{6,5},{7,6},{8,11},{9,8},{10,9... | collective-permute-start | bytes 49160 | tf_op jit(solution)/shard_map/ppermute | solution.py:543
  25.0 9.3 %copy-start.3 = (s32[1,1,64]{2,1,0:T(1,128)S(1)}, s32[1,1,64]{2,1,0:T(1,128)}, u32[]{:S(2)}) copy-start(s32[1,1,64]{2,1,0:T(1,128)} %cols_hbm.1) | copy-start | bytes 772
  25.0 9.3 %copy-start.4 = (s32[1,1,64]{2,1,0:T(1,128)S(1)}, s32[1,1,64]{2,1,0:T(1,128)}, u32[]{:S(2)}) copy-start(s32[1,1,64]{2,1,0:T(1,128)} %rows_hbm.1) | copy-start | bytes 772
  29.6 15.3 %collective-permute-start.8 = (f16[2,256,256]{2,1,0:T(8,128)(2,1)S(1)}, f16[2,256,256]{2,1,0:T(8,128)(2,1)}, u32[]{:S(2)}, u32[]{:S(2)}) collective-permute-start(f16[2,256,256]{2,1,0:T(8,128)(2,1)S(1)} %convert_element_type.50), channel_id=1, source_target_pairs={{0,1},{1,2},{2,3},{3,0},{4,5},{5,6},{6,7},{7,4},{8,9},{9,10},{10,1... | collective-permute-start | bytes 786440 | tf_op jit(solution)/shard_map/ppermute | solution.py:558
  31.6 14.7 %collective-permute-start.9 = (f16[2,256,256]{2,1,0:T(8,128)(2,1)S(1)}, f16[2,256,256]{2,1,0:T(8,128)(2,1)}, u32[]{:S(2)}, u32[]{:S(2)}) collective-permute-start(f16[2,256,256]{2,1,0:T(8,128)(2,1)S(1)} %convert_element_type.50), channel_id=1, source_target_pairs={{0,2},{1,3},{2,0},{3,1},{4,6},{5,7},{6,4},{7,5},{8,10},{9,11},{10,... | collective-permute-start | bytes 786440 | tf_op jit(solution)/shard_map/ppermute | solution.py:558
  33.7 13.0 %collective-permute-start.10 = (f16[2,256,256]{2,1,0:T(8,128)(2,1)S(1)}, f16[2,256,256]{2,1,0:T(8,128)(2,1)}, u32[]{:S(2)}, u32[]{:S(2)}) collective-permute-start(f16[2,256,256]{2,1,0:T(8,128)(2,1)S(1)} %convert_element_type.50), channel_id=1, source_target_pairs={{0,3},{1,0},{2,1},{3,2},{4,7},{5,4},{6,5},{7,6},{8,11},{9,8},{10,9... | collective-permute-start | bytes 786440 | tf_op jit(solution)/shard_map/ppermute | solution.py:558
  34.4 21.8 %all-to-all-start = ((f32[640,1,128]{2,1,0:T(1,128)}), f32[640,1,128]{2,1,0:T(1,128)S(1)}, u32[]{:S(2)}, u32[]{:S(2)}) async-start(f32[640,1,128]{2,1,0:T(1,128)} %bitcast.12), calls=%async_computation | async-start | bytes 655360 | tf_op jit(solution)/shard_map/all_to_all | solution.py:560
  61.2 1.6 %copy-start = (bf16[1,1,64,128,128]{4,3,2,1,0:T(8,128)(2,1)S(1)}, bf16[1,1,64,128,128]{4,3,2,1,0:T(8,128)(2,1)}, u32[]{:S(2)}) copy-start(bf16[1,1,64,128,128]{4,3,2,1,0:T(8,128)(2,1)} %tiles.1) | copy-start | bytes 6291460
  61.4 3.7 %collective-permute-start.11 = (f16[16,136,256]{2,1,0:T(8,128)(2,1)S(1)}, f16[16,136,256]{2,1,0:T(8,128)(2,1)S(1)}, u32[]{:S(2)}, u32[]{:S(2)}) collective-permute-start(f16[16,136,256]{2,1,0:T(8,128)(2,1)S(1)} %convert_element_type.52), channel_id=1, source_target_pairs={{0,4},{4,0},{1,5},{5,1},{2,6},{6,2},{3,7},{7,3},{8,12},{12,8},{9,1... | collective-permute-start | bytes 3342344 | tf_op jit(solution)/shard_map/ppermute | solution.py:576
  65.4 21.0 %copy-start.2 = (f32[2048,256]{1,0:T(8,128)S(1)}, f32[2048,256]{1,0:T(8,128)}, u32[]{:S(2)}) copy-start(f32[2048,256]{1,0:T(8,128)} %factors_hbm.1) | copy-start | bytes 6291460
  86.3 1.4 %collective-permute-start.12 = (f32[136,256]{1,0:T(8,128)S(1)}, f32[136,256]{1,0:T(8,128)S(1)}, u32[]{:S(2)}, u32[]{:S(2)}) collective-permute-start(f32[136,256]{1,0:T(8,128)S(1)} %convert_reduce_fusion.mine), channel_id=1, source_target_pairs={{0,4},{4,0},{1,5},{5,1},{2,6},{6,2},{3,7},{7,3},{8,12},{12,8},{9,1... | collective-permute-start | bytes 417800 | tf_op jit(solution)/shard_map/ppermute | solution.py:587
  110.7 8.6 %collective-permute-start.16 = (f16[16,136,256]{2,1,0:T(8,128)(2,1)S(1)}, f16[16,136,256]{2,1,0:T(8,128)(2,1)S(1)}, u32[]{:S(2)}, u32[]{:S(2)}) collective-permute-start(f16[16,136,256]{2,1,0:T(8,128)(2,1)S(1)} %all_to_all.16), channel_id=1, source_target_pairs={{0,4},{4,0},{1,5},{5,1},{2,6},{6,2},{3,7},{7,3},{8,12},{12,8},{9,1... | collective-permute-start | bytes 3342344 | tf_op jit(solution)/shard_map/ppermute | solution.py:594
  111.0 4.8 %collective-permute-start.13 = (f32[8,128]{1,0:T(8,128)S(1)}, f32[8,128]{1,0:T(8,128)S(1)}, u32[]{:S(2)}, u32[]{:S(2)}) collective-permute-start(f32[8,128]{1,0:T(8,128)S(1)} %shard_map.83.own), channel_id=1, source_target_pairs={{0,1},{1,2},{2,3},{3,0},{4,5},{5,6},{6,7},{7,4},{8,9},{9,10},{10,1... | collective-permute-start | bytes 12296 | tf_op jit(solution)/shard_map/ppermute | solution.py:597
  112.1 5.1 %collective-permute-start.14 = (f32[8,128]{1,0:T(8,128)S(1)}, f32[8,128]{1,0:T(8,128)S(1)}, u32[]{:S(2)}, u32[]{:S(2)}) collective-permute-start(f32[8,128]{1,0:T(8,128)S(1)} %shard_map.83.own), channel_id=1, source_target_pairs={{0,2},{1,3},{2,0},{3,1},{4,6},{5,7},{6,4},{7,5},{8,10},{9,11},{10,... | collective-permute-start | bytes 12296 | tf_op jit(solution)/shard_map/ppermute | solution.py:597
  114.9 3.6 %collective-permute-start.15 = (f32[8,128]{1,0:T(8,128)S(1)}, f32[8,128]{1,0:T(8,128)S(1)}, u32[]{:S(2)}, u32[]{:S(2)}) collective-permute-start(f32[8,128]{1,0:T(8,128)S(1)} %shard_map.83.own), channel_id=1, source_target_pairs={{0,3},{1,0},{2,1},{3,2},{4,7},{5,4},{6,5},{7,6},{8,11},{9,8},{10,9... | collective-permute-start | bytes 12296 | tf_op jit(solution)/shard_map/ppermute | solution.py:597

commit v6 on v5

--- a/solution.py
+++ b/solution.py
@@ -60,7 +60,7 @@
     )
 
 
-def scatter(row_of, col_of, live, tiles, dense, mask=None):
+def scatter(row_of, col_of, live, tiles, dense, mask=None, begin=0, end=NB):
     def four(step, carry):
         for k in range(4):
             s = jnp.minimum(step * 4 + k, live - 1)
@@ -72,11 +72,11 @@
                 mask[row * COLS + col] = 1.0
         return carry
 
-    lax.fori_loop(0, (live + 3) // 4, four, 0)
-
-
-def fill(ids, tiles, dense):
-    scatter(lambda s: ids[s], lambda s: ids[NB + s], ids[2 * NB], tiles, dense)
+    lax.fori_loop(begin // 4, jnp.minimum((live + 3) // 4, end // 4), four, 0)
+
+
+def fill(ids, tiles, dense, **bounds):
+    scatter(lambda s: ids[s], lambda s: ids[NB + s], ids[2 * NB], tiles, dense, **bounds)
 
 
 def variant_sums(
@@ -300,10 +300,10 @@
 
 
 def new_variants(
-    meta, ids, table, start, pieces, tiles_hbm, new_hbm, rounded, scales, dense, new, tiles, sems
+    meta, ids, table, start, pieces, tiles_hbm, new, rounded, scales, dense, tiles, sem
 ):
     me, core, slab = meta[0], meta[1], meta[2]
-    load = pltpu.make_async_copy(tiles_hbm.at[0, 0], tiles, sems.at[4])
+    load = pltpu.make_async_copy(tiles_hbm.at[0, 0], tiles, sem)
     load.start()
 
     @pl.when(core == 1)
@@ -321,7 +321,6 @@
     rr, ra, aa, aaa = (sums[:, k : k + 1] for k in range(4))
     on_resid, on_applied, _, _ = curve_of(rr, ra, aa, aaa - 2.0 * smooth_weight * total_of(across))
     n = 2 * BS
-    keeps = []
     for k in range(4):
         owner = lax.rem(me - k + 4, 4)
         rows = pl.ds(pl.multiple_of(owner * n, n), n)
@@ -335,9 +334,6 @@
         )
         new[rows, :] = value
         rounded[rows, :] = value.astype(bf16)
-        keep = pltpu.make_async_copy(new.at[rows, :], new_hbm.at[rows, :], sems.at[k])
-        keep.start()
-        keeps.append(keep)
     top = jnp.abs(on_resid) * peaks[:, 4:5] + jnp.abs(on_applied) * peaks[:, 5:6] + 1.5
     scale_e = 30000.0 / (2.0 * 6.0 * COLS * BS * top)
     scale_h = 30000.0 / (2.0 * COLS * BS * top * top)
@@ -347,9 +343,6 @@
     @pl.when(core == 1)
     def _():
         fill(ids, tiles, dense)
-
-    for keep in keeps:
-        keep.wait()
 
 
 def tile_sums(scale, dense, rounded, pay):
@@ -386,7 +379,10 @@
         pay[r, BS:, :] = jnp.where(lines == 0, row, 0.0)
 
 
-def sums_to_send(meta, mask, scales, dense, rounded, pay, grams, diags):
+def sums_to_send(meta, mask, scales, dense, rounded, new, pay, new_hbm, grams, diags, sem):
+    keep = pltpu.make_async_copy(new, new_hbm, sem)
+    keep.start()
+
     @pl.when(meta[1] == 1)
     def _():
         tile_sums(scales[0:1, 0:1], dense, rounded, pay)
@@ -395,12 +391,27 @@
     def _():
         gram_sums(scales[0:1, 1:2], mask, rounded, pay, grams, diags)
 
-
-def sums_to_keep(meta, ids, mask, scales, rounded, tiles, pay, dense, grams, diags):
+    keep.wait()
+
+
+def sums_to_keep(meta, ids, mask, scales, rounded, tiles_hbm, pay, dense, tiles, grams, diags, sems):
     @pl.when(meta[1] == 0)
     def _():
+        quarter = NB // 4
+        loads = [
+            pltpu.make_async_copy(
+                tiles_hbm.at[0, 0, pl.ds(k * quarter, quarter)],
+                tiles.at[pl.ds(k * quarter, quarter)],
+                sems.at[k],
+            )
+            for k in range(4)
+        ]
+        for load in loads:
+            load.start()
         dense[...] = jnp.zeros_like(dense)
-        fill(ids, tiles.at[0, 0], dense)
+        for k, load in enumerate(loads):
+            load.wait()
+            fill(ids, tiles, dense, begin=k * quarter, end=(k + 1) * quarter)
         tile_sums(scales[0:1, 0:1], dense, rounded, pay)
 
     @pl.when(meta[1] == 1)
@@ -562,23 +573,31 @@
     ).reshape(4 * slabs * 5, BS)
 
     whole = ((ROWS * BS, COLS * BS), bf16, V)
-    variant_new, rounded, scales, dense = call(
+    new, rounded, scales, dense = call(
         new_variants,
         [S, S, V, V, V, H],
-        [((COLS * BS, R), f32, H), ((COLS * BS, R), bf16, V), row, whole],
-        [pltpu.VMEM((COLS * BS, R), f32), big, pltpu.SemaphoreType.DMA((5,))],
+        [((COLS * BS, R), f32, V), ((COLS * BS, R), bf16, V), row, whole],
+        [big, pltpu.SemaphoreType.DMA],
     )(meta, ids, table, variant_factors, pieces, dosage_tiles)
     sums = ((ROWS, PAY_I, R), f32, V)
     scratch = [pltpu.VMEM((COLS, BS, R), f32), pltpu.VMEM((COLS, BS), f32)]
-    (pay,) = call(sums_to_send, [S, S, V, V, V], [sums], scratch)(
-        meta, mask, scales, dense, rounded
-    )
+    pay, variant_new = call(
+        sums_to_send,
+        [S, S, V, V, V, V],
+        [sums, ((COLS * BS, R), f32, H)],
+        scratch + [pltpu.SemaphoreType.DMA],
+    )(meta, mask, scales, dense, rounded, new)
     from_other = lax.ppermute(pay.astype(f16), "c", swap)
     (pay,) = call(
         sums_to_keep,
-        [S, S, S, V, V, V],
+        [S, S, S, V, V, H],
         [sums],
-        [pltpu.VMEM((ROWS * BS, COLS * BS), bf16), *scratch],
+        [
+            pltpu.VMEM((ROWS * BS, COLS * BS), bf16),
+            big,
+            *scratch,
+            pltpu.SemaphoreType.DMA((4,)),
+        ],
         8 << 20,
     )(meta, ids, mask, scales, rounded, dosage_tiles)
     of_chip = (pay + from_other.astype(f32)).astype(f16)

time: 122 us -> 121 us (level)
  Pallas kernels: 18.9 us -> 20.5 us
  local copies, waits for them, and re-layouts: 1.8 us -> 0.49 us
    pallas_call x8, Pallas kernels: 18.9 us -> 20.5 us  [run(): pl.pallas_call(kernel, out_shape=tuple((placed(*out) for out in outs)), i...]
    unnamed x11 -> x9, local copies, waits for them, and re-layouts: 1.33 us -> 0.02 us
  transfers between devices with their start and end apart: 18 -> 18, of which waited for: 12 -> 12; matrix products, arithmetic and copies ran while one was open for 2% -> 2% of each run, Pallas kernels for 3% -> 4%
where the time goes in v6:
time: 121 us
  blocking collectives  41.8 us (35%)
  starting transfers between devices  31.3 us (26%)
  waiting for transfers between devices  20.9 us (17%)
  Pallas kernels  20.5 us (17%)
  other arithmetic  4.58 us (4%)
  between operations  1.52 us (1%)
    all_to_all x1, blocking collectives, on_device(): here = lax.all_to_all(sent, CHIP, 0, 0)  21.4 us
    pallas_call x8, Pallas kernels, run(): pl.pallas_call(kernel, out_shape=tuple((placed(*out) for out in outs)), i...  20.5 us
    all_to_all x1, blocking collectives, on_device(): arrived = lax.all_to_all(of_chip, CHIP, 0, 0)  20.4 us
    all_to_all x1, starting transfers between devices, on_device(): lax.all_to_all(table.reshape(4 * slabs * 5, 1, BS), ALL, 0, 0, tiled=True)  10.8 us
    all_to_all x1, waiting for transfers between devices, on_device(): lax.all_to_all(table.reshape(4 * slabs * 5, 1, BS), ALL, 0, 0, tiled=True)  8.47 us
    ppermute x3, starting transfers between devices, on_device(): got = [lax.ppermute(far[k - 1], 'x', ring(k)) for k in (1, 2, 3)]  5.79 us
    ppermute x3, starting transfers between devices, on_device(): lax.ppermute(sent, 'x', ring(k))  4.69 us
    ppermute x3, starting transfers between devices, on_device(): nexts = [lax.ppermute(moments, 'x', ring(k)) for k in (1, 2, 3)]  3.98 us
  transfers between devices with their start and end apart: 18, of which 12 were waited for; matrix products, arithmetic and copies ran while one was open for 2% of the time, Pallas kernels for 4%

profile of v6, /device:TPU:0, one launch (start us, length us, event | category | flops | bytes accessed | tf_op | source)
XLA Modules:
  0.0 121.0 jit_solution(5114594845938806276)
XLA Ops:
  1.3 0.1 pad_add_fusion.1.meta
  1.4 7.7 %shard_map.77 = (f32[520,256]{1,0:T(8,128)S(1)}, f32[3,520,256]{2,1,0:T(8,128)S(1)}, f32[128]{0:T(128)S(1)}, f32[8,256]{1,0:T(8,128)S(1)}, f32[8,256]{1,0:T(8,128)S(1)}) custom-call(s32[3]{0:T(128)S(1)} %pad_add_fusion.1.meta, s32[1,1]{1,0:T(1,128)} %copy.17.live, s32[1,1,64]{2,1,0:T(1,128)} %rows_hbm.1, s32[1,1,64]{2,1,0:T(1,128)} %cols_hbm.1, ...), custom_call_target="tpu_custom_call" | custom-call | bytes 20971520 | tf_op jit(solution)/shard_map/pallas_call | solution.py:502
  9.0 0.2 convert_element_type.46
  9.2 0.0 copy-start
  9.2 0.2 slice_bitcast_fusion.2
  9.4 1.6 %collective-permute-start = (f16[520,256]{1,0:T(8,128)(2,1)S(1)}, f16[520,256]{1,0:T(8,128)(2,1)S(1)}, u32[]{:S(2)}, u32[]{:S(2)}) collective-permute-start(f16[520,256]{1,0:T(8,128)(2,1)S(1)} %get-tuple-element.30), channel_id=1, source_target_pairs={{0,1},{1,2},{2,3},{3,0},{4,5},{5,6},{6,7},{7,4},{8,9},{9,10},{10,1... | collective-permute-start | bytes 798728 | tf_op jit(solution)/shard_map/ppermute | solution.py:549
  11.0 2.7 %collective-permute-start.1 = (f16[520,256]{1,0:T(8,128)(2,1)S(1)}, f16[520,256]{1,0:T(8,128)(2,1)S(1)}, u32[]{:S(2)}, u32[]{:S(2)}) collective-permute-start(f16[520,256]{1,0:T(8,128)(2,1)S(1)} %get-tuple-element.32), channel_id=1, source_target_pairs={{0,2},{1,3},{2,0},{3,1},{4,6},{5,7},{6,4},{7,5},{8,10},{9,11},{10,... | collective-permute-start | bytes 798728 | tf_op jit(solution)/shard_map/ppermute | solution.py:549
  13.7 1.4 %collective-permute-start.2 = (f16[520,256]{1,0:T(8,128)(2,1)S(1)}, f16[520,256]{1,0:T(8,128)(2,1)S(1)}, u32[]{:S(2)}, u32[]{:S(2)}) collective-permute-start(f16[520,256]{1,0:T(8,128)(2,1)S(1)} %get-tuple-element.31), channel_id=1, source_target_pairs={{0,3},{1,0},{2,1},{3,2},{4,7},{5,4},{6,5},{7,6},{8,11},{9,8},{10,9... | collective-permute-start | bytes 798728 | tf_op jit(solution)/shard_map/ppermute | solution.py:549
  15.2 1.3 %collective-permute-start.3 = (f32[8,256]{1,0:T(8,128)S(1)}, f32[8,256]{1,0:T(8,128)S(1)}, u32[]{:S(2)}, u32[]{:S(2)}) collective-permute-start(f32[8,256]{1,0:T(8,128)S(1)} %get-tuple-element.18), channel_id=1, source_target_pairs={{0,4},{4,8},{8,12},{12,16},{16,20},{20,24},{24,28},{28,32},{32,36}... | collective-permute-start | bytes 24584 | tf_op jit(solution)/shard_map/ppermute | solution.py:550
  16.5 1.3 %collective-permute-start.4 = (f32[8,256]{1,0:T(8,128)S(1)}, f32[8,256]{1,0:T(8,128)S(1)}, u32[]{:S(2)}, u32[]{:S(2)}) collective-permute-start(f32[8,256]{1,0:T(8,128)S(1)} %get-tuple-element.19), channel_id=1, source_target_pairs={{4,0},{8,4},{12,8},{16,12},{20,16},{24,20},{28,24},{32,28},{36,32}... | collective-permute-start | bytes 24584 | tf_op jit(solution)/shard_map/ppermute | solution.py:551
  17.8 0.1 pad_add_fusion.2.meta
  17.8 0.0 collective-permute-done.3
  17.8 3.5 %collective-permute-done.4 = f32[8,256]{1,0:T(8,128)S(1)} collective-permute-done((f32[8,256]{1,0:T(8,128)S(1)}, f32[8,256]{1,0:T(8,128)S(1)}, u32[]{:S(2)}, u32[]{:S(2)}) %collective-permute-start.4) | collective-permute-done | bytes 8224 | tf_op jit(solution)/shard_map/ppermute | solution.py:551
  21.3 0.6 collective-permute-start.5
  21.9 0.9 collective-permute-start.6
  22.8 0.0 collective-permute-done
  22.8 1.8 %collective-permute-start.7 = (f32[16,256]{1,0:T(8,128)S(1)}, f32[16,256]{1,0:T(8,128)S(1)}, u32[]{:S(2)}, u32[]{:S(2)}) collective-permute-start(f32[16,256]{1,0:T(8,128)S(1)} %constant_dynamic-update-slice_fusion.near0), channel_id=1, source_target_pairs={{0,3},{1,0},{2,1},{3,2},{4,7},{5,4},{6,5},{7,6},{8,11},{9,8},{10,9... | collective-permute-start | bytes 49160 | tf_op jit(solution)/shard_map/ppermute | solution.py:554
  24.6 0.3 collective-permute-done.1
  24.9 0.0 collective-permute-done.2
  24.9 0.1 convert_add_fusion.total
  25.1 1.2 collective-permute-done.5.near1
  26.3 0.9 collective-permute-done.6.near2
  27.2 0.1 collective-permute-done.7.near3
  27.3 0.0 copy-done
  27.3 2.3 %shard_map.78 = (f32[2,256,256]{2,1,0:T(8,128)S(1)}, f32[640,128]{1,0:T(8,128)}) custom-call(s32[3]{0:T(128)S(1)} %pad_add_fusion.2.meta, f32[520,256]{1,0:T(8,128)S(1)} %convert_add_fusion.total, f32[1024,256]{1,0:T(8,128)S(1)} %copy-done, f32[16,256]{1,0:T(8,128)S(1)} %constant_dynamic-update-slice_fusion.near0, ...), custom_call_target="tpu_custom_call" | custom-call | bytes 1048576 | tf_op jit(solution)/shard_map/pallas_call | solution.py:502
  29.7 1.9 %collective-permute-start.8 = (f16[2,256,256]{2,1,0:T(8,128)(2,1)S(1)}, f16[2,256,256]{2,1,0:T(8,128)(2,1)}, u32[]{:S(2)}, u32[]{:S(2)}) collective-permute-start(f16[2,256,256]{2,1,0:T(8,128)(2,1)S(1)} %convert_element_type.50), channel_id=1, source_target_pairs={{0,1},{1,2},{2,3},{3,0},{4,5},{5,6},{6,7},{7,4},{8,9},{9,10},{10,1... | collective-permute-start | bytes 786440 | tf_op jit(solution)/shard_map/ppermute | solution.py:569
  31.6 2.1 %collective-permute-start.9 = (f16[2,256,256]{2,1,0:T(8,128)(2,1)S(1)}, f16[2,256,256]{2,1,0:T(8,128)(2,1)}, u32[]{:S(2)}, u32[]{:S(2)}) collective-permute-start(f16[2,256,256]{2,1,0:T(8,128)(2,1)S(1)} %convert_element_type.50), channel_id=1, source_target_pairs={{0,2},{1,3},{2,0},{3,1},{4,6},{5,7},{6,4},{7,5},{8,10},{9,11},{10,... | collective-permute-start | bytes 786440 | tf_op jit(solution)/shard_map/ppermute | solution.py:569
  33.7 0.7 collective-permute-start.10
  34.3 0.0 copy-done.2
  34.3 0.1 pad_add_fusion.ids
  34.4 10.8 %all-to-all-start = ((f32[640,1,128]{2,1,0:T(1,128)}), f32[640,1,128]{2,1,0:T(1,128)S(1)}, u32[]{:S(2)}, u32[]{:S(2)}) async-start(f32[640,1,128]{2,1,0:T(1,128)} %bitcast.12), calls=%async_computation | async-start | bytes 655360 | tf_op jit(solution)/shard_map/all_to_all | solution.py:571
  45.3 0.0 collective-permute-done.8
  45.3 1.0 collective-permute-done.9
  46.3 0.5 collective-permute-done.10
  46.7 1.3 %maximum_convert_fusion.pieces = f32[4,2,256,256]{3,2,1,0:T(8,128)S(1)} fusion(f16[1,2,256,256]{3,2,1,0:T(8,128)(2,1)} %bitcast.17, f16[1,2,256,256]{3,2,1,0:T(8,128)(2,1)} %bitcast.16, f16[1,2,256,256]{3,2,1,0:T(8,128)(2,1)} %bitcast.15, f16[1,2,256,256]{3,2,1,0:T(8,128)(2,1)S(1)} %convert_bitcast_fusion), kind=kLoop, calls=%fused_computation.3 | loop fusion | flops 2097152 | bytes 3145728 | tf_op jit(solution)/shard_map/convert_element_type | solution.py:570
  48.1 8.5 %all-to-all-done = f32[640,1,128]{2,1,0:T(1,128)S(1)} async-done(((f32[640,1,128]{2,1,0:T(1,128)}), f32[640,1,128]{2,1,0:T(1,128)S(1)}, u32[]{:S(2)}, u32[]{:S(2)}) %all-to-all-start) | async-done | bytes 327712 | tf_op jit(solution)/shard_map/all_to_all | solution.py:571
  56.5 2.2 %shard_map.79 = (f32[1024,256]{1,0:T(8,128)S(1)}, bf16[1024,256]{1,0:T(8,128)(2,1)S(1)}, f32[8,128]{1,0:T(8,128)S(1)}, bf16[2048,1024]{1,0:T(8,128)(2,1)S(1)}) custom-call(s32[3]{0:T(128)S(1)} %pad_add_fusion.1.meta, s32[129]{0:T(256)S(1)} %pad_add_fusion.ids, f32[640,128]{1,0:T(8,128)S(1)} %bitcast.31, f32[1024,256]{1,0:T(8,128)S(1)} %copy-done, ...), custom_call_target="tpu_custom_call" | custom-call | bytes 1048576 | tf_op jit(solution)/shard_map/pallas_call | solution.py:502
  58.7 2.4 %shard_map.80 = (f32[16,136,256]{2,1,0:T(8,128)S(1)}, f32[1024,256]{1,0:T(8,128)}) custom-call(s32[3]{0:T(128)S(1)} %pad_add_fusion.1.meta, f32[128]{0:T(128)S(1)} %get-tuple-element.15.mask, f32[8,128]{1,0:T(8,128)S(1)} %get-tuple-element.22.scales, bf16[2048,1024]{1,0:T(8,128)(2,1)S(1)} %get-tuple-element.23.dense, ...), custom_call_target="tpu_custom_call" | custom-call | bytes 1048576 | tf_op jit(solution)/shard_map/pallas_call | solution.py:502
  61.1 0.2 convert_element_type.52
  61.3 0.1 collective-permute-start.11
  61.4 3.7 %shard_map.81 = f32[16,136,256]{2,1,0:T(8,128)S(1)} custom-call(s32[3]{0:T(128)S(1)} %pad_add_fusion.1.meta, s32[129]{0:T(256)S(1)} %pad_add_fusion.ids, f32[128]{0:T(128)S(1)} %get-tuple-element.15.mask, f32[8,128]{1,0:T(8,128)S(1)} %get-tuple-element.22.scales, bf16[1024,256]{1,0:T(8,128)(2,1)S(1)} %get-tuple-element.24.rounded, ...), custom_call_target="tpu_custom_call" | custom-call | bytes 8388608 | tf_op jit(solution)/shard_map/pallas_call | solution.py:502
  65.1 0.0 collective-permute-done.11
  65.1 0.4 add_convert_fusion
  65.5 0.0 copy-start.1
  65.5 20.4 %all_to_all.15 = f16[16,136,256]{2,1,0:T(8,128)(2,1)S(1)} all-to-all(f16[16,136,256]{2,1,0:T(8,128)(2,1)S(1)} %add_convert_fusion), channel_id=1, replica_groups=mesh['z'=4,'y'=4,'c'=2,'x'=4] {'z','y'}, dimensions={0} | all-to-all | bytes 2228224 | tf_op jit(solution)/shard_map/all_to_all | solution.py:604
  85.8 0.2 convert_reduce_fusion.mine
  86.0 0.1 collective-permute-start.12
  86.1 0.0 copy-done.1
  86.1 1.3 %collective-permute-done.12.theirs = f32[136,256]{1,0:T(8,128)S(1)} collective-permute-done((f32[136,256]{1,0:T(8,128)S(1)}, f32[136,256]{1,0:T(8,128)S(1)}, u32[]{:S(2)}, u32[]{:S(2)}) %collective-permute-start.12) | collective-permute-done | bytes 139296 | tf_op jit(solution)/shard_map/ppermute | solution.py:606
  87.4 1.4 %shard_map.82 = f32[136,256]{1,0:T(8,128)S(1)} custom-call(s32[3]{0:T(128)S(1)} %pad_add_fusion.1.meta, f32[136,256]{1,0:T(8,128)S(1)} %convert_reduce_fusion.mine, f32[136,256]{1,0:T(8,128)S(1)} %collective-permute-done.12.theirs, f32[128,256]{1,0:T(8,128)S(1)} %constant_dynamic-slice_fusion.start, f32[8,128]{1,0:T(8,128)S(1)} %get-tuple-element.22.scales), custom_call_target="tpu_custom_call" | custom-call | bytes 1048576 | tf_op jit(solution)/shard_map/pallas_call | solution.py:502
  88.9 0.1 broadcast_in_dim.2
  89.0 21.4 %all_to_all.16 = f16[16,136,256]{2,1,0:T(8,128)(2,1)S(1)} all-to-all(f16[16,136,256]{2,1,0:T(8,128)(2,1)S(1)} %broadcast_in_dim.2), channel_id=1, replica_groups=mesh['z'=4,'y'=4,'c'=2,'x'=4] {'z','y'}, dimensions={0} | all-to-all | bytes 2228224 | tf_op jit(solution)/shard_map/all_to_all | solution.py:612
  110.4 0.0 collective-permute-start.16
  110.4 0.2 shard_map.83.own
  110.6 1.2 collective-permute-start.13
  111.8 2.8 %collective-permute-start.14 = (f32[8,128]{1,0:T(8,128)S(1)}, f32[8,128]{1,0:T(8,128)S(1)}, u32[]{:S(2)}, u32[]{:S(2)}) collective-permute-start(f32[8,128]{1,0:T(8,128)S(1)} %shard_map.83.own), channel_id=1, source_target_pairs={{0,2},{1,3},{2,0},{3,1},{4,6},{5,7},{6,4},{7,5},{8,10},{9,11},{10,... | collective-permute-start | bytes 12296 | tf_op jit(solution)/shard_map/ppermute | solution.py:616
  114.6 0.0 collective-permute-start.15
  114.6 0.8 collective-permute-done.13.next1
  115.5 1.4 %collective-permute-done.14.next2 = f32[8,128]{1,0:T(8,128)S(1)} collective-permute-done((f32[8,128]{1,0:T(8,128)S(1)}, f32[8,128]{1,0:T(8,128)S(1)}, u32[]{:S(2)}, u32[]{:S(2)}) %collective-permute-start.14) | collective-permute-done | bytes 4128 | tf_op jit(solution)/shard_map/ppermute | solution.py:616
  116.9 1.3 %collective-permute-done.15.next3 = f32[8,128]{1,0:T(8,128)S(1)} collective-permute-done((f32[8,128]{1,0:T(8,128)S(1)}, f32[8,128]{1,0:T(8,128)S(1)}, u32[]{:S(2)}, u32[]{:S(2)}) %collective-permute-start.15) | collective-permute-done | bytes 4128 | tf_op jit(solution)/shard_map/ppermute | solution.py:616
  118.2 0.7 shard_map.84
  118.9 0.2 slice_reduce_fusion.1
  119.1 0.0 collective-permute-done.16
  119.1 1.9 %add_add_fusion = f32[16,128,256]{2,1,0:T(8,128)} fusion(f32[16,128,256]{2,1,0:T(8,128)S(1)} %bitcast.32, f16[16,136,256]{2,1,0:T(8,128)(2,1)S(1)} %collective-permute-done.16, f16[16,136,256]{2,1,0:T(8,128)(2,1)S(1)} %all_to_all.16, f32[16]{0:T(128)S(1)} %get-tuple-element.29, f32[16]{0:T(128)S(1)} %get-tuple-element.28), kind=kLoop, calls=%fused_computation.2 | loop fusion | flops 3145728 | bytes 6291584 | tf_op jit(solution)/shard_map/add | solution.py:624
  (11 shorter events, 0.1 us)
Async XLA Ops:
  9.2 18.1 %copy-start = (f32[1024,256]{1,0:T(8,128)S(1)}, f32[1024,256]{1,0:T(8,128)}, u32[]{:S(2)}) copy-start(f32[1024,256]{1,0:T(8,128)} %start.3) | copy-start | bytes 3145732
  9.4 13.4 %collective-permute-start = (f16[520,256]{1,0:T(8,128)(2,1)S(1)}, f16[520,256]{1,0:T(8,128)(2,1)S(1)}, u32[]{:S(2)}, u32[]{:S(2)}) collective-permute-start(f16[520,256]{1,0:T(8,128)(2,1)S(1)} %get-tuple-element.30), channel_id=1, source_target_pairs={{0,1},{1,2},{2,3},{3,0},{4,5},{5,6},{6,7},{7,4},{8,9},{9,10},{10,1... | collective-permute-start | bytes 798728 | tf_op jit(solution)/shard_map/ppermute | solution.py:549
  11.0 13.9 %collective-permute-start.1 = (f16[520,256]{1,0:T(8,128)(2,1)S(1)}, f16[520,256]{1,0:T(8,128)(2,1)S(1)}, u32[]{:S(2)}, u32[]{:S(2)}) collective-permute-start(f16[520,256]{1,0:T(8,128)(2,1)S(1)} %get-tuple-element.32), channel_id=1, source_target_pairs={{0,2},{1,3},{2,0},{3,1},{4,6},{5,7},{6,4},{7,5},{8,10},{9,11},{10,... | collective-permute-start | bytes 798728 | tf_op jit(solution)/shard_map/ppermute | solution.py:549
  13.7 11.2 %collective-permute-start.2 = (f16[520,256]{1,0:T(8,128)(2,1)S(1)}, f16[520,256]{1,0:T(8,128)(2,1)S(1)}, u32[]{:S(2)}, u32[]{:S(2)}) collective-permute-start(f16[520,256]{1,0:T(8,128)(2,1)S(1)} %get-tuple-element.31), channel_id=1, source_target_pairs={{0,3},{1,0},{2,1},{3,2},{4,7},{5,4},{6,5},{7,6},{8,11},{9,8},{10,9... | collective-permute-start | bytes 798728 | tf_op jit(solution)/shard_map/ppermute | solution.py:549
  15.2 2.7 %collective-permute-start.3 = (f32[8,256]{1,0:T(8,128)S(1)}, f32[8,256]{1,0:T(8,128)S(1)}, u32[]{:S(2)}, u32[]{:S(2)}) collective-permute-start(f32[8,256]{1,0:T(8,128)S(1)} %get-tuple-element.18), channel_id=1, source_target_pairs={{0,4},{4,8},{8,12},{12,16},{16,20},{20,24},{24,28},{28,32},{32,36}... | collective-permute-start | bytes 24584 | tf_op jit(solution)/shard_map/ppermute | solution.py:550
  16.5 4.9 %collective-permute-start.4 = (f32[8,256]{1,0:T(8,128)S(1)}, f32[8,256]{1,0:T(8,128)S(1)}, u32[]{:S(2)}, u32[]{:S(2)}) collective-permute-start(f32[8,256]{1,0:T(8,128)S(1)} %get-tuple-element.19), channel_id=1, source_target_pairs={{4,0},{8,4},{12,8},{16,12},{20,16},{24,20},{28,24},{32,28},{36,32}... | collective-permute-start | bytes 24584 | tf_op jit(solution)/shard_map/ppermute | solution.py:551
  21.3 4.9 %collective-permute-start.5 = (f32[16,256]{1,0:T(8,128)S(1)}, f32[16,256]{1,0:T(8,128)S(1)}, u32[]{:S(2)}, u32[]{:S(2)}) collective-permute-start(f32[16,256]{1,0:T(8,128)S(1)} %constant_dynamic-update-slice_fusion.near0), channel_id=1, source_target_pairs={{0,1},{1,2},{2,3},{3,0},{4,5},{5,6},{6,7},{7,4},{8,9},{9,10},{10,1... | collective-permute-start | bytes 49160 | tf_op jit(solution)/shard_map/ppermute | solution.py:554
  21.9 5.2 %collective-permute-start.6 = (f32[16,256]{1,0:T(8,128)S(1)}, f32[16,256]{1,0:T(8,128)S(1)}, u32[]{:S(2)}, u32[]{:S(2)}) collective-permute-start(f32[16,256]{1,0:T(8,128)S(1)} %constant_dynamic-update-slice_fusion.near0), channel_id=1, source_target_pairs={{0,2},{1,3},{2,0},{3,1},{4,6},{5,7},{6,4},{7,5},{8,10},{9,11},{10,... | collective-permute-start | bytes 49160 | tf_op jit(solution)/shard_map/ppermute | solution.py:554
  22.8 4.5 %collective-permute-start.7 = (f32[16,256]{1,0:T(8,128)S(1)}, f32[16,256]{1,0:T(8,128)S(1)}, u32[]{:S(2)}, u32[]{:S(2)}) collective-permute-start(f32[16,256]{1,0:T(8,128)S(1)} %constant_dynamic-update-slice_fusion.near0), channel_id=1, source_target_pairs={{0,3},{1,0},{2,1},{3,2},{4,7},{5,4},{6,5},{7,6},{8,11},{9,8},{10,9... | collective-permute-start | bytes 49160 | tf_op jit(solution)/shard_map/ppermute | solution.py:554
  24.9 9.4 %copy-start.2 = (s32[1,1,64]{2,1,0:T(1,128)S(1)}, s32[1,1,64]{2,1,0:T(1,128)}, u32[]{:S(2)}) copy-start(s32[1,1,64]{2,1,0:T(1,128)} %rows_hbm.1) | copy-start | bytes 772
  24.9 9.4 %copy-start.3 = (s32[1,1,64]{2,1,0:T(1,128)S(1)}, s32[1,1,64]{2,1,0:T(1,128)}, u32[]{:S(2)}) copy-start(s32[1,1,64]{2,1,0:T(1,128)} %cols_hbm.1) | copy-start | bytes 772
  29.7 15.6 %collective-permute-start.8 = (f16[2,256,256]{2,1,0:T(8,128)(2,1)S(1)}, f16[2,256,256]{2,1,0:T(8,128)(2,1)}, u32[]{:S(2)}, u32[]{:S(2)}) collective-permute-start(f16[2,256,256]{2,1,0:T(8,128)(2,1)S(1)} %convert_element_type.50), channel_id=1, source_target_pairs={{0,1},{1,2},{2,3},{3,0},{4,5},{5,6},{6,7},{7,4},{8,9},{9,10},{10,1... | collective-permute-start | bytes 786440 | tf_op jit(solution)/shard_map/ppermute | solution.py:569
  31.6 14.7 %collective-permute-start.9 = (f16[2,256,256]{2,1,0:T(8,128)(2,1)S(1)}, f16[2,256,256]{2,1,0:T(8,128)(2,1)}, u32[]{:S(2)}, u32[]{:S(2)}) collective-permute-start(f16[2,256,256]{2,1,0:T(8,128)(2,1)S(1)} %convert_element_type.50), channel_id=1, source_target_pairs={{0,2},{1,3},{2,0},{3,1},{4,6},{5,7},{6,4},{7,5},{8,10},{9,11},{10,... | collective-permute-start | bytes 786440 | tf_op jit(solution)/shard_map/ppermute | solution.py:569
  33.7 13.0 %collective-permute-start.10 = (f16[2,256,256]{2,1,0:T(8,128)(2,1)S(1)}, f16[2,256,256]{2,1,0:T(8,128)(2,1)}, u32[]{:S(2)}, u32[]{:S(2)}) collective-permute-start(f16[2,256,256]{2,1,0:T(8,128)(2,1)S(1)} %convert_element_type.50), channel_id=1, source_target_pairs={{0,3},{1,0},{2,1},{3,2},{4,7},{5,4},{6,5},{7,6},{8,11},{9,8},{10,9... | collective-permute-start | bytes 786440 | tf_op jit(solution)/shard_map/ppermute | solution.py:569
  34.4 22.1 %all-to-all-start = ((f32[640,1,128]{2,1,0:T(1,128)}), f32[640,1,128]{2,1,0:T(1,128)S(1)}, u32[]{:S(2)}, u32[]{:S(2)}) async-start(f32[640,1,128]{2,1,0:T(1,128)} %bitcast.12), calls=%async_computation | async-start | bytes 655360 | tf_op jit(solution)/shard_map/all_to_all | solution.py:571
  61.3 3.8 %collective-permute-start.11 = (f16[16,136,256]{2,1,0:T(8,128)(2,1)S(1)}, f16[16,136,256]{2,1,0:T(8,128)(2,1)S(1)}, u32[]{:S(2)}, u32[]{:S(2)}) collective-permute-start(f16[16,136,256]{2,1,0:T(8,128)(2,1)S(1)} %convert_element_type.52), channel_id=1, source_target_pairs={{0,4},{4,0},{1,5},{5,1},{2,6},{6,2},{3,7},{7,3},{8,12},{12,8},{9,1... | collective-permute-start | bytes 3342344 | tf_op jit(solution)/shard_map/ppermute | solution.py:590
  65.5 20.6 %copy-start.1 = (f32[2048,256]{1,0:T(8,128)S(1)}, f32[2048,256]{1,0:T(8,128)}, u32[]{:S(2)}) copy-start(f32[2048,256]{1,0:T(8,128)} %factors_hbm.1) | copy-start | bytes 6291460
  86.0 1.4 %collective-permute-start.12 = (f32[136,256]{1,0:T(8,128)S(1)}, f32[136,256]{1,0:T(8,128)S(1)}, u32[]{:S(2)}, u32[]{:S(2)}) collective-permute-start(f32[136,256]{1,0:T(8,128)S(1)} %convert_reduce_fusion.mine), channel_id=1, source_target_pairs={{0,4},{4,0},{1,5},{5,1},{2,6},{6,2},{3,7},{7,3},{8,12},{12,8},{9,1... | collective-permute-start | bytes 417800 | tf_op jit(solution)/shard_map/ppermute | solution.py:606
  110.4 8.7 %collective-permute-start.16 = (f16[16,136,256]{2,1,0:T(8,128)(2,1)S(1)}, f16[16,136,256]{2,1,0:T(8,128)(2,1)S(1)}, u32[]{:S(2)}, u32[]{:S(2)}) collective-permute-start(f16[16,136,256]{2,1,0:T(8,128)(2,1)S(1)} %all_to_all.16), channel_id=1, source_target_pairs={{0,4},{4,0},{1,5},{5,1},{2,6},{6,2},{3,7},{7,3},{8,12},{12,8},{9,1... | collective-permute-start | bytes 3342344 | tf_op jit(solution)/shard_map/ppermute | solution.py:613
  110.6 4.8 %collective-permute-start.13 = (f32[8,128]{1,0:T(8,128)S(1)}, f32[8,128]{1,0:T(8,128)S(1)}, u32[]{:S(2)}, u32[]{:S(2)}) collective-permute-start(f32[8,128]{1,0:T(8,128)S(1)} %shard_map.83.own), channel_id=1, source_target_pairs={{0,1},{1,2},{2,3},{3,0},{4,5},{5,6},{6,7},{7,4},{8,9},{9,10},{10,1... | collective-permute-start | bytes 12296 | tf_op jit(solution)/shard_map/ppermute | solution.py:616
  111.8 5.1 %collective-permute-start.14 = (f32[8,128]{1,0:T(8,128)S(1)}, f32[8,128]{1,0:T(8,128)S(1)}, u32[]{:S(2)}, u32[]{:S(2)}) collective-permute-start(f32[8,128]{1,0:T(8,128)S(1)} %shard_map.83.own), channel_id=1, source_target_pairs={{0,2},{1,3},{2,0},{3,1},{4,6},{5,7},{6,4},{7,5},{8,10},{9,11},{10,... | collective-permute-start | bytes 12296 | tf_op jit(solution)/shard_map/ppermute | solution.py:616
  114.6 3.6 %collective-permute-start.15 = (f32[8,128]{1,0:T(8,128)S(1)}, f32[8,128]{1,0:T(8,128)S(1)}, u32[]{:S(2)}, u32[]{:S(2)}) collective-permute-start(f32[8,128]{1,0:T(8,128)S(1)} %shard_map.83.own), channel_id=1, source_target_pairs={{0,3},{1,0},{2,1},{3,2},{4,7},{5,4},{6,5},{7,6},{8,11},{9,8},{10,9... | collective-permute-start | bytes 12296 | tf_op jit(solution)/shard_map/ppermute | solution.py:616

commit v7 on v6

--- a/solution.py
+++ b/solution.py
@@ -14,6 +14,8 @@
 COLS = 8
 smooth_weight = 32.0
 ridge_weight = 1.0
+damping = 2.0**-12
+resid_unit = 64.0
 f32, bf16, f16 = jnp.float32, jnp.bfloat16, jnp.float16
 ALL = ("z", "y", "c", "x")
 GEN = ("z", "y", "c")
@@ -173,8 +175,10 @@
     for k in range(4):
         part = lax.rem(me + k, 4)
         out = own if k == 0 else far.at[k - 1]
-        out[4 * BS + 2 : 4 * BS + 3, :] = rims[pl.ds(jnp.maximum(2 * part - 1, 0), 1), :]
-        out[4 * BS + 3 : 4 * BS + 4, :] = rims[pl.ds(jnp.minimum(2 * part + 2, COLS - 1), 1), :]
+        before = rims[pl.ds(jnp.maximum(2 * part - 1, 0), 1), :]
+        after = rims[pl.ds(jnp.minimum(2 * part + 2, COLS - 1), 1), :]
+        out[4 * BS + 2 : 4 * BS + 3, :] = before * (1.0 / resid_unit)
+        out[4 * BS + 3 : 4 * BS + 4, :] = after * (1.0 / resid_unit)
     upward[...] = jnp.concatenate(
         [sides[8 * COLS - 2 : 8 * COLS, :], rims[COLS - 1 : COLS, :], jnp.zeros((5, R), f32)], axis=0
     )
@@ -216,8 +220,8 @@
         - 2.0 * (1.0 + ratio) * first * aa
         + first * first * aaa
     )
-    second = rr_next / curve
-    return first + second * (1.0 + ratio), second * first, rr_next, curve
+    second = jnp.where((rr_next > 2e-6 * rr) & (curve > 0.0), rr_next / curve, 0.0)
+    return damping * (first + second * (1.0 + ratio)), damping * second * first, rr_next, curve
 
 
 def variant_moments(
@@ -254,8 +258,8 @@
     value = jnp.concatenate(pieces, axis=0)
     low = near0[2:3, :] + near1[2:3, :] + near2[2:3, :] + near3[2:3, :]
     high = near0[10:11, :] + near1[10:11, :] + near2[10:11, :] + near3[10:11, :]
-    low = jnp.where(at_low, low, total[4 * BS + 2 : 4 * BS + 3, :])
-    high = jnp.where(at_high, high, total[4 * BS + 3 : 4 * BS + 4, :])
+    low = jnp.where(at_low, low, resid_unit * total[4 * BS + 2 : 4 * BS + 3, :])
+    high = jnp.where(at_high, high, resid_unit * total[4 * BS + 3 : 4 * BS + 4, :])
     low = low - ridge_weight * before - smooth_weight * (2.0 * before - before2 - mine[0:1, :])
     high = high - ridge_weight * after - smooth_weight * (2.0 * after - after2 - mine[n - 1 : n, :])
     zero = jnp.zeros((1, R), f32)
@@ -266,8 +270,8 @@
         data = [times(values[k * BS : (k + 1) * BS], g_high[k], g_low[k]) for k in range(2)]
         return jnp.concatenate(data, axis=0) + ridge_weight * values + smooth_weight * banded
 
-    first = operator(value, band_of(value, low, high, ext))
-    second = operator(first, band_of(first, zero, zero, ext))
+    first = damping * operator(value, band_of(value, low, high, ext))
+    second = damping * operator(first, band_of(first, zero, zero, ext))
     rr, ra = total_of(value * value), total_of(value * first)
     aa, aaa = total_of(first * first), total_of(first * second)
     near, far, rr_next, curve = curve_of(rr, ra, aa, aaa)
@@ -319,7 +323,7 @@
         for half in range(2)
     )
     rr, ra, aa, aaa = (sums[:, k : k + 1] for k in range(4))
-    on_resid, on_applied, _, _ = curve_of(rr, ra, aa, aaa - 2.0 * smooth_weight * total_of(across))
+    on_resid, on_applied, _, _ = curve_of(rr, ra, aa, aaa - 2.0 * damping * smooth_weight * total_of(across))
     n = 2 * BS
     for k in range(4):
         owner = lax.rem(me - k + 4, 4)
@@ -462,6 +466,7 @@
         return jnp.sum(value * power, axis=0, keepdims=True)
 
     one, two, three = (jnp.exp2(lines[:, j : j + 1]) for j in (12, 13, 14))
+    two, three = damping * two, damping * damping * three
     moments[...] = as_row(
         [
             moment(0, one * one),
@@ -476,7 +481,7 @@
     sums = own[0:1, :] + next1[0:1, :] + next2[0:1, :] + next3[0:1, :]
     on_resid, on_applied, _, _ = curve_of(*(sums[:, k : k + 1] for k in range(4)))
     of_resid = on_resid * jnp.exp2(lines[:, 12:13]) * (1.0 / 16384.0)
-    of_applied = -on_applied * jnp.exp2(lines[:, 13:14]) * (1.0 / 16384.0)
+    of_applied = -on_applied * jnp.exp2(lines[:, 13:14]) * (damping / 16384.0)
     core = meta[1]
     lanes = lax.broadcasted_iota(jnp.int32, (ROWS, BS), 1)
     here = jnp.where(core == 0, of_resid, of_applied)

time: 121 us -> 121 us (level)
  transfers between devices with their start and end apart: 18 -> 18, of which waited for: 12 -> 11; matrix products, arithmetic and copies ran while one was open for 2% -> 2% of each run, Pallas kernels for 4% -> 4%
where the time goes in v7:
time: 121 us
  blocking collectives  41.9 us (35%)
  starting transfers between devices  31.8 us (26%)
  waiting for transfers between devices  20.4 us (17%)
  Pallas kernels  19.8 us (16%)
  other arithmetic  4.58 us (4%)
  between operations  1.52 us (1%)
    all_to_all x1, blocking collectives, on_device(): here = lax.all_to_all(sent, CHIP, 0, 0)  21.4 us
    all_to_all x1, blocking collectives, on_device(): arrived = lax.all_to_all(of_chip, CHIP, 0, 0)  20.6 us
    pallas_call x8, Pallas kernels, run(): pl.pallas_call(kernel, out_shape=tuple((placed(*out) for out in outs)), i...  19.8 us
    all_to_all x1, starting transfers between devices, on_device(): lax.all_to_all(table.reshape(4 * slabs * 5, 1, BS), ALL, 0, 0, tiled=True)  11 us
    all_to_all x1, waiting for transfers between devices, on_device(): lax.all_to_all(table.reshape(4 * slabs * 5, 1, BS), ALL, 0, 0, tiled=True)  8.72 us
    ppermute x3, starting transfers between devices, on_device(): got = [lax.ppermute(far[k - 1], 'x', ring(k)) for k in (1, 2, 3)]  5.84 us
    ppermute x3, starting transfers between devices, on_device(): lax.ppermute(sent, 'x', ring(k))  4.74 us
    ppermute x3, starting transfers between devices, on_device(): nexts = [lax.ppermute(moments, 'x', ring(k)) for k in (1, 2, 3)]  4.03 us
  transfers between devices with their start and end apart: 18, of which 11 were waited for; matrix products, arithmetic and copies ran while one was open for 2% of the time, Pallas kernels for 4%

profile of v7, /device:TPU:0, one launch (start us, length us, event | category | flops | bytes accessed | tf_op | source)
XLA Modules:
  0.0 120.5 jit_solution(7134266526410352285)
XLA Ops:
  1.3 0.1 pad_add_fusion.1.meta
  1.4 7.1 %shard_map.77 = (f32[520,256]{1,0:T(8,128)S(1)}, f32[3,520,256]{2,1,0:T(8,128)S(1)}, f32[128]{0:T(128)S(1)}, f32[8,256]{1,0:T(8,128)S(1)}, f32[8,256]{1,0:T(8,128)S(1)}) custom-call(s32[3]{0:T(128)S(1)} %pad_add_fusion.1.meta, s32[1,1]{1,0:T(1,128)} %copy.17.live, s32[1,1,64]{2,1,0:T(1,128)} %rows_hbm.1, s32[1,1,64]{2,1,0:T(1,128)} %cols_hbm.1, ...), custom_call_target="tpu_custom_call" | custom-call | bytes 20971520 | tf_op jit(solution)/shard_map/pallas_call | solution.py:507
  8.4 0.2 convert_element_type.46
  8.6 0.0 copy-start
  8.6 0.2 slice_bitcast_fusion.2
  8.8 1.4 %collective-permute-start = (f16[520,256]{1,0:T(8,128)(2,1)S(1)}, f16[520,256]{1,0:T(8,128)(2,1)S(1)}, u32[]{:S(2)}, u32[]{:S(2)}) collective-permute-start(f16[520,256]{1,0:T(8,128)(2,1)S(1)} %get-tuple-element.30), channel_id=1, source_target_pairs={{0,1},{1,2},{2,3},{3,0},{4,5},{5,6},{6,7},{7,4},{8,9},{9,10},{10,1... | collective-permute-start | bytes 798728 | tf_op jit(solution)/shard_map/ppermute | solution.py:554
  10.2 2.7 %collective-permute-start.1 = (f16[520,256]{1,0:T(8,128)(2,1)S(1)}, f16[520,256]{1,0:T(8,128)(2,1)S(1)}, u32[]{:S(2)}, u32[]{:S(2)}) collective-permute-start(f16[520,256]{1,0:T(8,128)(2,1)S(1)} %get-tuple-element.32), channel_id=1, source_target_pairs={{0,2},{1,3},{2,0},{3,1},{4,6},{5,7},{6,4},{7,5},{8,10},{9,11},{10,... | collective-permute-start | bytes 798728 | tf_op jit(solution)/shard_map/ppermute | solution.py:554
  12.9 1.7 %collective-permute-start.2 = (f16[520,256]{1,0:T(8,128)(2,1)S(1)}, f16[520,256]{1,0:T(8,128)(2,1)S(1)}, u32[]{:S(2)}, u32[]{:S(2)}) collective-permute-start(f16[520,256]{1,0:T(8,128)(2,1)S(1)} %get-tuple-element.31), channel_id=1, source_target_pairs={{0,3},{1,0},{2,1},{3,2},{4,7},{5,4},{6,5},{7,6},{8,11},{9,8},{10,9... | collective-permute-start | bytes 798728 | tf_op jit(solution)/shard_map/ppermute | solution.py:554
  14.6 1.3 %collective-permute-start.3 = (f32[8,256]{1,0:T(8,128)S(1)}, f32[8,256]{1,0:T(8,128)S(1)}, u32[]{:S(2)}, u32[]{:S(2)}) collective-permute-start(f32[8,256]{1,0:T(8,128)S(1)} %get-tuple-element.18), channel_id=1, source_target_pairs={{0,4},{4,8},{8,12},{12,16},{16,20},{20,24},{24,28},{28,32},{32,36}... | collective-permute-start | bytes 24584 | tf_op jit(solution)/shard_map/ppermute | solution.py:555
  15.9 1.3 %collective-permute-start.4 = (f32[8,256]{1,0:T(8,128)S(1)}, f32[8,256]{1,0:T(8,128)S(1)}, u32[]{:S(2)}, u32[]{:S(2)}) collective-permute-start(f32[8,256]{1,0:T(8,128)S(1)} %get-tuple-element.19), channel_id=1, source_target_pairs={{4,0},{8,4},{12,8},{16,12},{20,16},{24,20},{28,24},{32,28},{36,32}... | collective-permute-start | bytes 24584 | tf_op jit(solution)/shard_map/ppermute | solution.py:556
  17.2 0.1 pad_add_fusion.2.meta
  17.3 0.0 collective-permute-done.3
  17.3 3.3 %collective-permute-done.4 = f32[8,256]{1,0:T(8,128)S(1)} collective-permute-done((f32[8,256]{1,0:T(8,128)S(1)}, f32[8,256]{1,0:T(8,128)S(1)}, u32[]{:S(2)}, u32[]{:S(2)}) %collective-permute-start.4) | collective-permute-done | bytes 8224 | tf_op jit(solution)/shard_map/ppermute | solution.py:556
  20.6 0.8 collective-permute-start.5
  21.4 0.7 collective-permute-start.6
  22.1 0.0 collective-permute-done
  22.1 2.0 %collective-permute-start.7 = (f32[16,256]{1,0:T(8,128)S(1)}, f32[16,256]{1,0:T(8,128)S(1)}, u32[]{:S(2)}, u32[]{:S(2)}) collective-permute-start(f32[16,256]{1,0:T(8,128)S(1)} %constant_dynamic-update-slice_fusion.near0), channel_id=1, source_target_pairs={{0,3},{1,0},{2,1},{3,2},{4,7},{5,4},{6,5},{7,6},{8,11},{9,8},{10,9... | collective-permute-start | bytes 49160 | tf_op jit(solution)/shard_map/ppermute | solution.py:559
  24.1 0.9 collective-permute-done.1
  25.1 0.0 collective-permute-done.2
  25.1 0.1 convert_add_fusion.total
  25.2 0.4 collective-permute-done.5.near1
  25.6 1.1 collective-permute-done.6.near2
  26.7 0.0 collective-permute-done.7.near3
  26.7 0.0 copy-done
  26.7 2.3 %shard_map.78 = (f32[2,256,256]{2,1,0:T(8,128)S(1)}, f32[640,128]{1,0:T(8,128)}) custom-call(s32[3]{0:T(128)S(1)} %pad_add_fusion.2.meta, f32[520,256]{1,0:T(8,128)S(1)} %convert_add_fusion.total, f32[1024,256]{1,0:T(8,128)S(1)} %copy-done, f32[16,256]{1,0:T(8,128)S(1)} %constant_dynamic-update-slice_fusion.near0, ...), custom_call_target="tpu_custom_call" | custom-call | bytes 1048576 | tf_op jit(solution)/shard_map/pallas_call | solution.py:507
  29.0 2.0 %collective-permute-start.8 = (f16[2,256,256]{2,1,0:T(8,128)(2,1)S(1)}, f16[2,256,256]{2,1,0:T(8,128)(2,1)}, u32[]{:S(2)}, u32[]{:S(2)}) collective-permute-start(f16[2,256,256]{2,1,0:T(8,128)(2,1)S(1)} %convert_element_type.50), channel_id=1, source_target_pairs={{0,1},{1,2},{2,3},{3,0},{4,5},{5,6},{6,7},{7,4},{8,9},{9,10},{10,1... | collective-permute-start | bytes 786440 | tf_op jit(solution)/shard_map/ppermute | solution.py:574
  31.0 2.1 %collective-permute-start.9 = (f16[2,256,256]{2,1,0:T(8,128)(2,1)S(1)}, f16[2,256,256]{2,1,0:T(8,128)(2,1)}, u32[]{:S(2)}, u32[]{:S(2)}) collective-permute-start(f16[2,256,256]{2,1,0:T(8,128)(2,1)S(1)} %convert_element_type.50), channel_id=1, source_target_pairs={{0,2},{1,3},{2,0},{3,1},{4,6},{5,7},{6,4},{7,5},{8,10},{9,11},{10,... | collective-permute-start | bytes 786440 | tf_op jit(solution)/shard_map/ppermute | solution.py:574
  33.1 0.6 collective-permute-start.10
  33.8 0.0 copy-done.2
  33.8 0.0 copy-done.3
  33.8 0.1 pad_add_fusion.ids
  33.9 11.0 %all-to-all-start = ((f32[640,1,128]{2,1,0:T(1,128)}), f32[640,1,128]{2,1,0:T(1,128)S(1)}, u32[]{:S(2)}, u32[]{:S(2)}) async-start(f32[640,1,128]{2,1,0:T(1,128)} %bitcast.12), calls=%async_computation | async-start | bytes 655360 | tf_op jit(solution)/shard_map/all_to_all | solution.py:576
  44.9 0.0 collective-permute-done.8
  44.9 0.8 collective-permute-done.9
  45.7 0.4 collective-permute-done.10
  46.1 1.3 %maximum_convert_fusion.pieces = f32[4,2,256,256]{3,2,1,0:T(8,128)S(1)} fusion(f16[1,2,256,256]{3,2,1,0:T(8,128)(2,1)} %bitcast.17, f16[1,2,256,256]{3,2,1,0:T(8,128)(2,1)} %bitcast.16, f16[1,2,256,256]{3,2,1,0:T(8,128)(2,1)} %bitcast.15, f16[1,2,256,256]{3,2,1,0:T(8,128)(2,1)S(1)} %convert_bitcast_fusion), kind=kLoop, calls=%fused_computation.3 | loop fusion | flops 2097152 | bytes 3145728 | tf_op jit(solution)/shard_map/convert_element_type | solution.py:575
  47.5 8.7 %all-to-all-done = f32[640,1,128]{2,1,0:T(1,128)S(1)} async-done(((f32[640,1,128]{2,1,0:T(1,128)}), f32[640,1,128]{2,1,0:T(1,128)S(1)}, u32[]{:S(2)}, u32[]{:S(2)}) %all-to-all-start) | async-done | bytes 327712 | tf_op jit(solution)/shard_map/all_to_all | solution.py:576
  56.2 2.2 %shard_map.79 = (f32[1024,256]{1,0:T(8,128)S(1)}, bf16[1024,256]{1,0:T(8,128)(2,1)S(1)}, f32[8,128]{1,0:T(8,128)S(1)}, bf16[2048,1024]{1,0:T(8,128)(2,1)S(1)}) custom-call(s32[3]{0:T(128)S(1)} %pad_add_fusion.1.meta, s32[129]{0:T(256)S(1)} %pad_add_fusion.ids, f32[640,128]{1,0:T(8,128)S(1)} %bitcast.31, f32[1024,256]{1,0:T(8,128)S(1)} %copy-done, ...), custom_call_target="tpu_custom_call" | custom-call | bytes 1048576 | tf_op jit(solution)/shard_map/pallas_call | solution.py:507
  58.3 2.4 %shard_map.80 = (f32[16,136,256]{2,1,0:T(8,128)S(1)}, f32[1024,256]{1,0:T(8,128)}) custom-call(s32[3]{0:T(128)S(1)} %pad_add_fusion.1.meta, f32[128]{0:T(128)S(1)} %get-tuple-element.15.mask, f32[8,128]{1,0:T(8,128)S(1)} %get-tuple-element.22.scales, bf16[2048,1024]{1,0:T(8,128)(2,1)S(1)} %get-tuple-element.23.dense, ...), custom_call_target="tpu_custom_call" | custom-call | bytes 1048576 | tf_op jit(solution)/shard_map/pallas_call | solution.py:507
  60.7 0.2 convert_element_type.52
  60.9 0.1 collective-permute-start.11
  61.0 3.5 %shard_map.81 = f32[16,136,256]{2,1,0:T(8,128)S(1)} custom-call(s32[3]{0:T(128)S(1)} %pad_add_fusion.1.meta, s32[129]{0:T(256)S(1)} %pad_add_fusion.ids, f32[128]{0:T(128)S(1)} %get-tuple-element.15.mask, f32[8,128]{1,0:T(8,128)S(1)} %get-tuple-element.22.scales, bf16[1024,256]{1,0:T(8,128)(2,1)S(1)} %get-tuple-element.24.rounded, ...), custom_call_target="tpu_custom_call" | custom-call | bytes 8388608 | tf_op jit(solution)/shard_map/pallas_call | solution.py:507
  64.5 0.0 collective-permute-done.11
  64.5 0.4 add_convert_fusion
  64.9 0.0 copy-start.1
  64.9 20.6 %all_to_all.15 = f16[16,136,256]{2,1,0:T(8,128)(2,1)S(1)} all-to-all(f16[16,136,256]{2,1,0:T(8,128)(2,1)S(1)} %add_convert_fusion), channel_id=1, replica_groups=mesh['z'=4,'y'=4,'c'=2,'x'=4] {'z','y'}, dimensions={0} | all-to-all | bytes 2228224 | tf_op jit(solution)/shard_map/all_to_all | solution.py:609
  85.5 0.2 convert_reduce_fusion.mine
  85.7 0.1 collective-permute-start.12
  85.8 1.3 %collective-permute-done.12.theirs = f32[136,256]{1,0:T(8,128)S(1)} collective-permute-done((f32[136,256]{1,0:T(8,128)S(1)}, f32[136,256]{1,0:T(8,128)S(1)}, u32[]{:S(2)}, u32[]{:S(2)}) %collective-permute-start.12) | collective-permute-done | bytes 139296 | tf_op jit(solution)/shard_map/ppermute | solution.py:611
  87.1 1.4 %shard_map.82 = f32[136,256]{1,0:T(8,128)S(1)} custom-call(s32[3]{0:T(128)S(1)} %pad_add_fusion.1.meta, f32[136,256]{1,0:T(8,128)S(1)} %convert_reduce_fusion.mine, f32[136,256]{1,0:T(8,128)S(1)} %collective-permute-done.12.theirs, f32[128,256]{1,0:T(8,128)S(1)} %constant_dynamic-slice_fusion.start, f32[8,128]{1,0:T(8,128)S(1)} %get-tuple-element.22.scales), custom_call_target="tpu_custom_call" | custom-call | bytes 1048576 | tf_op jit(solution)/shard_map/pallas_call | solution.py:507
  88.6 0.1 broadcast_in_dim.2
  88.6 21.4 %all_to_all.16 = f16[16,136,256]{2,1,0:T(8,128)(2,1)S(1)} all-to-all(f16[16,136,256]{2,1,0:T(8,128)(2,1)S(1)} %broadcast_in_dim.2), channel_id=1, replica_groups=mesh['z'=4,'y'=4,'c'=2,'x'=4] {'z','y'}, dimensions={0} | all-to-all | bytes 2228224 | tf_op jit(solution)/shard_map/all_to_all | solution.py:617
  110.0 0.0 collective-permute-start.16
  110.0 0.2 shard_map.83.own
  110.3 1.1 collective-permute-start.13
  111.4 2.7 %collective-permute-start.14 = (f32[8,128]{1,0:T(8,128)S(1)}, f32[8,128]{1,0:T(8,128)S(1)}, u32[]{:S(2)}, u32[]{:S(2)}) collective-permute-start(f32[8,128]{1,0:T(8,128)S(1)} %shard_map.83.own), channel_id=1, source_target_pairs={{0,2},{1,3},{2,0},{3,1},{4,6},{5,7},{6,4},{7,5},{8,10},{9,11},{10,... | collective-permute-start | bytes 12296 | tf_op jit(solution)/shard_map/ppermute | solution.py:621
  114.1 0.2 collective-permute-start.15
  114.3 0.8 collective-permute-done.13.next1
  115.1 1.4 %collective-permute-done.14.next2 = f32[8,128]{1,0:T(8,128)S(1)} collective-permute-done((f32[8,128]{1,0:T(8,128)S(1)}, f32[8,128]{1,0:T(8,128)S(1)}, u32[]{:S(2)}, u32[]{:S(2)}) %collective-permute-start.14) | collective-permute-done | bytes 4128 | tf_op jit(solution)/shard_map/ppermute | solution.py:621
  116.5 1.2 %collective-permute-done.15.next3 = f32[8,128]{1,0:T(8,128)S(1)} collective-permute-done((f32[8,128]{1,0:T(8,128)S(1)}, f32[8,128]{1,0:T(8,128)S(1)}, u32[]{:S(2)}, u32[]{:S(2)}) %collective-permute-start.15) | collective-permute-done | bytes 4128 | tf_op jit(solution)/shard_map/ppermute | solution.py:621
  117.7 0.7 shard_map.84
  118.4 0.2 slice_reduce_fusion.1
  118.6 0.0 collective-permute-done.16
  118.6 1.9 %add_add_fusion = f32[16,128,256]{2,1,0:T(8,128)} fusion(f32[16,128,256]{2,1,0:T(8,128)S(1)} %bitcast.32, f16[16,136,256]{2,1,0:T(8,128)(2,1)S(1)} %collective-permute-done.16, f16[16,136,256]{2,1,0:T(8,128)(2,1)S(1)} %all_to_all.16, f32[16]{0:T(128)S(1)} %get-tuple-element.29, f32[16]{0:T(128)S(1)} %get-tuple-element.28), kind=kLoop, calls=%fused_computation.2 | loop fusion | flops 3145728 | bytes 6291584 | tf_op jit(solution)/shard_map/add | solution.py:629
  (11 shorter events, 0.1 us)
Async XLA Ops:
  8.6 18.1 %copy-start = (f32[1024,256]{1,0:T(8,128)S(1)}, f32[1024,256]{1,0:T(8,128)}, u32[]{:S(2)}) copy-start(f32[1024,256]{1,0:T(8,128)} %start.3) | copy-start | bytes 3145732
  8.8 13.4 %collective-permute-start = (f16[520,256]{1,0:T(8,128)(2,1)S(1)}, f16[520,256]{1,0:T(8,128)(2,1)S(1)}, u32[]{:S(2)}, u32[]{:S(2)}) collective-permute-start(f16[520,256]{1,0:T(8,128)(2,1)S(1)} %get-tuple-element.30), channel_id=1, source_target_pairs={{0,1},{1,2},{2,3},{3,0},{4,5},{5,6},{6,7},{7,4},{8,9},{9,10},{10,1... | collective-permute-start | bytes 798728 | tf_op jit(solution)/shard_map/ppermute | solution.py:554
  10.2 14.8 %collective-permute-start.1 = (f16[520,256]{1,0:T(8,128)(2,1)S(1)}, f16[520,256]{1,0:T(8,128)(2,1)S(1)}, u32[]{:S(2)}, u32[]{:S(2)}) collective-permute-start(f16[520,256]{1,0:T(8,128)(2,1)S(1)} %get-tuple-element.32), channel_id=1, source_target_pairs={{0,2},{1,3},{2,0},{3,1},{4,6},{5,7},{6,4},{7,5},{8,10},{9,11},{10,... | collective-permute-start | bytes 798728 | tf_op jit(solution)/shard_map/ppermute | solution.py:554
  12.9 12.1 %collective-permute-start.2 = (f16[520,256]{1,0:T(8,128)(2,1)S(1)}, f16[520,256]{1,0:T(8,128)(2,1)S(1)}, u32[]{:S(2)}, u32[]{:S(2)}) collective-permute-start(f16[520,256]{1,0:T(8,128)(2,1)S(1)} %get-tuple-element.31), channel_id=1, source_target_pairs={{0,3},{1,0},{2,1},{3,2},{4,7},{5,4},{6,5},{7,6},{8,11},{9,8},{10,9... | collective-permute-start | bytes 798728 | tf_op jit(solution)/shard_map/ppermute | solution.py:554
  14.6 2.7 %collective-permute-start.3 = (f32[8,256]{1,0:T(8,128)S(1)}, f32[8,256]{1,0:T(8,128)S(1)}, u32[]{:S(2)}, u32[]{:S(2)}) collective-permute-start(f32[8,256]{1,0:T(8,128)S(1)} %get-tuple-element.18), channel_id=1, source_target_pairs={{0,4},{4,8},{8,12},{12,16},{16,20},{20,24},{24,28},{28,32},{32,36}... | collective-permute-start | bytes 24584 | tf_op jit(solution)/shard_map/ppermute | solution.py:555
  15.9 4.7 %collective-permute-start.4 = (f32[8,256]{1,0:T(8,128)S(1)}, f32[8,256]{1,0:T(8,128)S(1)}, u32[]{:S(2)}, u32[]{:S(2)}) collective-permute-start(f32[8,256]{1,0:T(8,128)S(1)} %get-tuple-element.19), channel_id=1, source_target_pairs={{4,0},{8,4},{12,8},{16,12},{20,16},{24,20},{28,24},{32,28},{36,32}... | collective-permute-start | bytes 24584 | tf_op jit(solution)/shard_map/ppermute | solution.py:556
  20.6 4.9 %collective-permute-start.5 = (f32[16,256]{1,0:T(8,128)S(1)}, f32[16,256]{1,0:T(8,128)S(1)}, u32[]{:S(2)}, u32[]{:S(2)}) collective-permute-start(f32[16,256]{1,0:T(8,128)S(1)} %constant_dynamic-update-slice_fusion.near0), channel_id=1, source_target_pairs={{0,1},{1,2},{2,3},{3,0},{4,5},{5,6},{6,7},{7,4},{8,9},{9,10},{10,1... | collective-permute-start | bytes 49160 | tf_op jit(solution)/shard_map/ppermute | solution.py:559
  21.4 5.2 %collective-permute-start.6 = (f32[16,256]{1,0:T(8,128)S(1)}, f32[16,256]{1,0:T(8,128)S(1)}, u32[]{:S(2)}, u32[]{:S(2)}) collective-permute-start(f32[16,256]{1,0:T(8,128)S(1)} %constant_dynamic-update-slice_fusion.near0), channel_id=1, source_target_pairs={{0,2},{1,3},{2,0},{3,1},{4,6},{5,7},{6,4},{7,5},{8,10},{9,11},{10,... | collective-permute-start | bytes 49160 | tf_op jit(solution)/shard_map/ppermute | solution.py:559
  22.1 4.5 %collective-permute-start.7 = (f32[16,256]{1,0:T(8,128)S(1)}, f32[16,256]{1,0:T(8,128)S(1)}, u32[]{:S(2)}, u32[]{:S(2)}) collective-permute-start(f32[16,256]{1,0:T(8,128)S(1)} %constant_dynamic-update-slice_fusion.near0), channel_id=1, source_target_pairs={{0,3},{1,0},{2,1},{3,2},{4,7},{5,4},{6,5},{7,6},{8,11},{9,8},{10,9... | collective-permute-start | bytes 49160 | tf_op jit(solution)/shard_map/ppermute | solution.py:559
  25.1 8.7 %copy-start.2 = (s32[1,1,64]{2,1,0:T(1,128)S(1)}, s32[1,1,64]{2,1,0:T(1,128)}, u32[]{:S(2)}) copy-start(s32[1,1,64]{2,1,0:T(1,128)} %rows_hbm.1) | copy-start | bytes 772
  25.1 8.7 %copy-start.3 = (s32[1,1,64]{2,1,0:T(1,128)S(1)}, s32[1,1,64]{2,1,0:T(1,128)}, u32[]{:S(2)}) copy-start(s32[1,1,64]{2,1,0:T(1,128)} %cols_hbm.1) | copy-start | bytes 772
  29.0 15.9 %collective-permute-start.8 = (f16[2,256,256]{2,1,0:T(8,128)(2,1)S(1)}, f16[2,256,256]{2,1,0:T(8,128)(2,1)}, u32[]{:S(2)}, u32[]{:S(2)}) collective-permute-start(f16[2,256,256]{2,1,0:T(8,128)(2,1)S(1)} %convert_element_type.50), channel_id=1, source_target_pairs={{0,1},{1,2},{2,3},{3,0},{4,5},{5,6},{6,7},{7,4},{8,9},{9,10},{10,1... | collective-permute-start | bytes 786440 | tf_op jit(solution)/shard_map/ppermute | solution.py:574
  31.0 14.7 %collective-permute-start.9 = (f16[2,256,256]{2,1,0:T(8,128)(2,1)S(1)}, f16[2,256,256]{2,1,0:T(8,128)(2,1)}, u32[]{:S(2)}, u32[]{:S(2)}) collective-permute-start(f16[2,256,256]{2,1,0:T(8,128)(2,1)S(1)} %convert_element_type.50), channel_id=1, source_target_pairs={{0,2},{1,3},{2,0},{3,1},{4,6},{5,7},{6,4},{7,5},{8,10},{9,11},{10,... | collective-permute-start | bytes 786440 | tf_op jit(solution)/shard_map/ppermute | solution.py:574
  33.1 13.0 %collective-permute-start.10 = (f16[2,256,256]{2,1,0:T(8,128)(2,1)S(1)}, f16[2,256,256]{2,1,0:T(8,128)(2,1)}, u32[]{:S(2)}, u32[]{:S(2)}) collective-permute-start(f16[2,256,256]{2,1,0:T(8,128)(2,1)S(1)} %convert_element_type.50), channel_id=1, source_target_pairs={{0,3},{1,0},{2,1},{3,2},{4,7},{5,4},{6,5},{7,6},{8,11},{9,8},{10,9... | collective-permute-start | bytes 786440 | tf_op jit(solution)/shard_map/ppermute | solution.py:574
  33.9 22.3 %all-to-all-start = ((f32[640,1,128]{2,1,0:T(1,128)}), f32[640,1,128]{2,1,0:T(1,128)S(1)}, u32[]{:S(2)}, u32[]{:S(2)}) async-start(f32[640,1,128]{2,1,0:T(1,128)} %bitcast.12), calls=%async_computation | async-start | bytes 655360 | tf_op jit(solution)/shard_map/all_to_all | solution.py:576
  60.9 3.6 %collective-permute-start.11 = (f16[16,136,256]{2,1,0:T(8,128)(2,1)S(1)}, f16[16,136,256]{2,1,0:T(8,128)(2,1)S(1)}, u32[]{:S(2)}, u32[]{:S(2)}) collective-permute-start(f16[16,136,256]{2,1,0:T(8,128)(2,1)S(1)} %convert_element_type.52), channel_id=1, source_target_pairs={{0,4},{4,0},{1,5},{5,1},{2,6},{6,2},{3,7},{7,3},{8,12},{12,8},{9,1... | collective-permute-start | bytes 3342344 | tf_op jit(solution)/shard_map/ppermute | solution.py:595
  64.9 20.8 %copy-start.1 = (f32[2048,256]{1,0:T(8,128)S(1)}, f32[2048,256]{1,0:T(8,128)}, u32[]{:S(2)}) copy-start(f32[2048,256]{1,0:T(8,128)} %factors_hbm.1) | copy-start | bytes 6291460
  85.7 1.4 %collective-permute-start.12 = (f32[136,256]{1,0:T(8,128)S(1)}, f32[136,256]{1,0:T(8,128)S(1)}, u32[]{:S(2)}, u32[]{:S(2)}) collective-permute-start(f32[136,256]{1,0:T(8,128)S(1)} %convert_reduce_fusion.mine), channel_id=1, source_target_pairs={{0,4},{4,0},{1,5},{5,1},{2,6},{6,2},{3,7},{7,3},{8,12},{12,8},{9,1... | collective-permute-start | bytes 417800 | tf_op jit(solution)/shard_map/ppermute | solution.py:611
  110.0 8.6 %collective-permute-start.16 = (f16[16,136,256]{2,1,0:T(8,128)(2,1)S(1)}, f16[16,136,256]{2,1,0:T(8,128)(2,1)S(1)}, u32[]{:S(2)}, u32[]{:S(2)}) collective-permute-start(f16[16,136,256]{2,1,0:T(8,128)(2,1)S(1)} %all_to_all.16), channel_id=1, source_target_pairs={{0,4},{4,0},{1,5},{5,1},{2,6},{6,2},{3,7},{7,3},{8,12},{12,8},{9,1... | collective-permute-start | bytes 3342344 | tf_op jit(solution)/shard_map/ppermute | solution.py:618
  110.3 4.8 %collective-permute-start.13 = (f32[8,128]{1,0:T(8,128)S(1)}, f32[8,128]{1,0:T(8,128)S(1)}, u32[]{:S(2)}, u32[]{:S(2)}) collective-permute-start(f32[8,128]{1,0:T(8,128)S(1)} %shard_map.83.own), channel_id=1, source_target_pairs={{0,1},{1,2},{2,3},{3,0},{4,5},{5,6},{6,7},{7,4},{8,9},{9,10},{10,1... | collective-permute-start | bytes 12296 | tf_op jit(solution)/shard_map/ppermute | solution.py:621
  111.4 5.1 %collective-permute-start.14 = (f32[8,128]{1,0:T(8,128)S(1)}, f32[8,128]{1,0:T(8,128)S(1)}, u32[]{:S(2)}, u32[]{:S(2)}) collective-permute-start(f32[8,128]{1,0:T(8,128)S(1)} %shard_map.83.own), channel_id=1, source_target_pairs={{0,2},{1,3},{2,0},{3,1},{4,6},{5,7},{6,4},{7,5},{8,10},{9,11},{10,... | collective-permute-start | bytes 12296 | tf_op jit(solution)/shard_map/ppermute | solution.py:621
  114.1 3.6 %collective-permute-start.15 = (f32[8,128]{1,0:T(8,128)S(1)}, f32[8,128]{1,0:T(8,128)S(1)}, u32[]{:S(2)}, u32[]{:S(2)}) collective-permute-start(f32[8,128]{1,0:T(8,128)S(1)} %shard_map.83.own), channel_id=1, source_target_pairs={{0,3},{1,0},{2,1},{3,2},{4,7},{5,4},{6,5},{7,6},{8,11},{9,8},{10,9... | collective-permute-start | bytes 12296 | tf_op jit(solution)/shard_map/ppermute | solution.py:621

commit v8 on v7

--- a/solution.py
+++ b/solution.py
@@ -22,6 +22,7 @@
 CHIP = ("z", "y")
 PAY_V = 2 * BS + 2 * BS + 8
 PAY_I = BS + 8
+PAY_H = 2 * BS + 8
 VMEM_LIMIT = 16 * 1024 * 1024
 
 
@@ -354,8 +355,9 @@
         product = jnp.dot(
             dense[r * BS : (r + 1) * BS, :], rounded[...], preferred_element_type=f32
         )
-        pay[r, :BS, :] = scale * product
-        pay[r, BS:, :] = jnp.zeros((PAY_I - BS, R), f32)
+        pay[r, :BS, :] = scale * product[:, :BS]
+        pay[r, BS : 2 * BS, :] = scale * product[:, BS:]
+        pay[r, 2 * BS :, :] = jnp.zeros((PAY_H - 2 * BS, BS), f32)
 
 
 def gram_sums(scale, mask, rounded, pay, grams, diags):
@@ -367,7 +369,7 @@
         grams[c, :, :BS] = mixed
         grams[c, :, BS:] = cross
         diags[c : c + 1, :] = diag
-    lines = lax.broadcasted_iota(jnp.int32, (PAY_I - BS, R), 0)
+    lines = lax.broadcasted_iota(jnp.int32, (PAY_H - 2 * BS, BS), 0)
     for r in range(ROWS):
         weights = [mask[r * COLS + c] for c in range(COLS)]
         for piece in range(4):
@@ -375,12 +377,12 @@
             total = weights[0] * grams[0, rows, :]
             for c in range(1, COLS):
                 total += weights[c] * grams[c, rows, :]
-            pay[r, rows, :] = total
+            pay[r, rows, :] = total[:, :BS]
+            pay[r, BS + piece * 32 : BS + (piece + 1) * 32, :] = total[:, BS:]
         total = weights[0] * diags[0:1, :]
         for c in range(1, COLS):
             total += weights[c] * diags[c : c + 1, :]
-        row = jnp.concatenate([total, jnp.zeros((1, BS), f32)], axis=1)
-        pay[r, BS:, :] = jnp.where(lines == 0, row, 0.0)
+        pay[r, 2 * BS :, :] = jnp.where(lines == 0, total, 0.0)
 
 
 def sums_to_send(meta, mask, scales, dense, rounded, new, pay, new_hbm, grams, diags, sem):
@@ -439,9 +441,10 @@
     own, far = mine[...], theirs[...]
     data = jnp.where(core == 0, own, far) * scales[0:1, 2:3]
     packed = jnp.where(core == 0, far, own) * scales[0:1, 3:4]
-    high, low = split(unpack(packed[:BS, :BS], packed[:BS, BS:], packed[BS : BS + 1, :BS]))
+    high, low = split(unpack(packed[:BS], packed[BS : 2 * BS], packed[2 * BS : 2 * BS + 1]))
     begin = start[...]
-    value = data[:BS, :] - times(begin, high, low) - ridge_weight * begin
+    data = jnp.concatenate([data[:BS], data[BS : 2 * BS]], axis=1)
+    value = data - times(begin, high, low) - ridge_weight * begin
     first = times(value, high, low) + ridge_weight * value
     second = times(first, high, low) + ridge_weight * first
     powers = [exponent_of(largest(array)) for array in (value, first, second)]
@@ -584,7 +587,7 @@
         [((COLS * BS, R), f32, V), ((COLS * BS, R), bf16, V), row, whole],
         [big, pltpu.SemaphoreType.DMA],
     )(meta, ids, table, variant_factors, pieces, dosage_tiles)
-    sums = ((ROWS, PAY_I, R), f32, V)
+    sums = ((ROWS, PAY_H, BS), f32, V)
     scratch = [pltpu.VMEM((COLS, BS, R), f32), pltpu.VMEM((COLS, BS), f32)]
     pay, variant_new = call(
         sums_to_send,

time: 121 us -> 120 us (level)
  no operation moved by 1% of the time
where the time goes in v8:
time: 120 us
  blocking collectives  41.3 us (34%)
  starting transfers between devices  32.1 us (27%)
  waiting for transfers between devices  20.6 us (17%)
  Pallas kernels  19.6 us (16%)
  other arithmetic  4.41 us (4%)
  between operations  1.53 us (1%)
    all_to_all x1, blocking collectives, on_device(): here = lax.all_to_all(sent, CHIP, 0, 0)  21.3 us
    all_to_all x1, blocking collectives, on_device(): arrived = lax.all_to_all(of_chip, CHIP, 0, 0)  20 us
    pallas_call x8, Pallas kernels, run(): pl.pallas_call(kernel, out_shape=tuple((placed(*out) for out in outs)), i...  19.6 us
    all_to_all x1, starting transfers between devices, on_device(): lax.all_to_all(table.reshape(4 * slabs * 5, 1, BS), ALL, 0, 0, tiled=True)  10.9 us
    all_to_all x1, waiting for transfers between devices, on_device(): lax.all_to_all(table.reshape(4 * slabs * 5, 1, BS), ALL, 0, 0, tiled=True)  8.57 us
    ppermute x3, starting transfers between devices, on_device(): got = [lax.ppermute(far[k - 1], 'x', ring(k)) for k in (1, 2, 3)]  6.03 us
    ppermute x3, starting transfers between devices, on_device(): lax.ppermute(sent, 'x', ring(k))  4.72 us
    ppermute x3, starting transfers between devices, on_device(): nexts = [lax.ppermute(moments, 'x', ring(k)) for k in (1, 2, 3)]  3.96 us
  transfers between devices with their start and end apart: 18, of which 11 were waited for; matrix products, arithmetic and copies ran while one was open for 2% of the time, Pallas kernels for 4%

profile of v8, /device:TPU:0, one launch (start us, length us, event | category | flops | bytes accessed | tf_op | source)
XLA Modules:
  0.0 120.1 jit_solution(14112713988621656727)
XLA Ops:
  1.3 0.1 pad_add_fusion.1.meta
  1.4 6.9 %shard_map.77 = (f32[520,256]{1,0:T(8,128)S(1)}, f32[3,520,256]{2,1,0:T(8,128)S(1)}, f32[128]{0:T(128)S(1)}, f32[8,256]{1,0:T(8,128)S(1)}, f32[8,256]{1,0:T(8,128)S(1)}) custom-call(s32[3]{0:T(128)S(1)} %pad_add_fusion.1.meta, s32[1,1]{1,0:T(1,128)} %copy.17.live, s32[1,1,64]{2,1,0:T(1,128)} %rows_hbm.1, s32[1,1,64]{2,1,0:T(1,128)} %cols_hbm.1, ...), custom_call_target="tpu_custom_call" | custom-call | bytes 20971520 | tf_op jit(solution)/shard_map/pallas_call | solution.py:510
  8.3 0.2 convert_element_type.46
  8.4 0.0 copy-start
  8.5 0.2 slice_bitcast_fusion.2
  8.6 1.8 %collective-permute-start = (f16[520,256]{1,0:T(8,128)(2,1)S(1)}, f16[520,256]{1,0:T(8,128)(2,1)S(1)}, u32[]{:S(2)}, u32[]{:S(2)}) collective-permute-start(f16[520,256]{1,0:T(8,128)(2,1)S(1)} %get-tuple-element.30), channel_id=1, source_target_pairs={{0,1},{1,2},{2,3},{3,0},{4,5},{5,6},{6,7},{7,4},{8,9},{9,10},{10,1... | collective-permute-start | bytes 798728 | tf_op jit(solution)/shard_map/ppermute | solution.py:557
  10.5 2.6 %collective-permute-start.1 = (f16[520,256]{1,0:T(8,128)(2,1)S(1)}, f16[520,256]{1,0:T(8,128)(2,1)S(1)}, u32[]{:S(2)}, u32[]{:S(2)}) collective-permute-start(f16[520,256]{1,0:T(8,128)(2,1)S(1)} %get-tuple-element.32), channel_id=1, source_target_pairs={{0,2},{1,3},{2,0},{3,1},{4,6},{5,7},{6,4},{7,5},{8,10},{9,11},{10,... | collective-permute-start | bytes 798728 | tf_op jit(solution)/shard_map/ppermute | solution.py:557
  13.1 1.6 %collective-permute-start.2 = (f16[520,256]{1,0:T(8,128)(2,1)S(1)}, f16[520,256]{1,0:T(8,128)(2,1)S(1)}, u32[]{:S(2)}, u32[]{:S(2)}) collective-permute-start(f16[520,256]{1,0:T(8,128)(2,1)S(1)} %get-tuple-element.31), channel_id=1, source_target_pairs={{0,3},{1,0},{2,1},{3,2},{4,7},{5,4},{6,5},{7,6},{8,11},{9,8},{10,9... | collective-permute-start | bytes 798728 | tf_op jit(solution)/shard_map/ppermute | solution.py:557
  14.7 1.3 %collective-permute-start.3 = (f32[8,256]{1,0:T(8,128)S(1)}, f32[8,256]{1,0:T(8,128)S(1)}, u32[]{:S(2)}, u32[]{:S(2)}) collective-permute-start(f32[8,256]{1,0:T(8,128)S(1)} %get-tuple-element.18), channel_id=1, source_target_pairs={{0,4},{4,8},{8,12},{12,16},{16,20},{20,24},{24,28},{28,32},{32,36}... | collective-permute-start | bytes 24584 | tf_op jit(solution)/shard_map/ppermute | solution.py:558
  16.0 1.3 %collective-permute-start.4 = (f32[8,256]{1,0:T(8,128)S(1)}, f32[8,256]{1,0:T(8,128)S(1)}, u32[]{:S(2)}, u32[]{:S(2)}) collective-permute-start(f32[8,256]{1,0:T(8,128)S(1)} %get-tuple-element.19), channel_id=1, source_target_pairs={{4,0},{8,4},{12,8},{16,12},{20,16},{24,20},{28,24},{32,28},{36,32}... | collective-permute-start | bytes 24584 | tf_op jit(solution)/shard_map/ppermute | solution.py:559
  17.3 0.1 pad_add_fusion.2.meta
  17.3 0.0 collective-permute-done.3
  17.3 3.4 %collective-permute-done.4 = f32[8,256]{1,0:T(8,128)S(1)} collective-permute-done((f32[8,256]{1,0:T(8,128)S(1)}, f32[8,256]{1,0:T(8,128)S(1)}, u32[]{:S(2)}, u32[]{:S(2)}) %collective-permute-start.4) | collective-permute-done | bytes 8224 | tf_op jit(solution)/shard_map/ppermute | solution.py:559
  20.7 0.7 collective-permute-start.5
  21.4 0.7 collective-permute-start.6
  22.2 0.0 collective-permute-done
  22.2 1.9 %collective-permute-start.7 = (f32[16,256]{1,0:T(8,128)S(1)}, f32[16,256]{1,0:T(8,128)S(1)}, u32[]{:S(2)}, u32[]{:S(2)}) collective-permute-start(f32[16,256]{1,0:T(8,128)S(1)} %constant_dynamic-update-slice_fusion.near0), channel_id=1, source_target_pairs={{0,3},{1,0},{2,1},{3,2},{4,7},{5,4},{6,5},{7,6},{8,11},{9,8},{10,9... | collective-permute-start | bytes 49160 | tf_op jit(solution)/shard_map/ppermute | solution.py:562
  24.1 1.3 %collective-permute-done.1 = f16[520,256]{1,0:T(8,128)(2,1)S(1)} collective-permute-done((f16[520,256]{1,0:T(8,128)(2,1)S(1)}, f16[520,256]{1,0:T(8,128)(2,1)S(1)}, u32[]{:S(2)}, u32[]{:S(2)}) %collective-permute-start.1) | collective-permute-done | bytes 266272 | tf_op jit(solution)/shard_map/ppermute | solution.py:557
  25.4 0.0 collective-permute-done.2
  25.4 0.1 convert_add_fusion.total
  25.6 0.1 collective-permute-done.5.near1
  25.7 1.0 collective-permute-done.6.near2
  26.7 0.0 collective-permute-done.7.near3
  26.7 0.0 copy-done
  26.7 2.3 %shard_map.78 = (f32[2,256,256]{2,1,0:T(8,128)S(1)}, f32[640,128]{1,0:T(8,128)}) custom-call(s32[3]{0:T(128)S(1)} %pad_add_fusion.2.meta, f32[520,256]{1,0:T(8,128)S(1)} %convert_add_fusion.total, f32[1024,256]{1,0:T(8,128)S(1)} %copy-done, f32[16,256]{1,0:T(8,128)S(1)} %constant_dynamic-update-slice_fusion.near0, ...), custom_call_target="tpu_custom_call" | custom-call | bytes 1048576 | tf_op jit(solution)/shard_map/pallas_call | solution.py:510
  29.1 2.0 %collective-permute-start.8 = (f16[2,256,256]{2,1,0:T(8,128)(2,1)S(1)}, f16[2,256,256]{2,1,0:T(8,128)(2,1)}, u32[]{:S(2)}, u32[]{:S(2)}) collective-permute-start(f16[2,256,256]{2,1,0:T(8,128)(2,1)S(1)} %convert_element_type.50), channel_id=1, source_target_pairs={{0,1},{1,2},{2,3},{3,0},{4,5},{5,6},{6,7},{7,4},{8,9},{9,10},{10,1... | collective-permute-start | bytes 786440 | tf_op jit(solution)/shard_map/ppermute | solution.py:577
  31.0 2.1 %collective-permute-start.9 = (f16[2,256,256]{2,1,0:T(8,128)(2,1)S(1)}, f16[2,256,256]{2,1,0:T(8,128)(2,1)}, u32[]{:S(2)}, u32[]{:S(2)}) collective-permute-start(f16[2,256,256]{2,1,0:T(8,128)(2,1)S(1)} %convert_element_type.50), channel_id=1, source_target_pairs={{0,2},{1,3},{2,0},{3,1},{4,6},{5,7},{6,4},{7,5},{8,10},{9,11},{10,... | collective-permute-start | bytes 786440 | tf_op jit(solution)/shard_map/ppermute | solution.py:577
  33.1 0.6 collective-permute-start.10
  33.8 0.0 copy-done.2
  33.8 0.0 copy-done.3
  33.8 0.1 pad_add_fusion.ids
  33.9 10.9 %all-to-all-start = ((f32[640,1,128]{2,1,0:T(1,128)}), f32[640,1,128]{2,1,0:T(1,128)S(1)}, u32[]{:S(2)}, u32[]{:S(2)}) async-start(f32[640,1,128]{2,1,0:T(1,128)} %bitcast.12), calls=%async_computation | async-start | bytes 655360 | tf_op jit(solution)/shard_map/all_to_all | solution.py:579
  44.8 0.0 collective-permute-done.8
  44.8 0.9 collective-permute-done.9
  45.7 0.4 collective-permute-done.10
  46.1 1.3 %maximum_convert_fusion.pieces = f32[4,2,256,256]{3,2,1,0:T(8,128)S(1)} fusion(f16[1,2,256,256]{3,2,1,0:T(8,128)(2,1)} %bitcast.17, f16[1,2,256,256]{3,2,1,0:T(8,128)(2,1)} %bitcast.16, f16[1,2,256,256]{3,2,1,0:T(8,128)(2,1)} %bitcast.15, f16[1,2,256,256]{3,2,1,0:T(8,128)(2,1)S(1)} %convert_bitcast_fusion), kind=kLoop, calls=%fused_computation.3 | loop fusion | flops 2097152 | bytes 3145728 | tf_op jit(solution)/shard_map/convert_element_type | solution.py:578
  47.5 8.6 %all-to-all-done = f32[640,1,128]{2,1,0:T(1,128)S(1)} async-done(((f32[640,1,128]{2,1,0:T(1,128)}), f32[640,1,128]{2,1,0:T(1,128)S(1)}, u32[]{:S(2)}, u32[]{:S(2)}) %all-to-all-start) | async-done | bytes 327712 | tf_op jit(solution)/shard_map/all_to_all | solution.py:579
  56.0 2.2 %shard_map.79 = (f32[1024,256]{1,0:T(8,128)S(1)}, bf16[1024,256]{1,0:T(8,128)(2,1)S(1)}, f32[8,128]{1,0:T(8,128)S(1)}, bf16[2048,1024]{1,0:T(8,128)(2,1)S(1)}) custom-call(s32[3]{0:T(128)S(1)} %pad_add_fusion.1.meta, s32[129]{0:T(256)S(1)} %pad_add_fusion.ids, f32[640,128]{1,0:T(8,128)S(1)} %bitcast.31, f32[1024,256]{1,0:T(8,128)S(1)} %copy-done, ...), custom_call_target="tpu_custom_call" | custom-call | bytes 1048576 | tf_op jit(solution)/shard_map/pallas_call | solution.py:510
  58.2 2.4 %shard_map.80 = (f32[16,264,128]{2,1,0:T(8,128)S(1)}, f32[1024,256]{1,0:T(8,128)}) custom-call(s32[3]{0:T(128)S(1)} %pad_add_fusion.1.meta, f32[128]{0:T(128)S(1)} %get-tuple-element.15.mask, f32[8,128]{1,0:T(8,128)S(1)} %get-tuple-element.22.scales, bf16[2048,1024]{1,0:T(8,128)(2,1)S(1)} %get-tuple-element.23.dense, ...), custom_call_target="tpu_custom_call" | custom-call | bytes 1048576 | tf_op jit(solution)/shard_map/pallas_call | solution.py:510
  60.6 0.1 convert_element_type.52
  60.7 0.5 collective-permute-start.11
  61.2 3.5 %shard_map.81 = f32[16,264,128]{2,1,0:T(8,128)S(1)} custom-call(s32[3]{0:T(128)S(1)} %pad_add_fusion.1.meta, s32[129]{0:T(256)S(1)} %pad_add_fusion.ids, f32[128]{0:T(128)S(1)} %get-tuple-element.15.mask, f32[8,128]{1,0:T(8,128)S(1)} %get-tuple-element.22.scales, bf16[1024,256]{1,0:T(8,128)(2,1)S(1)} %get-tuple-element.24.rounded, ...), custom_call_target="tpu_custom_call" | custom-call | bytes 8388608 | tf_op jit(solution)/shard_map/pallas_call | solution.py:510
  64.7 0.0 collective-permute-done.11
  64.7 0.3 add_convert_fusion
  65.0 0.0 copy-start.1
  65.0 20.0 %all_to_all.15 = f16[16,264,128]{2,1,0:T(8,128)(2,1)S(1)} all-to-all(f16[16,264,128]{2,1,0:T(8,128)(2,1)S(1)} %add_convert_fusion), channel_id=1, replica_groups=mesh['z'=4,'y'=4,'c'=2,'x'=4] {'z','y'}, dimensions={0} | all-to-all | bytes 2162688 | tf_op jit(solution)/shard_map/all_to_all | solution.py:612
  85.0 0.1 convert_reduce_fusion.mine
  85.2 0.1 collective-permute-start.12
  85.3 1.3 %collective-permute-done.12.theirs = f32[264,128]{1,0:T(8,128)S(1)} collective-permute-done((f32[264,128]{1,0:T(8,128)S(1)}, f32[264,128]{1,0:T(8,128)S(1)}, u32[]{:S(2)}, u32[]{:S(2)}) %collective-permute-start.12) | collective-permute-done | bytes 135200 | tf_op jit(solution)/shard_map/ppermute | solution.py:614
  86.6 1.4 %shard_map.82 = f32[136,256]{1,0:T(8,128)S(1)} custom-call(s32[3]{0:T(128)S(1)} %pad_add_fusion.1.meta, f32[264,128]{1,0:T(8,128)S(1)} %convert_reduce_fusion.mine, f32[264,128]{1,0:T(8,128)S(1)} %collective-permute-done.12.theirs, f32[128,256]{1,0:T(8,128)S(1)} %constant_dynamic-slice_fusion.start, f32[8,128]{1,0:T(8,128)S(1)} %get-tuple-element.22.scales), custom_call_target="tpu_custom_call" | custom-call | bytes 1048576 | tf_op jit(solution)/shard_map/pallas_call | solution.py:510
  88.1 0.1 broadcast_in_dim.2
  88.2 21.3 %all_to_all.16 = f16[16,136,256]{2,1,0:T(8,128)(2,1)S(1)} all-to-all(f16[16,136,256]{2,1,0:T(8,128)(2,1)S(1)} %broadcast_in_dim.2), channel_id=1, replica_groups=mesh['z'=4,'y'=4,'c'=2,'x'=4] {'z','y'}, dimensions={0} | all-to-all | bytes 2228224 | tf_op jit(solution)/shard_map/all_to_all | solution.py:620
  109.5 0.0 collective-permute-start.16
  109.5 0.2 shard_map.83.own
  109.7 1.0 collective-permute-start.13
  110.7 2.9 %collective-permute-start.14 = (f32[8,128]{1,0:T(8,128)S(1)}, f32[8,128]{1,0:T(8,128)S(1)}, u32[]{:S(2)}, u32[]{:S(2)}) collective-permute-start(f32[8,128]{1,0:T(8,128)S(1)} %shard_map.83.own), channel_id=1, source_target_pairs={{0,2},{1,3},{2,0},{3,1},{4,6},{5,7},{6,4},{7,5},{8,10},{9,11},{10,... | collective-permute-start | bytes 12296 | tf_op jit(solution)/shard_map/ppermute | solution.py:624
  113.7 0.0 collective-permute-start.15
  113.7 0.9 collective-permute-done.13.next1
  114.5 1.3 %collective-permute-done.14.next2 = f32[8,128]{1,0:T(8,128)S(1)} collective-permute-done((f32[8,128]{1,0:T(8,128)S(1)}, f32[8,128]{1,0:T(8,128)S(1)}, u32[]{:S(2)}, u32[]{:S(2)}) %collective-permute-start.14) | collective-permute-done | bytes 4128 | tf_op jit(solution)/shard_map/ppermute | solution.py:624
  115.9 1.4 %collective-permute-done.15.next3 = f32[8,128]{1,0:T(8,128)S(1)} collective-permute-done((f32[8,128]{1,0:T(8,128)S(1)}, f32[8,128]{1,0:T(8,128)S(1)}, u32[]{:S(2)}, u32[]{:S(2)}) %collective-permute-start.15) | collective-permute-done | bytes 4128 | tf_op jit(solution)/shard_map/ppermute | solution.py:624
  117.3 0.7 shard_map.84
  118.0 0.2 slice_reduce_fusion.1
  118.2 0.0 collective-permute-done.16
  118.2 1.9 %add_add_fusion = f32[16,128,256]{2,1,0:T(8,128)} fusion(f32[16,128,256]{2,1,0:T(8,128)S(1)} %bitcast.32, f16[16,136,256]{2,1,0:T(8,128)(2,1)S(1)} %collective-permute-done.16, f16[16,136,256]{2,1,0:T(8,128)(2,1)S(1)} %all_to_all.16, f32[16]{0:T(128)S(1)} %get-tuple-element.29, f32[16]{0:T(128)S(1)} %get-tuple-element.28), kind=kLoop, calls=%fused_computation.2 | loop fusion | flops 3145728 | bytes 6291584 | tf_op jit(solution)/shard_map/add | solution.py:632
  (11 shorter events, 0.1 us)
Async XLA Ops:
  8.4 18.2 %copy-start = (f32[1024,256]{1,0:T(8,128)S(1)}, f32[1024,256]{1,0:T(8,128)}, u32[]{:S(2)}) copy-start(f32[1024,256]{1,0:T(8,128)} %start.3) | copy-start | bytes 3145732
  8.6 13.5 %collective-permute-start = (f16[520,256]{1,0:T(8,128)(2,1)S(1)}, f16[520,256]{1,0:T(8,128)(2,1)S(1)}, u32[]{:S(2)}, u32[]{:S(2)}) collective-permute-start(f16[520,256]{1,0:T(8,128)(2,1)S(1)} %get-tuple-element.30), channel_id=1, source_target_pairs={{0,1},{1,2},{2,3},{3,0},{4,5},{5,6},{6,7},{7,4},{8,9},{9,10},{10,1... | collective-permute-start | bytes 798728 | tf_op jit(solution)/shard_map/ppermute | solution.py:557
  10.5 15.0 %collective-permute-start.1 = (f16[520,256]{1,0:T(8,128)(2,1)S(1)}, f16[520,256]{1,0:T(8,128)(2,1)S(1)}, u32[]{:S(2)}, u32[]{:S(2)}) collective-permute-start(f16[520,256]{1,0:T(8,128)(2,1)S(1)} %get-tuple-element.32), channel_id=1, source_target_pairs={{0,2},{1,3},{2,0},{3,1},{4,6},{5,7},{6,4},{7,5},{8,10},{9,11},{10,... | collective-permute-start | bytes 798728 | tf_op jit(solution)/shard_map/ppermute | solution.py:557
  13.1 12.3 %collective-permute-start.2 = (f16[520,256]{1,0:T(8,128)(2,1)S(1)}, f16[520,256]{1,0:T(8,128)(2,1)S(1)}, u32[]{:S(2)}, u32[]{:S(2)}) collective-permute-start(f16[520,256]{1,0:T(8,128)(2,1)S(1)} %get-tuple-element.31), channel_id=1, source_target_pairs={{0,3},{1,0},{2,1},{3,2},{4,7},{5,4},{6,5},{7,6},{8,11},{9,8},{10,9... | collective-permute-start | bytes 798728 | tf_op jit(solution)/shard_map/ppermute | solution.py:557
  14.7 2.7 %collective-permute-start.3 = (f32[8,256]{1,0:T(8,128)S(1)}, f32[8,256]{1,0:T(8,128)S(1)}, u32[]{:S(2)}, u32[]{:S(2)}) collective-permute-start(f32[8,256]{1,0:T(8,128)S(1)} %get-tuple-element.18), channel_id=1, source_target_pairs={{0,4},{4,8},{8,12},{12,16},{16,20},{20,24},{24,28},{28,32},{32,36}... | collective-permute-start | bytes 24584 | tf_op jit(solution)/shard_map/ppermute | solution.py:558
  16.0 4.7 %collective-permute-start.4 = (f32[8,256]{1,0:T(8,128)S(1)}, f32[8,256]{1,0:T(8,128)S(1)}, u32[]{:S(2)}, u32[]{:S(2)}) collective-permute-start(f32[8,256]{1,0:T(8,128)S(1)} %get-tuple-element.19), channel_id=1, source_target_pairs={{4,0},{8,4},{12,8},{16,12},{20,16},{24,20},{28,24},{32,28},{36,32}... | collective-permute-start | bytes 24584 | tf_op jit(solution)/shard_map/ppermute | solution.py:559
  20.7 4.9 %collective-permute-start.5 = (f32[16,256]{1,0:T(8,128)S(1)}, f32[16,256]{1,0:T(8,128)S(1)}, u32[]{:S(2)}, u32[]{:S(2)}) collective-permute-start(f32[16,256]{1,0:T(8,128)S(1)} %constant_dynamic-update-slice_fusion.near0), channel_id=1, source_target_pairs={{0,1},{1,2},{2,3},{3,0},{4,5},{5,6},{6,7},{7,4},{8,9},{9,10},{10,1... | collective-permute-start | bytes 49160 | tf_op jit(solution)/shard_map/ppermute | solution.py:562
  21.4 5.2 %collective-permute-start.6 = (f32[16,256]{1,0:T(8,128)S(1)}, f32[16,256]{1,0:T(8,128)S(1)}, u32[]{:S(2)}, u32[]{:S(2)}) collective-permute-start(f32[16,256]{1,0:T(8,128)S(1)} %constant_dynamic-update-slice_fusion.near0), channel_id=1, source_target_pairs={{0,2},{1,3},{2,0},{3,1},{4,6},{5,7},{6,4},{7,5},{8,10},{9,11},{10,... | collective-permute-start | bytes 49160 | tf_op jit(solution)/shard_map/ppermute | solution.py:562
  22.2 4.5 %collective-permute-start.7 = (f32[16,256]{1,0:T(8,128)S(1)}, f32[16,256]{1,0:T(8,128)S(1)}, u32[]{:S(2)}, u32[]{:S(2)}) collective-permute-start(f32[16,256]{1,0:T(8,128)S(1)} %constant_dynamic-update-slice_fusion.near0), channel_id=1, source_target_pairs={{0,3},{1,0},{2,1},{3,2},{4,7},{5,4},{6,5},{7,6},{8,11},{9,8},{10,9... | collective-permute-start | bytes 49160 | tf_op jit(solution)/shard_map/ppermute | solution.py:562
  25.4 8.4 %copy-start.2 = (s32[1,1,64]{2,1,0:T(1,128)S(1)}, s32[1,1,64]{2,1,0:T(1,128)}, u32[]{:S(2)}) copy-start(s32[1,1,64]{2,1,0:T(1,128)} %rows_hbm.1) | copy-start | bytes 772
  25.4 8.4 %copy-start.3 = (s32[1,1,64]{2,1,0:T(1,128)S(1)}, s32[1,1,64]{2,1,0:T(1,128)}, u32[]{:S(2)}) copy-start(s32[1,1,64]{2,1,0:T(1,128)} %cols_hbm.1) | copy-start | bytes 772
  29.1 15.7 %collective-permute-start.8 = (f16[2,256,256]{2,1,0:T(8,128)(2,1)S(1)}, f16[2,256,256]{2,1,0:T(8,128)(2,1)}, u32[]{:S(2)}, u32[]{:S(2)}) collective-permute-start(f16[2,256,256]{2,1,0:T(8,128)(2,1)S(1)} %convert_element_type.50), channel_id=1, source_target_pairs={{0,1},{1,2},{2,3},{3,0},{4,5},{5,6},{6,7},{7,4},{8,9},{9,10},{10,1... | collective-permute-start | bytes 786440 | tf_op jit(solution)/shard_map/ppermute | solution.py:577
  31.0 14.7 %collective-permute-start.9 = (f16[2,256,256]{2,1,0:T(8,128)(2,1)S(1)}, f16[2,256,256]{2,1,0:T(8,128)(2,1)}, u32[]{:S(2)}, u32[]{:S(2)}) collective-permute-start(f16[2,256,256]{2,1,0:T(8,128)(2,1)S(1)} %convert_element_type.50), channel_id=1, source_target_pairs={{0,2},{1,3},{2,0},{3,1},{4,6},{5,7},{6,4},{7,5},{8,10},{9,11},{10,... | collective-permute-start | bytes 786440 | tf_op jit(solution)/shard_map/ppermute | solution.py:577
  33.1 13.0 %collective-permute-start.10 = (f16[2,256,256]{2,1,0:T(8,128)(2,1)S(1)}, f16[2,256,256]{2,1,0:T(8,128)(2,1)}, u32[]{:S(2)}, u32[]{:S(2)}) collective-permute-start(f16[2,256,256]{2,1,0:T(8,128)(2,1)S(1)} %convert_element_type.50), channel_id=1, source_target_pairs={{0,3},{1,0},{2,1},{3,2},{4,7},{5,4},{6,5},{7,6},{8,11},{9,8},{10,9... | collective-permute-start | bytes 786440 | tf_op jit(solution)/shard_map/ppermute | solution.py:577
  33.9 22.2 %all-to-all-start = ((f32[640,1,128]{2,1,0:T(1,128)}), f32[640,1,128]{2,1,0:T(1,128)S(1)}, u32[]{:S(2)}, u32[]{:S(2)}) async-start(f32[640,1,128]{2,1,0:T(1,128)} %bitcast.12), calls=%async_computation | async-start | bytes 655360 | tf_op jit(solution)/shard_map/all_to_all | solution.py:579
  60.7 4.0 %collective-permute-start.11 = (f16[16,264,128]{2,1,0:T(8,128)(2,1)S(1)}, f16[16,264,128]{2,1,0:T(8,128)(2,1)S(1)}, u32[]{:S(2)}, u32[]{:S(2)}) collective-permute-start(f16[16,264,128]{2,1,0:T(8,128)(2,1)S(1)} %convert_element_type.52), channel_id=1, source_target_pairs={{0,4},{4,0},{1,5},{5,1},{2,6},{6,2},{3,7},{7,3},{8,12},{12,8},{9,1... | collective-permute-start | bytes 3244040 | tf_op jit(solution)/shard_map/ppermute | solution.py:598
  65.0 20.3 %copy-start.1 = (f32[2048,256]{1,0:T(8,128)S(1)}, f32[2048,256]{1,0:T(8,128)}, u32[]{:S(2)}) copy-start(f32[2048,256]{1,0:T(8,128)} %factors_hbm.1) | copy-start | bytes 6291460
  85.2 1.4 %collective-permute-start.12 = (f32[264,128]{1,0:T(8,128)S(1)}, f32[264,128]{1,0:T(8,128)S(1)}, u32[]{:S(2)}, u32[]{:S(2)}) collective-permute-start(f32[264,128]{1,0:T(8,128)S(1)} %convert_reduce_fusion.mine), channel_id=1, source_target_pairs={{0,4},{4,0},{1,5},{5,1},{2,6},{6,2},{3,7},{7,3},{8,12},{12,8},{9,1... | collective-permute-start | bytes 405512 | tf_op jit(solution)/shard_map/ppermute | solution.py:614
  109.5 8.7 %collective-permute-start.16 = (f16[16,136,256]{2,1,0:T(8,128)(2,1)S(1)}, f16[16,136,256]{2,1,0:T(8,128)(2,1)S(1)}, u32[]{:S(2)}, u32[]{:S(2)}) collective-permute-start(f16[16,136,256]{2,1,0:T(8,128)(2,1)S(1)} %all_to_all.16), channel_id=1, source_target_pairs={{0,4},{4,0},{1,5},{5,1},{2,6},{6,2},{3,7},{7,3},{8,12},{12,8},{9,1... | collective-permute-start | bytes 3342344 | tf_op jit(solution)/shard_map/ppermute | solution.py:621
  109.7 4.8 %collective-permute-start.13 = (f32[8,128]{1,0:T(8,128)S(1)}, f32[8,128]{1,0:T(8,128)S(1)}, u32[]{:S(2)}, u32[]{:S(2)}) collective-permute-start(f32[8,128]{1,0:T(8,128)S(1)} %shard_map.83.own), channel_id=1, source_target_pairs={{0,1},{1,2},{2,3},{3,0},{4,5},{5,6},{6,7},{7,4},{8,9},{9,10},{10,1... | collective-permute-start | bytes 12296 | tf_op jit(solution)/shard_map/ppermute | solution.py:624
  110.7 5.1 %collective-permute-start.14 = (f32[8,128]{1,0:T(8,128)S(1)}, f32[8,128]{1,0:T(8,128)S(1)}, u32[]{:S(2)}, u32[]{:S(2)}) collective-permute-start(f32[8,128]{1,0:T(8,128)S(1)} %shard_map.83.own), channel_id=1, source_target_pairs={{0,2},{1,3},{2,0},{3,1},{4,6},{5,7},{6,4},{7,5},{8,10},{9,11},{10,... | collective-permute-start | bytes 12296 | tf_op jit(solution)/shard_map/ppermute | solution.py:624
  113.7 3.6 %collective-permute-start.15 = (f32[8,128]{1,0:T(8,128)S(1)}, f32[8,128]{1,0:T(8,128)S(1)}, u32[]{:S(2)}, u32[]{:S(2)}) collective-permute-start(f32[8,128]{1,0:T(8,128)S(1)} %shard_map.83.own), channel_id=1, source_target_pairs={{0,3},{1,0},{2,1},{3,2},{4,7},{5,4},{6,5},{7,6},{8,11},{9,8},{10,9... | collective-permute-start | bytes 12296 | tf_op jit(solution)/shard_map/ppermute | solution.py:624

commit v9 on v8

--- a/solution.py
+++ b/solution.py
@@ -457,9 +457,11 @@
         total_of(first * first),
         total_of(first * second),
     ]
-    sent[:BS, :] = jnp.where(core == 0, value, first) * 16384.0
+    chosen = jnp.where(core == 0, value, first) * 16384.0
+    sent[:BS, :] = chosen[:, :BS]
+    sent[BS : 2 * BS, :] = chosen[:, BS:]
     row = as_row([part for moment in moments for part in pieces_of(moment)] + powers)
-    sent[BS:, :] = jnp.concatenate([row, row], axis=1)
+    sent[2 * BS :, :] = row
 
 
 def chip_moments(lines, moments):
@@ -613,21 +615,24 @@
     mine = jnp.sum(arrived.astype(f32), axis=0)
     theirs = lax.ppermute(mine, "c", swap)
     begin = lax.dynamic_slice_in_dim(indiv_factors, chip * BS, BS, 0)
-    (sent,) = call(indiv_moments, [S, V, V, V, V], [((PAY_I, R), f32, V)])(
+    (sent,) = call(indiv_moments, [S, V, V, V, V], [((PAY_H, BS), f32, V)])(
         meta, mine, theirs, begin, scales
     )
-    sent = jnp.broadcast_to(sent.astype(f16)[None], (ROWS, PAY_I, R))
+    sent = jnp.broadcast_to(sent.astype(f16)[None], (ROWS, PAY_H, BS))
     here = lax.all_to_all(sent, CHIP, 0, 0)
     there = lax.ppermute(here, "c", swap)
-    lines = here[:, BS, :BS].astype(f32)
+    lines = here[:, 2 * BS].astype(f32)
     (moments,) = call(chip_moments, [V], [row])(lines)
     nexts = [lax.ppermute(moments, "x", ring(k)) for k in (1, 2, 3)]
     (shares,) = call(indiv_shares, [S] + [V] * 5, [((ROWS, BS), f32, V)])(
         meta, lines, moments, *nexts
     )
+    def halves(array):
+        return jnp.concatenate([array[:, :BS], array[:, BS : 2 * BS]], axis=2).astype(f32)
+
     change = (
-        shares[:, 0].reshape(ROWS, 1, 1) * here[:, :BS].astype(f32)
-        + shares[:, 1].reshape(ROWS, 1, 1) * there[:, :BS].astype(f32)
+        shares[:, 0].reshape(ROWS, 1, 1) * halves(here)
+        + shares[:, 1].reshape(ROWS, 1, 1) * halves(there)
     )
     indiv_new = indiv_factors.reshape(ROWS, BS, R) + change
     return variant_new, indiv_new.reshape(ROWS * BS, R)

time: 120 us -> 120 us (level)
  transfers between devices with their start and end apart: 18 -> 18, of which waited for: 11 -> 12; matrix products, arithmetic and copies ran while one was open for 2% -> 2% of each run, Pallas kernels for 4% -> 4%
where the time goes in v9:
time: 120 us
  blocking collectives  41.4 us (34%)
  starting transfers between devices  31.6 us (26%)
  Pallas kernels  20.4 us (17%)
  waiting for transfers between devices  19.5 us (16%)
  other arithmetic  4.23 us (4%)
  between operations  1.54 us (1%)
    all_to_all x1, blocking collectives, on_device(): here = lax.all_to_all(sent, CHIP, 0, 0)  21 us
    pallas_call x8, Pallas kernels, run(): pl.pallas_call(kernel, out_shape=tuple((placed(*out) for out in outs)), i...  20.4 us
    all_to_all x1, blocking collectives, on_device(): arrived = lax.all_to_all(of_chip, CHIP, 0, 0)  20.4 us
    all_to_all x1, starting transfers between devices, on_device(): lax.all_to_all(table.reshape(4 * slabs * 5, 1, BS), ALL, 0, 0, tiled=True)  11.2 us
    all_to_all x1, waiting for transfers between devices, on_device(): lax.all_to_all(table.reshape(4 * slabs * 5, 1, BS), ALL, 0, 0, tiled=True)  8.87 us
    ppermute x3, starting transfers between devices, on_device(): got = [lax.ppermute(far[k - 1], 'x', ring(k)) for k in (1, 2, 3)]  5.79 us
    ppermute x3, starting transfers between devices, on_device(): lax.ppermute(sent, 'x', ring(k))  4.69 us
    ppermute x3, starting transfers between devices, on_device(): nexts = [lax.ppermute(moments, 'x', ring(k)) for k in (1, 2, 3)]  3.97 us
  transfers between devices with their start and end apart: 18, of which 12 were waited for; matrix products, arithmetic and copies ran while one was open for 2% of the time, Pallas kernels for 4%

profile of v9, /device:TPU:0, one launch (start us, length us, event | category | flops | bytes accessed | tf_op | source)
XLA Modules:
  0.0 119.9 jit_solution(12679381933995370207)
XLA Ops:
  1.3 0.1 pad_add_fusion.1.meta
  1.4 7.5 %shard_map.77 = (f32[520,256]{1,0:T(8,128)S(1)}, f32[3,520,256]{2,1,0:T(8,128)S(1)}, f32[128]{0:T(128)S(1)}, f32[8,256]{1,0:T(8,128)S(1)}, f32[8,256]{1,0:T(8,128)S(1)}) custom-call(s32[3]{0:T(128)S(1)} %pad_add_fusion.1.meta, s32[1,1]{1,0:T(1,128)} %copy.19.live, s32[1,1,64]{2,1,0:T(1,128)} %rows_hbm.1, s32[1,1,64]{2,1,0:T(1,128)} %cols_hbm.1, ...), custom_call_target="tpu_custom_call" | custom-call | bytes 20971520 | tf_op jit(solution)/shard_map/pallas_call | solution.py:512
  8.9 0.2 convert_element_type.48
  9.1 0.0 copy-start
  9.1 0.2 slice_bitcast_fusion.2
  9.2 1.6 %collective-permute-start = (f16[520,256]{1,0:T(8,128)(2,1)S(1)}, f16[520,256]{1,0:T(8,128)(2,1)S(1)}, u32[]{:S(2)}, u32[]{:S(2)}) collective-permute-start(f16[520,256]{1,0:T(8,128)(2,1)S(1)} %get-tuple-element.34), channel_id=1, source_target_pairs={{0,1},{1,2},{2,3},{3,0},{4,5},{5,6},{6,7},{7,4},{8,9},{9,10},{10,1... | collective-permute-start | bytes 798728 | tf_op jit(solution)/shard_map/ppermute | solution.py:559
  10.9 2.7 %collective-permute-start.1 = (f16[520,256]{1,0:T(8,128)(2,1)S(1)}, f16[520,256]{1,0:T(8,128)(2,1)S(1)}, u32[]{:S(2)}, u32[]{:S(2)}) collective-permute-start(f16[520,256]{1,0:T(8,128)(2,1)S(1)} %get-tuple-element.36), channel_id=1, source_target_pairs={{0,2},{1,3},{2,0},{3,1},{4,6},{5,7},{6,4},{7,5},{8,10},{9,11},{10,... | collective-permute-start | bytes 798728 | tf_op jit(solution)/shard_map/ppermute | solution.py:559
  13.6 1.4 %collective-permute-start.2 = (f16[520,256]{1,0:T(8,128)(2,1)S(1)}, f16[520,256]{1,0:T(8,128)(2,1)S(1)}, u32[]{:S(2)}, u32[]{:S(2)}) collective-permute-start(f16[520,256]{1,0:T(8,128)(2,1)S(1)} %get-tuple-element.35), channel_id=1, source_target_pairs={{0,3},{1,0},{2,1},{3,2},{4,7},{5,4},{6,5},{7,6},{8,11},{9,8},{10,9... | collective-permute-start | bytes 798728 | tf_op jit(solution)/shard_map/ppermute | solution.py:559
  15.0 1.3 %collective-permute-start.3 = (f32[8,256]{1,0:T(8,128)S(1)}, f32[8,256]{1,0:T(8,128)S(1)}, u32[]{:S(2)}, u32[]{:S(2)}) collective-permute-start(f32[8,256]{1,0:T(8,128)S(1)} %get-tuple-element.18), channel_id=1, source_target_pairs={{0,4},{4,8},{8,12},{12,16},{16,20},{20,24},{24,28},{28,32},{32,36}... | collective-permute-start | bytes 24584 | tf_op jit(solution)/shard_map/ppermute | solution.py:560
  16.3 1.3 %collective-permute-start.4 = (f32[8,256]{1,0:T(8,128)S(1)}, f32[8,256]{1,0:T(8,128)S(1)}, u32[]{:S(2)}, u32[]{:S(2)}) collective-permute-start(f32[8,256]{1,0:T(8,128)S(1)} %get-tuple-element.19), channel_id=1, source_target_pairs={{4,0},{8,4},{12,8},{16,12},{20,16},{24,20},{28,24},{32,28},{36,32}... | collective-permute-start | bytes 24584 | tf_op jit(solution)/shard_map/ppermute | solution.py:561
  17.6 0.1 pad_add_fusion.2.meta
  17.7 0.0 collective-permute-done.3
  17.7 3.0 %collective-permute-done.4 = f32[8,256]{1,0:T(8,128)S(1)} collective-permute-done((f32[8,256]{1,0:T(8,128)S(1)}, f32[8,256]{1,0:T(8,128)S(1)}, u32[]{:S(2)}, u32[]{:S(2)}) %collective-permute-start.4) | collective-permute-done | bytes 8224 | tf_op jit(solution)/shard_map/ppermute | solution.py:561
  20.7 0.5 collective-permute-start.5
  21.3 1.0 collective-permute-start.6
  22.2 0.0 collective-permute-done
  22.2 1.7 %collective-permute-start.7 = (f32[16,256]{1,0:T(8,128)S(1)}, f32[16,256]{1,0:T(8,128)S(1)}, u32[]{:S(2)}, u32[]{:S(2)}) collective-permute-start(f32[16,256]{1,0:T(8,128)S(1)} %constant_dynamic-update-slice_fusion.near0), channel_id=1, source_target_pairs={{0,3},{1,0},{2,1},{3,2},{4,7},{5,4},{6,5},{7,6},{8,11},{9,8},{10,9... | collective-permute-start | bytes 49160 | tf_op jit(solution)/shard_map/ppermute | solution.py:564
  24.0 0.8 collective-permute-done.1
  24.8 0.0 collective-permute-done.2
  24.8 0.1 convert_add_fusion.total
  25.0 0.7 collective-permute-done.5.near1
  25.7 0.8 collective-permute-done.6.near2
  26.5 0.2 collective-permute-done.7.near3
  26.7 2.3 %shard_map.78 = (f32[2,256,256]{2,1,0:T(8,128)S(1)}, f32[640,128]{1,0:T(8,128)}) custom-call(s32[3]{0:T(128)S(1)} %pad_add_fusion.2.meta, f32[520,256]{1,0:T(8,128)S(1)} %convert_add_fusion.total, f32[1024,256]{1,0:T(8,128)S(1)} %copy-done, f32[16,256]{1,0:T(8,128)S(1)} %constant_dynamic-update-slice_fusion.near0, ...), custom_call_target="tpu_custom_call" | custom-call | bytes 1048576 | tf_op jit(solution)/shard_map/pallas_call | solution.py:512
  29.1 1.9 %collective-permute-start.8 = (f16[2,256,256]{2,1,0:T(8,128)(2,1)S(1)}, f16[2,256,256]{2,1,0:T(8,128)(2,1)}, u32[]{:S(2)}, u32[]{:S(2)}) collective-permute-start(f16[2,256,256]{2,1,0:T(8,128)(2,1)S(1)} %convert_element_type.52), channel_id=1, source_target_pairs={{0,1},{1,2},{2,3},{3,0},{4,5},{5,6},{6,7},{7,4},{8,9},{9,10},{10,1... | collective-permute-start | bytes 786440 | tf_op jit(solution)/shard_map/ppermute | solution.py:579
  31.0 2.1 %collective-permute-start.9 = (f16[2,256,256]{2,1,0:T(8,128)(2,1)S(1)}, f16[2,256,256]{2,1,0:T(8,128)(2,1)}, u32[]{:S(2)}, u32[]{:S(2)}) collective-permute-start(f16[2,256,256]{2,1,0:T(8,128)(2,1)S(1)} %convert_element_type.52), channel_id=1, source_target_pairs={{0,2},{1,3},{2,0},{3,1},{4,6},{5,7},{6,4},{7,5},{8,10},{9,11},{10,... | collective-permute-start | bytes 786440 | tf_op jit(solution)/shard_map/ppermute | solution.py:579
  33.1 0.7 collective-permute-start.10
  33.8 0.1 pad_add_fusion.ids
  33.9 11.2 %all-to-all-start = ((f32[640,1,128]{2,1,0:T(1,128)}), f32[640,1,128]{2,1,0:T(1,128)S(1)}, u32[]{:S(2)}, u32[]{:S(2)}) async-start(f32[640,1,128]{2,1,0:T(1,128)} %bitcast.12), calls=%async_computation | async-start | bytes 655360 | tf_op jit(solution)/shard_map/all_to_all | solution.py:581
  45.1 0.0 collective-permute-done.8
  45.1 0.6 collective-permute-done.9
  45.7 0.5 collective-permute-done.10
  46.2 1.3 %maximum_convert_fusion.pieces = f32[4,2,256,256]{3,2,1,0:T(8,128)S(1)} fusion(f16[1,2,256,256]{3,2,1,0:T(8,128)(2,1)} %bitcast.17, f16[1,2,256,256]{3,2,1,0:T(8,128)(2,1)} %bitcast.16, f16[1,2,256,256]{3,2,1,0:T(8,128)(2,1)} %bitcast.15, f16[1,2,256,256]{3,2,1,0:T(8,128)(2,1)S(1)} %convert_bitcast_fusion), kind=kLoop, calls=%fused_computation.3 | loop fusion | flops 2097152 | bytes 3145728 | tf_op jit(solution)/shard_map/convert_element_type | solution.py:580
  47.5 8.9 %all-to-all-done = f32[640,1,128]{2,1,0:T(1,128)S(1)} async-done(((f32[640,1,128]{2,1,0:T(1,128)}), f32[640,1,128]{2,1,0:T(1,128)S(1)}, u32[]{:S(2)}, u32[]{:S(2)}) %all-to-all-start) | async-done | bytes 327712 | tf_op jit(solution)/shard_map/all_to_all | solution.py:581
  56.4 2.2 %shard_map.79 = (f32[1024,256]{1,0:T(8,128)S(1)}, bf16[1024,256]{1,0:T(8,128)(2,1)S(1)}, f32[8,128]{1,0:T(8,128)S(1)}, bf16[2048,1024]{1,0:T(8,128)(2,1)S(1)}) custom-call(s32[3]{0:T(128)S(1)} %pad_add_fusion.1.meta, s32[129]{0:T(256)S(1)} %pad_add_fusion.ids, f32[640,128]{1,0:T(8,128)S(1)} %bitcast.37, f32[1024,256]{1,0:T(8,128)S(1)} %copy-done, ...), custom_call_target="tpu_custom_call" | custom-call | bytes 1048576 | tf_op jit(solution)/shard_map/pallas_call | solution.py:512
  58.5 2.4 %shard_map.80 = (f32[16,264,128]{2,1,0:T(8,128)S(1)}, f32[1024,256]{1,0:T(8,128)}) custom-call(s32[3]{0:T(128)S(1)} %pad_add_fusion.1.meta, f32[128]{0:T(128)S(1)} %get-tuple-element.15.mask, f32[8,128]{1,0:T(8,128)S(1)} %get-tuple-element.22.scales, bf16[2048,1024]{1,0:T(8,128)(2,1)S(1)} %get-tuple-element.23.dense, ...), custom_call_target="tpu_custom_call" | custom-call | bytes 1048576 | tf_op jit(solution)/shard_map/pallas_call | solution.py:512
  60.9 0.1 convert_element_type.54
  61.1 0.1 collective-permute-start.11
  61.1 3.7 %shard_map.81 = f32[16,264,128]{2,1,0:T(8,128)S(1)} custom-call(s32[3]{0:T(128)S(1)} %pad_add_fusion.1.meta, s32[129]{0:T(256)S(1)} %pad_add_fusion.ids, f32[128]{0:T(128)S(1)} %get-tuple-element.15.mask, f32[8,128]{1,0:T(8,128)S(1)} %get-tuple-element.22.scales, bf16[1024,256]{1,0:T(8,128)(2,1)S(1)} %get-tuple-element.24.rounded, ...), custom_call_target="tpu_custom_call" | custom-call | bytes 8388608 | tf_op jit(solution)/shard_map/pallas_call | solution.py:512
  64.8 0.0 collective-permute-done.11
  64.8 0.3 add_convert_fusion
  65.1 0.0 copy-start.1
  65.1 20.4 %all_to_all.15 = f16[16,264,128]{2,1,0:T(8,128)(2,1)S(1)} all-to-all(f16[16,264,128]{2,1,0:T(8,128)(2,1)S(1)} %add_convert_fusion), channel_id=1, replica_groups=mesh['z'=4,'y'=4,'c'=2,'x'=4] {'z','y'}, dimensions={0} | all-to-all | bytes 2162688 | tf_op jit(solution)/shard_map/all_to_all | solution.py:614
  85.5 0.1 convert_reduce_fusion.mine
  85.7 0.1 collective-permute-start.12
  85.8 1.3 %collective-permute-done.12.theirs = f32[264,128]{1,0:T(8,128)S(1)} collective-permute-done((f32[264,128]{1,0:T(8,128)S(1)}, f32[264,128]{1,0:T(8,128)S(1)}, u32[]{:S(2)}, u32[]{:S(2)}) %collective-permute-start.12) | collective-permute-done | bytes 135200 | tf_op jit(solution)/shard_map/ppermute | solution.py:616
  87.1 1.4 %shard_map.82 = f32[264,128]{1,0:T(8,128)S(1)} custom-call(s32[3]{0:T(128)S(1)} %pad_add_fusion.1.meta, f32[264,128]{1,0:T(8,128)S(1)} %convert_reduce_fusion.mine, f32[264,128]{1,0:T(8,128)S(1)} %collective-permute-done.12.theirs, f32[128,256]{1,0:T(8,128)S(1)} %constant_dynamic-slice_fusion.start, f32[8,128]{1,0:T(8,128)S(1)} %get-tuple-element.22.scales), custom_call_target="tpu_custom_call" | custom-call | bytes 1048576 | tf_op jit(solution)/shard_map/pallas_call | solution.py:512
  88.6 0.1 broadcast_in_dim.2
  88.7 21.0 %all_to_all.16 = f16[16,264,128]{2,1,0:T(8,128)(2,1)S(1)} all-to-all(f16[16,264,128]{2,1,0:T(8,128)(2,1)S(1)} %broadcast_in_dim.2), channel_id=1, replica_groups=mesh['z'=4,'y'=4,'c'=2,'x'=4] {'z','y'}, dimensions={0} | all-to-all | bytes 2162688 | tf_op jit(solution)/shard_map/all_to_all | solution.py:622
  109.7 0.0 collective-permute-start.16
  109.8 0.2 shard_map.83.own
  110.0 0.6 collective-permute-start.13
  110.6 2.8 %collective-permute-start.14 = (f32[8,128]{1,0:T(8,128)S(1)}, f32[8,128]{1,0:T(8,128)S(1)}, u32[]{:S(2)}, u32[]{:S(2)}) collective-permute-start(f32[8,128]{1,0:T(8,128)S(1)} %shard_map.83.own), channel_id=1, source_target_pairs={{0,2},{1,3},{2,0},{3,1},{4,6},{5,7},{6,4},{7,5},{8,10},{9,11},{10,... | collective-permute-start | bytes 12296 | tf_op jit(solution)/shard_map/ppermute | solution.py:626
  113.3 0.6 collective-permute-start.15
  114.0 0.3 fusion.2
  114.2 0.6 collective-permute-done.13.next1
  114.8 0.9 collective-permute-done.14.next2
  115.7 1.3 %collective-permute-done.15.next3 = f32[8,128]{1,0:T(8,128)S(1)} collective-permute-done((f32[8,128]{1,0:T(8,128)S(1)}, f32[8,128]{1,0:T(8,128)S(1)}, u32[]{:S(2)}, u32[]{:S(2)}) %collective-permute-start.15) | collective-permute-done | bytes 4128 | tf_op jit(solution)/shard_map/ppermute | solution.py:626
  117.0 0.7 shard_map.84
  117.7 0.2 slice_reduce_fusion.1
  117.8 0.1 broadcast_bitcast_fusion
  117.9 0.0 collective-permute-done.16
  117.9 0.3 fusion.1
  118.2 1.7 %add_add_fusion = f32[2048,256]{1,0:T(8,128)} fusion(f32[2048,256]{1,0:T(8,128)S(1)} %copy-done.1, f16[2048,128]{1,0:T(8,128)(2,1)S(1)} %bitcast.39, f16[2048,128]{1,0:T(8,128)(2,1)S(1)} %bitcast.38, f16[2048,128]{1,0:T(8,128)(2,1)S(1)} %bitcast.41, f16[2048,128]{1,0:T(8,128)(2,1)S(1)} %bitcast.40, f32[2048]{0:T(1024)S(1)} %get-tuple-element.37, ...), kind=kLoop, calls=%fused_computation.2 | loop fusion | flops 4194304 | bytes 6307840 | tf_op jit(solution)/shard_map/add | solution.py:637
  (14 shorter events, 0.1 us)
Async XLA Ops:
  9.1 17.7 %copy-start = (f32[1024,256]{1,0:T(8,128)S(1)}, f32[1024,256]{1,0:T(8,128)}, u32[]{:S(2)}) copy-start(f32[1024,256]{1,0:T(8,128)} %start.3) | copy-start | bytes 3145732
  9.2 13.0 %collective-permute-start = (f16[520,256]{1,0:T(8,128)(2,1)S(1)}, f16[520,256]{1,0:T(8,128)(2,1)S(1)}, u32[]{:S(2)}, u32[]{:S(2)}) collective-permute-start(f16[520,256]{1,0:T(8,128)(2,1)S(1)} %get-tuple-element.34), channel_id=1, source_target_pairs={{0,1},{1,2},{2,3},{3,0},{4,5},{5,6},{6,7},{7,4},{8,9},{9,10},{10,1... | collective-permute-start | bytes 798728 | tf_op jit(solution)/shard_map/ppermute | solution.py:559
  10.9 13.9 %collective-permute-start.1 = (f16[520,256]{1,0:T(8,128)(2,1)S(1)}, f16[520,256]{1,0:T(8,128)(2,1)S(1)}, u32[]{:S(2)}, u32[]{:S(2)}) collective-permute-start(f16[520,256]{1,0:T(8,128)(2,1)S(1)} %get-tuple-element.36), channel_id=1, source_target_pairs={{0,2},{1,3},{2,0},{3,1},{4,6},{5,7},{6,4},{7,5},{8,10},{9,11},{10,... | collective-permute-start | bytes 798728 | tf_op jit(solution)/shard_map/ppermute | solution.py:559
  13.6 11.2 %collective-permute-start.2 = (f16[520,256]{1,0:T(8,128)(2,1)S(1)}, f16[520,256]{1,0:T(8,128)(2,1)S(1)}, u32[]{:S(2)}, u32[]{:S(2)}) collective-permute-start(f16[520,256]{1,0:T(8,128)(2,1)S(1)} %get-tuple-element.35), channel_id=1, source_target_pairs={{0,3},{1,0},{2,1},{3,2},{4,7},{5,4},{6,5},{7,6},{8,11},{9,8},{10,9... | collective-permute-start | bytes 798728 | tf_op jit(solution)/shard_map/ppermute | solution.py:559
  15.0 2.7 %collective-permute-start.3 = (f32[8,256]{1,0:T(8,128)S(1)}, f32[8,256]{1,0:T(8,128)S(1)}, u32[]{:S(2)}, u32[]{:S(2)}) collective-permute-start(f32[8,256]{1,0:T(8,128)S(1)} %get-tuple-element.18), channel_id=1, source_target_pairs={{0,4},{4,8},{8,12},{12,16},{16,20},{20,24},{24,28},{28,32},{32,36}... | collective-permute-start | bytes 24584 | tf_op jit(solution)/shard_map/ppermute | solution.py:560
  16.3 4.4 %collective-permute-start.4 = (f32[8,256]{1,0:T(8,128)S(1)}, f32[8,256]{1,0:T(8,128)S(1)}, u32[]{:S(2)}, u32[]{:S(2)}) collective-permute-start(f32[8,256]{1,0:T(8,128)S(1)} %get-tuple-element.19), channel_id=1, source_target_pairs={{4,0},{8,4},{12,8},{16,12},{20,16},{24,20},{28,24},{32,28},{36,32}... | collective-permute-start | bytes 24584 | tf_op jit(solution)/shard_map/ppermute | solution.py:561
  20.7 4.9 %collective-permute-start.5 = (f32[16,256]{1,0:T(8,128)S(1)}, f32[16,256]{1,0:T(8,128)S(1)}, u32[]{:S(2)}, u32[]{:S(2)}) collective-permute-start(f32[16,256]{1,0:T(8,128)S(1)} %constant_dynamic-update-slice_fusion.near0), channel_id=1, source_target_pairs={{0,1},{1,2},{2,3},{3,0},{4,5},{5,6},{6,7},{7,4},{8,9},{9,10},{10,1... | collective-permute-start | bytes 49160 | tf_op jit(solution)/shard_map/ppermute | solution.py:564
  21.3 5.2 %collective-permute-start.6 = (f32[16,256]{1,0:T(8,128)S(1)}, f32[16,256]{1,0:T(8,128)S(1)}, u32[]{:S(2)}, u32[]{:S(2)}) collective-permute-start(f32[16,256]{1,0:T(8,128)S(1)} %constant_dynamic-update-slice_fusion.near0), channel_id=1, source_target_pairs={{0,2},{1,3},{2,0},{3,1},{4,6},{5,7},{6,4},{7,5},{8,10},{9,11},{10,... | collective-permute-start | bytes 49160 | tf_op jit(solution)/shard_map/ppermute | solution.py:564
  22.2 4.5 %collective-permute-start.7 = (f32[16,256]{1,0:T(8,128)S(1)}, f32[16,256]{1,0:T(8,128)S(1)}, u32[]{:S(2)}, u32[]{:S(2)}) collective-permute-start(f32[16,256]{1,0:T(8,128)S(1)} %constant_dynamic-update-slice_fusion.near0), channel_id=1, source_target_pairs={{0,3},{1,0},{2,1},{3,2},{4,7},{5,4},{6,5},{7,6},{8,11},{9,8},{10,9... | collective-permute-start | bytes 49160 | tf_op jit(solution)/shard_map/ppermute | solution.py:564
  24.8 9.0 %copy-start.2 = (s32[1,1,64]{2,1,0:T(1,128)S(1)}, s32[1,1,64]{2,1,0:T(1,128)}, u32[]{:S(2)}) copy-start(s32[1,1,64]{2,1,0:T(1,128)} %rows_hbm.1) | copy-start | bytes 772
  24.8 9.0 %copy-start.3 = (s32[1,1,64]{2,1,0:T(1,128)S(1)}, s32[1,1,64]{2,1,0:T(1,128)}, u32[]{:S(2)}) copy-start(s32[1,1,64]{2,1,0:T(1,128)} %cols_hbm.1) | copy-start | bytes 772
  29.1 16.0 %collective-permute-start.8 = (f16[2,256,256]{2,1,0:T(8,128)(2,1)S(1)}, f16[2,256,256]{2,1,0:T(8,128)(2,1)}, u32[]{:S(2)}, u32[]{:S(2)}) collective-permute-start(f16[2,256,256]{2,1,0:T(8,128)(2,1)S(1)} %convert_element_type.52), channel_id=1, source_target_pairs={{0,1},{1,2},{2,3},{3,0},{4,5},{5,6},{6,7},{7,4},{8,9},{9,10},{10,1... | collective-permute-start | bytes 786440 | tf_op jit(solution)/shard_map/ppermute | solution.py:579
  31.0 14.7 %collective-permute-start.9 = (f16[2,256,256]{2,1,0:T(8,128)(2,1)S(1)}, f16[2,256,256]{2,1,0:T(8,128)(2,1)}, u32[]{:S(2)}, u32[]{:S(2)}) collective-permute-start(f16[2,256,256]{2,1,0:T(8,128)(2,1)S(1)} %convert_element_type.52), channel_id=1, source_target_pairs={{0,2},{1,3},{2,0},{3,1},{4,6},{5,7},{6,4},{7,5},{8,10},{9,11},{10,... | collective-permute-start | bytes 786440 | tf_op jit(solution)/shard_map/ppermute | solution.py:579
  33.1 13.0 %collective-permute-start.10 = (f16[2,256,256]{2,1,0:T(8,128)(2,1)S(1)}, f16[2,256,256]{2,1,0:T(8,128)(2,1)}, u32[]{:S(2)}, u32[]{:S(2)}) collective-permute-start(f16[2,256,256]{2,1,0:T(8,128)(2,1)S(1)} %convert_element_type.52), channel_id=1, source_target_pairs={{0,3},{1,0},{2,1},{3,2},{4,7},{5,4},{6,5},{7,6},{8,11},{9,8},{10,9... | collective-permute-start | bytes 786440 | tf_op jit(solution)/shard_map/ppermute | solution.py:579
  33.9 22.5 %all-to-all-start = ((f32[640,1,128]{2,1,0:T(1,128)}), f32[640,1,128]{2,1,0:T(1,128)S(1)}, u32[]{:S(2)}, u32[]{:S(2)}) async-start(f32[640,1,128]{2,1,0:T(1,128)} %bitcast.12), calls=%async_computation | async-start | bytes 655360 | tf_op jit(solution)/shard_map/all_to_all | solution.py:581
  61.1 3.8 %collective-permute-start.11 = (f16[16,264,128]{2,1,0:T(8,128)(2,1)S(1)}, f16[16,264,128]{2,1,0:T(8,128)(2,1)S(1)}, u32[]{:S(2)}, u32[]{:S(2)}) collective-permute-start(f16[16,264,128]{2,1,0:T(8,128)(2,1)S(1)} %convert_element_type.54), channel_id=1, source_target_pairs={{0,4},{4,0},{1,5},{5,1},{2,6},{6,2},{3,7},{7,3},{8,12},{12,8},{9,1... | collective-permute-start | bytes 3244040 | tf_op jit(solution)/shard_map/ppermute | solution.py:600
  65.1 20.7 %copy-start.1 = (f32[2048,256]{1,0:T(8,128)S(1)}, f32[2048,256]{1,0:T(8,128)}, u32[]{:S(2)}) copy-start(f32[2048,256]{1,0:T(8,128)} %factors_hbm.1) | copy-start | bytes 6291460
  85.7 1.4 %collective-permute-start.12 = (f32[264,128]{1,0:T(8,128)S(1)}, f32[264,128]{1,0:T(8,128)S(1)}, u32[]{:S(2)}, u32[]{:S(2)}) collective-permute-start(f32[264,128]{1,0:T(8,128)S(1)} %convert_reduce_fusion.mine), channel_id=1, source_target_pairs={{0,4},{4,0},{1,5},{5,1},{2,6},{6,2},{3,7},{7,3},{8,12},{12,8},{9,1... | collective-permute-start | bytes 405512 | tf_op jit(solution)/shard_map/ppermute | solution.py:616
  109.7 8.2 %collective-permute-start.16 = (f16[16,264,128]{2,1,0:T(8,128)(2,1)S(1)}, f16[16,264,128]{2,1,0:T(8,128)(2,1)S(1)}, u32[]{:S(2)}, u32[]{:S(2)}) collective-permute-start(f16[16,264,128]{2,1,0:T(8,128)(2,1)S(1)} %all_to_all.16), channel_id=1, source_target_pairs={{0,4},{4,0},{1,5},{5,1},{2,6},{6,2},{3,7},{7,3},{8,12},{12,8},{9,1... | collective-permute-start | bytes 3244040 | tf_op jit(solution)/shard_map/ppermute | solution.py:623
  110.0 4.8 %collective-permute-start.13 = (f32[8,128]{1,0:T(8,128)S(1)}, f32[8,128]{1,0:T(8,128)S(1)}, u32[]{:S(2)}, u32[]{:S(2)}) collective-permute-start(f32[8,128]{1,0:T(8,128)S(1)} %shard_map.83.own), channel_id=1, source_target_pairs={{0,1},{1,2},{2,3},{3,0},{4,5},{5,6},{6,7},{7,4},{8,9},{9,10},{10,1... | collective-permute-start | bytes 12296 | tf_op jit(solution)/shard_map/ppermute | solution.py:626
  110.6 5.1 %collective-permute-start.14 = (f32[8,128]{1,0:T(8,128)S(1)}, f32[8,128]{1,0:T(8,128)S(1)}, u32[]{:S(2)}, u32[]{:S(2)}) collective-permute-start(f32[8,128]{1,0:T(8,128)S(1)} %shard_map.83.own), channel_id=1, source_target_pairs={{0,2},{1,3},{2,0},{3,1},{4,6},{5,7},{6,4},{7,5},{8,10},{9,11},{10,... | collective-permute-start | bytes 12296 | tf_op jit(solution)/shard_map/ppermute | solution.py:626
  113.3 3.6 %collective-permute-start.15 = (f32[8,128]{1,0:T(8,128)S(1)}, f32[8,128]{1,0:T(8,128)S(1)}, u32[]{:S(2)}, u32[]{:S(2)}) collective-permute-start(f32[8,128]{1,0:T(8,128)S(1)} %shard_map.83.own), channel_id=1, source_target_pairs={{0,3},{1,0},{2,1},{3,2},{4,7},{5,4},{6,5},{7,6},{8,11},{9,8},{10,9... | collective-permute-start | bytes 12296 | tf_op jit(solution)/shard_map/ppermute | solution.py:626
